TPU v7x, 256 devices: a whole 4x4x8 slice. The times are simulated.
256 devices in a mesh: row: 8 (over x_lo, y), col: 32 (over z, x_hi, core).
Axes of the slice: x: 4 (x_hi: 2, x_lo: 2; x = x_hi * 2 + x_lo), y: 4, z: 8, core: 2. Of those that a mesh axis runs over, the one named last changes fastest.
Arguments:
- corners: bfloat16 [8, 32, 128, 128], P('row', 'col'), may hold values from -6 to 6
- edges: bfloat16 [8, 32, 128, 4608], P('row', 'col'), may hold values from -0.5 to 0.5
- projectors: bfloat16 [32, 4608, 128], P('col'), may hold values from -0.09375 to 0.09375
- cotangent: bfloat16 [8, 32, 128, 128], P('row', 'col'), may hold values from -6 to 6
Outputs:
- corner_grad: bfloat16 [8, 32, 128, 128], P('row', 'col')
- edge_grad: bfloat16 [8, 32, 128, 4608], P('row', 'col')
- projector_grad: float32 [32, 4608, 128], P('col', 'row')
All inputs are finite; a program needn't handle non-finite values.
Results may differ from a plain program's by a relative error of at most 0.028.
Values may be sent and summed in bfloat16 or wider, within the bound.
No kernel may reach another device: no remote copies, remote signals or barrier semaphores. Data moves between devices by JAX's collectives and lax.ppermute only.
A program may use at most 128 MiB of HBM per device.

v0:
```python
import jax
import jax.numpy as jnp
from jax import lax
from jax.sharding import PartitionSpec as P

MOVES = 6


def shifted(value, axis, by):
    devices = lax.axis_size(axis)
    return lax.ppermute(value, axis, [(i, (i + by) % devices) for i in range(devices)])


def shards(corners, edges, projectors, cotangent):
    corner_first = corners[0, 0]
    site_edge = edges[0, 0]
    projector = projectors[0]
    chi_width = corner_first.shape[0]
    edge_width = site_edge.shape[1]
    row_parts = lax.axis_size("row")
    share_rows = edge_width // row_parts
    states = []
    merges = []
    corner_now = corner_first
    for move_index in range(MOVES):
        product = jnp.dot(corner_now, site_edge, preferred_element_type=jnp.float32)
        merged = product.astype(jnp.bfloat16).reshape(edge_width, chi_width)
        states.append(corner_now)
        merges.append(merged)
        if move_index + 1 < MOVES:
            absorbed = lax.dot_general(
                projector, merged, (((0,), (0,)), ((), ())), preferred_element_type=jnp.float32
            ).astype(jnp.bfloat16)
            corner_now = shifted(absorbed, "col", 1)
    adjoint = cotangent[0, 0]
    edge_total = jnp.zeros((chi_width, edge_width), jnp.float32)
    arrivals = [None] * MOVES
    for move_index in reversed(range(MOVES)):
        arrived = shifted(adjoint, "col", -1)
        arrivals[move_index] = arrived
        merged_bar = jnp.dot(projector, arrived, preferred_element_type=jnp.float32).astype(
            jnp.bfloat16
        )
        flat_bar = merged_bar.reshape(chi_width, edge_width)
        edge_total = edge_total + lax.dot_general(
            states[move_index],
            flat_bar,
            (((0,), (0,)), ((), ())),
            preferred_element_type=jnp.float32,
        )
        adjoint = lax.dot_general(
            flat_bar, site_edge, (((1,), (1,)), ((), ())), preferred_element_type=jnp.float32
        ).astype(jnp.bfloat16)
    summed = jnp.zeros((share_rows * lax.axis_size("row"), chi_width), jnp.float32)
    for move_index in range(MOVES):
        block_rows = merges[move_index]
        summed = summed + lax.dot_general(
            block_rows,
            arrivals[move_index],
            (((1,), (1,)), ((), ())),
            preferred_element_type=jnp.float32,
        )
    proj_share = lax.psum_scatter(
        summed.astype(jnp.bfloat16), "row", scatter_dimension=0, tiled=True
    ).astype(jnp.float32)
    corner_grad = adjoint.reshape(1, 1, chi_width, chi_width)
    edge_grad = edge_total.astype(jnp.bfloat16).reshape(1, 1, chi_width, edge_width)
    return (corner_grad, edge_grad, proj_share.reshape(1, share_rows, chi_width))


def solution(mesh):
    placed = (
        P("row", "col", None, None),
        P("row", "col", None, None),
        P("col", None, None),
        P("row", "col", None, None),
    )
    return jax.shard_map(
        shards,
        mesh=mesh,
        in_specs=placed,
        out_specs=(P("row", "col", None, None), P("row", "col", None, None), P("col", "row", None)),
        check_vma=False,
    )
```

profile of v0, /device:TPU:4, one launch (start us, length us, event | category | flops | bytes accessed | tf_op | source)
XLA Modules:
  0.0 196.1 jit_solution(4448858349681403788)
XLA Ops:
  10.7 2.6 %reshape.61 = bf16[4608,128]{1,0:T(8,128)(2,1)S(1)} reshape(bf16[128,4608]{1,0:T(8,128)(2,1)} %convolution_convert_fusion.5) | data formatting | bytes 2359296 | tf_op jit(solution)/shard_map/reshape | solution.py:27
  16.7 2.4 %reshape.54 = bf16[128,4608]{1,0:T(8,128)(2,1)S(1)} reshape(bf16[4608,128]{1,0:T(8,128)(2,1)} %convolution_convert_fusion.11) | data formatting | bytes 2359296 | tf_op jit(solution)/shard_map/reshape | solution.py:44
  20.2 3.2 %collective-permute-start.1 = (bf16[128,128]{1,0:T(8,128)(2,1)}, bf16[128,128]{1,0:T(8,128)(2,1)}, u32[]{:S(2)}, u32[]{:S(2)}) collective-permute-start(bf16[128,128]{1,0:T(8,128)(2,1)} %fusion.65), channel_id=1, source_target_pairs={{0,31},{1,0},{2,1},{3,2},{4,3},{5,4},{6,5},{7,6},{8,7},{9,8},{10,9... | collective-permute-start | bytes 98312 | tf_op jit(solution)/shard_map/ppermute | solution.py:11
  25.7 3.3 %reshape.62 = bf16[4608,128]{1,0:T(8,128)(2,1)} reshape(bf16[128,4608]{1,0:T(8,128)(2,1)} %convolution_convert_fusion.4) | data formatting | bytes 2359296 | tf_op jit(solution)/shard_map/reshape | solution.py:27
  29.1 2.4 %fusion.95 = bf16[128,128]{0,1:T(8,128)(2,1)} fusion(bf16[4608,128]{1,0:T(8,128)(2,1)} %reshape.62, bf16[1,4608,128]{2,1,0:T(8,128)(2,1)S(1)} %copy-done.1), kind=kOutput, calls=%fused_computation.80 | convolution fusion | flops 151011328 | bytes 2392064 | tf_op jit(solution)/shard_map/dot_general | solution.py:31
  31.5 2.3 %fusion.10 = bf16[4608,128]{0,1:T(8,128)(2,1)} fusion(bf16[128,128]{1,0:T(8,128)(2,1)} %collective-permute-done.1, bf16[1,4608,128]{2,1,0:T(8,128)(2,1)S(1)} %copy-done.1), kind=kOutput, calls=%fused_computation.25 | convolution fusion | flops 151584768 | bytes 2392064 | tf_op jit(solution)/shard_map/dot_general | solution.py:41
  33.7 2.4 %copy.8 = bf16[4608,128]{1,0:T(8,128)(2,1)} copy(bf16[4608,128]{0,1:T(8,128)(2,1)} %fusion.10) | data formatting | bytes 2359296 | tf_op jit(solution)/shard_map/convert_element_type | solution.py:41
  36.1 3.2 %reshape.55 = bf16[128,4608]{1,0:T(8,128)(2,1)} reshape(bf16[4608,128]{1,0:T(8,128)(2,1)} %copy.8) | data formatting | bytes 2359296 | tf_op jit(solution)/shard_map/reshape | solution.py:44
  39.3 2.4 %fusion.68 = bf16[128,128]{1,0:T(8,128)(2,1)} fusion(bf16[128,4608]{1,0:T(8,128)(2,1)} %reshape.55, bf16[1,1,128,4608]{3,2,1,0:T(8,128)(2,1)S(1)} %copy-done), kind=kOutput, calls=%fused_computation.71 | convolution fusion | flops 151011328 | bytes 2392064 | tf_op jit(solution)/shard_map/dot_general | solution.py:51
  41.7 4.0 %collective-permute-start.2 = (bf16[128,128]{1,0:T(8,128)(2,1)}, bf16[128,128]{1,0:T(8,128)(2,1)}, u32[]{:S(2)}, u32[]{:S(2)}) collective-permute-start(bf16[128,128]{1,0:T(8,128)(2,1)} %fusion.68), channel_id=1, source_target_pairs={{0,31},{1,0},{2,1},{3,2},{4,3},{5,4},{6,5},{7,6},{8,7},{9,8},{10,9... | collective-permute-start | bytes 98312 | tf_op jit(solution)/shard_map/ppermute | solution.py:11
  45.7 2.3 %convolution_convert_fusion.3 = bf16[128,4608]{1,0:T(8,128)(2,1)} fusion(bf16[128,128]{0,1:T(8,128)(2,1)} %collective-permute-done.7, bf16[1,1,128,4608]{3,2,1,0:T(8,128)(2,1)S(1)} %copy-done), kind=kOutput, calls=%fused_computation.16 | convolution fusion | flops 151584768 | bytes 2392064 | tf_op jit(solution)/shard_map/dot_general | solution.py:26
  48.0 3.3 %reshape.63 = bf16[4608,128]{1,0:T(8,128)(2,1)} reshape(bf16[128,4608]{1,0:T(8,128)(2,1)} %convolution_convert_fusion.3) | data formatting | bytes 2359296 | tf_op jit(solution)/shard_map/reshape | solution.py:27
  51.3 2.4 %fusion.92 = bf16[128,128]{0,1:T(8,128)(2,1)} fusion(bf16[4608,128]{1,0:T(8,128)(2,1)} %reshape.63, bf16[1,4608,128]{2,1,0:T(8,128)(2,1)S(1)} %copy-done.1), kind=kOutput, calls=%fused_computation.79 | convolution fusion | flops 151011328 | bytes 2392064 | tf_op jit(solution)/shard_map/dot_general | solution.py:31
  53.7 2.3 %fusion.11 = bf16[4608,128]{0,1:T(8,128)(2,1)} fusion(bf16[128,128]{1,0:T(8,128)(2,1)} %collective-permute-done.2, bf16[1,4608,128]{2,1,0:T(8,128)(2,1)S(1)} %copy-done.1), kind=kOutput, calls=%fused_computation.26 | convolution fusion | flops 151584768 | bytes 2392064 | tf_op jit(solution)/shard_map/dot_general | solution.py:41
  56.0 2.4 %copy.9 = bf16[4608,128]{1,0:T(8,128)(2,1)} copy(bf16[4608,128]{0,1:T(8,128)(2,1)} %fusion.11) | data formatting | bytes 2359296 | tf_op jit(solution)/shard_map/convert_element_type | solution.py:41
  58.4 3.2 %reshape.56 = bf16[128,4608]{1,0:T(8,128)(2,1)} reshape(bf16[4608,128]{1,0:T(8,128)(2,1)} %copy.9) | data formatting | bytes 2359296 | tf_op jit(solution)/shard_map/reshape | solution.py:44
  61.6 2.3 %fusion.71 = bf16[128,128]{1,0:T(8,128)(2,1)} fusion(bf16[128,4608]{1,0:T(8,128)(2,1)} %reshape.56, bf16[1,1,128,4608]{3,2,1,0:T(8,128)(2,1)S(1)} %copy-done), kind=kOutput, calls=%fused_computation.72 | convolution fusion | flops 151011328 | bytes 2392064 | tf_op jit(solution)/shard_map/dot_general | solution.py:51
  64.0 5.3 %collective-permute-start.3 = (bf16[128,128]{1,0:T(8,128)(2,1)}, bf16[128,128]{1,0:T(8,128)(2,1)}, u32[]{:S(2)}, u32[]{:S(2)}) collective-permute-start(bf16[128,128]{1,0:T(8,128)(2,1)} %fusion.71), channel_id=1, source_target_pairs={{0,31},{1,0},{2,1},{3,2},{4,3},{5,4},{6,5},{7,6},{8,7},{9,8},{10,9... | collective-permute-start | bytes 98312 | tf_op jit(solution)/shard_map/ppermute | solution.py:11
  69.3 2.3 %convolution_convert_fusion.2 = bf16[128,4608]{1,0:T(8,128)(2,1)} fusion(bf16[128,128]{0,1:T(8,128)(2,1)} %collective-permute-done.8, bf16[1,1,128,4608]{3,2,1,0:T(8,128)(2,1)S(1)} %copy-done), kind=kOutput, calls=%fused_computation.15 | convolution fusion | flops 151584768 | bytes 2392064 | tf_op jit(solution)/shard_map/dot_general | solution.py:26
  71.6 3.3 %reshape.64 = bf16[4608,128]{1,0:T(8,128)(2,1)} reshape(bf16[128,4608]{1,0:T(8,128)(2,1)} %convolution_convert_fusion.2) | data formatting | bytes 2359296 | tf_op jit(solution)/shard_map/reshape | solution.py:27
  74.9 2.5 %fusion.89 = bf16[128,128]{0,1:T(8,128)(2,1)} fusion(bf16[4608,128]{1,0:T(8,128)(2,1)} %reshape.64, bf16[1,4608,128]{2,1,0:T(8,128)(2,1)S(1)} %copy-done.1), kind=kOutput, calls=%fused_computation.78 | convolution fusion | flops 151011328 | bytes 2392064 | tf_op jit(solution)/shard_map/dot_general | solution.py:31
  77.4 2.8 %fusion.104 = f32[128,4608]{1,0:T(8,128)} fusion(bf16[128,128]{0,1:T(8,128)(2,1)} %collective-permute-done.8, bf16[128,4608]{1,0:T(8,128)(2,1)S(1)} %copy-done.7), kind=kOutput, calls=%fused_computation.86 | convolution fusion | flops 150994944 | bytes 3571712 | tf_op jit(solution)/shard_map/dot_general | solution.py:45
  80.2 2.7 %fusion.109 = f32[4608,128]{1,0:T(8,128)} fusion(bf16[4608,128]{1,0:T(8,128)(2,1)S(1)} %copy-done.8, bf16[128,128]{1,0:T(8,128)(2,1)} %collective-permute-done.2), kind=kOutput, calls=%fused_computation.91 | convolution fusion | flops 150994944 | bytes 3571712 | tf_op jit(solution)/shard_map/dot_general | solution.py:57
  82.8 2.3 %fusion.12 = bf16[4608,128]{0,1:T(8,128)(2,1)} fusion(bf16[128,128]{1,0:T(8,128)(2,1)} %collective-permute-done.3, bf16[1,4608,128]{2,1,0:T(8,128)(2,1)S(1)} %copy-done.1), kind=kOutput, calls=%fused_computation.27 | convolution fusion | flops 151584768 | bytes 2392064 | tf_op jit(solution)/shard_map/dot_general | solution.py:41
  85.2 2.4 %copy.10 = bf16[4608,128]{1,0:T(8,128)(2,1)} copy(bf16[4608,128]{0,1:T(8,128)(2,1)} %fusion.12) | data formatting | bytes 2359296 | tf_op jit(solution)/shard_map/convert_element_type | solution.py:41
  87.6 3.2 %reshape.57 = bf16[128,4608]{1,0:T(8,128)(2,1)} reshape(bf16[4608,128]{1,0:T(8,128)(2,1)} %copy.10) | data formatting | bytes 2359296 | tf_op jit(solution)/shard_map/reshape | solution.py:44
  90.8 2.4 %fusion.74 = bf16[128,128]{1,0:T(8,128)(2,1)} fusion(bf16[128,4608]{1,0:T(8,128)(2,1)} %reshape.57, bf16[1,1,128,4608]{3,2,1,0:T(8,128)(2,1)S(1)} %copy-done), kind=kOutput, calls=%fused_computation.73 | convolution fusion | flops 151011328 | bytes 2392064 | tf_op jit(solution)/shard_map/dot_general | solution.py:51
  93.2 5.4 %collective-permute-start.4 = (bf16[128,128]{1,0:T(8,128)(2,1)}, bf16[128,128]{1,0:T(8,128)(2,1)}, u32[]{:S(2)}, u32[]{:S(2)}) collective-permute-start(bf16[128,128]{1,0:T(8,128)(2,1)} %fusion.74), channel_id=1, source_target_pairs={{0,31},{1,0},{2,1},{3,2},{4,3},{5,4},{6,5},{7,6},{8,7},{9,8},{10,9... | collective-permute-start | bytes 98312 | tf_op jit(solution)/shard_map/ppermute | solution.py:11
  98.5 2.3 %convolution_convert_fusion.1 = bf16[128,4608]{1,0:T(8,128)(2,1)} fusion(bf16[128,128]{0,1:T(8,128)(2,1)} %collective-permute-done.9, bf16[1,1,128,4608]{3,2,1,0:T(8,128)(2,1)S(1)} %copy-done), kind=kOutput, calls=%fused_computation.14 | convolution fusion | flops 151584768 | bytes 2392064 | tf_op jit(solution)/shard_map/dot_general | solution.py:26
  100.9 3.3 %reshape.65 = bf16[4608,128]{1,0:T(8,128)(2,1)} reshape(bf16[128,4608]{1,0:T(8,128)(2,1)} %convolution_convert_fusion.1) | data formatting | bytes 2359296 | tf_op jit(solution)/shard_map/reshape | solution.py:27
  104.2 2.5 %fusion.86 = bf16[128,128]{0,1:T(8,128)(2,1)} fusion(bf16[4608,128]{1,0:T(8,128)(2,1)} %reshape.65, bf16[1,4608,128]{2,1,0:T(8,128)(2,1)S(1)} %copy-done.1), kind=kOutput, calls=%fused_computation.77 | convolution fusion | flops 151011328 | bytes 2392064 | tf_op jit(solution)/shard_map/dot_general | solution.py:31
  106.7 2.8 %fusion.110 = f32[4608,128]{1,0:T(8,128)} fusion(bf16[4608,128]{1,0:T(8,128)(2,1)S(1)} %copy-done.9, bf16[128,128]{1,0:T(8,128)(2,1)} %collective-permute-done.1), kind=kOutput, calls=%fused_computation.92 | convolution fusion | flops 150994944 | bytes 3571712 | tf_op jit(solution)/shard_map/dot_general | solution.py:57
  109.5 2.7 %fusion.108 = f32[4608,128]{1,0:T(8,128)} fusion(bf16[4608,128]{1,0:T(8,128)(2,1)S(1)} %copy-done.5, bf16[128,128]{1,0:T(8,128)(2,1)} %collective-permute-done.3), kind=kOutput, calls=%fused_computation.90 | convolution fusion | flops 150994944 | bytes 3571712 | tf_op jit(solution)/shard_map/dot_general | solution.py:57
  112.2 2.3 %fusion.13 = bf16[4608,128]{0,1:T(8,128)(2,1)} fusion(bf16[128,128]{1,0:T(8,128)(2,1)} %collective-permute-done.4, bf16[1,4608,128]{2,1,0:T(8,128)(2,1)S(1)} %copy-done.1), kind=kOutput, calls=%fused_computation.28 | convolution fusion | flops 151584768 | bytes 2392064 | tf_op jit(solution)/shard_map/dot_general | solution.py:41
  114.4 2.4 %copy.11 = bf16[4608,128]{1,0:T(8,128)(2,1)} copy(bf16[4608,128]{0,1:T(8,128)(2,1)} %fusion.13) | data formatting | bytes 2359296 | tf_op jit(solution)/shard_map/convert_element_type | solution.py:41
  116.8 3.2 %reshape.58 = bf16[128,4608]{1,0:T(8,128)(2,1)} reshape(bf16[4608,128]{1,0:T(8,128)(2,1)} %copy.11) | data formatting | bytes 2359296 | tf_op jit(solution)/shard_map/reshape | solution.py:44
  120.1 2.4 %fusion.77 = bf16[128,128]{1,0:T(8,128)(2,1)} fusion(bf16[128,4608]{1,0:T(8,128)(2,1)} %reshape.58, bf16[1,1,128,4608]{3,2,1,0:T(8,128)(2,1)S(1)} %copy-done), kind=kOutput, calls=%fused_computation.74 | convolution fusion | flops 151011328 | bytes 2392064 | tf_op jit(solution)/shard_map/dot_general | solution.py:51
  122.4 5.4 %collective-permute-start.5 = (bf16[128,128]{1,0:T(8,128)(2,1)}, bf16[128,128]{1,0:T(8,128)(2,1)}, u32[]{:S(2)}, u32[]{:S(2)}) collective-permute-start(bf16[128,128]{1,0:T(8,128)(2,1)} %fusion.77), channel_id=1, source_target_pairs={{0,31},{1,0},{2,1},{3,2},{4,3},{5,4},{6,5},{7,6},{8,7},{9,8},{10,9... | collective-permute-start | bytes 98312 | tf_op jit(solution)/shard_map/ppermute | solution.py:11
  130.1 3.4 %reshape.67 = bf16[4608,128]{1,0:T(8,128)(2,1)} reshape(bf16[128,4608]{1,0:T(8,128)(2,1)} %convolution_convert_fusion) | data formatting | bytes 2359296 | tf_op jit(solution)/shard_map/reshape | solution.py:27
  137.5 3.5 %fusion.8 = bf16[4608,128]{1,0:T(8,128)(2,1)} fusion(f32[4608,128]{1,0:T(8,128)S(1)} %fusion.111, f32[4608,128]{1,0:T(8,128)S(1)} %copy-done.12, f32[4608,128]{1,0:T(8,128)S(1)} %copy-done.11, f32[4608,128]{1,0:T(8,128)} %fusion.108, f32[4608,128]{1,0:T(8,128)S(1)} %fusion.107, bf16[4608,128]{1,0:T(8,128)(2,1)S(1)} %copy-done.3, ...), kind=kOutput, calls=%fused_computation.11 | convolution fusion | flops 154533888 | bytes 14188544 | tf_op jit(solution)/shard_map/dot_general | solution.py:57
  141.1 3.3 %fusion.105 = f32[128,4608]{1,0:T(8,128)} fusion(bf16[128,128]{0,1:T(8,128)(2,1)} %collective-permute-done.7, bf16[128,4608]{1,0:T(8,128)(2,1)} %reshape.57), kind=kOutput, calls=%fused_computation.87 | convolution fusion | flops 150994944 | bytes 3571712 | tf_op jit(solution)/shard_map/dot_general | solution.py:45
  144.3 2.7 %fusion.103 = f32[128,4608]{1,0:T(8,128)} fusion(bf16[128,128]{0,1:T(8,128)(2,1)} %collective-permute-done.9, bf16[128,4608]{1,0:T(8,128)(2,1)S(1)} %copy-done.4), kind=kOutput, calls=%fused_computation.85 | convolution fusion | flops 150994944 | bytes 3571712 | tf_op jit(solution)/shard_map/dot_general | solution.py:45
  147.1 2.7 %fusion.106 = f32[128,4608]{1,0:T(8,128)} fusion(bf16[128,128]{0,1:T(8,128)(2,1)} %collective-permute-done.6, bf16[128,4608]{1,0:T(8,128)(2,1)S(1)} %copy-done.6), kind=kOutput, calls=%fused_computation.88 | convolution fusion | flops 150994944 | bytes 3571712 | tf_op jit(solution)/shard_map/dot_general | solution.py:45
  149.8 2.3 %fusion.14 = bf16[4608,128]{0,1:T(8,128)(2,1)} fusion(bf16[128,128]{1,0:T(8,128)(2,1)} %collective-permute-done.5, bf16[1,4608,128]{2,1,0:T(8,128)(2,1)S(1)} %copy-done.1), kind=kOutput, calls=%fused_computation.29 | convolution fusion | flops 151584768 | bytes 2392064 | tf_op jit(solution)/shard_map/dot_general | solution.py:41
  152.1 2.4 %copy.12 = bf16[4608,128]{1,0:T(8,128)(2,1)} copy(bf16[4608,128]{0,1:T(8,128)(2,1)} %fusion.14) | data formatting | bytes 2359296 | tf_op jit(solution)/shard_map/convert_element_type | solution.py:41
  154.4 2.4 %reshape.59 = bf16[128,4608]{1,0:T(8,128)(2,1)S(1)} reshape(bf16[4608,128]{1,0:T(8,128)(2,1)} %copy.12) | data formatting | bytes 2359296 | tf_op jit(solution)/shard_map/reshape | solution.py:44
  159.8 4.2 %fusion.15 = bf16[1,1,128,4608]{3,2,1,0:T(8,128)(2,1)} fusion(f32[128,4608]{1,0:T(8,128)S(1)} %convolution_bitcast_fusion, f32[128,4608]{1,0:T(8,128)} %fusion.106, f32[128,4608]{1,0:T(8,128)S(1)} %copy-done.13, f32[128,4608]{1,0:T(8,128)S(1)} %copy-done.10, f32[128,4608]{1,0:T(8,128)} %fusion.103, bf16[128,128]{0,1:T(8,128)(2,1)} %collective-permute-done.10, ...), kind=kOutput, calls=%fused_computation.30 | convolution fusion | flops 154533888 | bytes 14188544 | tf_op jit(solution)/shard_map/dot_general | solution.py:45
  164.0 23.6 %reduce-scatter.2.cloned.1.call-done = bf16[576,128]{1,0:T(8,128)(2,1)} async-done(((bf16[4608,128]{1,0:T(8,128)(2,1)}), bf16[576,128]{1,0:T(8,128)(2,1)}) %reduce-scatter.2.cloned.1.call-update) | async-done | bytes 147472 | tf_op jit(solution)/shard_map/reduce_scatter | solution.py:63
  (62 shorter events, 21.1 us)
Async XLA Ops:
  7.2 1.3 copy-start
  7.2 180.5 %reduce-scatter.2.cloned.1.call-start = ((), (), s32[]{:S(2)}) async-start(), calls=%async_computation.1 | async-start | bytes 1327104 | tf_op jit(solution)/shard_map/reduce_scatter | solution.py:63
  7.2 7.2 %collective-permute-start = (bf16[128,128]{1,0:T(8,128)(2,1)}, bf16[128,128]{1,0:T(8,128)(2,1)}, u32[]{:S(2)}, u32[]{:S(2)}) collective-permute-start(bf16[128,128]{1,0:T(8,128)(2,1)} %bitcast.162), channel_id=1, source_target_pairs={{0,31},{1,0},{2,1},{3,2},{4,3},{5,4},{6,5},{7,6},{8,7},{9,8},{10,9... | collective-permute-start | bytes 98312 | tf_op jit(solution)/shard_map/ppermute | solution.py:11
  10.7 2.6 %copy-start.1 = (bf16[1,4608,128]{2,1,0:T(8,128)(2,1)S(1)}, bf16[1,4608,128]{2,1,0:T(8,128)(2,1)}, u32[]{:S(2)}) copy-start(bf16[1,4608,128]{2,1,0:T(8,128)(2,1)} %param.6) | copy-start | bytes 3538948
  13.3 1.1 copy-start.2
  14.5 9.0 %collective-permute-start.6 = (bf16[128,128]{0,1:T(8,128)(2,1)}, bf16[128,128]{0,1:T(8,128)(2,1)}, u32[]{:S(2)}, u32[]{:S(2)}) collective-permute-start(bf16[128,128]{0,1:T(8,128)(2,1)} %fusion.98), channel_id=1, source_target_pairs={{0,1},{1,2},{2,3},{3,4},{4,5},{5,6},{6,7},{7,8},{8,9},{9,10},{10,1... | collective-permute-start | bytes 98312 | tf_op jit(solution)/shard_map/ppermute | solution.py:11
  20.2 11.3 %collective-permute-start.1 = (bf16[128,128]{1,0:T(8,128)(2,1)}, bf16[128,128]{1,0:T(8,128)(2,1)}, u32[]{:S(2)}, u32[]{:S(2)}) collective-permute-start(bf16[128,128]{1,0:T(8,128)(2,1)} %fusion.65), channel_id=1, source_target_pairs={{0,31},{1,0},{2,1},{3,2},{4,3},{5,4},{6,5},{7,6},{8,7},{9,8},{10,9... | collective-permute-start | bytes 98312 | tf_op jit(solution)/shard_map/ppermute | solution.py:11
  31.4 14.2 %collective-permute-start.7 = (bf16[128,128]{0,1:T(8,128)(2,1)}, bf16[128,128]{0,1:T(8,128)(2,1)}, u32[]{:S(2)}, u32[]{:S(2)}) collective-permute-start(bf16[128,128]{0,1:T(8,128)(2,1)} %fusion.95), channel_id=1, source_target_pairs={{0,1},{1,2},{2,3},{3,4},{4,5},{5,6},{6,7},{7,8},{8,9},{9,10},{10,1... | collective-permute-start | bytes 98312 | tf_op jit(solution)/shard_map/ppermute | solution.py:11
  41.7 12.0 %collective-permute-start.2 = (bf16[128,128]{1,0:T(8,128)(2,1)}, bf16[128,128]{1,0:T(8,128)(2,1)}, u32[]{:S(2)}, u32[]{:S(2)}) collective-permute-start(bf16[128,128]{1,0:T(8,128)(2,1)} %fusion.68), channel_id=1, source_target_pairs={{0,31},{1,0},{2,1},{3,2},{4,3},{5,4},{6,5},{7,6},{8,7},{9,8},{10,9... | collective-permute-start | bytes 98312 | tf_op jit(solution)/shard_map/ppermute | solution.py:11
  53.7 15.6 %collective-permute-start.8 = (bf16[128,128]{0,1:T(8,128)(2,1)}, bf16[128,128]{0,1:T(8,128)(2,1)}, u32[]{:S(2)}, u32[]{:S(2)}) collective-permute-start(bf16[128,128]{0,1:T(8,128)(2,1)} %fusion.92), channel_id=1, source_target_pairs={{0,1},{1,2},{2,3},{3,4},{4,5},{5,6},{6,7},{7,8},{8,9},{9,10},{10,1... | collective-permute-start | bytes 98312 | tf_op jit(solution)/shard_map/ppermute | solution.py:11
  64.0 18.9 %collective-permute-start.3 = (bf16[128,128]{1,0:T(8,128)(2,1)}, bf16[128,128]{1,0:T(8,128)(2,1)}, u32[]{:S(2)}, u32[]{:S(2)}) collective-permute-start(bf16[128,128]{1,0:T(8,128)(2,1)} %fusion.71), channel_id=1, source_target_pairs={{0,31},{1,0},{2,1},{3,2},{4,3},{5,4},{6,5},{7,6},{8,7},{9,8},{10,9... | collective-permute-start | bytes 98312 | tf_op jit(solution)/shard_map/ppermute | solution.py:11
  74.9 2.5 %copy-start.7 = (bf16[128,4608]{1,0:T(8,128)(2,1)S(1)}, bf16[128,4608]{1,0:T(8,128)(2,1)}, u32[]{:S(2)}) copy-start(bf16[128,4608]{1,0:T(8,128)(2,1)} %reshape.56) | copy-start | bytes 3538948
  77.4 2.8 %copy-start.8 = (bf16[4608,128]{1,0:T(8,128)(2,1)S(1)}, bf16[4608,128]{1,0:T(8,128)(2,1)}, u32[]{:S(2)}) copy-start(bf16[4608,128]{1,0:T(8,128)(2,1)} %reshape.64) | copy-start | bytes 3538948
  77.4 21.1 %collective-permute-start.9 = (bf16[128,128]{0,1:T(8,128)(2,1)}, bf16[128,128]{0,1:T(8,128)(2,1)}, u32[]{:S(2)}, u32[]{:S(2)}) collective-permute-start(bf16[128,128]{0,1:T(8,128)(2,1)} %fusion.89), channel_id=1, source_target_pairs={{0,1},{1,2},{2,3},{3,4},{4,5},{5,6},{6,7},{7,8},{8,9},{9,10},{10,1... | collective-permute-start | bytes 98312 | tf_op jit(solution)/shard_map/ppermute | solution.py:11
  93.2 19.0 %collective-permute-start.4 = (bf16[128,128]{1,0:T(8,128)(2,1)}, bf16[128,128]{1,0:T(8,128)(2,1)}, u32[]{:S(2)}, u32[]{:S(2)}) collective-permute-start(bf16[128,128]{1,0:T(8,128)(2,1)} %fusion.74), channel_id=1, source_target_pairs={{0,31},{1,0},{2,1},{3,2},{4,3},{5,4},{6,5},{7,6},{8,7},{9,8},{10,9... | collective-permute-start | bytes 98312 | tf_op jit(solution)/shard_map/ppermute | solution.py:11
  104.2 2.5 %copy-start.9 = (bf16[4608,128]{1,0:T(8,128)(2,1)S(1)}, bf16[4608,128]{1,0:T(8,128)(2,1)}, u32[]{:S(2)}) copy-start(bf16[4608,128]{1,0:T(8,128)(2,1)} %reshape.65) | copy-start | bytes 3538948
  106.7 2.8 %copy-start.5 = (bf16[4608,128]{1,0:T(8,128)(2,1)S(1)}, bf16[4608,128]{1,0:T(8,128)(2,1)}, u32[]{:S(2)}) copy-start(bf16[4608,128]{1,0:T(8,128)(2,1)} %reshape.63) | copy-start | bytes 3538948
  106.7 21.1 %collective-permute-start.10 = (bf16[128,128]{0,1:T(8,128)(2,1)}, bf16[128,128]{0,1:T(8,128)(2,1)}, u32[]{:S(2)}, u32[]{:S(2)}) collective-permute-start(bf16[128,128]{0,1:T(8,128)(2,1)} %fusion.86), channel_id=1, source_target_pairs={{0,1},{1,2},{2,3},{3,4},{4,5},{5,6},{6,7},{7,8},{8,9},{9,10},{10,1... | collective-permute-start | bytes 98312 | tf_op jit(solution)/shard_map/ppermute | solution.py:11
  122.4 14.3 %collective-permute-start.5 = (bf16[128,128]{1,0:T(8,128)(2,1)}, bf16[128,128]{1,0:T(8,128)(2,1)}, u32[]{:S(2)}, u32[]{:S(2)}) collective-permute-start(bf16[128,128]{1,0:T(8,128)(2,1)} %fusion.77), channel_id=1, source_target_pairs={{0,31},{1,0},{2,1},{3,2},{4,3},{5,4},{6,5},{7,6},{8,7},{9,8},{10,9... | collective-permute-start | bytes 98312 | tf_op jit(solution)/shard_map/ppermute | solution.py:11
  133.4 1.9 copy-start.14
  133.4 3.3 %copy-start.12 = (f32[4608,128]{1,0:T(8,128)S(1)}, f32[4608,128]{1,0:T(8,128)}, u32[]{:S(2)}) copy-start(f32[4608,128]{1,0:T(8,128)} %fusion.110) | copy-start | bytes 7077892
  135.4 1.4 copy-start.3
  135.4 2.1 %copy-start.11 = (f32[4608,128]{1,0:T(8,128)S(1)}, f32[4608,128]{1,0:T(8,128)}, u32[]{:S(2)}) copy-start(f32[4608,128]{1,0:T(8,128)} %fusion.109) | copy-start | bytes 7077892
  141.1 3.3 %copy-start.4 = (bf16[128,4608]{1,0:T(8,128)(2,1)S(1)}, bf16[128,4608]{1,0:T(8,128)(2,1)}, u32[]{:S(2)}) copy-start(bf16[128,4608]{1,0:T(8,128)(2,1)} %reshape.55) | copy-start | bytes 3538948
  144.3 2.7 %copy-start.6 = (bf16[128,4608]{1,0:T(8,128)(2,1)S(1)}, bf16[128,4608]{1,0:T(8,128)(2,1)}, u32[]{:S(2)}) copy-start(bf16[128,4608]{1,0:T(8,128)(2,1)} %reshape.58) | copy-start | bytes 3538948
  156.8 1.1 copy-start.15
  156.9 1.7 copy-start.13
  158.0 1.8 copy-start.10
Sparse Core Ops, SparseCore 0:
  141.2 46.4 reduce-scatter.1
where the time goes:
time: 198 us; the launch traced here: 196 us
  matrix products  80.9 us (41%)
  local copies, waits for them, and re-layouts  52.2 us (26%)
  waiting for transfers between devices  23.7 us (12%)
  starting transfers between devices  23.5 us (12%)
  between operations  14.2 us (7%)
    reduce_scatter x1, waiting for transfers between devices, shards(): lax.psum_scatter(summed.astype(jnp.bfloat16), 'row', scatter_dimension=0,...  23.6 us
    ppermute x11, starting transfers between devices, shifted(): lax.ppermute(value, axis, [(i, (i + by) % devices) for i in range(devices)])  23.4 us
    reshape x6, local copies, waits for them, and re-layouts, shards(): merged = product.astype(jnp.bfloat16).reshape(edge_width, chi_width)  19.4 us
    reshape x6, local copies, waits for them, and re-layouts, shards(): flat_bar = merged_bar.reshape(chi_width, edge_width)  17.7 us
    dot_general x6, matrix products, shards(): lax.dot_general(states[move_index], flat_bar, (((0,), (0,)), ((), ())), p...  16.2 us
    dot_general x6, matrix products, shards(): lax.dot_general(block_rows, arrivals[move_index], (((1,), (1,)), ((), ())...  14.9 us
    dot_general x6, matrix products, shards(): jnp.dot(projector, arrived, preferred_element_type=jnp.float32)  13.7 us
    dot_general x6, matrix products, shards(): product = jnp.dot(corner_now, site_edge, preferred_element_type=jnp.float32)  13.6 us
  transfers between devices with their start and end apart: 12, of which 1 were waited for; matrix products, arithmetic and copies ran while one was open for 64% of the time, Pallas kernels for 0%

commit v1 on v0

v1 whole, which is shorter than its diff:
```python
import jax
import jax.numpy as jnp
from jax import lax
from jax.experimental import pallas as pl
from jax.experimental.pallas import tpu as pltpu
from jax.sharding import PartitionSpec as P


W = 128
BF = jnp.bfloat16
F32 = jnp.float32


def dot(a, b):
    return jnp.dot(a, b, preferred_element_type=F32)


def step(z, x_ref, y_ref):
    n = z.shape[0] // W
    total = None
    for t in range(x_ref.shape[1] // (2 * W)):
        cols = slice(2 * W * t, 2 * W * (t + 1))
        mid = dot(z, x_ref[:, cols]).astype(BF)
        tall = jnp.concatenate(
            [jnp.concatenate([mid[W * b : W * (b + 1), :W], mid[W * b : W * (b + 1), W:]], 0) for b in range(n)], 1
        )
        part = dot(y_ref[:, cols], tall)
        total = part if total is None else total + part
    return total.astype(BF)


def split(wide):
    return [wide[:, W * b : W * (b + 1)] for b in range(wide.shape[1] // W)]


def by_role(core_ref, body, edge, turned):
    @pl.when(core_ref[0] == 0)
    def _():
        body(edge, turned)

    @pl.when(core_ref[0] != 0)
    def _():
        body(turned, edge)


def turn_kernel(proj_ref, cot_ref, turned_ref, cot_t_ref, wide_ref):
    planes = turned_ref.shape[1] // W
    wide_ref[...] = proj_ref[...].astype(F32)
    for p in range(planes):
        turned_ref[:, W * p : W * (p + 1)] = wide_ref[pl.ds(p, W, stride=planes), :].T.astype(BF)
    cot_t_ref[...] = cot_ref[...].astype(F32).T.astype(BF)


def own_kernel(corner_ref, edge_ref, turned_ref, cot_t_ref, out_ref):
    out_ref[:W, :] = step(corner_ref[...], edge_ref, turned_ref)
    out_ref[W:, :] = cot_t_ref[...]


def first_kernel(core_ref, own_ref, mate_ref, edge_ref, turned_ref, out_ref):
    def body(x_ref, y_ref):
        start = jnp.where(core_ref[0] == 0, own_ref[:W, :], own_ref[W:, :])
        out_ref[:W, :] = jnp.where(core_ref[0] == 0, mate_ref[:W, :], mate_ref[W:, :])
        out_ref[W:, :] = step(start, x_ref, y_ref)

    by_role(core_ref, body, edge_ref, turned_ref)


def double_kernel(core_ref, come_ref, edge_ref, turned_ref, mate_edge_ref, mate_turned_ref, near_ref, far_ref):
    def run(x1, y1, x2, y2):
        near = jnp.concatenate(split(step(come_ref[...], x1, y1)), 0)
        near_ref[...] = near
        far_ref[...] = jnp.concatenate(split(step(near, x2, y2)), 0)

    @pl.when(core_ref[0] == 0)
    def _():
        run(edge_ref, turned_ref, mate_edge_ref, mate_turned_ref)

    @pl.when(core_ref[0] != 0)
    def _():
        run(turned_ref, edge_ref, mate_turned_ref, mate_edge_ref)


def last_kernel(core_ref, come_ref, edge_ref, turned_ref, mate_edge_ref, mate_turned_ref, out_ref, own_ref):
    @pl.when(core_ref[0] != 0)
    def _():
        got = split(step(come_ref[...], turned_ref, edge_ref))
        out_ref[:W, :] = got[0]
        own_ref[...] = got[1]
        out_ref[W:, :] = step(got[0], mate_turned_ref, mate_edge_ref)

    @pl.when(core_ref[0] == 0)
    def _():
        out_ref[...] = jnp.zeros_like(out_ref)
        own_ref[...] = jnp.zeros_like(own_ref)


def blocks(ref):
    return [ref[W * b : W * (b + 1), :] for b in range(ref.shape[0] // W)]


def fill(ref, parts):
    for b, part in enumerate(parts):
        ref[W * b : W * (b + 1), :] = part


def pairs_of(z_ref, x_ref, w_ref, put):
    n = z_ref.shape[0] // W
    for t in range(x_ref.shape[1] // (2 * W)):
        mid = dot(z_ref[...], x_ref[:, 2 * W * t : 2 * W * (t + 1)]).astype(BF)
        for half in range(2):
            flat = jnp.concatenate([mid[W * k : W * (k + 1), W * half : W * (half + 1)] for k in range(n)], 1)
            put(2 * t + half, dot(flat, w_ref[...]))


def proj_early_kernel(core_ref, r1_ref, r2_ref, m2_ref, m3_ref, edge_ref, out_ref, z_ref, w_ref):
    r1, r2, m2, m3 = blocks(r1_ref), blocks(r2_ref), blocks(m2_ref), blocks(m3_ref)

    @pl.when(core_ref[0] == 0)
    def _():
        fill(z_ref, [r1[0], r1[1], r2[0], r2[1]])
        fill(w_ref, [m3[1], m3[0], m2[1], m2[0]])

    @pl.when(core_ref[0] != 0)
    def _():
        fill(z_ref, [m2[0], m2[1], m3[0], m3[1]])
        fill(w_ref, [r2[1], r2[0], r1[1], r1[0]])

    def put(p, value):
        out_ref[:, W * p : W * (p + 1)] = value

    pairs_of(z_ref, edge_ref, w_ref, put)


def proj_late_kernel(core_ref, corner_ref, r3_ref, m1_ref, m4_ref, edge_ref, early_ref, out_ref, z_ref, w_ref):
    r3, m1, m4 = blocks(r3_ref), blocks(m1_ref), blocks(m4_ref)

    @pl.when(core_ref[0] == 0)
    def _():
        fill(z_ref, [corner_ref[...], r3[0]])
        fill(w_ref, [m4[0], m1[1]])

    @pl.when(core_ref[0] != 0)
    def _():
        fill(z_ref, [corner_ref[...], m1[0]])
        fill(w_ref, [r3[1], r3[0]])

    def put(p, value):
        out_ref[:, W * p : W * (p + 1)] = (early_ref[:, W * p : W * (p + 1)] + value).astype(BF)

    pairs_of(z_ref, edge_ref, w_ref, put)


def edge_kernel(
    core_ref, corner_ref, r1_ref, r2_ref, r3_ref, m1_ref, m2_ref, m3_ref, m4_ref, own_ref, turned_ref,
    out_ref, grad_ref, z_ref, w_ref,
):
    r1, r2, r3 = blocks(r1_ref), blocks(r2_ref), blocks(r3_ref)
    m1, m2, m3, m4 = blocks(m1_ref), blocks(m2_ref), blocks(m3_ref), blocks(m4_ref)

    @pl.when(core_ref[0] == 0)
    def _():
        fill(w_ref, [corner_ref[...], r1[0], r1[1], r2[0], r2[1], r3[0]])
        fill(z_ref, [m4[0], m3[1], m3[0], m2[1], m2[0], m1[1]])
        grad_ref[...] = m4[1].astype(F32).T.astype(BF)

    @pl.when(core_ref[0] != 0)
    def _():
        fill(w_ref, [corner_ref[...], m1[0], m2[0], m2[1], m3[0], m3[1]])
        fill(z_ref, [r3[1], r3[0], r2[1], r2[0], r1[1], r1[0]])
        grad_ref[...] = own_ref[...].astype(F32).T.astype(BF)

    def put(p, value):
        out_ref[:, W * p : W * (p + 1)] = value.T.astype(BF)

    pairs_of(z_ref, turned_ref, w_ref, put)


def gather_kernel(parts_ref, out_ref):
    rows = parts_ref.shape[1]
    planes = parts_ref.shape[2] // W
    for p in range(planes):
        out_ref[pl.ds(p, rows, stride=planes), :] = jnp.sum(
            parts_ref[:, :, W * p : W * (p + 1)].astype(F32), axis=0
        )


def call(kernel, shapes, *args, scratch=(), flops=0):
    specs = [
        pl.BlockSpec(memory_space=pltpu.SMEM if arg.dtype == jnp.int32 else pltpu.VMEM) for arg in args
    ]
    moved = sum(arg.size * arg.dtype.itemsize for arg in args)
    single = len(shapes) == 1
    outs = [jax.ShapeDtypeStruct(shape, kind) for shape, kind in shapes]
    out_specs = [pl.BlockSpec(memory_space=pltpu.VMEM) for _ in shapes]
    return pl.pallas_call(
        kernel,
        out_shape=outs[0] if single else outs,
        in_specs=specs,
        out_specs=out_specs[0] if single else out_specs,
        scratch_shapes=[pltpu.VMEM(shape, kind) for shape, kind in scratch],
        compiler_params=pltpu.CompilerParams(vmem_limit_bytes=24 * 1024 * 1024),
        cost_estimate=pl.CostEstimate(flops=flops, bytes_accessed=moved, transcendentals=0),
    )(*args)


def shards(corners, edges, projectors, cotangent):
    corner = corners[0, 0]
    edge = edges[0, 0]
    projector = projectors[0]
    cot = cotangent[0, 0]
    width = edge.shape[1]
    rows = lax.axis_size("row")
    cols = lax.axis_size("col")
    core = (lax.axis_index("col") % 2).astype(jnp.int32).reshape(1)
    unit = 2 * W * W * width

    def swap(value):
        return lax.ppermute(value, "col", [(i, i ^ 1) for i in range(cols)])

    def onward(value):
        return lax.ppermute(value, "col", [(i, (i + (2 if i % 2 == 0 else -2)) % cols) for i in range(cols)])

    two = ((2 * W, W), BF)
    mate_edge = swap(edge)
    turned, cot_t = call(
        turn_kernel, [((W, width), BF), ((W, W), BF)], projector, cot, scratch=[((width, W), F32)], flops=unit
    )
    mate_turned = swap(turned)
    own = call(own_kernel, [two], corner, edge, turned, cot_t, flops=2 * unit)
    m1 = swap(own)
    go1 = call(first_kernel, [two], core, own, m1, mate_edge, mate_turned, flops=2 * unit)
    tensors = (edge, turned, mate_edge, mate_turned)
    r1 = onward(go1)
    s1, go2 = call(double_kernel, [two, two], core, r1, *tensors, flops=8 * unit)
    r2 = onward(go2)
    m2 = swap(s1)
    s2, go3 = call(double_kernel, [two, two], core, r2, *tensors, flops=8 * unit)
    r3 = onward(go3)
    m3 = swap(s2)
    early = call(
        proj_early_kernel, [((W, width), F32)], core, r1, r2, m2, m3, edge,
        scratch=[((4 * W, W), BF), ((4 * W, W), BF)], flops=8 * unit,
    )
    s3, own_grad = call(last_kernel, [two, ((W, W), BF)], core, r3, *tensors, flops=6 * unit)
    m4 = swap(s3)
    late = call(
        proj_late_kernel, [((W, width), BF)], core, corner, r3, m1, m4, edge, early,
        scratch=[((2 * W, W), BF), ((2 * W, W), BF)], flops=4 * unit,
    )
    share = W // rows
    parts = lax.all_to_all(late.reshape(rows, share, width), "row", 0, 0, tiled=True)
    edge_grad, corner_grad = call(
        edge_kernel, [((W, width), BF), ((W, W), BF)], core, corner, r1, r2, r3, m1, m2, m3, m4, own_grad, turned,
        scratch=[((6 * W, W), BF), ((6 * W, W), BF)], flops=12 * unit,
    )
    proj = call(gather_kernel, [((share * width // W, W), F32)], parts, flops=unit)
    return (corner_grad[None, None], edge_grad[None, None], proj[None])


def solution(mesh):
    placed = (
        P("row", "col", None, None),
        P("row", "col", None, None),
        P("col", None, None),
        P("row", "col", None, None),
    )
    return jax.shard_map(
        shards,
        mesh=mesh,
        in_specs=placed,
        out_specs=(P("row", "col", None, None), P("row", "col", None, None), P("col", "row", None)),
        check_vma=False,
    )
```

time: 198 us -> 77.6 us (0.39)
  the two profiles are of different devices: /device:TPU:4 before, /device:TPU:1 now
where the time goes in v1:
time: 77.6 us; the launch traced here: 77 us
  Pallas kernels  31.9 us (41%)
  starting transfers between devices  27.1 us (35%)
  waiting for transfers between devices  14.9 us (19%)
  local copies, waits for them, and re-layouts  2.19 us (3%)
  between operations  0.85 us (1%)
    pallas_call x10, Pallas kernels, call(): pl.pallas_call(kernel, out_shape=outs[0] if single else outs, in_specs=sp...  31.9 us
    ppermute x3, starting transfers between devices, onward(): lax.ppermute(value, 'col', [(i, (i + (2 if i % 2 == 0 else -2)) % cols) f...  17.3 us
    all_to_all x1, waiting for transfers between devices, shards(): lax.all_to_all(late.reshape(rows, share, width), 'row', 0, 0, tiled=True)  10.2 us
    ppermute x6, starting transfers between devices, swap(): return lax.ppermute(value, 'col', [(i, i ^ 1) for i in range(cols)])  5.44 us
    all_to_all x1, starting transfers between devices, shards(): lax.all_to_all(late.reshape(rows, share, width), 'row', 0, 0, tiled=True)  4.36 us
    ppermute x3, waiting for transfers between devices, onward(): lax.ppermute(value, 'col', [(i, (i + (2 if i % 2 == 0 else -2)) % cols) f...  3.49 us
    unnamed x34, local copies, waits for them, and re-layouts  2.19 us
  transfers between devices with their start and end apart: 10, of which 5 were waited for; matrix products, arithmetic and copies ran while one was open for 0% of the time, Pallas kernels for 20%

profile of v1, /device:TPU:1, one launch (start us, length us, event | category | flops | bytes accessed | tf_op | source)
XLA Modules:
  0.0 77.0 jit_solution(13697418841647977536)
XLA Ops:
  0.6 0.0 copy-start
  0.6 3.3 %collective-permute-start.1 = (bf16[128,4608]{1,0:T(8,128)(2,1)}, bf16[128,4608]{1,0:T(8,128)(2,1)S(1)}, u32[]{:S(2)}, u32[]{:S(2)}) collective-permute-start(bf16[128,4608]{1,0:T(8,128)(2,1)} %bitcast.9), channel_id=1, source_target_pairs={{0,1},{1,0},{2,3},{3,2},{4,5},{5,4},{6,7},{7,6},{8,9},{9,8},{10,11... | collective-permute-start | bytes 3538952 | tf_op jit(solution)/shard_map/ppermute | solution.py:218
  4.0 1.3 %copy-done.1 = bf16[1,4608,128]{2,1,0:T(8,128)(2,1)S(1)} copy-done((bf16[1,4608,128]{2,1,0:T(8,128)(2,1)S(1)}, bf16[1,4608,128]{2,1,0:T(8,128)(2,1)}, u32[]{:S(2)}) %copy-start.1) | copy-done | bytes 1179672
  5.2 0.8 copy-done.10
  6.0 0.5 shard_map.67
  6.5 0.2 collective-permute-start.2
  6.7 0.0 copy-done
  6.7 0.1 copy-done.4
  6.8 1.7 %shard_map.68.own_ref = bf16[256,128]{1,0:T(8,128)(2,1)} custom-call(bf16[128,128]{1,0:T(8,128)(2,1)S(1)} %bitcast.17, bf16[128,4608]{1,0:T(8,128)(2,1)S(1)} %bitcast.10, bf16[128,4608]{1,0:T(8,128)(2,1)S(1)} %get-tuple-element.13.turned_ref, bf16[128,128]{1,0:T(8,128)(2,1)S(1)} %get-tuple-element.14.cot_t_ref), custom_call_target="tpu_custom_call" | custom-call | flops 301989888 | bytes 2424832 | tf_op jit(solution)/shard_map/pallas_call | solution.py:195
  8.4 0.3 collective-permute-start
  8.7 1.3 %collective-permute-done.mate_ref.m1_ref = bf16[256,128]{1,0:T(8,128)(2,1)} collective-permute-done((bf16[256,128]{1,0:T(8,128)(2,1)}, bf16[256,128]{1,0:T(8,128)(2,1)}, u32[]{:S(2)}, u32[]{:S(2)}) %collective-permute-start) | collective-permute-done | bytes 65568 | tf_op jit(solution)/shard_map/ppermute | solution.py:218
  10.0 0.0 collective-permute-done.1.edge_ref.mate_edge_ref
  10.0 0.0 collective-permute-done.2.turned_ref.mate_turned_ref
  10.0 2.4 %shard_map.69 = bf16[256,128]{1,0:T(8,128)(2,1)S(1)} custom-call(s32[1]{0:T(128)} %bitcast.core_ref, bf16[256,128]{1,0:T(8,128)(2,1)} %shard_map.68.own_ref, bf16[256,128]{1,0:T(8,128)(2,1)} %collective-permute-done.mate_ref.m1_ref, bf16[128,4608]{1,0:T(8,128)(2,1)S(1)} %collective-permute-done.1.edge_ref.mate_edge_ref, ...), custom_call_target="tpu_custom_call" | custom-call | flops 301989888 | bytes 2490372 | tf_op jit(solution)/shard_map/pallas_call | solution.py:195
  12.4 6.4 %collective-permute-start.3 = (bf16[256,128]{1,0:T(8,128)(2,1)S(1)}, bf16[256,128]{1,0:T(8,128)(2,1)S(1)}, u32[]{:S(2)}, u32[]{:S(2)}) collective-permute-start(bf16[256,128]{1,0:T(8,128)(2,1)S(1)} %shard_map.69), channel_id=1, source_target_pairs={{0,2},{1,31},{2,4},{3,1},{4,6},{5,3},{6,8},{7,5},{8,10},{9,7},{10,... | collective-permute-start | bytes 196616 | tf_op jit(solution)/shard_map/ppermute | solution.py:221
  18.8 1.3 %collective-permute-done.3.come_ref.r1_ref = bf16[256,128]{1,0:T(8,128)(2,1)S(1)} collective-permute-done((bf16[256,128]{1,0:T(8,128)(2,1)S(1)}, bf16[256,128]{1,0:T(8,128)(2,1)S(1)}, u32[]{:S(2)}, u32[]{:S(2)}) %collective-permute-start.3) | collective-permute-done | bytes 65568 | tf_op jit(solution)/shard_map/ppermute | solution.py:221
  20.1 4.8 %shard_map.70 = (bf16[256,128]{1,0:T(8,128)(2,1)S(1)}, bf16[256,128]{1,0:T(8,128)(2,1)S(1)}) custom-call(s32[1]{0:T(128)} %bitcast.core_ref, bf16[256,128]{1,0:T(8,128)(2,1)S(1)} %collective-permute-done.3.come_ref.r1_ref, bf16[128,4608]{1,0:T(8,128)(2,1)S(1)} %bitcast.11, bf16[128,4608]{1,0:T(8,128)(2,1)S(1)} %get-tuple-element.13.turned_ref, ...), custom_call_target="tpu_custom_call" | custom-call | flops 1207959552 | bytes 4784132 | tf_op jit(solution)/shard_map/pallas_call | solution.py:195
  25.0 5.5 %collective-permute-start.4 = (bf16[256,128]{1,0:T(8,128)(2,1)S(1)}, bf16[256,128]{1,0:T(8,128)(2,1)S(1)}, u32[]{:S(2)}, u32[]{:S(2)}) collective-permute-start(bf16[256,128]{1,0:T(8,128)(2,1)S(1)} %get-tuple-element.15), channel_id=1, source_target_pairs={{0,2},{1,31},{2,4},{3,1},{4,6},{5,3},{6,8},{7,5},{8,10},{9,7},{10,... | collective-permute-start | bytes 196616 | tf_op jit(solution)/shard_map/ppermute | solution.py:221
  30.5 1.3 %collective-permute-done.4.come_ref.r2_ref = bf16[256,128]{1,0:T(8,128)(2,1)S(1)} collective-permute-done((bf16[256,128]{1,0:T(8,128)(2,1)S(1)}, bf16[256,128]{1,0:T(8,128)(2,1)S(1)}, u32[]{:S(2)}, u32[]{:S(2)}) %collective-permute-start.4) | collective-permute-done | bytes 65568 | tf_op jit(solution)/shard_map/ppermute | solution.py:221
  31.8 4.8 %shard_map.71 = (bf16[256,128]{1,0:T(8,128)(2,1)S(1)}, bf16[256,128]{1,0:T(8,128)(2,1)S(1)}) custom-call(s32[1]{0:T(128)} %bitcast.core_ref, bf16[256,128]{1,0:T(8,128)(2,1)S(1)} %collective-permute-done.4.come_ref.r2_ref, bf16[128,4608]{1,0:T(8,128)(2,1)S(1)} %bitcast.12, bf16[128,4608]{1,0:T(8,128)(2,1)S(1)} %get-tuple-element.13.turned_ref, ...), custom_call_target="tpu_custom_call" | custom-call | flops 1207959552 | bytes 4784132 | tf_op jit(solution)/shard_map/pallas_call | solution.py:195
  36.7 5.5 %collective-permute-start.5 = (bf16[256,128]{1,0:T(8,128)(2,1)S(1)}, bf16[256,128]{1,0:T(8,128)(2,1)S(1)}, u32[]{:S(2)}, u32[]{:S(2)}) collective-permute-start(bf16[256,128]{1,0:T(8,128)(2,1)S(1)} %get-tuple-element.16), channel_id=1, source_target_pairs={{0,2},{1,31},{2,4},{3,1},{4,6},{5,3},{6,8},{7,5},{8,10},{9,7},{10,... | collective-permute-start | bytes 196616 | tf_op jit(solution)/shard_map/ppermute | solution.py:221
  42.1 0.0 collective-permute-start.6
  42.1 0.5 collective-permute-start.7
  42.6 0.8 %collective-permute-done.5.come_ref.r3_ref = bf16[256,128]{1,0:T(8,128)(2,1)S(1)} collective-permute-done((bf16[256,128]{1,0:T(8,128)(2,1)S(1)}, bf16[256,128]{1,0:T(8,128)(2,1)S(1)}, u32[]{:S(2)}, u32[]{:S(2)}) %collective-permute-start.5) | collective-permute-done | bytes 65568 | tf_op jit(solution)/shard_map/ppermute | solution.py:221
  43.5 4.1 %shard_map.72 = (bf16[256,128]{1,0:T(8,128)(2,1)S(1)}, bf16[128,128]{1,0:T(8,128)(2,1)S(1)}) custom-call(s32[1]{0:T(128)} %bitcast.core_ref, bf16[256,128]{1,0:T(8,128)(2,1)S(1)} %collective-permute-done.5.come_ref.r3_ref, bf16[128,4608]{1,0:T(8,128)(2,1)S(1)} %bitcast.13, bf16[128,4608]{1,0:T(8,128)(2,1)S(1)} %get-tuple-element.13.turned_ref, ...), custom_call_target="tpu_custom_call" | custom-call | flops 905969664 | bytes 4784132 | tf_op jit(solution)/shard_map/pallas_call | solution.py:195
  47.6 0.0 copy-start.15
  47.6 0.0 copy-start.5
  47.6 1.1 %collective-permute-start.8 = (bf16[256,128]{1,0:T(8,128)(2,1)S(1)}, bf16[256,128]{1,0:T(8,128)(2,1)S(1)}, u32[]{:S(2)}, u32[]{:S(2)}) collective-permute-start(bf16[256,128]{1,0:T(8,128)(2,1)S(1)} %get-tuple-element.19), channel_id=1, source_target_pairs={{0,1},{1,0},{2,3},{3,2},{4,5},{5,4},{6,7},{7,6},{8,9},{9,8},{10,11... | collective-permute-start | bytes 196616 | tf_op jit(solution)/shard_map/ppermute | solution.py:218
  48.7 0.0 collective-permute-done.6.m2_ref
  48.7 0.0 collective-permute-done.7.m3_ref
  48.8 3.1 %shard_map.74.early_ref = f32[128,4608]{1,0:T(8,128)S(1)} custom-call(s32[1]{0:T(128)} %bitcast.core_ref, bf16[256,128]{1,0:T(8,128)(2,1)S(1)} %collective-permute-done.3.come_ref.r1_ref, bf16[256,128]{1,0:T(8,128)(2,1)S(1)} %collective-permute-done.4.come_ref.r2_ref, bf16[256,128]{1,0:T(8,128)(2,1)S(1)} %collective-permute-done.6.m2_ref, ...), custom_call_target="tpu_custom_call" | custom-call | flops 1207959552 | bytes 1441796 | tf_op jit(solution)/shard_map/pallas_call | solution.py:195
  51.9 0.0 copy-done.15
  51.9 0.0 copy-done.11
  51.9 0.0 copy-done.13
  51.9 0.0 collective-permute-done.8.m4_ref
  51.9 3.4 %shard_map.75 = bf16[128,4608]{1,0:T(8,128)(2,1)} custom-call(s32[1]{0:T(128)} %bitcast.core_ref, bf16[128,128]{1,0:T(8,128)(2,1)S(1)} %bitcast.18, bf16[256,128]{1,0:T(8,128)(2,1)S(1)} %collective-permute-done.5.come_ref.r3_ref, bf16[256,128]{1,0:T(8,128)(2,1)} %collective-permute-done.mate_ref.m1_ref, bf16[256,128]{1,0:T(8,128)(2,1)S(1)} %collective-permute-done.8.m4_ref, ...), custom_call_target="tpu_custom_call" | custom-call | flops 603979776 | bytes 3768324 | tf_op jit(solution)/shard_map/pallas_call | solution.py:195
  55.4 0.0 copy-start.14
  55.4 0.0 copy-start.16
  55.4 4.4 %all-to-all-start = ((bf16[8,16,4608]{2,1,0:T(8,128)(2,1)}), bf16[8,16,4608]{2,1,0:T(8,128)(2,1)S(1)}, u32[]{:S(2)}, u32[]{:S(2)}) async-start(bf16[8,16,4608]{2,1,0:T(8,128)(2,1)} %bitcast.7), calls=%async_computation | async-start | bytes 2359296 | tf_op jit(solution)/shard_map/all_to_all | solution.py:251
  59.7 0.0 copy-done.3
  59.7 0.0 copy-done.7
  59.8 0.0 copy-done.9
  59.8 0.0 copy-done.12
  59.8 0.0 copy-done.14
  59.8 0.0 copy-done.16
  59.8 6.2 %shard_map.73 = (bf16[128,4608]{1,0:T(8,128)(2,1)}, bf16[128,128]{1,0:T(8,128)(2,1)}) custom-call(s32[1]{0:T(128)} %bitcast.core_ref, bf16[128,128]{1,0:T(8,128)(2,1)S(1)} %bitcast.19, bf16[256,128]{1,0:T(8,128)(2,1)S(1)} %copy-done.7, bf16[256,128]{1,0:T(8,128)(2,1)S(1)} %copy-done.9, bf16[256,128]{1,0:T(8,128)(2,1)S(1)} %copy-done.3, ...), custom_call_target="tpu_custom_call" | custom-call | flops 1811939328 | bytes 1703940 | tf_op jit(solution)/shard_map/pallas_call | solution.py:195
  66.0 10.2 %all-to-all-done.parts_ref = bf16[8,16,4608]{2,1,0:T(8,128)(2,1)S(1)} async-done(((bf16[8,16,4608]{2,1,0:T(8,128)(2,1)}), bf16[8,16,4608]{2,1,0:T(8,128)(2,1)S(1)}, u32[]{:S(2)}, u32[]{:S(2)}) %all-to-all-start) | async-done | bytes 1179680 | tf_op jit(solution)/shard_map/all_to_all | solution.py:251
  76.1 0.9 %shard_map.76 = f32[576,128]{1,0:T(8,128)} custom-call(bf16[8,16,4608]{2,1,0:T(8,128)(2,1)S(1)} %all-to-all-done.parts_ref), custom_call_target="tpu_custom_call" | custom-call | flops 150994944 | bytes 1179648 | tf_op jit(solution)/shard_map/pallas_call | solution.py:195
  (16 shorter events, 0.0 us)
Async XLA Ops:
  0.6 6.0 %copy-start = (bf16[1,1,128,4608]{3,2,1,0:T(8,128)(2,1)S(1)}, bf16[1,1,128,4608]{3,2,1,0:T(8,128)(2,1)}, u32[]{:S(2)}) copy-start(bf16[1,1,128,4608]{3,2,1,0:T(8,128)(2,1)} %param.5) | copy-start | bytes 3538948
  0.6 9.4 %collective-permute-start.1 = (bf16[128,4608]{1,0:T(8,128)(2,1)}, bf16[128,4608]{1,0:T(8,128)(2,1)S(1)}, u32[]{:S(2)}, u32[]{:S(2)}) collective-permute-start(bf16[128,4608]{1,0:T(8,128)(2,1)} %bitcast.9), channel_id=1, source_target_pairs={{0,1},{1,0},{2,3},{3,2},{4,5},{5,4},{6,7},{7,6},{8,9},{9,8},{10,11... | collective-permute-start | bytes 3538952 | tf_op jit(solution)/shard_map/ppermute | solution.py:218
  4.0 1.3 %copy-start.1 = (bf16[1,4608,128]{2,1,0:T(8,128)(2,1)S(1)}, bf16[1,4608,128]{2,1,0:T(8,128)(2,1)}, u32[]{:S(2)}) copy-start(bf16[1,4608,128]{2,1,0:T(8,128)(2,1)} %param.6) | copy-start | bytes 3538948
  5.2 0.8 copy-start.10
  6.0 0.8 copy-start.4
  6.5 3.5 %collective-permute-start.2 = (bf16[128,4608]{1,0:T(8,128)(2,1)S(1)}, bf16[128,4608]{1,0:T(8,128)(2,1)}, u32[]{:S(2)}, u32[]{:S(2)}) collective-permute-start(bf16[128,4608]{1,0:T(8,128)(2,1)S(1)} %get-tuple-element.13.turned_ref), channel_id=1, source_target_pairs={{0,1},{1,0},{2,3},{3,2},{4,5},{5,4},{6,7},{7,6},{8,9},{9,8},{10,11... | collective-permute-start | bytes 3538952 | tf_op jit(solution)/shard_map/ppermute | solution.py:218
  8.4 1.6 %collective-permute-start = (bf16[256,128]{1,0:T(8,128)(2,1)}, bf16[256,128]{1,0:T(8,128)(2,1)}, u32[]{:S(2)}, u32[]{:S(2)}) collective-permute-start(bf16[256,128]{1,0:T(8,128)(2,1)} %shard_map.68.own_ref), channel_id=1, source_target_pairs={{0,1},{1,0},{2,3},{3,2},{4,5},{5,4},{6,7},{7,6},{8,9},{9,8},{10,11... | collective-permute-start | bytes 196616 | tf_op jit(solution)/shard_map/ppermute | solution.py:218
  12.4 7.7 %collective-permute-start.3 = (bf16[256,128]{1,0:T(8,128)(2,1)S(1)}, bf16[256,128]{1,0:T(8,128)(2,1)S(1)}, u32[]{:S(2)}, u32[]{:S(2)}) collective-permute-start(bf16[256,128]{1,0:T(8,128)(2,1)S(1)} %shard_map.69), channel_id=1, source_target_pairs={{0,2},{1,31},{2,4},{3,1},{4,6},{5,3},{6,8},{7,5},{8,10},{9,7},{10,... | collective-permute-start | bytes 196616 | tf_op jit(solution)/shard_map/ppermute | solution.py:221
  20.1 28.6 %copy-start.6 = (bf16[256,128]{1,0:T(8,128)(2,1)}, bf16[256,128]{1,0:T(8,128)(2,1)S(1)}, u32[]{:S(2)}) copy-start(bf16[256,128]{1,0:T(8,128)(2,1)S(1)} %collective-permute-done.3.come_ref.r1_ref) | copy-start | bytes 196612
  25.0 6.8 %collective-permute-start.4 = (bf16[256,128]{1,0:T(8,128)(2,1)S(1)}, bf16[256,128]{1,0:T(8,128)(2,1)S(1)}, u32[]{:S(2)}, u32[]{:S(2)}) collective-permute-start(bf16[256,128]{1,0:T(8,128)(2,1)S(1)} %get-tuple-element.15), channel_id=1, source_target_pairs={{0,2},{1,31},{2,4},{3,1},{4,6},{5,3},{6,8},{7,5},{8,10},{9,7},{10,... | collective-permute-start | bytes 196616 | tf_op jit(solution)/shard_map/ppermute | solution.py:221
  31.8 17.0 %copy-start.8 = (bf16[256,128]{1,0:T(8,128)(2,1)}, bf16[256,128]{1,0:T(8,128)(2,1)S(1)}, u32[]{:S(2)}) copy-start(bf16[256,128]{1,0:T(8,128)(2,1)S(1)} %collective-permute-done.4.come_ref.r2_ref) | copy-start | bytes 196612
  36.7 6.8 %collective-permute-start.5 = (bf16[256,128]{1,0:T(8,128)(2,1)S(1)}, bf16[256,128]{1,0:T(8,128)(2,1)S(1)}, u32[]{:S(2)}, u32[]{:S(2)}) collective-permute-start(bf16[256,128]{1,0:T(8,128)(2,1)S(1)} %get-tuple-element.16), channel_id=1, source_target_pairs={{0,2},{1,31},{2,4},{3,1},{4,6},{5,3},{6,8},{7,5},{8,10},{9,7},{10,... | collective-permute-start | bytes 196616 | tf_op jit(solution)/shard_map/ppermute | solution.py:221
  42.1 6.6 %collective-permute-start.6 = (bf16[256,128]{1,0:T(8,128)(2,1)S(1)}, bf16[256,128]{1,0:T(8,128)(2,1)S(1)}, u32[]{:S(2)}, u32[]{:S(2)}) collective-permute-start(bf16[256,128]{1,0:T(8,128)(2,1)S(1)} %get-tuple-element.17), channel_id=1, source_target_pairs={{0,1},{1,0},{2,3},{3,2},{4,5},{5,4},{6,7},{7,6},{8,9},{9,8},{10,11... | collective-permute-start | bytes 196616 | tf_op jit(solution)/shard_map/ppermute | solution.py:218
  42.1 6.6 %collective-permute-start.7 = (bf16[256,128]{1,0:T(8,128)(2,1)S(1)}, bf16[256,128]{1,0:T(8,128)(2,1)S(1)}, u32[]{:S(2)}, u32[]{:S(2)}) collective-permute-start(bf16[256,128]{1,0:T(8,128)(2,1)S(1)} %get-tuple-element.18), channel_id=1, source_target_pairs={{0,1},{1,0},{2,3},{3,2},{4,5},{5,4},{6,7},{7,6},{8,9},{9,8},{10,11... | collective-permute-start | bytes 196616 | tf_op jit(solution)/shard_map/ppermute | solution.py:218
  43.5 8.4 %copy-start.2 = (bf16[256,128]{1,0:T(8,128)(2,1)}, bf16[256,128]{1,0:T(8,128)(2,1)S(1)}, u32[]{:S(2)}) copy-start(bf16[256,128]{1,0:T(8,128)(2,1)S(1)} %collective-permute-done.5.come_ref.r3_ref) | copy-start | bytes 196612
  47.6 4.3 %copy-start.15 = (bf16[128,128]{1,0:T(8,128)(2,1)}, bf16[128,128]{1,0:T(8,128)(2,1)S(1)}, u32[]{:S(2)}) copy-start(bf16[128,128]{1,0:T(8,128)(2,1)S(1)} %get-tuple-element.20.own_ref) | copy-start | bytes 98308
  47.6 4.3 %copy-start.5 = (bf16[1,1,128,128]{3,2,1,0:T(8,128)(2,1)S(1)}, bf16[1,1,128,128]{3,2,1,0:T(8,128)(2,1)}, u32[]{:S(2)}) copy-start(bf16[1,1,128,128]{3,2,1,0:T(8,128)(2,1)} %param.4) | copy-start | bytes 98308
  47.6 4.3 %collective-permute-start.8 = (bf16[256,128]{1,0:T(8,128)(2,1)S(1)}, bf16[256,128]{1,0:T(8,128)(2,1)S(1)}, u32[]{:S(2)}, u32[]{:S(2)}) collective-permute-start(bf16[256,128]{1,0:T(8,128)(2,1)S(1)} %get-tuple-element.19), channel_id=1, source_target_pairs={{0,1},{1,0},{2,3},{3,2},{4,5},{5,4},{6,7},{7,6},{8,9},{9,8},{10,11... | collective-permute-start | bytes 196616 | tf_op jit(solution)/shard_map/ppermute | solution.py:218
  48.7 3.1 %copy-start.11 = (bf16[256,128]{1,0:T(8,128)(2,1)}, bf16[256,128]{1,0:T(8,128)(2,1)S(1)}, u32[]{:S(2)}) copy-start(bf16[256,128]{1,0:T(8,128)(2,1)S(1)} %collective-permute-done.6.m2_ref) | copy-start | bytes 196612
  48.8 3.1 %copy-start.13 = (bf16[256,128]{1,0:T(8,128)(2,1)}, bf16[256,128]{1,0:T(8,128)(2,1)S(1)}, u32[]{:S(2)}) copy-start(bf16[256,128]{1,0:T(8,128)(2,1)S(1)} %collective-permute-done.7.m3_ref) | copy-start | bytes 196612
  55.3 4.4 %copy-start.3 = (bf16[256,128]{1,0:T(8,128)(2,1)S(1)}, bf16[256,128]{1,0:T(8,128)(2,1)}, u32[]{:S(2)}) copy-start(bf16[256,128]{1,0:T(8,128)(2,1)} %copy-done.2) | copy-start | bytes 196612
  55.3 4.4 %copy-start.7 = (bf16[256,128]{1,0:T(8,128)(2,1)S(1)}, bf16[256,128]{1,0:T(8,128)(2,1)}, u32[]{:S(2)}) copy-start(bf16[256,128]{1,0:T(8,128)(2,1)} %copy-done.6) | copy-start | bytes 196612
  55.3 4.4 %copy-start.9 = (bf16[256,128]{1,0:T(8,128)(2,1)S(1)}, bf16[256,128]{1,0:T(8,128)(2,1)}, u32[]{:S(2)}) copy-start(bf16[256,128]{1,0:T(8,128)(2,1)} %copy-done.8) | copy-start | bytes 196612
  55.4 4.4 %copy-start.12 = (bf16[256,128]{1,0:T(8,128)(2,1)S(1)}, bf16[256,128]{1,0:T(8,128)(2,1)}, u32[]{:S(2)}) copy-start(bf16[256,128]{1,0:T(8,128)(2,1)} %copy-done.11) | copy-start | bytes 196612
  55.4 4.4 %copy-start.14 = (bf16[256,128]{1,0:T(8,128)(2,1)S(1)}, bf16[256,128]{1,0:T(8,128)(2,1)}, u32[]{:S(2)}) copy-start(bf16[256,128]{1,0:T(8,128)(2,1)} %copy-done.13) | copy-start | bytes 196612
  55.4 4.4 %copy-start.16 = (bf16[128,128]{1,0:T(8,128)(2,1)S(1)}, bf16[128,128]{1,0:T(8,128)(2,1)}, u32[]{:S(2)}) copy-start(bf16[128,128]{1,0:T(8,128)(2,1)} %copy-done.15) | copy-start | bytes 98308
  55.4 20.8 %all-to-all-start = ((bf16[8,16,4608]{2,1,0:T(8,128)(2,1)}), bf16[8,16,4608]{2,1,0:T(8,128)(2,1)S(1)}, u32[]{:S(2)}, u32[]{:S(2)}) async-start(bf16[8,16,4608]{2,1,0:T(8,128)(2,1)} %bitcast.7), calls=%async_computation | async-start | bytes 2359296 | tf_op jit(solution)/shard_map/all_to_all | solution.py:251

commit v2 on v1

v2 whole, which is shorter than its diff:
```python
import jax
import jax.numpy as jnp
from jax import lax
from jax.experimental import pallas as pl
from jax.experimental.pallas import tpu as pltpu
from jax.sharding import PartitionSpec as P


W = 128
BF = jnp.bfloat16
F32 = jnp.float32


def dot(a, b):
    return jnp.dot(a, b, preferred_element_type=F32)


def step(z, x_ref, y_ref):
    n = z.shape[0] // W
    total = None
    for t in range(x_ref.shape[1] // (2 * W)):
        cols = slice(2 * W * t, 2 * W * (t + 1))
        mid = dot(z, x_ref[:, cols]).astype(BF)
        tall = jnp.concatenate(
            [jnp.concatenate([mid[W * b : W * (b + 1), :W], mid[W * b : W * (b + 1), W:]], 0) for b in range(n)], 1
        )
        part = dot(y_ref[:, cols], tall)
        total = part if total is None else total + part
    return total.astype(BF)


def split(wide):
    return [wide[:, W * b : W * (b + 1)] for b in range(wide.shape[1] // W)]


def turn_kernel(proj_ref, cot_ref, turned_ref, cot_t_ref, wide_ref):
    planes = turned_ref.shape[1] // W
    wide_ref[...] = proj_ref[...].astype(F32)
    for p in range(planes):
        turned_ref[:, W * p : W * (p + 1)] = wide_ref[pl.ds(p, W, stride=planes), :].T.astype(BF)
    cot_t_ref[...] = cot_ref[...].astype(F32).T.astype(BF)


def own_kernel(core_ref, corner_ref, edge_ref, turned_ref, cot_t_ref, keep_ref, send_ref):
    moved = step(corner_ref[...], edge_ref, turned_ref)
    keep_ref[...] = jnp.where(core_ref[0] == 0, moved, cot_t_ref[...])
    send_ref[...] = jnp.where(core_ref[0] == 0, cot_t_ref[...], moved)


def by_role(core_ref, body, tensors):
    edge, turned, mate_edge, mate_turned = tensors

    @pl.when(core_ref[0] == 0)
    def _():
        body(edge, turned, mate_edge, mate_turned)

    @pl.when(core_ref[0] != 0)
    def _():
        body(turned, edge, mate_turned, mate_edge)


def ahead_kernel(core_ref, keep_ref, mate_edge_ref, mate_turned_ref, out_ref):
    def body(x1, y1, x2, y2):
        out_ref[...] = step(keep_ref[...], x2, y2)

    by_role(core_ref, body, (None, None, mate_edge_ref, mate_turned_ref))


def single_kernel(core_ref, come_ref, ahead_ref, e_ref, t_ref, me_ref, mt_ref, near_ref, far_ref):
    far_ref[:W, :] = ahead_ref[...]

    def body(x1, y1, x2, y2):
        near = step(come_ref[...], x1, y1)
        near_ref[...] = near
        far_ref[W:, :] = step(near, x2, y2)

    by_role(core_ref, body, (e_ref, t_ref, me_ref, mt_ref))


def double_kernel(core_ref, come_ref, e_ref, t_ref, me_ref, mt_ref, m1_ref, m2_ref, near_ref, far_ref):
    def body(x1, y1, x2, y2):
        near = jnp.concatenate(split(step(come_ref[...], x1, y1)), 0)
        near_ref[...] = near
        far_ref[...] = jnp.concatenate(split(step(near, x2, y2)), 0)

    by_role(core_ref, body, (e_ref, t_ref, me_ref, mt_ref))


def turn_back_kernel(core_ref, come_ref, e_ref, t_ref, early_ref, near_ref):
    @pl.when(core_ref[0] == 0)
    def _():
        near_ref[:W, :] = step(come_ref[:W, :], e_ref, t_ref)
        near_ref[W:, :] = jnp.zeros((W, W), BF)

    @pl.when(core_ref[0] != 0)
    def _():
        fill(near_ref, split(step(come_ref[...], t_ref, e_ref)))


def blocks(ref):
    return [ref[W * b : W * (b + 1), :] for b in range(ref.shape[0] // W)]


def fill(ref, parts):
    for b, part in enumerate(parts):
        ref[W * b : W * (b + 1), :] = part


def pairs_of(z_ref, x_ref, w_ref, put):
    n = z_ref.shape[0] // W
    for t in range(x_ref.shape[1] // (2 * W)):
        mid = dot(z_ref[...], x_ref[:, 2 * W * t : 2 * W * (t + 1)]).astype(BF)
        for half in range(2):
            flat = jnp.concatenate([mid[W * k : W * (k + 1), W * half : W * (half + 1)] for k in range(n)], 1)
            put(2 * t + half, dot(flat, w_ref[...]))


def proj_first_kernel(core_ref, r1_ref, m3_ref, edge_ref, out_ref, z_ref, w_ref):
    r1, m3 = blocks(r1_ref), blocks(m3_ref)

    @pl.when(core_ref[0] == 0)
    def _():
        fill(z_ref, r1)
        fill(w_ref, m3[::-1])

    @pl.when(core_ref[0] != 0)
    def _():
        fill(z_ref, m3)
        fill(w_ref, r1[::-1])

    def put(p, value):
        out_ref[:, W * p : W * (p + 1)] = value

    pairs_of(z_ref, edge_ref, w_ref, put)


def adder(from_ref, to_ref):
    def put(p, value):
        at = slice(W * p, W * (p + 1))
        to_ref[:, at] = (from_ref[:, at] + value).astype(to_ref.dtype)

    return put


def proj_second_kernel(
    core_ref, r2_ref, m1_ref, m2_ref, near_ref, edge_ref, me_ref, mt_ref, early_ref, far_ref, out_ref, z_ref, w_ref
):
    @pl.when(core_ref[0] == 0)
    def _():
        fill(z_ref, blocks(r2_ref))
        fill(w_ref, [m2_ref[...], m1_ref[...]])
        pairs_of(z_ref, edge_ref, w_ref, adder(early_ref, out_ref))
        far_ref[...] = jnp.zeros_like(far_ref)

    @pl.when(core_ref[0] != 0)
    def _():
        far_ref[...] = step(near_ref[:W, :], mt_ref, me_ref)


def proj_third_kernel(
    core_ref, corner_ref, r0_ref, r2_ref, m1_ref, m2_ref, m4_ref, edge_ref, early_ref, sum_ref, out_ref, z_ref, w_ref
):
    @pl.when(core_ref[0] == 0)
    def _():
        fill(z_ref, [corner_ref[...], r0_ref[...]])
        fill(w_ref, blocks(m4_ref)[::-1])
        two = slice(0, 2 * W)
        pairs_of(z_ref.at[two], edge_ref, w_ref.at[two], adder(early_ref, out_ref))

    @pl.when(core_ref[0] != 0)
    def _():
        fill(z_ref, [m1_ref[...], m2_ref[...], m4_ref[:W, :]])
        fill(w_ref, blocks(r2_ref)[::-1] + [r0_ref[...]])
        pairs_of(z_ref, edge_ref, w_ref, adder(early_ref, sum_ref))


def proj_last_kernel(core_ref, corner_ref, r3_ref, edge_ref, sum_ref, done_ref, out_ref):
    @pl.when(core_ref[0] != 0)
    def _():
        pairs_of(corner_ref, edge_ref, r3_ref, adder(sum_ref, out_ref))


def edge_kernel(
    core_ref, corner_ref, r0_ref, r1_ref, r2_ref, r3_ref, m1_ref, m2_ref, m3_ref, m4_ref, edge_ref, turned_ref,
    out_ref, grad_ref, z_ref, w_ref,
):
    come = [r0_ref[...]] + blocks(r1_ref) + blocks(r2_ref)
    mate = [m1_ref[...], m2_ref[...]] + blocks(m3_ref) + blocks(m4_ref)

    @pl.when(core_ref[0] == 0)
    def _():
        fill(w_ref, [corner_ref[...]] + come)
        fill(z_ref, mate[::-1])

    @pl.when(core_ref[0] != 0)
    def _():
        fill(w_ref, [corner_ref[...]] + mate[:5])
        fill(z_ref, [r3_ref[...]] + come[::-1])

    def put(p, value):
        out_ref[:, W * p : W * (p + 1)] = value.T.astype(BF)

    pairs_of(z_ref, turned_ref, w_ref, put)
    grad_ref[...] = step(z_ref[:W, :], turned_ref, edge_ref).astype(F32).T.astype(BF)


def gather_kernel(parts_ref, out_ref):
    rows = parts_ref.shape[1]
    planes = parts_ref.shape[2] // W
    for p in range(planes):
        out_ref[pl.ds(p, rows, stride=planes), :] = jnp.sum(
            parts_ref[:, :, W * p : W * (p + 1)].astype(F32), axis=0
        )


def call(kernel, shapes, *args, scratch=(), flops=0, order=(), alias=None):
    def space(n, arg):
        if n in order:
            return pl.ANY
        return pltpu.SMEM if arg.dtype == jnp.int32 else pltpu.VMEM

    moved = sum(arg.size * arg.dtype.itemsize for n, arg in enumerate(args) if n not in order)
    single = len(shapes) == 1
    outs = [jax.ShapeDtypeStruct(shape, kind) for shape, kind in shapes]
    out_specs = [pl.BlockSpec(memory_space=pltpu.VMEM) for _ in shapes]
    return pl.pallas_call(
        kernel,
        out_shape=outs[0] if single else outs,
        in_specs=[pl.BlockSpec(memory_space=space(n, arg)) for n, arg in enumerate(args)],
        out_specs=out_specs[0] if single else out_specs,
        scratch_shapes=[pltpu.VMEM(shape, kind) for shape, kind in scratch],
        input_output_aliases=alias or {},
        compiler_params=pltpu.CompilerParams(vmem_limit_bytes=16 * 1024 * 1024),
        cost_estimate=pl.CostEstimate(flops=flops, bytes_accessed=moved, transcendentals=0),
    )(*args)


def shards(corners, edges, projectors, cotangent):
    corner = corners[0, 0]
    edge = edges[0, 0]
    projector = projectors[0]
    cot = cotangent[0, 0]
    width = edge.shape[1]
    rows = lax.axis_size("row")
    cols = lax.axis_size("col")
    core = (lax.axis_index("col") % 2).astype(jnp.int32).reshape(1)
    unit = 2 * W * W * width

    def send(value, to):
        pairs = [(i, to(i) % cols) for i in range(cols) if to(i) is not None]
        return lax.ppermute(value, "col", pairs)

    def swap(value):
        return send(value, lambda i: i ^ 1)

    def onward(value):
        return send(value, lambda i: i + 2 if i % 2 == 0 else i - 2)

    one, two = ((W, W), BF), ((2 * W, W), BF)
    whole, wide = ((W, width), BF), ((W, width), F32)

    def stacks(n):
        return [((n * W, W), BF), ((n * W, W), BF)]

    mate_edge = swap(edge)
    turned, cot_t = call(turn_kernel, [whole, one], projector, cot, scratch=[((width, W), F32)], flops=unit)
    mate_turned = swap(turned)
    keep, first = call(own_kernel, [one, one], core, corner, edge, turned, cot_t, flops=2 * unit)
    r0 = send(first, lambda i: i - 1 if i % 2 == 0 else i + 1)
    tensors = (edge, turned, mate_edge, mate_turned)
    ahead = call(ahead_kernel, [one], core, keep, mate_edge, mate_turned, flops=2 * unit)
    near1, go1 = call(single_kernel, [one, two], core, r0, ahead, *tensors, flops=4 * unit)
    r1 = onward(go1)
    m1, m2 = swap(keep), swap(near1)
    near2, go2 = call(double_kernel, [two, two], core, r1, *tensors, m1, m2, flops=8 * unit, order=(6, 7))
    r2 = onward(go2)
    m3 = swap(near2)
    early = call(proj_first_kernel, [wide], core, r1, m3, edge, scratch=stacks(2), flops=4 * unit)
    near3 = call(turn_back_kernel, [two], core, r2, edge, turned, early, flops=4 * unit, order=(4,))
    m4 = swap(near3)
    go3, early = call(
        proj_second_kernel, [one, wide], core, r2, m1, m2, near3, edge, mate_edge, mate_turned, early,
        scratch=stacks(2), flops=4 * unit, alias={8: 1},
    )
    r3 = send(go3, lambda i: None if i % 2 == 0 else i - 2)
    part, done = call(
        proj_third_kernel, [wide, whole], core, corner, r0, r2, m1, m2, m4, edge, early,
        scratch=stacks(3), flops=6 * unit, alias={8: 0},
    )
    done = call(proj_last_kernel, [whole], core, corner, r3, edge, part, done, flops=2 * unit, alias={5: 0})
    share = W // rows
    parts = lax.all_to_all(done.reshape(rows, share, width), "row", 0, 0, tiled=True)
    edge_grad, corner_grad = call(
        edge_kernel, [whole, one], core, corner, r0, r1, r2, r3, m1, m2, m3, m4, edge, turned,
        scratch=stacks(6), flops=14 * unit,
    )
    proj = call(gather_kernel, [((share * width // W, W), F32)], parts, flops=unit)
    return (corner_grad[None, None], edge_grad[None, None], proj[None])


def solution(mesh):
    placed = (
        P("row", "col", None, None),
        P("row", "col", None, None),
        P("col", None, None),
        P("row", "col", None, None),
    )
    return jax.shard_map(
        shards,
        mesh=mesh,
        in_specs=placed,
        out_specs=(P("row", "col", None, None), P("row", "col", None, None), P("col", "row", None)),
        check_vma=False,
    )
```

time: 77.6 us -> 75.2 us (0.969)
  waiting for transfers between devices: 14.9 us -> 2.09 us
  local copies, waits for them, and re-layouts: 2.19 us -> 12.4 us
  Pallas kernels: 31.9 us -> 28.1 us
  starting transfers between devices: 27.1 us -> 30.7 us
    unnamed x34 -> x50, local copies, waits for them, and re-layouts: 2.19 us -> 12.4 us
    all_to_all x1, waiting for transfers between devices: 10.2 us -> 0.01 us  [shards(): lax.all_to_all(done.reshape(rows, share, width), 'row', 0, 0, tiled=True)]
    pallas_call x10 -> x12, Pallas kernels: 31.9 us -> 28.1 us  [call(): pl.pallas_call(kernel, out_shape=outs[0] if single else outs, in_specs=[p...]
    ppermute x9 -> x10, starting transfers between devices: 22.8 us -> 26.5 us  [send(): return lax.ppermute(value, 'col', pairs)]
    ppermute x9 -> x10, waiting for transfers between devices: 4.77 us -> 2.09 us  [send(): return lax.ppermute(value, 'col', pairs)]
  transfers between devices with their start and end apart: 10 -> 11, of which waited for: 5 -> 3; matrix products, arithmetic and copies ran while one was open for 0% -> 0% of each run, Pallas kernels for 20% -> 22%
where the time goes in v2:
time: 75.2 us; the launch traced here: 74.1 us
  starting transfers between devices  30.7 us (41%)
  Pallas kernels  28.1 us (37%)
  local copies, waits for them, and re-layouts  12.4 us (16%)
  waiting for transfers between devices  2.09 us (3%)
  between operations  0.88 us (1%)
    pallas_call x12, Pallas kernels, call(): pl.pallas_call(kernel, out_shape=outs[0] if single else outs, in_specs=[p...  28.1 us
    ppermute x10, starting transfers between devices, send(): return lax.ppermute(value, 'col', pairs)  26.5 us
    unnamed x50, local copies, waits for them, and re-layouts  12.4 us
    all_to_all x1, starting transfers between devices, shards(): lax.all_to_all(done.reshape(rows, share, width), 'row', 0, 0, tiled=True)  4.22 us
    ppermute x10, waiting for transfers between devices, send(): return lax.ppermute(value, 'col', pairs)  2.09 us
  transfers between devices with their start and end apart: 11, of which 3 were waited for; matrix products, arithmetic and copies ran while one was open for 0% of the time, Pallas kernels for 22%

profile of v2, /device:TPU:1, one launch (start us, length us, event | category | flops | bytes accessed | tf_op | source)
XLA Modules:
  0.0 74.1 jit_solution(16035717912030471694)
XLA Ops:
  0.6 3.3 %collective-permute-start.1 = (bf16[128,4608]{1,0:T(8,128)(2,1)}, bf16[128,4608]{1,0:T(8,128)(2,1)S(1)}, u32[]{:S(2)}, u32[]{:S(2)}) collective-permute-start(bf16[128,4608]{1,0:T(8,128)(2,1)} %bitcast.9), channel_id=1, source_target_pairs={{0,1},{1,0},{2,3},{3,2},{4,5},{5,4},{6,7},{7,6},{8,9},{9,8},{10,11... | collective-permute-start | bytes 3538952 | tf_op jit(solution)/shard_map/ppermute | solution.py:251
  4.0 1.3 %copy-done.2 = bf16[1,4608,128]{2,1,0:T(8,128)(2,1)S(1)} copy-done((bf16[1,4608,128]{2,1,0:T(8,128)(2,1)S(1)}, bf16[1,4608,128]{2,1,0:T(8,128)(2,1)}, u32[]{:S(2)}) %copy-start.2) | copy-done | bytes 1179672
  5.2 0.8 %copy-done.24 = bf16[1,1,128,128]{3,2,1,0:T(8,128)(2,1)S(1)} copy-done((bf16[1,1,128,128]{3,2,1,0:T(8,128)(2,1)S(1)}, bf16[1,1,128,128]{3,2,1,0:T(8,128)(2,1)}, u32[]{:S(2)}) %copy-start.24) | copy-done | bytes 32792
  6.0 0.5 shard_map.67
  6.5 0.0 copy-start.20
  6.5 0.6 copy-done.20
  7.1 0.1 collective-permute-start.2
  7.2 0.8 %copy-done.5 = bf16[1,1,128,128]{3,2,1,0:T(8,128)(2,1)S(1)} copy-done((bf16[1,1,128,128]{3,2,1,0:T(8,128)(2,1)S(1)}, bf16[1,1,128,128]{3,2,1,0:T(8,128)(2,1)}, u32[]{:S(2)}) %copy-start.5) | copy-done | bytes 32792
  7.9 0.8 %copy-done.21 = bf16[128,128]{1,0:T(8,128)(2,1)S(1)} copy-done((bf16[128,128]{1,0:T(8,128)(2,1)S(1)}, bf16[128,128]{1,0:T(8,128)(2,1)}, u32[]{:S(2)}) %copy-start.21) | copy-done | bytes 32792
  8.7 1.0 %shard_map.68 = (bf16[128,128]{1,0:T(8,128)(2,1)S(1)}, bf16[128,128]{1,0:T(8,128)(2,1)S(1)}) custom-call(s32[1]{0:T(128)} %bitcast.core_ref, bf16[128,128]{1,0:T(8,128)(2,1)S(1)} %bitcast.21, bf16[128,4608]{1,0:T(8,128)(2,1)S(1)} %bitcast.10, bf16[128,4608]{1,0:T(8,128)(2,1)S(1)} %get-tuple-element.17.turned_ref.t_ref, bf16[128,128]{1,0:T(8,128)(2,1)S(1)} %copy-done.21), custom_call_target="tpu_custom_call" | custom-call | flops 301989888 | bytes 2424836 | tf_op jit(solution)/shard_map/pallas_call | solution.py:226
  9.7 1.4 %collective-permute-start = (bf16[128,128]{1,0:T(8,128)(2,1)S(1)}, bf16[128,128]{1,0:T(8,128)(2,1)S(1)}, u32[]{:S(2)}, u32[]{:S(2)}) collective-permute-start(bf16[128,128]{1,0:T(8,128)(2,1)S(1)} %get-tuple-element.19), channel_id=1, source_target_pairs={{0,31},{1,2},{2,1},{3,4},{4,3},{5,6},{6,5},{7,8},{8,7},{9,10},{10,... | collective-permute-start | bytes 98312 | tf_op jit(solution)/shard_map/ppermute | solution.py:251
  11.1 0.0 collective-permute-done.1.mate_edge_ref.me_ref
  11.2 0.0 collective-permute-done.2.mate_turned_ref.mt_ref
  11.2 2.3 %shard_map.69.ahead_ref = bf16[128,128]{1,0:T(8,128)(2,1)S(1)} custom-call(s32[1]{0:T(128)} %bitcast.core_ref, bf16[128,128]{1,0:T(8,128)(2,1)S(1)} %get-tuple-element.20.keep_ref, bf16[128,4608]{1,0:T(8,128)(2,1)S(1)} %collective-permute-done.1.mate_edge_ref.me_ref, bf16[128,4608]{1,0:T(8,128)(2,1)} %collective-permute-done.2.mate_turned_ref.mt_ref), custom_call_target="tpu_custom_call" | custom-call | flops 301989888 | bytes 2392068 | tf_op jit(solution)/shard_map/pallas_call | solution.py:226
  13.5 1.2 %collective-permute-done.come_ref.r0_ref = bf16[128,128]{1,0:T(8,128)(2,1)S(1)} collective-permute-done((bf16[128,128]{1,0:T(8,128)(2,1)S(1)}, bf16[128,128]{1,0:T(8,128)(2,1)S(1)}, u32[]{:S(2)}, u32[]{:S(2)}) %collective-permute-start) | collective-permute-done | bytes 32800 | tf_op jit(solution)/shard_map/ppermute | solution.py:251
  14.7 3.3 %shard_map.70 = (bf16[128,128]{1,0:T(8,128)(2,1)S(1)}, bf16[256,128]{1,0:T(8,128)(2,1)S(1)}) custom-call(s32[1]{0:T(128)} %bitcast.core_ref, bf16[128,128]{1,0:T(8,128)(2,1)S(1)} %collective-permute-done.come_ref.r0_ref, bf16[128,128]{1,0:T(8,128)(2,1)S(1)} %shard_map.69.ahead_ref, bf16[128,4608]{1,0:T(8,128)(2,1)S(1)} %bitcast.11, ...), custom_call_target="tpu_custom_call" | custom-call | flops 603979776 | bytes 4784132 | tf_op jit(solution)/shard_map/pallas_call | solution.py:226
  18.0 8.5 %collective-permute-start.3 = (bf16[256,128]{1,0:T(8,128)(2,1)S(1)}, bf16[256,128]{1,0:T(8,128)(2,1)S(1)}, u32[]{:S(2)}, u32[]{:S(2)}) collective-permute-start(bf16[256,128]{1,0:T(8,128)(2,1)S(1)} %get-tuple-element.21), channel_id=1, source_target_pairs={{0,2},{1,31},{2,4},{3,1},{4,6},{5,3},{6,8},{7,5},{8,10},{9,7},{10,... | collective-permute-start | bytes 196616 | tf_op jit(solution)/shard_map/ppermute | solution.py:251
  26.5 0.0 collective-permute-start.4
  26.5 0.5 collective-permute-start.5
  27.0 0.7 collective-permute-done.4.m1_ref
  27.7 0.2 collective-permute-done.5.m2_ref
  27.9 0.0 collective-permute-done.3.come_ref.r1_ref
  27.9 4.8 %shard_map.71 = (bf16[256,128]{1,0:T(8,128)(2,1)S(1)}, bf16[256,128]{1,0:T(8,128)(2,1)S(1)}) custom-call(s32[1]{0:T(128)} %bitcast.core_ref, bf16[256,128]{1,0:T(8,128)(2,1)S(1)} %collective-permute-done.3.come_ref.r1_ref, bf16[128,4608]{1,0:T(8,128)(2,1)S(1)} %bitcast.12, bf16[128,4608]{1,0:T(8,128)(2,1)S(1)} %get-tuple-element.17.turned_ref.t_ref, ...), custom_call_target="tpu_custom_call" | custom-call | flops 1207959552 | bytes 4784132 | tf_op jit(solution)/shard_map/pallas_call | solution.py:226
  32.7 2.4 %collective-permute-start.7 = (bf16[256,128]{1,0:T(8,128)(2,1)S(1)}, bf16[256,128]{1,0:T(8,128)(2,1)S(1)}, u32[]{:S(2)}, u32[]{:S(2)}) collective-permute-start(bf16[256,128]{1,0:T(8,128)(2,1)S(1)} %get-tuple-element.24), channel_id=1, source_target_pairs={{0,1},{1,0},{2,3},{3,2},{4,5},{5,4},{6,7},{7,6},{8,9},{9,8},{10,11... | collective-permute-start | bytes 196616 | tf_op jit(solution)/shard_map/ppermute | solution.py:251
  35.1 3.1 %collective-permute-start.6 = (bf16[256,128]{1,0:T(8,128)(2,1)S(1)}, bf16[256,128]{1,0:T(8,128)(2,1)S(1)}, u32[]{:S(2)}, u32[]{:S(2)}) collective-permute-start(bf16[256,128]{1,0:T(8,128)(2,1)S(1)} %get-tuple-element.23), channel_id=1, source_target_pairs={{0,2},{1,31},{2,4},{3,1},{4,6},{5,3},{6,8},{7,5},{8,10},{9,7},{10,... | collective-permute-start | bytes 196616 | tf_op jit(solution)/shard_map/ppermute | solution.py:251
  38.2 1.5 %shard_map.72.early_ref = f32[128,4608]{1,0:T(8,128)S(1)} custom-call(s32[1]{0:T(128)} %bitcast.core_ref, bf16[256,128]{1,0:T(8,128)(2,1)S(1)} %collective-permute-done.3.come_ref.r1_ref, bf16[256,128]{1,0:T(8,128)(2,1)S(1)} %collective-permute-done.7.m3_ref, bf16[128,4608]{1,0:T(8,128)(2,1)S(1)} %bitcast.13), custom_call_target="tpu_custom_call" | custom-call | flops 603979776 | bytes 1310724 | tf_op jit(solution)/shard_map/pallas_call | solution.py:226
  39.8 0.0 collective-permute-done.6.come_ref.r2_ref
  39.8 0.0 copy-start.3
  39.8 1.9 %shard_map.73.near_ref = bf16[256,128]{1,0:T(8,128)(2,1)S(1)} custom-call(s32[1]{0:T(128)} %bitcast.core_ref, bf16[256,128]{1,0:T(8,128)(2,1)S(1)} %collective-permute-done.6.come_ref.r2_ref, bf16[128,4608]{1,0:T(8,128)(2,1)S(1)} %bitcast.14, bf16[128,4608]{1,0:T(8,128)(2,1)S(1)} %get-tuple-element.17.turned_ref.t_ref, f32[128,4608]{1,0:T(8,128)S(1)} %shard_map.72.early_ref), custom_call_target="tpu_custom_call" | custom-call | flops 603979776 | bytes 2424836 | tf_op jit(solution)/shard_map/pallas_call | solution.py:226
  41.7 0.0 copy-start.6
  41.7 2.5 %collective-permute-start.9 = (bf16[256,128]{1,0:T(8,128)(2,1)S(1)}, bf16[256,128]{1,0:T(8,128)(2,1)S(1)}, u32[]{:S(2)}, u32[]{:S(2)}) collective-permute-start(bf16[256,128]{1,0:T(8,128)(2,1)S(1)} %shard_map.73.near_ref), channel_id=1, source_target_pairs={{0,1},{1,0},{2,3},{3,2},{4,5},{5,4},{6,7},{7,6},{8,9},{9,8},{10,11... | collective-permute-start | bytes 196616 | tf_op jit(solution)/shard_map/ppermute | solution.py:251
  44.2 2.3 %shard_map.74 = (bf16[128,128]{1,0:T(8,128)(2,1)S(1)}, f32[128,4608]{1,0:T(8,128)S(1)}) custom-call(s32[1]{0:T(128)} %bitcast.core_ref, bf16[256,128]{1,0:T(8,128)(2,1)S(1)} %collective-permute-done.6.come_ref.r2_ref, bf16[128,128]{1,0:T(8,128)(2,1)S(1)} %collective-permute-done.4.m1_ref, ...), custom_call_target="tpu_custom_call", output_to_operand_aliasing={{1}: (8, {})} | custom-call | flops 603979776 | bytes 6094852 | tf_op jit(solution)/shard_map/pallas_call | solution.py:226
  46.5 4.6 %collective-permute-start.8 = (bf16[128,128]{1,0:T(8,128)(2,1)S(1)}, bf16[128,128]{1,0:T(8,128)(2,1)S(1)}, u32[]{:S(2)}, u32[]{:S(2)}) collective-permute-start(bf16[128,128]{1,0:T(8,128)(2,1)S(1)} %get-tuple-element.25), channel_id=1, source_target_pairs={{1,31},{3,1},{5,3},{7,5},{9,7},{11,9},{13,11},{15,13},{17,15},{19,... | collective-permute-start | bytes 98312 | tf_op jit(solution)/shard_map/ppermute | solution.py:251
  51.2 2.3 %shard_map.76 = (f32[128,4608]{1,0:T(8,128)S(1)}, bf16[128,4608]{1,0:T(8,128)(2,1)S(1)}) custom-call(s32[1]{0:T(128)} %bitcast.core_ref, bf16[128,128]{1,0:T(8,128)(2,1)S(1)} %bitcast.22, bf16[128,128]{1,0:T(8,128)(2,1)S(1)} %collective-permute-done.come_ref.r0_ref, ...), custom_call_target="tpu_custom_call", output_to_operand_aliasing={{0}: (8, {})} | custom-call | flops 905969664 | bytes 3801092 | tf_op jit(solution)/shard_map/pallas_call | solution.py:226
  53.6 0.9 %shard_map.77 = bf16[128,4608]{1,0:T(8,128)(2,1)S(1)} custom-call(s32[1]{0:T(128)} %bitcast.core_ref, bf16[128,128]{1,0:T(8,128)(2,1)S(1)} %bitcast.23, bf16[128,128]{1,0:T(8,128)(2,1)S(1)} %collective-permute-done.8.r3_ref, bf16[128,4608]{1,0:T(8,128)(2,1)S(1)} %bitcast.17, ...), custom_call_target="tpu_custom_call", output_to_operand_aliasing={{}: (5, {})} | custom-call | flops 301989888 | bytes 4784132 | tf_op jit(solution)/shard_map/pallas_call | solution.py:226
  54.5 1.0 %copy-done.1 = bf16[128,4608]{1,0:T(8,128)(2,1)} copy-done((bf16[128,4608]{1,0:T(8,128)(2,1)}, bf16[128,4608]{1,0:T(8,128)(2,1)S(1)}, u32[]{:S(2)}) %copy-start.1) | copy-done | bytes 1179672
  55.6 4.2 %all-to-all-start = ((bf16[8,16,4608]{2,1,0:T(8,128)(2,1)}), bf16[8,16,4608]{2,1,0:T(8,128)(2,1)S(1)}, u32[]{:S(2)}, u32[]{:S(2)}) async-start(bf16[8,16,4608]{2,1,0:T(8,128)(2,1)} %bitcast.19), calls=%async_computation | async-start | bytes 2359296 | tf_op jit(solution)/shard_map/all_to_all | solution.py:292
  59.8 0.8 %copy-done.4 = bf16[256,128]{1,0:T(8,128)(2,1)S(1)} copy-done((bf16[256,128]{1,0:T(8,128)(2,1)S(1)}, bf16[256,128]{1,0:T(8,128)(2,1)}, u32[]{:S(2)}) %copy-start.4) | copy-done | bytes 65560
  60.6 0.8 %copy-done.7 = bf16[1,1,128,128]{3,2,1,0:T(8,128)(2,1)S(1)} copy-done((bf16[1,1,128,128]{3,2,1,0:T(8,128)(2,1)S(1)}, bf16[1,1,128,128]{3,2,1,0:T(8,128)(2,1)}, u32[]{:S(2)}) %copy-start.7) | copy-done | bytes 32792
  61.4 0.8 %copy-done.9 = bf16[128,128]{1,0:T(8,128)(2,1)S(1)} copy-done((bf16[128,128]{1,0:T(8,128)(2,1)S(1)}, bf16[128,128]{1,0:T(8,128)(2,1)}, u32[]{:S(2)}) %copy-start.9) | copy-done | bytes 32792
  62.1 0.8 %copy-done.11 = bf16[128,128]{1,0:T(8,128)(2,1)S(1)} copy-done((bf16[128,128]{1,0:T(8,128)(2,1)S(1)}, bf16[128,128]{1,0:T(8,128)(2,1)}, u32[]{:S(2)}) %copy-start.11) | copy-done | bytes 32792
  62.9 0.8 %copy-done.13 = bf16[256,128]{1,0:T(8,128)(2,1)S(1)} copy-done((bf16[256,128]{1,0:T(8,128)(2,1)S(1)}, bf16[256,128]{1,0:T(8,128)(2,1)}, u32[]{:S(2)}) %copy-start.13) | copy-done | bytes 65560
  63.7 0.8 %copy-done.15 = bf16[128,128]{1,0:T(8,128)(2,1)S(1)} copy-done((bf16[128,128]{1,0:T(8,128)(2,1)S(1)}, bf16[128,128]{1,0:T(8,128)(2,1)}, u32[]{:S(2)}) %copy-start.15) | copy-done | bytes 32792
  64.5 0.8 %copy-done.17 = bf16[256,128]{1,0:T(8,128)(2,1)S(1)} copy-done((bf16[256,128]{1,0:T(8,128)(2,1)S(1)}, bf16[256,128]{1,0:T(8,128)(2,1)}, u32[]{:S(2)}) %copy-start.17) | copy-done | bytes 65560
  65.3 0.8 %copy-done.19 = bf16[256,128]{1,0:T(8,128)(2,1)S(1)} copy-done((bf16[256,128]{1,0:T(8,128)(2,1)S(1)}, bf16[256,128]{1,0:T(8,128)(2,1)}, u32[]{:S(2)}) %copy-start.19) | copy-done | bytes 65560
  66.2 0.8 %copy-done.23 = bf16[128,128]{1,0:T(8,128)(2,1)S(1)} copy-done((bf16[128,128]{1,0:T(8,128)(2,1)S(1)}, bf16[128,128]{1,0:T(8,128)(2,1)}, u32[]{:S(2)}) %copy-start.23) | copy-done | bytes 32792
  66.9 6.3 %shard_map.75 = (bf16[128,4608]{1,0:T(8,128)(2,1)}, bf16[128,128]{1,0:T(8,128)(2,1)}) custom-call(s32[1]{0:T(128)} %bitcast.core_ref, bf16[128,128]{1,0:T(8,128)(2,1)S(1)} %bitcast.24, bf16[128,128]{1,0:T(8,128)(2,1)S(1)} %copy-done.15, bf16[256,128]{1,0:T(8,128)(2,1)S(1)} %copy-done.13, bf16[256,128]{1,0:T(8,128)(2,1)S(1)} %copy-done.4, ...), custom_call_target="tpu_custom_call" | custom-call | flops 2113929216 | bytes 2785284 | tf_op jit(solution)/shard_map/pallas_call | solution.py:226
  73.2 0.9 %shard_map.78 = f32[576,128]{1,0:T(8,128)} custom-call(bf16[8,16,4608]{2,1,0:T(8,128)(2,1)S(1)} %all-to-all-done.parts_ref), custom_call_target="tpu_custom_call" | custom-call | flops 150994944 | bytes 1179648 | tf_op jit(solution)/shard_map/pallas_call | solution.py:226
  (36 shorter events, 0.1 us)
Async XLA Ops:
  0.6 6.6 %copy-start = (bf16[1,1,128,4608]{3,2,1,0:T(8,128)(2,1)S(1)}, bf16[1,1,128,4608]{3,2,1,0:T(8,128)(2,1)}, u32[]{:S(2)}) copy-start(bf16[1,1,128,4608]{3,2,1,0:T(8,128)(2,1)} %param.5) | copy-start | bytes 3538948
  0.6 10.5 %collective-permute-start.1 = (bf16[128,4608]{1,0:T(8,128)(2,1)}, bf16[128,4608]{1,0:T(8,128)(2,1)S(1)}, u32[]{:S(2)}, u32[]{:S(2)}) collective-permute-start(bf16[128,4608]{1,0:T(8,128)(2,1)} %bitcast.9), channel_id=1, source_target_pairs={{0,1},{1,0},{2,3},{3,2},{4,5},{5,4},{6,7},{7,6},{8,9},{9,8},{10,11... | collective-permute-start | bytes 3538952 | tf_op jit(solution)/shard_map/ppermute | solution.py:251
  4.0 1.3 %copy-start.2 = (bf16[1,4608,128]{2,1,0:T(8,128)(2,1)S(1)}, bf16[1,4608,128]{2,1,0:T(8,128)(2,1)}, u32[]{:S(2)}) copy-start(bf16[1,4608,128]{2,1,0:T(8,128)(2,1)} %param.6) | copy-start | bytes 3538948
  5.2 0.8 %copy-start.24 = (bf16[1,1,128,128]{3,2,1,0:T(8,128)(2,1)S(1)}, bf16[1,1,128,128]{3,2,1,0:T(8,128)(2,1)}, u32[]{:S(2)}) copy-start(bf16[1,1,128,128]{3,2,1,0:T(8,128)(2,1)} %param.7) | copy-start | bytes 98308
  6.5 0.6 copy-start.20
  7.1 4.1 %collective-permute-start.2 = (bf16[128,4608]{1,0:T(8,128)(2,1)S(1)}, bf16[128,4608]{1,0:T(8,128)(2,1)}, u32[]{:S(2)}, u32[]{:S(2)}) collective-permute-start(bf16[128,4608]{1,0:T(8,128)(2,1)S(1)} %get-tuple-element.17.turned_ref.t_ref), channel_id=1, source_target_pairs={{0,1},{1,0},{2,3},{3,2},{4,5},{5,4},{6,7},{7,6},{8,9},{9,8},{10,11... | collective-permute-start | bytes 3538952 | tf_op jit(solution)/shard_map/ppermute | solution.py:251
  7.2 0.8 %copy-start.5 = (bf16[1,1,128,128]{3,2,1,0:T(8,128)(2,1)S(1)}, bf16[1,1,128,128]{3,2,1,0:T(8,128)(2,1)}, u32[]{:S(2)}) copy-start(bf16[1,1,128,128]{3,2,1,0:T(8,128)(2,1)} %param.4) | copy-start | bytes 98308
  7.9 0.8 %copy-start.21 = (bf16[128,128]{1,0:T(8,128)(2,1)S(1)}, bf16[128,128]{1,0:T(8,128)(2,1)}, u32[]{:S(2)}) copy-start(bf16[128,128]{1,0:T(8,128)(2,1)} %copy-done.20) | copy-start | bytes 98308
  9.7 4.9 %collective-permute-start = (bf16[128,128]{1,0:T(8,128)(2,1)S(1)}, bf16[128,128]{1,0:T(8,128)(2,1)S(1)}, u32[]{:S(2)}, u32[]{:S(2)}) collective-permute-start(bf16[128,128]{1,0:T(8,128)(2,1)S(1)} %get-tuple-element.19), channel_id=1, source_target_pairs={{0,31},{1,2},{2,1},{3,4},{4,3},{5,6},{6,5},{7,8},{8,7},{9,10},{10,... | collective-permute-start | bytes 98312 | tf_op jit(solution)/shard_map/ppermute | solution.py:251
  14.7 36.5 %copy-start.14 = (bf16[128,128]{1,0:T(8,128)(2,1)}, bf16[128,128]{1,0:T(8,128)(2,1)S(1)}, u32[]{:S(2)}) copy-start(bf16[128,128]{1,0:T(8,128)(2,1)S(1)} %collective-permute-done.come_ref.r0_ref) | copy-start | bytes 98308
  18.0 9.9 %collective-permute-start.3 = (bf16[256,128]{1,0:T(8,128)(2,1)S(1)}, bf16[256,128]{1,0:T(8,128)(2,1)S(1)}, u32[]{:S(2)}, u32[]{:S(2)}) collective-permute-start(bf16[256,128]{1,0:T(8,128)(2,1)S(1)} %get-tuple-element.21), channel_id=1, source_target_pairs={{0,2},{1,31},{2,4},{3,1},{4,6},{5,3},{6,8},{7,5},{8,10},{9,7},{10,... | collective-permute-start | bytes 196616 | tf_op jit(solution)/shard_map/ppermute | solution.py:251
  26.5 1.2 %collective-permute-start.4 = (bf16[128,128]{1,0:T(8,128)(2,1)S(1)}, bf16[128,128]{1,0:T(8,128)(2,1)S(1)}, u32[]{:S(2)}, u32[]{:S(2)}) collective-permute-start(bf16[128,128]{1,0:T(8,128)(2,1)S(1)} %get-tuple-element.20.keep_ref), channel_id=1, source_target_pairs={{0,1},{1,0},{2,3},{3,2},{4,5},{5,4},{6,7},{7,6},{8,9},{9,8},{10,11... | collective-permute-start | bytes 98312 | tf_op jit(solution)/shard_map/ppermute | solution.py:251
  26.5 1.4 %collective-permute-start.5 = (bf16[128,128]{1,0:T(8,128)(2,1)S(1)}, bf16[128,128]{1,0:T(8,128)(2,1)S(1)}, u32[]{:S(2)}, u32[]{:S(2)}) collective-permute-start(bf16[128,128]{1,0:T(8,128)(2,1)S(1)} %get-tuple-element.22), channel_id=1, source_target_pairs={{0,1},{1,0},{2,3},{3,2},{4,5},{5,4},{6,7},{7,6},{8,9},{9,8},{10,11... | collective-permute-start | bytes 98312 | tf_op jit(solution)/shard_map/ppermute | solution.py:251
  27.7 23.5 %copy-start.8 = (bf16[128,128]{1,0:T(8,128)(2,1)}, bf16[128,128]{1,0:T(8,128)(2,1)S(1)}, u32[]{:S(2)}) copy-start(bf16[128,128]{1,0:T(8,128)(2,1)S(1)} %collective-permute-done.4.m1_ref) | copy-start | bytes 98308
  27.8 23.4 %copy-start.10 = (bf16[128,128]{1,0:T(8,128)(2,1)}, bf16[128,128]{1,0:T(8,128)(2,1)S(1)}, u32[]{:S(2)}) copy-start(bf16[128,128]{1,0:T(8,128)(2,1)S(1)} %collective-permute-done.5.m2_ref) | copy-start | bytes 98308
  27.9 10.4 %copy-start.12 = (bf16[256,128]{1,0:T(8,128)(2,1)}, bf16[256,128]{1,0:T(8,128)(2,1)S(1)}, u32[]{:S(2)}) copy-start(bf16[256,128]{1,0:T(8,128)(2,1)S(1)} %collective-permute-done.3.come_ref.r1_ref) | copy-start | bytes 196612
  32.7 5.5 %collective-permute-start.7 = (bf16[256,128]{1,0:T(8,128)(2,1)S(1)}, bf16[256,128]{1,0:T(8,128)(2,1)S(1)}, u32[]{:S(2)}, u32[]{:S(2)}) collective-permute-start(bf16[256,128]{1,0:T(8,128)(2,1)S(1)} %get-tuple-element.24), channel_id=1, source_target_pairs={{0,1},{1,0},{2,3},{3,2},{4,5},{5,4},{6,7},{7,6},{8,9},{9,8},{10,11... | collective-permute-start | bytes 196616 | tf_op jit(solution)/shard_map/ppermute | solution.py:251
  35.1 4.7 %collective-permute-start.6 = (bf16[256,128]{1,0:T(8,128)(2,1)S(1)}, bf16[256,128]{1,0:T(8,128)(2,1)S(1)}, u32[]{:S(2)}, u32[]{:S(2)}) collective-permute-start(bf16[256,128]{1,0:T(8,128)(2,1)S(1)} %get-tuple-element.23), channel_id=1, source_target_pairs={{0,2},{1,31},{2,4},{3,1},{4,6},{5,3},{6,8},{7,5},{8,10},{9,7},{10,... | collective-permute-start | bytes 196616 | tf_op jit(solution)/shard_map/ppermute | solution.py:251
  38.2 1.6 %copy-start.16 = (bf16[256,128]{1,0:T(8,128)(2,1)}, bf16[256,128]{1,0:T(8,128)(2,1)S(1)}, u32[]{:S(2)}) copy-start(bf16[256,128]{1,0:T(8,128)(2,1)S(1)} %collective-permute-done.7.m3_ref) | copy-start | bytes 196612
  39.8 11.4 %copy-start.3 = (bf16[256,128]{1,0:T(8,128)(2,1)}, bf16[256,128]{1,0:T(8,128)(2,1)S(1)}, u32[]{:S(2)}) copy-start(bf16[256,128]{1,0:T(8,128)(2,1)S(1)} %collective-permute-done.6.come_ref.r2_ref) | copy-start | bytes 196612
  41.7 9.5 %copy-start.6 = (bf16[1,1,128,128]{3,2,1,0:T(8,128)(2,1)S(1)}, bf16[1,1,128,128]{3,2,1,0:T(8,128)(2,1)}, u32[]{:S(2)}) copy-start(bf16[1,1,128,128]{3,2,1,0:T(8,128)(2,1)} %param.4) | copy-start | bytes 98308
  41.7 9.5 %collective-permute-start.9 = (bf16[256,128]{1,0:T(8,128)(2,1)S(1)}, bf16[256,128]{1,0:T(8,128)(2,1)S(1)}, u32[]{:S(2)}, u32[]{:S(2)}) collective-permute-start(bf16[256,128]{1,0:T(8,128)(2,1)S(1)} %shard_map.73.near_ref), channel_id=1, source_target_pairs={{0,1},{1,0},{2,3},{3,2},{4,5},{5,4},{6,7},{7,6},{8,9},{9,8},{10,11... | collective-permute-start | bytes 196616 | tf_op jit(solution)/shard_map/ppermute | solution.py:251
  46.5 7.1 %collective-permute-start.8 = (bf16[128,128]{1,0:T(8,128)(2,1)S(1)}, bf16[128,128]{1,0:T(8,128)(2,1)S(1)}, u32[]{:S(2)}, u32[]{:S(2)}) collective-permute-start(bf16[128,128]{1,0:T(8,128)(2,1)S(1)} %get-tuple-element.25), channel_id=1, source_target_pairs={{1,31},{3,1},{5,3},{7,5},{9,7},{11,9},{13,11},{15,13},{17,15},{19,... | collective-permute-start | bytes 98312 | tf_op jit(solution)/shard_map/ppermute | solution.py:251
  51.2 2.4 %copy-start.18 = (bf16[256,128]{1,0:T(8,128)(2,1)}, bf16[256,128]{1,0:T(8,128)(2,1)S(1)}, u32[]{:S(2)}) copy-start(bf16[256,128]{1,0:T(8,128)(2,1)S(1)} %collective-permute-done.9.m4_ref) | copy-start | bytes 196612
  53.6 0.9 %copy-start.22 = (bf16[128,128]{1,0:T(8,128)(2,1)}, bf16[128,128]{1,0:T(8,128)(2,1)S(1)}, u32[]{:S(2)}) copy-start(bf16[128,128]{1,0:T(8,128)(2,1)S(1)} %collective-permute-done.8.r3_ref) | copy-start | bytes 98308
  54.5 1.0 %copy-start.1 = (bf16[128,4608]{1,0:T(8,128)(2,1)}, bf16[128,4608]{1,0:T(8,128)(2,1)S(1)}, u32[]{:S(2)}) copy-start(bf16[128,4608]{1,0:T(8,128)(2,1)S(1)} %shard_map.77) | copy-start | bytes 3538948
  55.6 17.7 %all-to-all-start = ((bf16[8,16,4608]{2,1,0:T(8,128)(2,1)}), bf16[8,16,4608]{2,1,0:T(8,128)(2,1)S(1)}, u32[]{:S(2)}, u32[]{:S(2)}) async-start(bf16[8,16,4608]{2,1,0:T(8,128)(2,1)} %bitcast.19), calls=%async_computation | async-start | bytes 2359296 | tf_op jit(solution)/shard_map/all_to_all | solution.py:292
  59.8 0.8 %copy-start.4 = (bf16[256,128]{1,0:T(8,128)(2,1)S(1)}, bf16[256,128]{1,0:T(8,128)(2,1)}, u32[]{:S(2)}) copy-start(bf16[256,128]{1,0:T(8,128)(2,1)} %copy-done.3) | copy-start | bytes 196612
  60.6 0.8 %copy-start.7 = (bf16[1,1,128,128]{3,2,1,0:T(8,128)(2,1)S(1)}, bf16[1,1,128,128]{3,2,1,0:T(8,128)(2,1)}, u32[]{:S(2)}) copy-start(bf16[1,1,128,128]{3,2,1,0:T(8,128)(2,1)} %param.4) | copy-start | bytes 98308
  61.4 0.8 %copy-start.9 = (bf16[128,128]{1,0:T(8,128)(2,1)S(1)}, bf16[128,128]{1,0:T(8,128)(2,1)}, u32[]{:S(2)}) copy-start(bf16[128,128]{1,0:T(8,128)(2,1)} %copy-done.8) | copy-start | bytes 98308
  62.1 0.8 %copy-start.11 = (bf16[128,128]{1,0:T(8,128)(2,1)S(1)}, bf16[128,128]{1,0:T(8,128)(2,1)}, u32[]{:S(2)}) copy-start(bf16[128,128]{1,0:T(8,128)(2,1)} %copy-done.10) | copy-start | bytes 98308
  62.9 0.8 %copy-start.13 = (bf16[256,128]{1,0:T(8,128)(2,1)S(1)}, bf16[256,128]{1,0:T(8,128)(2,1)}, u32[]{:S(2)}) copy-start(bf16[256,128]{1,0:T(8,128)(2,1)} %copy-done.12) | copy-start | bytes 196612
  63.7 0.8 %copy-start.15 = (bf16[128,128]{1,0:T(8,128)(2,1)S(1)}, bf16[128,128]{1,0:T(8,128)(2,1)}, u32[]{:S(2)}) copy-start(bf16[128,128]{1,0:T(8,128)(2,1)} %copy-done.14) | copy-start | bytes 98308
  64.5 0.8 %copy-start.17 = (bf16[256,128]{1,0:T(8,128)(2,1)S(1)}, bf16[256,128]{1,0:T(8,128)(2,1)}, u32[]{:S(2)}) copy-start(bf16[256,128]{1,0:T(8,128)(2,1)} %copy-done.16) | copy-start | bytes 196612
  65.3 0.8 %copy-start.19 = (bf16[256,128]{1,0:T(8,128)(2,1)S(1)}, bf16[256,128]{1,0:T(8,128)(2,1)}, u32[]{:S(2)}) copy-start(bf16[256,128]{1,0:T(8,128)(2,1)} %copy-done.18) | copy-start | bytes 196612
  66.2 0.8 %copy-start.23 = (bf16[128,128]{1,0:T(8,128)(2,1)S(1)}, bf16[128,128]{1,0:T(8,128)(2,1)}, u32[]{:S(2)}) copy-start(bf16[128,128]{1,0:T(8,128)(2,1)} %copy-done.22) | copy-start | bytes 98308

commit v3 on v2

v3 whole, which is shorter than its diff:
```python
import jax
import jax.numpy as jnp
from jax import lax
from jax.experimental import pallas as pl
from jax.experimental.pallas import tpu as pltpu
from jax.sharding import PartitionSpec as P


W = 128
BF = jnp.bfloat16
F32 = jnp.float32


def dot(a, b):
    return jnp.dot(a, b, preferred_element_type=F32)


def step(z, x_ref, y_ref):
    n = z.shape[0] // W
    total = None
    for t in range(x_ref.shape[1] // (2 * W)):
        cols = slice(2 * W * t, 2 * W * (t + 1))
        mid = dot(z, x_ref[:, cols]).astype(BF)
        tall = jnp.concatenate(
            [jnp.concatenate([mid[W * b : W * (b + 1), :W], mid[W * b : W * (b + 1), W:]], 0) for b in range(n)], 1
        )
        part = dot(y_ref[:, cols], tall)
        total = part if total is None else total + part
    return total.astype(BF)


def split(wide):
    return [wide[:, W * b : W * (b + 1)] for b in range(wide.shape[1] // W)]


def start_kernel(
    core_ref, proj_ref, edge_ref, corner_ref, cot_ref, turned_ref, keep_ref, send_ref,
    proj_in, wide_ref, edge_in, corner_in, cot_in, proj_sem, sem,
):
    pieces = proj_sem.shape[0]
    size = proj_ref.shape[0] // pieces
    loads = []
    for n in range(pieces):
        at = pl.ds(n * size, size)
        loads.append(pltpu.make_async_copy(proj_ref.at[at], proj_in.at[at], proj_sem.at[n]))
    others = [
        pltpu.make_async_copy(cot_ref, cot_in, sem.at[0]),
        pltpu.make_async_copy(corner_ref, corner_in, sem.at[1]),
        pltpu.make_async_copy(edge_ref, edge_in, sem.at[2]),
    ]
    for copy in loads + others:
        copy.start()
    for n, copy in enumerate(loads):
        copy.wait()
        at = slice(n * size, (n + 1) * size)
        wide_ref[at, :] = proj_in[at, :].astype(F32)
    planes = turned_ref.shape[1] // W
    for p in range(planes):
        turned_ref[:, W * p : W * (p + 1)] = wide_ref[pl.ds(p, W, stride=planes), :].T.astype(BF)
    for copy in others:
        copy.wait()
    cot_t = cot_in[...].astype(F32).T.astype(BF)
    moved = step(corner_in[...], edge_in, turned_ref)
    keep_ref[...] = jnp.where(core_ref[0] == 0, moved, cot_t)
    send_ref[...] = jnp.where(core_ref[0] == 0, cot_t, moved)


def by_role(core_ref, body, tensors):
    edge, turned, mate_edge, mate_turned = tensors

    @pl.when(core_ref[0] == 0)
    def _():
        body(edge, turned, mate_edge, mate_turned)

    @pl.when(core_ref[0] != 0)
    def _():
        body(turned, edge, mate_turned, mate_edge)


def ahead_kernel(core_ref, keep_ref, far_edge_ref, far_turned_ref, out_ref, mate_edge_ref, mate_turned_ref, sem):
    copies = [
        pltpu.make_async_copy(far_edge_ref, mate_edge_ref, sem.at[0]),
        pltpu.make_async_copy(far_turned_ref, mate_turned_ref, sem.at[1]),
    ]
    for copy in copies:
        copy.start()
    for copy in copies:
        copy.wait()

    def body(x1, y1, x2, y2):
        out_ref[...] = step(keep_ref[...], x2, y2)

    by_role(core_ref, body, (None, None, mate_edge_ref, mate_turned_ref))


def single_kernel(core_ref, come_ref, ahead_ref, e_ref, t_ref, me_ref, mt_ref, near_ref, far_ref):
    far_ref[:W, :] = ahead_ref[...]

    def body(x1, y1, x2, y2):
        near = step(come_ref[...], x1, y1)
        near_ref[...] = near
        far_ref[W:, :] = step(near, x2, y2)

    by_role(core_ref, body, (e_ref, t_ref, me_ref, mt_ref))


def double_kernel(core_ref, come_ref, e_ref, t_ref, me_ref, mt_ref, m1_ref, m2_ref, near_ref, far_ref):
    def body(x1, y1, x2, y2):
        near = jnp.concatenate(split(step(come_ref[...], x1, y1)), 0)
        near_ref[...] = near
        far_ref[...] = jnp.concatenate(split(step(near, x2, y2)), 0)

    by_role(core_ref, body, (e_ref, t_ref, me_ref, mt_ref))


def turn_back_kernel(core_ref, come_ref, e_ref, t_ref, me_ref, mt_ref, early_ref, near_ref, far_ref):
    @pl.when(core_ref[0] == 0)
    def _():
        near_ref[...] = step(come_ref[:W, :], e_ref, t_ref)
        far_ref[...] = jnp.zeros_like(far_ref)

    @pl.when(core_ref[0] != 0)
    def _():
        near = step(come_ref[:W, :], t_ref, e_ref)
        near_ref[...] = near
        far_ref[...] = step(near, mt_ref, me_ref)


def blocks(ref):
    return [ref[W * b : W * (b + 1), :] for b in range(ref.shape[0] // W)]


def fill(ref, parts):
    for b, part in enumerate(parts):
        ref[W * b : W * (b + 1), :] = part


def pairs_of(z_ref, x_ref, w_ref, put):
    n = z_ref.shape[0] // W
    for t in range(x_ref.shape[1] // (2 * W)):
        mid = dot(z_ref[...], x_ref[:, 2 * W * t : 2 * W * (t + 1)]).astype(BF)
        for half in range(2):
            flat = jnp.concatenate([mid[W * k : W * (k + 1), W * half : W * (half + 1)] for k in range(n)], 1)
            put(2 * t + half, dot(flat, w_ref[...]))


def proj_first_kernel(core_ref, r1_ref, m3_ref, edge_ref, out_ref, z_ref, w_ref):
    r1, m3 = blocks(r1_ref), blocks(m3_ref)

    @pl.when(core_ref[0] == 0)
    def _():
        fill(z_ref, r1)
        fill(w_ref, m3[::-1])

    @pl.when(core_ref[0] != 0)
    def _():
        fill(z_ref, m3)
        fill(w_ref, r1[::-1])

    def put(p, value):
        out_ref[:, W * p : W * (p + 1)] = value

    pairs_of(z_ref, edge_ref, w_ref, put)


def adder(from_ref, to_ref):
    def put(p, value):
        at = slice(W * p, W * (p + 1))
        to_ref[:, at] = (from_ref[:, at] + value).astype(to_ref.dtype)

    return put


def proj_second_kernel(
    core_ref, r0_ref, r2_ref, m1_ref, m2_ref, m4_ref, edge_ref, turned_ref, early_ref, near_ref, out_ref, z_ref, w_ref
):
    @pl.when(core_ref[0] == 0)
    def _():
        fill(z_ref, blocks(r2_ref) + [r0_ref[...]])
        fill(w_ref, [m2_ref[...], m1_ref[...], m4_ref[...]])
        pairs_of(z_ref, edge_ref, w_ref, adder(early_ref, out_ref))
        near_ref[...] = jnp.zeros_like(near_ref)

    @pl.when(core_ref[0] != 0)
    def _():
        near_ref[...] = step(r2_ref[W:, :], turned_ref, edge_ref)


def finish(z_ref, edge_ref, w_ref, sum_ref, out_ref, stage_ref, sem):
    pieces = sem.shape[0]
    planes = edge_ref.shape[1] // W
    each = planes // pieces
    add = adder(sum_ref, stage_ref)
    copies = []

    def put(p, value):
        add(p, value)
        if (p + 1) % each == 0:
            at = pl.ds(W * (p + 1 - each), W * each)
            copies.append(pltpu.make_async_copy(stage_ref.at[:, at], out_ref.at[:, at], sem.at[p // each]))
            copies[-1].start()

    pairs_of(z_ref, edge_ref, w_ref, put)
    for copy in copies:
        copy.wait()


def proj_third_kernel(
    core_ref, corner_ref, r0_ref, r2_ref, m1_ref, m2_ref, m4_ref, m5_ref, edge_ref, early_ref, sum_ref, out_ref,
    z_ref, w_ref, stage_ref, sem,
):
    @pl.when(core_ref[0] == 0)
    def _():
        finish(corner_ref, edge_ref, m5_ref, early_ref, out_ref, stage_ref, sem)

    @pl.when(core_ref[0] != 0)
    def _():
        fill(z_ref, [m1_ref[...], m2_ref[...], m4_ref[...]])
        fill(w_ref, blocks(r2_ref)[::-1] + [r0_ref[...]])
        pairs_of(z_ref, edge_ref, w_ref, adder(early_ref, sum_ref))


def proj_last_kernel(core_ref, corner_ref, r3_ref, edge_ref, sum_ref, done_ref, out_ref, stage_ref, sem):
    @pl.when(core_ref[0] != 0)
    def _():
        finish(corner_ref, edge_ref, r3_ref, sum_ref, out_ref, stage_ref, sem)


def edge_kernel(
    core_ref, corner_ref, r0_ref, r1_ref, r2_ref, r3_ref, m1_ref, m2_ref, m3_ref, m4_ref, m5_ref, edge_ref, turned_ref,
    out_ref, grad_ref, z_ref, w_ref, sem,
):
    def halves(ref):
        return [ref.at[pl.ds(0, W)], ref.at[pl.ds(W, W)]]

    come = [r0_ref] + halves(r1_ref) + halves(r2_ref)
    mate = [m1_ref, m2_ref] + halves(m3_ref) + [m4_ref, m5_ref]

    def fetch(z_parts, w_parts):
        copies = []
        for n, part in enumerate(z_parts + w_parts):
            k = n % len(z_parts)
            to = z_ref if n < len(z_parts) else w_ref
            copies.append(pltpu.make_async_copy(part, to.at[pl.ds(W * k, W)], sem.at[n]))
        for copy in copies:
            copy.start()
        for copy in copies:
            copy.wait()

    @pl.when(core_ref[0] == 0)
    def _():
        fetch(mate[::-1], [corner_ref] + come)

    @pl.when(core_ref[0] != 0)
    def _():
        fetch([r3_ref] + come[::-1], [corner_ref] + mate[:5])

    def put(p, value):
        out_ref[:, W * p : W * (p + 1)] = value.T.astype(BF)

    pairs_of(z_ref, turned_ref, w_ref, put)
    grad_ref[...] = step(z_ref[:W, :], turned_ref, edge_ref).astype(F32).T.astype(BF)


def gather_kernel(parts_ref, out_ref):
    rows = parts_ref.shape[1]
    planes = parts_ref.shape[2] // W
    for p in range(planes):
        out_ref[pl.ds(p, rows, stride=planes), :] = jnp.sum(
            parts_ref[:, :, W * p : W * (p + 1)].astype(F32), axis=0
        )


def call(kernel, shapes, *args, scratch=(), sems=(), flops=0, far=(), free=(), far_outs=(), alias=None):
    def spec(n, arg):
        if n in far or n in free:
            return pl.BlockSpec(memory_space=pl.ANY)
        return pl.BlockSpec(memory_space=pltpu.SMEM if arg.dtype == jnp.int32 else pltpu.VMEM)

    moved = sum(arg.size * arg.dtype.itemsize for arg in args)
    single = len(shapes) == 1
    outs = [
        pltpu.HBM(shape, kind) if n in far_outs else jax.ShapeDtypeStruct(shape, kind)
        for n, (shape, kind) in enumerate(shapes)
    ]
    out_specs = [pl.BlockSpec(memory_space=pl.ANY if n in far_outs else pltpu.VMEM) for n in range(len(shapes))]
    in_specs = [spec(n, arg) for n, arg in enumerate(args)]
    args = [pltpu.with_memory_space_constraint(arg, pltpu.HBM) if n in far else arg for n, arg in enumerate(args)]
    return pl.pallas_call(
        kernel,
        out_shape=outs[0] if single else outs,
        in_specs=in_specs,
        out_specs=out_specs[0] if single else out_specs,
        scratch_shapes=[pltpu.VMEM(shape, kind) for shape, kind in scratch]
        + [pltpu.SemaphoreType.DMA((count,)) for count in sems],
        input_output_aliases=alias or {},
        compiler_params=pltpu.CompilerParams(vmem_limit_bytes=16 * 1024 * 1024),
        cost_estimate=pl.CostEstimate(flops=flops, bytes_accessed=moved, transcendentals=0),
    )(*args)


def shards(corners, edges, projectors, cotangent):
    corner = corners[0, 0]
    edge = edges[0, 0]
    projector = projectors[0]
    cot = cotangent[0, 0]
    width = edge.shape[1]
    rows = lax.axis_size("row")
    cols = lax.axis_size("col")
    core = (lax.axis_index("col") % 2).astype(jnp.int32).reshape(1)
    unit = 2 * W * W * width

    def send(value, to):
        pairs = [(i, to(i) % cols) for i in range(cols) if to(i) is not None]
        return lax.ppermute(value, "col", pairs)

    def swap(value):
        return send(value, lambda i: i ^ 1)

    def onward(value):
        return send(value, lambda i: i + 2 if i % 2 == 0 else i - 2)

    one, two = ((W, W), BF), ((2 * W, W), BF)
    whole, wide = ((W, width), BF), ((W, width), F32)

    def stacks(n):
        return [((n * W, W), BF), ((n * W, W), BF)]

    far_edge = swap(edge)
    turned, keep, first = call(
        start_kernel, [whole, one, one], core, projector, edge, corner, cot,
        scratch=[((width, W), BF), ((width, W), F32), ((W, width), BF), ((W, W), BF), ((W, W), BF)], sems=(4, 3),
        flops=2 * unit, far=(1, 2, 3, 4),
    )
    r0 = send(first, lambda i: i - 1 if i % 2 == 0 else i + 1)
    far_turned = swap(turned)
    ahead, mate_edge, mate_turned = call(
        ahead_kernel, [one, whole, whole], core, keep, far_edge, far_turned, sems=(2,), flops=2 * unit, free=(2, 3)
    )
    tensors = (edge, turned, mate_edge, mate_turned)
    near1, go1 = call(single_kernel, [one, two], core, r0, ahead, *tensors, flops=4 * unit)
    r1 = onward(go1)
    m1, m2 = swap(keep), swap(near1)
    near2, go2 = call(double_kernel, [two, two], core, r1, *tensors, m1, m2, flops=8 * unit)
    r2 = onward(go2)
    m3 = swap(near2)
    early = call(proj_first_kernel, [wide], core, r1, m3, edge, scratch=stacks(2), flops=0)
    near3, go3 = call(turn_back_kernel, [one, one], core, r2, *tensors, early, flops=4 * unit)
    r3 = send(go3, lambda i: None if i % 2 == 0 else i - 2)
    m4 = swap(near3)
    near4, early = call(
        proj_second_kernel, [one, wide], core, r0, r2, m1, m2, m4, edge, turned, early,
        scratch=stacks(3), flops=6 * unit, alias={8: 1},
    )
    m5 = send(near4, lambda i: None if i % 2 == 0 else i - 1)
    part, done = call(
        proj_third_kernel, [wide, whole], core, corner, r0, r2, m1, m2, m4, m5, edge, early,
        scratch=stacks(3) + [whole], sems=(6,), flops=6 * unit, far_outs=(1,), alias={9: 0},
    )
    done = call(
        proj_last_kernel, [whole], core, corner, r3, edge, part, done,
        scratch=[whole], sems=(6,), flops=2 * unit, free=(5,), far_outs=(0,), alias={5: 0},
    )
    share = W // rows
    parts = lax.all_to_all(done.reshape(rows, share, width), "row", 0, 0, tiled=True)
    edge_grad, corner_grad = call(
        edge_kernel, [whole, one], core, corner, r0, r1, r2, r3, m1, m2, m3, m4, m5, edge, turned,
        scratch=stacks(6), sems=(12,), flops=14 * unit, far=range(1, 11),
    )
    proj = call(gather_kernel, [((share * width // W, W), F32)], parts, flops=unit)
    return (corner_grad[None, None], edge_grad[None, None], proj[None])


def solution(mesh):
    placed = (
        P("row", "col", None, None),
        P("row", "col", None, None),
        P("col", None, None),
        P("row", "col", None, None),
    )
    return jax.shard_map(
        shards,
        mesh=mesh,
        in_specs=placed,
        out_specs=(P("row", "col", None, None), P("row", "col", None, None), P("col", "row", None)),
        check_vma=False,
    )
```

time: 75.2 us -> 69.5 us (0.924); the launches traced: 74.1 us -> 69.2 us
  local copies, waits for them, and re-layouts: 12.4 us -> 0.04 us
  waiting for transfers between devices: 2.09 us -> 7.53 us
  starting transfers between devices: 30.7 us -> 34.3 us
  Pallas kernels: 28.1 us -> 26.5 us
    unnamed x50 -> x22, local copies, waits for them, and re-layouts: 12.4 us -> 0.04 us
    all_to_all x1, waiting for transfers between devices: 0.01 us -> 3.81 us  [shards(): lax.all_to_all(done.reshape(rows, share, width), 'row', 0, 0, tiled=True)]
    ppermute x10 -> x11, starting transfers between devices: 26.5 us -> 30.1 us  [send(): return lax.ppermute(value, 'col', pairs)]
    ppermute x10 -> x11, waiting for transfers between devices: 2.09 us -> 3.72 us  [send(): return lax.ppermute(value, 'col', pairs)]
    pallas_call x12 -> x11, Pallas kernels: 28.1 us -> 26.5 us  [call(): pl.pallas_call(kernel, out_shape=outs[0] if single else outs, in_specs=in...]
  transfers between devices with their start and end apart: 11 -> 12, of which waited for: 3 -> 6; matrix products, arithmetic and copies ran while one was open for 0% -> 0% of each run, Pallas kernels for 22% -> 22%
where the time goes in v3:
time: 69.5 us; the launch traced here: 69.2 us
  starting transfers between devices  34.3 us (49%)
  Pallas kernels  26.5 us (38%)
  waiting for transfers between devices  7.53 us (11%)
  between operations  0.86 us (1%)
    ppermute x11, starting transfers between devices, send(): return lax.ppermute(value, 'col', pairs)  30.1 us
    pallas_call x11, Pallas kernels, call(): pl.pallas_call(kernel, out_shape=outs[0] if single else outs, in_specs=in...  26.5 us
    all_to_all x1, starting transfers between devices, shards(): lax.all_to_all(done.reshape(rows, share, width), 'row', 0, 0, tiled=True)  4.22 us
    all_to_all x1, waiting for transfers between devices, shards(): lax.all_to_all(done.reshape(rows, share, width), 'row', 0, 0, tiled=True)  3.81 us
    ppermute x11, waiting for transfers between devices, send(): return lax.ppermute(value, 'col', pairs)  3.72 us
  transfers between devices with their start and end apart: 12, of which 6 were waited for; matrix products, arithmetic and copies ran while one was open for 0% of the time, Pallas kernels for 22%

profile of v3, /device:TPU:1, one launch (start us, length us, event | category | flops | bytes accessed | tf_op | source)
XLA Modules:
  0.0 69.2 jit_solution(387035055987675818)
XLA Ops:
  0.6 3.3 %collective-permute-start.1 = (bf16[128,4608]{1,0:T(8,128)(2,1)}, bf16[128,4608]{1,0:T(8,128)(2,1)S(1)}, u32[]{:S(2)}, u32[]{:S(2)}) collective-permute-start(bf16[128,4608]{1,0:T(8,128)(2,1)} %bitcast.9), channel_id=1, source_target_pairs={{0,1},{1,0},{2,3},{3,2},{4,5},{5,4},{6,7},{7,6},{8,9},{9,8},{10,11... | collective-permute-start | bytes 3538952 | tf_op jit(solution)/shard_map/ppermute | solution.py:315
  4.0 2.8 %shard_map.67 = (bf16[128,4608]{1,0:T(8,128)(2,1)S(1)}, bf16[128,128]{1,0:T(8,128)(2,1)S(1)}, bf16[128,128]{1,0:T(8,128)(2,1)S(1)}) custom-call(s32[1]{0:T(128)} %bitcast.core_ref, bf16[4608,128]{1,0:T(8,128)(2,1)} %bitcast.24, bf16[128,4608]{1,0:T(8,128)(2,1)} %bitcast.10, bf16[128,128]{1,0:T(8,128)(2,1)} %bitcast.19, bf16[128,128]{1,0:T(8,128)(2,1)} %bitcast.26), custom_call_target="tpu_custom_call" | custom-call | flops 301989888 | bytes 2424836 | tf_op jit(solution)/shard_map/pallas_call | solution.py:289
  6.7 0.1 collective-permute-start.2
  6.8 1.4 %collective-permute-start = (bf16[128,128]{1,0:T(8,128)(2,1)S(1)}, bf16[128,128]{1,0:T(8,128)(2,1)S(1)}, u32[]{:S(2)}, u32[]{:S(2)}) collective-permute-start(bf16[128,128]{1,0:T(8,128)(2,1)S(1)} %get-tuple-element.21), channel_id=1, source_target_pairs={{0,31},{1,2},{2,1},{3,4},{4,3},{5,6},{6,5},{7,8},{8,7},{9,10},{10,... | collective-permute-start | bytes 98312 | tf_op jit(solution)/shard_map/ppermute | solution.py:315
  8.2 0.0 collective-permute-done.1.far_edge_ref
  8.2 1.4 %collective-permute-done.2.far_turned_ref = bf16[128,4608]{1,0:T(8,128)(2,1)S(1)} collective-permute-done((bf16[128,4608]{1,0:T(8,128)(2,1)S(1)}, bf16[128,4608]{1,0:T(8,128)(2,1)S(1)}, u32[]{:S(2)}, u32[]{:S(2)}) %collective-permute-start.2) | collective-permute-done | bytes 1179680 | tf_op jit(solution)/shard_map/ppermute | solution.py:315
  9.7 1.5 %shard_map.68 = (bf16[128,128]{1,0:T(8,128)(2,1)S(1)}, bf16[128,4608]{1,0:T(8,128)(2,1)S(1)}, bf16[128,4608]{1,0:T(8,128)(2,1)S(1)}) custom-call(s32[1]{0:T(128)} %bitcast.core_ref, bf16[128,128]{1,0:T(8,128)(2,1)S(1)} %get-tuple-element.22.keep_ref, bf16[128,4608]{1,0:T(8,128)(2,1)S(1)} %collective-permute-done.1.far_edge_ref, ...), custom_call_target="tpu_custom_call" | custom-call | flops 301989888 | bytes 2392068 | tf_op jit(solution)/shard_map/pallas_call | solution.py:289
  11.2 0.5 collective-permute-done.come_ref.r0_ref
  11.8 0.0 copy-done
  11.8 2.0 %shard_map.69 = (bf16[128,128]{1,0:T(8,128)(2,1)S(1)}, bf16[256,128]{1,0:T(8,128)(2,1)S(1)}) custom-call(s32[1]{0:T(128)} %bitcast.core_ref, bf16[128,128]{1,0:T(8,128)(2,1)S(1)} %collective-permute-done.come_ref.r0_ref, bf16[128,128]{1,0:T(8,128)(2,1)S(1)} %get-tuple-element.24.ahead_ref, bf16[128,4608]{1,0:T(8,128)(2,1)S(1)} %bitcast.11, ...), custom_call_target="tpu_custom_call" | custom-call | flops 603979776 | bytes 4784132 | tf_op jit(solution)/shard_map/pallas_call | solution.py:289
  13.8 8.5 %collective-permute-start.3 = (bf16[256,128]{1,0:T(8,128)(2,1)S(1)}, bf16[256,128]{1,0:T(8,128)(2,1)S(1)}, u32[]{:S(2)}, u32[]{:S(2)}) collective-permute-start(bf16[256,128]{1,0:T(8,128)(2,1)S(1)} %get-tuple-element.27), channel_id=1, source_target_pairs={{0,2},{1,31},{2,4},{3,1},{4,6},{5,3},{6,8},{7,5},{8,10},{9,7},{10,... | collective-permute-start | bytes 196616 | tf_op jit(solution)/shard_map/ppermute | solution.py:315
  22.3 0.0 collective-permute-start.4
  22.3 0.5 collective-permute-start.5
  22.8 0.7 %collective-permute-done.4.m1_ref = bf16[128,128]{1,0:T(8,128)(2,1)S(1)} collective-permute-done((bf16[128,128]{1,0:T(8,128)(2,1)S(1)}, bf16[128,128]{1,0:T(8,128)(2,1)S(1)}, u32[]{:S(2)}, u32[]{:S(2)}) %collective-permute-start.4) | collective-permute-done | bytes 32800 | tf_op jit(solution)/shard_map/ppermute | solution.py:315
  23.5 0.2 collective-permute-done.5.m2_ref
  23.7 0.0 collective-permute-done.3.come_ref.r1_ref
  23.7 3.7 %shard_map.70 = (bf16[256,128]{1,0:T(8,128)(2,1)S(1)}, bf16[256,128]{1,0:T(8,128)(2,1)S(1)}) custom-call(s32[1]{0:T(128)} %bitcast.core_ref, bf16[256,128]{1,0:T(8,128)(2,1)S(1)} %collective-permute-done.3.come_ref.r1_ref, bf16[128,4608]{1,0:T(8,128)(2,1)S(1)} %bitcast.12, bf16[128,4608]{1,0:T(8,128)(2,1)S(1)} %get-tuple-element.23.t_ref.turned_ref, ...), custom_call_target="tpu_custom_call" | custom-call | flops 1207959552 | bytes 4849668 | tf_op jit(solution)/shard_map/pallas_call | solution.py:289
  27.3 1.5 %collective-permute-start.7 = (bf16[256,128]{1,0:T(8,128)(2,1)S(1)}, bf16[256,128]{1,0:T(8,128)(2,1)S(1)}, u32[]{:S(2)}, u32[]{:S(2)}) collective-permute-start(bf16[256,128]{1,0:T(8,128)(2,1)S(1)} %get-tuple-element.30), channel_id=1, source_target_pairs={{0,1},{1,0},{2,3},{3,2},{4,5},{5,4},{6,7},{7,6},{8,9},{9,8},{10,11... | collective-permute-start | bytes 196616 | tf_op jit(solution)/shard_map/ppermute | solution.py:315
  28.9 3.9 %collective-permute-start.6 = (bf16[256,128]{1,0:T(8,128)(2,1)S(1)}, bf16[256,128]{1,0:T(8,128)(2,1)S(1)}, u32[]{:S(2)}, u32[]{:S(2)}) collective-permute-start(bf16[256,128]{1,0:T(8,128)(2,1)S(1)} %get-tuple-element.29), channel_id=1, source_target_pairs={{0,2},{1,31},{2,4},{3,1},{4,6},{5,3},{6,8},{7,5},{8,10},{9,7},{10,... | collective-permute-start | bytes 196616 | tf_op jit(solution)/shard_map/ppermute | solution.py:315
  32.7 0.0 collective-permute-done.7.m3_ref
  32.7 0.0 copy-done.6
  32.7 1.5 %shard_map.71.early_ref = f32[128,4608]{1,0:T(8,128)S(1)} custom-call(s32[1]{0:T(128)} %bitcast.core_ref, bf16[256,128]{1,0:T(8,128)(2,1)S(1)} %collective-permute-done.3.come_ref.r1_ref, bf16[256,128]{1,0:T(8,128)(2,1)S(1)} %collective-permute-done.7.m3_ref, bf16[128,4608]{1,0:T(8,128)(2,1)S(1)} %bitcast.13), custom_call_target="tpu_custom_call" | custom-call | bytes 1310724 | tf_op jit(solution)/shard_map/pallas_call | solution.py:289
  34.3 0.0 copy-done.8
  34.3 0.0 collective-permute-done.6.come_ref.r2_ref
  34.3 0.0 copy-start.1
  34.3 2.0 %shard_map.72 = (bf16[128,128]{1,0:T(8,128)(2,1)S(1)}, bf16[128,128]{1,0:T(8,128)(2,1)S(1)}) custom-call(s32[1]{0:T(128)} %bitcast.core_ref, bf16[256,128]{1,0:T(8,128)(2,1)S(1)} %collective-permute-done.6.come_ref.r2_ref, bf16[128,4608]{1,0:T(8,128)(2,1)S(1)} %bitcast.14, bf16[128,4608]{1,0:T(8,128)(2,1)S(1)} %get-tuple-element.23.t_ref.turned_ref, ...), custom_call_target="tpu_custom_call" | custom-call | flops 603979776 | bytes 7143428 | tf_op jit(solution)/shard_map/pallas_call | solution.py:289
  36.4 0.0 copy-start.2
  36.4 1.6 %collective-permute-start.9 = (bf16[128,128]{1,0:T(8,128)(2,1)S(1)}, bf16[128,128]{1,0:T(8,128)(2,1)S(1)}, u32[]{:S(2)}, u32[]{:S(2)}) collective-permute-start(bf16[128,128]{1,0:T(8,128)(2,1)S(1)} %get-tuple-element.32), channel_id=1, source_target_pairs={{0,1},{1,0},{2,3},{3,2},{4,5},{5,4},{6,7},{7,6},{8,9},{9,8},{10,11... | collective-permute-start | bytes 98312 | tf_op jit(solution)/shard_map/ppermute | solution.py:315
  38.0 0.9 %collective-permute-done.9.m4_ref = bf16[128,128]{1,0:T(8,128)(2,1)S(1)} collective-permute-done((bf16[128,128]{1,0:T(8,128)(2,1)S(1)}, bf16[128,128]{1,0:T(8,128)(2,1)S(1)}, u32[]{:S(2)}, u32[]{:S(2)}) %collective-permute-start.9) | collective-permute-done | bytes 32800 | tf_op jit(solution)/shard_map/ppermute | solution.py:315
  38.8 1.0 %shard_map.73 = (bf16[128,128]{1,0:T(8,128)(2,1)S(1)}, f32[128,4608]{1,0:T(8,128)S(1)}) custom-call(s32[1]{0:T(128)} %bitcast.core_ref, bf16[128,128]{1,0:T(8,128)(2,1)S(1)} %collective-permute-done.come_ref.r0_ref, bf16[256,128]{1,0:T(8,128)(2,1)S(1)} %collective-permute-done.6.come_ref.r2_ref, ...), custom_call_target="tpu_custom_call", output_to_operand_aliasing={{1}: (8, {})} | custom-call | flops 905969664 | bytes 4915204 | tf_op jit(solution)/shard_map/pallas_call | solution.py:289
  39.9 3.5 %collective-permute-start.10 = (bf16[128,128]{1,0:T(8,128)(2,1)S(1)}, bf16[128,128]{1,0:T(8,128)(2,1)S(1)}, u32[]{:S(2)}, u32[]{:S(2)}) collective-permute-start(bf16[128,128]{1,0:T(8,128)(2,1)S(1)} %get-tuple-element.33), channel_id=1, source_target_pairs={{1,0},{3,2},{5,4},{7,6},{9,8},{11,10},{13,12},{15,14},{17,16},{19,... | collective-permute-start | bytes 98312 | tf_op jit(solution)/shard_map/ppermute | solution.py:315
  43.4 5.7 %collective-permute-start.8 = (bf16[128,128]{1,0:T(8,128)(2,1)S(1)}, bf16[128,128]{1,0:T(8,128)(2,1)S(1)}, u32[]{:S(2)}, u32[]{:S(2)}) collective-permute-start(bf16[128,128]{1,0:T(8,128)(2,1)S(1)} %get-tuple-element.31), channel_id=1, source_target_pairs={{1,31},{3,1},{5,3},{7,5},{9,7},{11,9},{13,11},{15,13},{17,15},{19,... | collective-permute-start | bytes 98312 | tf_op jit(solution)/shard_map/ppermute | solution.py:315
  49.1 0.0 collective-permute-done.10.m5_ref
  49.1 0.0 copy-start.9
  49.2 0.0 copy-done.3
  49.2 0.0 copy-done.4
  49.2 0.0 copy-done.5
  49.2 0.0 copy-done.1
  49.2 0.0 copy-done.7
  49.2 0.0 copy-done.2
  49.2 2.4 %shard_map.75 = (f32[128,4608]{1,0:T(8,128)S(1)}, bf16[128,4608]{1,0:T(8,128)(2,1)}) custom-call(s32[1]{0:T(128)} %bitcast.core_ref, bf16[128,128]{1,0:T(8,128)(2,1)S(1)} %bitcast.21, bf16[128,128]{1,0:T(8,128)(2,1)S(1)} %collective-permute-done.come_ref.r0_ref, ...), custom_call_target="tpu_custom_call", output_to_operand_aliasing={{0}: (9, {})} | custom-call | flops 905969664 | bytes 3801092 | tf_op jit(solution)/shard_map/pallas_call | solution.py:289
  51.6 0.0 copy-done.9
  51.6 0.0 collective-permute-done.8.r3_ref
  51.6 1.6 %shard_map.76 = bf16[128,4608]{1,0:T(8,128)(2,1)} custom-call(s32[1]{0:T(128)} %bitcast.core_ref, bf16[128,128]{1,0:T(8,128)(2,1)S(1)} %bitcast.22, bf16[128,128]{1,0:T(8,128)(2,1)S(1)} %collective-permute-done.8.r3_ref, bf16[128,4608]{1,0:T(8,128)(2,1)S(1)} %bitcast.17, f32[128,4608]{1,0:T(8,128)S(1)} %get-tuple-element.37.sum_ref, ...), custom_call_target="tpu_custom_call", output_to_operand_aliasing={{}: (5, {})} | custom-call | flops 301989888 | bytes 4784132 | tf_op jit(solution)/shard_map/pallas_call | solution.py:289
  53.3 4.2 %all-to-all-start = ((bf16[8,16,4608]{2,1,0:T(8,128)(2,1)}), bf16[8,16,4608]{2,1,0:T(8,128)(2,1)S(1)}, u32[]{:S(2)}, u32[]{:S(2)}) async-start(bf16[8,16,4608]{2,1,0:T(8,128)(2,1)} %bitcast.23), calls=%async_computation | async-start | bytes 2359296 | tf_op jit(solution)/shard_map/all_to_all | solution.py:365
  57.5 7.0 %shard_map.74 = (bf16[128,4608]{1,0:T(8,128)(2,1)}, bf16[128,128]{1,0:T(8,128)(2,1)}) custom-call(s32[1]{0:T(128)} %bitcast.core_ref, bf16[128,128]{1,0:T(8,128)(2,1)} %bitcast.20, bf16[128,128]{1,0:T(8,128)(2,1)} %copy-done.3, bf16[256,128]{1,0:T(8,128)(2,1)} %copy-done.6, bf16[256,128]{1,0:T(8,128)(2,1)} %copy-done.1, bf16[128,128]{1,0:T(8,128)(2,1)} %copy-done.10, ...), custom_call_target="tpu_custom_call" | custom-call | flops 2113929216 | bytes 2785284 | tf_op jit(solution)/shard_map/pallas_call | solution.py:289
  64.5 3.8 %all-to-all-done.parts_ref = bf16[8,16,4608]{2,1,0:T(8,128)(2,1)S(1)} async-done(((bf16[8,16,4608]{2,1,0:T(8,128)(2,1)}), bf16[8,16,4608]{2,1,0:T(8,128)(2,1)S(1)}, u32[]{:S(2)}, u32[]{:S(2)}) %all-to-all-start) | async-done | bytes 1179680 | tf_op jit(solution)/shard_map/all_to_all | solution.py:365
  68.4 0.9 %shard_map.77 = f32[576,128]{1,0:T(8,128)} custom-call(bf16[8,16,4608]{2,1,0:T(8,128)(2,1)S(1)} %all-to-all-done.parts_ref), custom_call_target="tpu_custom_call" | custom-call | flops 150994944 | bytes 1179648 | tf_op jit(solution)/shard_map/pallas_call | solution.py:289
  (9 shorter events, 0.0 us)
Async XLA Ops:
  0.6 7.6 %collective-permute-start.1 = (bf16[128,4608]{1,0:T(8,128)(2,1)}, bf16[128,4608]{1,0:T(8,128)(2,1)S(1)}, u32[]{:S(2)}, u32[]{:S(2)}) collective-permute-start(bf16[128,4608]{1,0:T(8,128)(2,1)} %bitcast.9), channel_id=1, source_target_pairs={{0,1},{1,0},{2,3},{3,2},{4,5},{5,4},{6,7},{7,6},{8,9},{9,8},{10,11... | collective-permute-start | bytes 3538952 | tf_op jit(solution)/shard_map/ppermute | solution.py:315
  6.7 2.9 %collective-permute-start.2 = (bf16[128,4608]{1,0:T(8,128)(2,1)S(1)}, bf16[128,4608]{1,0:T(8,128)(2,1)S(1)}, u32[]{:S(2)}, u32[]{:S(2)}) collective-permute-start(bf16[128,4608]{1,0:T(8,128)(2,1)S(1)} %get-tuple-element.23.t_ref.turned_ref), channel_id=1, source_target_pairs={{0,1},{1,0},{2,3},{3,2},{4,5},{5,4},{6,7},{7,6},{8,9},{9,8},{10,11... | collective-permute-start | bytes 3538952 | tf_op jit(solution)/shard_map/ppermute | solution.py:315
  6.8 4.9 %collective-permute-start = (bf16[128,128]{1,0:T(8,128)(2,1)S(1)}, bf16[128,128]{1,0:T(8,128)(2,1)S(1)}, u32[]{:S(2)}, u32[]{:S(2)}) collective-permute-start(bf16[128,128]{1,0:T(8,128)(2,1)S(1)} %get-tuple-element.21), channel_id=1, source_target_pairs={{0,31},{1,2},{2,1},{3,4},{4,3},{5,6},{6,5},{7,8},{8,7},{9,10},{10,... | collective-permute-start | bytes 98312 | tf_op jit(solution)/shard_map/ppermute | solution.py:315
  9.7 2.1 %copy-start = (bf16[1,1,128,4608]{3,2,1,0:T(8,128)(2,1)S(1)}, bf16[1,1,128,4608]{3,2,1,0:T(8,128)(2,1)}, u32[]{:S(2)}) copy-start(bf16[1,1,128,4608]{3,2,1,0:T(8,128)(2,1)} %param.5) | copy-start | bytes 3538948
  11.8 37.4 %copy-start.3 = (bf16[128,128]{1,0:T(8,128)(2,1)}, bf16[128,128]{1,0:T(8,128)(2,1)S(1)}, u32[]{:S(2)}) copy-start(bf16[128,128]{1,0:T(8,128)(2,1)S(1)} %collective-permute-done.come_ref.r0_ref) | copy-start | bytes 98308
  13.8 9.9 %collective-permute-start.3 = (bf16[256,128]{1,0:T(8,128)(2,1)S(1)}, bf16[256,128]{1,0:T(8,128)(2,1)S(1)}, u32[]{:S(2)}, u32[]{:S(2)}) collective-permute-start(bf16[256,128]{1,0:T(8,128)(2,1)S(1)} %get-tuple-element.27), channel_id=1, source_target_pairs={{0,2},{1,31},{2,4},{3,1},{4,6},{5,3},{6,8},{7,5},{8,10},{9,7},{10,... | collective-permute-start | bytes 196616 | tf_op jit(solution)/shard_map/ppermute | solution.py:315
  22.3 1.2 %collective-permute-start.4 = (bf16[128,128]{1,0:T(8,128)(2,1)S(1)}, bf16[128,128]{1,0:T(8,128)(2,1)S(1)}, u32[]{:S(2)}, u32[]{:S(2)}) collective-permute-start(bf16[128,128]{1,0:T(8,128)(2,1)S(1)} %get-tuple-element.22.keep_ref), channel_id=1, source_target_pairs={{0,1},{1,0},{2,3},{3,2},{4,5},{5,4},{6,7},{7,6},{8,9},{9,8},{10,11... | collective-permute-start | bytes 98312 | tf_op jit(solution)/shard_map/ppermute | solution.py:315
  22.3 1.4 %collective-permute-start.5 = (bf16[128,128]{1,0:T(8,128)(2,1)S(1)}, bf16[128,128]{1,0:T(8,128)(2,1)S(1)}, u32[]{:S(2)}, u32[]{:S(2)}) collective-permute-start(bf16[128,128]{1,0:T(8,128)(2,1)S(1)} %get-tuple-element.28), channel_id=1, source_target_pairs={{0,1},{1,0},{2,3},{3,2},{4,5},{5,4},{6,7},{7,6},{8,9},{9,8},{10,11... | collective-permute-start | bytes 98312 | tf_op jit(solution)/shard_map/ppermute | solution.py:315
  23.5 25.7 %copy-start.4 = (bf16[128,128]{1,0:T(8,128)(2,1)}, bf16[128,128]{1,0:T(8,128)(2,1)S(1)}, u32[]{:S(2)}) copy-start(bf16[128,128]{1,0:T(8,128)(2,1)S(1)} %collective-permute-done.4.m1_ref) | copy-start | bytes 98308
  23.7 25.5 %copy-start.5 = (bf16[128,128]{1,0:T(8,128)(2,1)}, bf16[128,128]{1,0:T(8,128)(2,1)S(1)}, u32[]{:S(2)}) copy-start(bf16[128,128]{1,0:T(8,128)(2,1)S(1)} %collective-permute-done.5.m2_ref) | copy-start | bytes 98308
  23.7 9.1 %copy-start.6 = (bf16[256,128]{1,0:T(8,128)(2,1)}, bf16[256,128]{1,0:T(8,128)(2,1)S(1)}, u32[]{:S(2)}) copy-start(bf16[256,128]{1,0:T(8,128)(2,1)S(1)} %collective-permute-done.3.come_ref.r1_ref) | copy-start | bytes 196612
  27.3 5.4 %collective-permute-start.7 = (bf16[256,128]{1,0:T(8,128)(2,1)S(1)}, bf16[256,128]{1,0:T(8,128)(2,1)S(1)}, u32[]{:S(2)}, u32[]{:S(2)}) collective-permute-start(bf16[256,128]{1,0:T(8,128)(2,1)S(1)} %get-tuple-element.30), channel_id=1, source_target_pairs={{0,1},{1,0},{2,3},{3,2},{4,5},{5,4},{6,7},{7,6},{8,9},{9,8},{10,11... | collective-permute-start | bytes 196616 | tf_op jit(solution)/shard_map/ppermute | solution.py:315
  28.9 5.5 %collective-permute-start.6 = (bf16[256,128]{1,0:T(8,128)(2,1)S(1)}, bf16[256,128]{1,0:T(8,128)(2,1)S(1)}, u32[]{:S(2)}, u32[]{:S(2)}) collective-permute-start(bf16[256,128]{1,0:T(8,128)(2,1)S(1)} %get-tuple-element.29), channel_id=1, source_target_pairs={{0,2},{1,31},{2,4},{3,1},{4,6},{5,3},{6,8},{7,5},{8,10},{9,7},{10,... | collective-permute-start | bytes 196616 | tf_op jit(solution)/shard_map/ppermute | solution.py:315
  32.7 1.6 %copy-start.8 = (bf16[256,128]{1,0:T(8,128)(2,1)}, bf16[256,128]{1,0:T(8,128)(2,1)S(1)}, u32[]{:S(2)}) copy-start(bf16[256,128]{1,0:T(8,128)(2,1)S(1)} %collective-permute-done.7.m3_ref) | copy-start | bytes 196612
  34.3 14.9 %copy-start.1 = (bf16[256,128]{1,0:T(8,128)(2,1)}, bf16[256,128]{1,0:T(8,128)(2,1)S(1)}, u32[]{:S(2)}) copy-start(bf16[256,128]{1,0:T(8,128)(2,1)S(1)} %collective-permute-done.6.come_ref.r2_ref) | copy-start | bytes 196612
  36.4 12.8 %copy-start.2 = (bf16[1,1,128,128]{3,2,1,0:T(8,128)(2,1)S(1)}, bf16[1,1,128,128]{3,2,1,0:T(8,128)(2,1)}, u32[]{:S(2)}) copy-start(bf16[1,1,128,128]{3,2,1,0:T(8,128)(2,1)} %param.4) | copy-start | bytes 98308
  36.4 2.4 %collective-permute-start.9 = (bf16[128,128]{1,0:T(8,128)(2,1)S(1)}, bf16[128,128]{1,0:T(8,128)(2,1)S(1)}, u32[]{:S(2)}, u32[]{:S(2)}) collective-permute-start(bf16[128,128]{1,0:T(8,128)(2,1)S(1)} %get-tuple-element.32), channel_id=1, source_target_pairs={{0,1},{1,0},{2,3},{3,2},{4,5},{5,4},{6,7},{7,6},{8,9},{9,8},{10,11... | collective-permute-start | bytes 98312 | tf_op jit(solution)/shard_map/ppermute | solution.py:315
  38.8 10.4 %copy-start.7 = (bf16[128,128]{1,0:T(8,128)(2,1)}, bf16[128,128]{1,0:T(8,128)(2,1)S(1)}, u32[]{:S(2)}) copy-start(bf16[128,128]{1,0:T(8,128)(2,1)S(1)} %collective-permute-done.9.m4_ref) | copy-start | bytes 98308
  39.9 9.3 %collective-permute-start.10 = (bf16[128,128]{1,0:T(8,128)(2,1)S(1)}, bf16[128,128]{1,0:T(8,128)(2,1)S(1)}, u32[]{:S(2)}, u32[]{:S(2)}) collective-permute-start(bf16[128,128]{1,0:T(8,128)(2,1)S(1)} %get-tuple-element.33), channel_id=1, source_target_pairs={{1,0},{3,2},{5,4},{7,6},{9,8},{11,10},{13,12},{15,14},{17,16},{19,... | collective-permute-start | bytes 98312 | tf_op jit(solution)/shard_map/ppermute | solution.py:315
  43.4 8.2 %collective-permute-start.8 = (bf16[128,128]{1,0:T(8,128)(2,1)S(1)}, bf16[128,128]{1,0:T(8,128)(2,1)S(1)}, u32[]{:S(2)}, u32[]{:S(2)}) collective-permute-start(bf16[128,128]{1,0:T(8,128)(2,1)S(1)} %get-tuple-element.31), channel_id=1, source_target_pairs={{1,31},{3,1},{5,3},{7,5},{9,7},{11,9},{13,11},{15,13},{17,15},{19,... | collective-permute-start | bytes 98312 | tf_op jit(solution)/shard_map/ppermute | solution.py:315
  49.1 2.5 %copy-start.9 = (bf16[128,128]{1,0:T(8,128)(2,1)}, bf16[128,128]{1,0:T(8,128)(2,1)S(1)}, u32[]{:S(2)}) copy-start(bf16[128,128]{1,0:T(8,128)(2,1)S(1)} %collective-permute-done.10.m5_ref) | copy-start | bytes 98308
  51.6 1.7 %copy-start.10 = (bf16[128,128]{1,0:T(8,128)(2,1)}, bf16[128,128]{1,0:T(8,128)(2,1)S(1)}, u32[]{:S(2)}) copy-start(bf16[128,128]{1,0:T(8,128)(2,1)S(1)} %collective-permute-done.8.r3_ref) | copy-start | bytes 98308
  53.3 15.1 %all-to-all-start = ((bf16[8,16,4608]{2,1,0:T(8,128)(2,1)}), bf16[8,16,4608]{2,1,0:T(8,128)(2,1)S(1)}, u32[]{:S(2)}, u32[]{:S(2)}) async-start(bf16[8,16,4608]{2,1,0:T(8,128)(2,1)} %bitcast.23), calls=%async_computation | async-start | bytes 2359296 | tf_op jit(solution)/shard_map/all_to_all | solution.py:365

commit v4 on v3

--- a/solution.py
+++ b/solution.py
@@ -113,19 +113,6 @@
     by_role(core_ref, body, (e_ref, t_ref, me_ref, mt_ref))
 
 
-def turn_back_kernel(core_ref, come_ref, e_ref, t_ref, me_ref, mt_ref, early_ref, near_ref, far_ref):
-    @pl.when(core_ref[0] == 0)
-    def _():
-        near_ref[...] = step(come_ref[:W, :], e_ref, t_ref)
-        far_ref[...] = jnp.zeros_like(far_ref)
-
-    @pl.when(core_ref[0] != 0)
-    def _():
-        near = step(come_ref[:W, :], t_ref, e_ref)
-        near_ref[...] = near
-        far_ref[...] = step(near, mt_ref, me_ref)
-
-
 def blocks(ref):
     return [ref[W * b : W * (b + 1), :] for b in range(ref.shape[0] // W)]
 
@@ -171,19 +158,22 @@
     return put
 
 
-def proj_second_kernel(
-    core_ref, r0_ref, r2_ref, m1_ref, m2_ref, m4_ref, edge_ref, turned_ref, early_ref, near_ref, out_ref, z_ref, w_ref
+def turn_back_kernel(
+    core_ref, come_ref, m1_ref, m2_ref, e_ref, t_ref, me_ref, mt_ref, early_ref, same_ref, far_ref, out_ref,
+    z_ref, w_ref,
 ):
-    @pl.when(core_ref[0] == 0)
-    def _():
-        fill(z_ref, blocks(r2_ref) + [r0_ref[...]])
-        fill(w_ref, [m2_ref[...], m1_ref[...], m4_ref[...]])
-        pairs_of(z_ref, edge_ref, w_ref, adder(early_ref, out_ref))
-        near_ref[...] = jnp.zeros_like(near_ref)
-
-    @pl.when(core_ref[0] != 0)
-    def _():
-        near_ref[...] = step(r2_ref[W:, :], turned_ref, edge_ref)
+    same_ref[...] = come_ref[...]
+
+    @pl.when(core_ref[0] == 0)
+    def _():
+        fill(z_ref, blocks(come_ref))
+        fill(w_ref, [m2_ref[...], m1_ref[...]])
+        pairs_of(z_ref, e_ref, w_ref, adder(early_ref, out_ref))
+        far_ref[...] = jnp.zeros_like(far_ref)
+
+    @pl.when(core_ref[0] != 0)
+    def _():
+        far_ref[...] = step(step(come_ref[:W, :], t_ref, e_ref), mt_ref, me_ref)
 
 
 def finish(z_ref, edge_ref, w_ref, sum_ref, out_ref, stage_ref, sem):
@@ -206,18 +196,25 @@
 
 
 def proj_third_kernel(
-    core_ref, corner_ref, r0_ref, r2_ref, m1_ref, m2_ref, m4_ref, m5_ref, edge_ref, early_ref, sum_ref, out_ref,
-    z_ref, w_ref, stage_ref, sem,
+    core_ref, corner_ref, r0_ref, r2_ref, m1_ref, m2_ref, m4_ref, e_ref, me_ref, mt_ref, early_ref,
+    near_ref, sum_ref, out_ref, z_ref, w_ref, stage_ref, sem,
 ):
     @pl.when(core_ref[0] == 0)
     def _():
-        finish(corner_ref, edge_ref, m5_ref, early_ref, out_ref, stage_ref, sem)
-
-    @pl.when(core_ref[0] != 0)
-    def _():
-        fill(z_ref, [m1_ref[...], m2_ref[...], m4_ref[...]])
+        near = split(step(m4_ref[...], mt_ref, me_ref))
+        fill(near_ref, near)
+        fill(z_ref, [corner_ref[...], r0_ref[...]])
+        fill(w_ref, near[::-1])
+        two = slice(0, 2 * W)
+        finish(z_ref.at[two], e_ref, w_ref.at[two], early_ref, out_ref, stage_ref, sem)
+
+    @pl.when(core_ref[0] != 0)
+    def _():
+        near = step(m4_ref[:W, :], me_ref, mt_ref)
+        fill(near_ref, [near, jnp.zeros_like(near)])
+        fill(z_ref, [m1_ref[...], m2_ref[...], near])
         fill(w_ref, blocks(r2_ref)[::-1] + [r0_ref[...]])
-        pairs_of(z_ref, edge_ref, w_ref, adder(early_ref, sum_ref))
+        pairs_of(z_ref, e_ref, w_ref, adder(early_ref, sum_ref))
 
 
 def proj_last_kernel(core_ref, corner_ref, r3_ref, edge_ref, sum_ref, done_ref, out_ref, stage_ref, sem):
@@ -227,14 +224,14 @@
 
 
 def edge_kernel(
-    core_ref, corner_ref, r0_ref, r1_ref, r2_ref, r3_ref, m1_ref, m2_ref, m3_ref, m4_ref, m5_ref, edge_ref, turned_ref,
+    core_ref, corner_ref, r0_ref, r1_ref, r2_ref, r3_ref, m1_ref, m2_ref, m3_ref, near_ref, edge_ref, turned_ref,
     out_ref, grad_ref, z_ref, w_ref, sem,
 ):
     def halves(ref):
         return [ref.at[pl.ds(0, W)], ref.at[pl.ds(W, W)]]
 
     come = [r0_ref] + halves(r1_ref) + halves(r2_ref)
-    mate = [m1_ref, m2_ref] + halves(m3_ref) + [m4_ref, m5_ref]
+    mate = [m1_ref, m2_ref] + halves(m3_ref) + halves(near_ref)
 
     def fetch(z_parts, w_parts):
         copies = []
@@ -345,17 +342,15 @@
     r2 = onward(go2)
     m3 = swap(near2)
     early = call(proj_first_kernel, [wide], core, r1, m3, edge, scratch=stacks(2), flops=0)
-    near3, go3 = call(turn_back_kernel, [one, one], core, r2, *tensors, early, flops=4 * unit)
+    same, go3, early = call(
+        turn_back_kernel, [two, one, wide], core, r2, m1, m2, *tensors, early,
+        scratch=stacks(2), flops=4 * unit, alias={8: 2},
+    )
     r3 = send(go3, lambda i: None if i % 2 == 0 else i - 2)
-    m4 = swap(near3)
-    near4, early = call(
-        proj_second_kernel, [one, wide], core, r0, r2, m1, m2, m4, edge, turned, early,
-        scratch=stacks(3), flops=6 * unit, alias={8: 1},
-    )
-    m5 = send(near4, lambda i: None if i % 2 == 0 else i - 1)
-    part, done = call(
-        proj_third_kernel, [wide, whole], core, corner, r0, r2, m1, m2, m4, m5, edge, early,
-        scratch=stacks(3) + [whole], sems=(6,), flops=6 * unit, far_outs=(1,), alias={9: 0},
+    m4 = swap(same)
+    near3, part, done = call(
+        proj_third_kernel, [two, wide, whole], core, corner, r0, r2, m1, m2, m4, edge, mate_edge, mate_turned, early,
+        scratch=stacks(3) + [whole], sems=(6,), flops=6 * unit, far_outs=(2,), alias={10: 1},
     )
     done = call(
         proj_last_kernel, [whole], core, corner, r3, edge, part, done,
@@ -364,8 +359,8 @@
     share = W // rows
     parts = lax.all_to_all(done.reshape(rows, share, width), "row", 0, 0, tiled=True)
     edge_grad, corner_grad = call(
-        edge_kernel, [whole, one], core, corner, r0, r1, r2, r3, m1, m2, m3, m4, m5, edge, turned,
-        scratch=stacks(6), sems=(12,), flops=14 * unit, far=range(1, 11),
+        edge_kernel, [whole, one], core, corner, r0, r1, r2, r3, m1, m2, m3, near3, edge, turned,
+        scratch=stacks(6), sems=(12,), flops=14 * unit, far=range(1, 10),
     )
     proj = call(gather_kernel, [((share * width // W, W), F32)], parts, flops=unit)
     return (corner_grad[None, None], edge_grad[None, None], proj[None])

time: 69.5 us -> 67.5 us (0.971)
  starting transfers between devices: 34.3 us -> 30.6 us
  waiting for transfers between devices: 7.53 us -> 9.22 us
    ppermute x11 -> x10, starting transfers between devices: 30.1 us -> 26.3 us  [send(): return lax.ppermute(value, 'col', pairs)]
    all_to_all x1, waiting for transfers between devices: 3.81 us -> 6.36 us  [shards(): lax.all_to_all(done.reshape(rows, share, width), 'row', 0, 0, tiled=True)]
    ppermute x11 -> x10, waiting for transfers between devices: 3.72 us -> 2.86 us  [send(): return lax.ppermute(value, 'col', pairs)]
    pallas_call x11 -> x10, Pallas kernels: 26.5 us -> 26.6 us  [call(): pl.pallas_call(kernel, out_shape=outs[0] if single else outs, in_specs=in...]
  transfers between devices with their start and end apart: 12 -> 11, of which waited for: 6 -> 5; matrix products, arithmetic and copies ran while one was open for 0% -> 0% of each run, Pallas kernels for 22% -> 24%
where the time goes in v4:
time: 67.5 us; the launch traced here: 67.3 us
  starting transfers between devices  30.6 us (45%)
  Pallas kernels  26.6 us (39%)
  waiting for transfers between devices  9.22 us (14%)
  between operations  0.84 us (1%)
    pallas_call x10, Pallas kernels, call(): pl.pallas_call(kernel, out_shape=outs[0] if single else outs, in_specs=in...  26.6 us
    ppermute x10, starting transfers between devices, send(): return lax.ppermute(value, 'col', pairs)  26.3 us
    all_to_all x1, waiting for transfers between devices, shards(): lax.all_to_all(done.reshape(rows, share, width), 'row', 0, 0, tiled=True)  6.36 us
    all_to_all x1, starting transfers between devices, shards(): lax.all_to_all(done.reshape(rows, share, width), 'row', 0, 0, tiled=True)  4.23 us
    ppermute x10, waiting for transfers between devices, send(): return lax.ppermute(value, 'col', pairs)  2.86 us
  transfers between devices with their start and end apart: 11, of which 5 were waited for; matrix products, arithmetic and copies ran while one was open for 0% of the time, Pallas kernels for 24%

profile of v4, /device:TPU:1, one launch (start us, length us, event | category | flops | bytes accessed | tf_op | source)
XLA Modules:
  0.0 67.3 jit_solution(9607083058084285294)
XLA Ops:
  0.6 3.3 %collective-permute-start.1 = (bf16[128,4608]{1,0:T(8,128)(2,1)}, bf16[128,4608]{1,0:T(8,128)(2,1)S(1)}, u32[]{:S(2)}, u32[]{:S(2)}) collective-permute-start(bf16[128,4608]{1,0:T(8,128)(2,1)} %bitcast.9), channel_id=1, source_target_pairs={{0,1},{1,0},{2,3},{3,2},{4,5},{5,4},{6,7},{7,6},{8,9},{9,8},{10,11... | collective-permute-start | bytes 3538952 | tf_op jit(solution)/shard_map/ppermute | solution.py:312
  4.0 2.8 %shard_map.67 = (bf16[128,4608]{1,0:T(8,128)(2,1)S(1)}, bf16[128,128]{1,0:T(8,128)(2,1)S(1)}, bf16[128,128]{1,0:T(8,128)(2,1)S(1)}) custom-call(s32[1]{0:T(128)} %bitcast.core_ref, bf16[4608,128]{1,0:T(8,128)(2,1)} %bitcast.23, bf16[128,4608]{1,0:T(8,128)(2,1)} %bitcast.10, bf16[128,128]{1,0:T(8,128)(2,1)} %bitcast.18, bf16[128,128]{1,0:T(8,128)(2,1)} %bitcast.25), custom_call_target="tpu_custom_call" | custom-call | flops 301989888 | bytes 2424836 | tf_op jit(solution)/shard_map/pallas_call | solution.py:286
  6.7 0.1 collective-permute-start.2
  6.8 1.4 %collective-permute-start = (bf16[128,128]{1,0:T(8,128)(2,1)S(1)}, bf16[128,128]{1,0:T(8,128)(2,1)S(1)}, u32[]{:S(2)}, u32[]{:S(2)}) collective-permute-start(bf16[128,128]{1,0:T(8,128)(2,1)S(1)} %get-tuple-element.21), channel_id=1, source_target_pairs={{0,31},{1,2},{2,1},{3,4},{4,3},{5,6},{6,5},{7,8},{8,7},{9,10},{10,... | collective-permute-start | bytes 98312 | tf_op jit(solution)/shard_map/ppermute | solution.py:312
  8.2 0.0 collective-permute-done.1.far_edge_ref
  8.2 1.4 %collective-permute-done.2.far_turned_ref = bf16[128,4608]{1,0:T(8,128)(2,1)S(1)} collective-permute-done((bf16[128,4608]{1,0:T(8,128)(2,1)S(1)}, bf16[128,4608]{1,0:T(8,128)(2,1)S(1)}, u32[]{:S(2)}, u32[]{:S(2)}) %collective-permute-start.2) | collective-permute-done | bytes 1179680 | tf_op jit(solution)/shard_map/ppermute | solution.py:312
  9.7 0.0 copy-start
  9.7 1.5 %shard_map.68 = (bf16[128,128]{1,0:T(8,128)(2,1)S(1)}, bf16[128,4608]{1,0:T(8,128)(2,1)S(1)}, bf16[128,4608]{1,0:T(8,128)(2,1)S(1)}) custom-call(s32[1]{0:T(128)} %bitcast.core_ref, bf16[128,128]{1,0:T(8,128)(2,1)S(1)} %get-tuple-element.22.keep_ref, bf16[128,4608]{1,0:T(8,128)(2,1)S(1)} %collective-permute-done.1.far_edge_ref, ...), custom_call_target="tpu_custom_call" | custom-call | flops 301989888 | bytes 2392068 | tf_op jit(solution)/shard_map/pallas_call | solution.py:286
  11.2 0.5 collective-permute-done.come_ref.r0_ref
  11.8 0.0 copy-start.6
  11.8 0.0 copy-done
  11.8 2.0 %shard_map.69 = (bf16[128,128]{1,0:T(8,128)(2,1)S(1)}, bf16[256,128]{1,0:T(8,128)(2,1)S(1)}) custom-call(s32[1]{0:T(128)} %bitcast.core_ref, bf16[128,128]{1,0:T(8,128)(2,1)S(1)} %collective-permute-done.come_ref.r0_ref, bf16[128,128]{1,0:T(8,128)(2,1)S(1)} %get-tuple-element.24.ahead_ref, bf16[128,4608]{1,0:T(8,128)(2,1)S(1)} %bitcast.11, ...), custom_call_target="tpu_custom_call" | custom-call | flops 603979776 | bytes 4784132 | tf_op jit(solution)/shard_map/pallas_call | solution.py:286
  13.8 8.5 %collective-permute-start.3 = (bf16[256,128]{1,0:T(8,128)(2,1)S(1)}, bf16[256,128]{1,0:T(8,128)(2,1)S(1)}, u32[]{:S(2)}, u32[]{:S(2)}) collective-permute-start(bf16[256,128]{1,0:T(8,128)(2,1)S(1)} %get-tuple-element.27), channel_id=1, source_target_pairs={{0,2},{1,31},{2,4},{3,1},{4,6},{5,3},{6,8},{7,5},{8,10},{9,7},{10,... | collective-permute-start | bytes 196616 | tf_op jit(solution)/shard_map/ppermute | solution.py:312
  22.3 0.0 collective-permute-start.4
  22.3 0.5 collective-permute-start.5
  22.8 0.7 %collective-permute-done.4.m1_ref = bf16[128,128]{1,0:T(8,128)(2,1)S(1)} collective-permute-done((bf16[128,128]{1,0:T(8,128)(2,1)S(1)}, bf16[128,128]{1,0:T(8,128)(2,1)S(1)}, u32[]{:S(2)}, u32[]{:S(2)}) %collective-permute-start.4) | collective-permute-done | bytes 32800 | tf_op jit(solution)/shard_map/ppermute | solution.py:312
  23.5 0.2 collective-permute-done.5.m2_ref
  23.7 0.0 collective-permute-done.3.come_ref.r1_ref
  23.7 3.7 %shard_map.70 = (bf16[256,128]{1,0:T(8,128)(2,1)S(1)}, bf16[256,128]{1,0:T(8,128)(2,1)S(1)}) custom-call(s32[1]{0:T(128)} %bitcast.core_ref, bf16[256,128]{1,0:T(8,128)(2,1)S(1)} %collective-permute-done.3.come_ref.r1_ref, bf16[128,4608]{1,0:T(8,128)(2,1)S(1)} %bitcast.12, bf16[128,4608]{1,0:T(8,128)(2,1)S(1)} %get-tuple-element.23.t_ref.turned_ref, ...), custom_call_target="tpu_custom_call" | custom-call | flops 1207959552 | bytes 4849668 | tf_op jit(solution)/shard_map/pallas_call | solution.py:286
  27.3 1.5 %collective-permute-start.7 = (bf16[256,128]{1,0:T(8,128)(2,1)S(1)}, bf16[256,128]{1,0:T(8,128)(2,1)S(1)}, u32[]{:S(2)}, u32[]{:S(2)}) collective-permute-start(bf16[256,128]{1,0:T(8,128)(2,1)S(1)} %get-tuple-element.30), channel_id=1, source_target_pairs={{0,1},{1,0},{2,3},{3,2},{4,5},{5,4},{6,7},{7,6},{8,9},{9,8},{10,11... | collective-permute-start | bytes 196616 | tf_op jit(solution)/shard_map/ppermute | solution.py:312
  28.9 3.9 %collective-permute-start.6 = (bf16[256,128]{1,0:T(8,128)(2,1)S(1)}, bf16[256,128]{1,0:T(8,128)(2,1)S(1)}, u32[]{:S(2)}, u32[]{:S(2)}) collective-permute-start(bf16[256,128]{1,0:T(8,128)(2,1)S(1)} %get-tuple-element.29), channel_id=1, source_target_pairs={{0,2},{1,31},{2,4},{3,1},{4,6},{5,3},{6,8},{7,5},{8,10},{9,7},{10,... | collective-permute-start | bytes 196616 | tf_op jit(solution)/shard_map/ppermute | solution.py:312
  32.7 0.0 collective-permute-done.7.m3_ref
  32.7 0.0 copy-done.4
  32.7 1.5 %shard_map.71.early_ref = f32[128,4608]{1,0:T(8,128)S(1)} custom-call(s32[1]{0:T(128)} %bitcast.core_ref, bf16[256,128]{1,0:T(8,128)(2,1)S(1)} %collective-permute-done.3.come_ref.r1_ref, bf16[256,128]{1,0:T(8,128)(2,1)S(1)} %collective-permute-done.7.m3_ref, bf16[128,4608]{1,0:T(8,128)(2,1)S(1)} %bitcast.13), custom_call_target="tpu_custom_call" | custom-call | bytes 1310724 | tf_op jit(solution)/shard_map/pallas_call | solution.py:286
  34.3 0.0 copy-done.7
  34.3 0.0 copy-start.1
  34.3 0.0 collective-permute-done.6.come_ref.r2_ref
  34.3 0.0 copy-start.5
  34.3 2.0 %shard_map.72 = (bf16[256,128]{1,0:T(8,128)(2,1)S(1)}, bf16[128,128]{1,0:T(8,128)(2,1)S(1)}, f32[128,4608]{1,0:T(8,128)S(1)}) custom-call(s32[1]{0:T(128)} %bitcast.core_ref, bf16[256,128]{1,0:T(8,128)(2,1)S(1)} %collective-permute-done.6.come_ref.r2_ref, bf16[128,128]{1,0:T(8,128)(2,1)S(1)} %collective-permute-done.4.m1_ref, ...), custom_call_target="tpu_custom_call", output_to_operand_aliasing={{2}: (8, {})} | custom-call | flops 603979776 | bytes 7208964 | tf_op jit(solution)/shard_map/pallas_call | solution.py:286
  36.4 2.4 %collective-permute-start.9 = (bf16[256,128]{1,0:T(8,128)(2,1)S(1)}, bf16[256,128]{1,0:T(8,128)(2,1)S(1)}, u32[]{:S(2)}, u32[]{:S(2)}) collective-permute-start(bf16[256,128]{1,0:T(8,128)(2,1)S(1)} %get-tuple-element.32), channel_id=1, source_target_pairs={{0,1},{1,0},{2,3},{3,2},{4,5},{5,4},{6,7},{7,6},{8,9},{9,8},{10,11... | collective-permute-start | bytes 196616 | tf_op jit(solution)/shard_map/ppermute | solution.py:312
  38.7 4.8 %collective-permute-start.8 = (bf16[128,128]{1,0:T(8,128)(2,1)S(1)}, bf16[128,128]{1,0:T(8,128)(2,1)S(1)}, u32[]{:S(2)}, u32[]{:S(2)}) collective-permute-start(bf16[128,128]{1,0:T(8,128)(2,1)S(1)} %get-tuple-element.31), channel_id=1, source_target_pairs={{1,31},{3,1},{5,3},{7,5},{9,7},{11,9},{13,11},{15,13},{17,15},{19,... | collective-permute-start | bytes 98312 | tf_op jit(solution)/shard_map/ppermute | solution.py:312
  43.5 0.0 collective-permute-done.9.m4_ref
  43.5 0.0 copy-done.6
  43.5 0.0 copy-done.2
  43.5 0.0 copy-done.3
  43.6 0.0 copy-done.5
  43.6 0.0 copy-done.1
  43.6 3.5 %shard_map.73 = (bf16[256,128]{1,0:T(8,128)(2,1)S(1)}, f32[128,4608]{1,0:T(8,128)S(1)}, bf16[128,4608]{1,0:T(8,128)(2,1)}) custom-call(s32[1]{0:T(128)} %bitcast.core_ref, bf16[128,128]{1,0:T(8,128)(2,1)S(1)} %bitcast.20, bf16[128,128]{1,0:T(8,128)(2,1)S(1)} %collective-permute-done.come_ref.r0_ref, ...), custom_call_target="tpu_custom_call", output_to_operand_aliasing={{1}: (10, {})} | custom-call | flops 905969664 | bytes 6160388 | tf_op jit(solution)/shard_map/pallas_call | solution.py:286
  47.1 0.0 copy-start.9
  47.1 0.0 collective-permute-done.8.r3_ref
  47.1 0.0 copy-start.8
  47.1 1.6 %shard_map.75 = bf16[128,4608]{1,0:T(8,128)(2,1)} custom-call(s32[1]{0:T(128)} %bitcast.core_ref, bf16[128,128]{1,0:T(8,128)(2,1)S(1)} %bitcast.21, bf16[128,128]{1,0:T(8,128)(2,1)S(1)} %collective-permute-done.8.r3_ref, bf16[128,4608]{1,0:T(8,128)(2,1)S(1)} %bitcast.16, f32[128,4608]{1,0:T(8,128)S(1)} %get-tuple-element.37.sum_ref, ...), custom_call_target="tpu_custom_call", output_to_operand_aliasing={{}: (5, {})} | custom-call | flops 301989888 | bytes 4784132 | tf_op jit(solution)/shard_map/pallas_call | solution.py:286
  48.8 0.0 copy-done.9
  48.8 0.0 copy-done.8
  48.8 4.2 %all-to-all-start = ((bf16[8,16,4608]{2,1,0:T(8,128)(2,1)}), bf16[8,16,4608]{2,1,0:T(8,128)(2,1)S(1)}, u32[]{:S(2)}, u32[]{:S(2)}) async-start(bf16[8,16,4608]{2,1,0:T(8,128)(2,1)} %bitcast.22), calls=%async_computation | async-start | bytes 2359296 | tf_op jit(solution)/shard_map/all_to_all | solution.py:360
  53.0 7.0 %shard_map.74 = (bf16[128,4608]{1,0:T(8,128)(2,1)}, bf16[128,128]{1,0:T(8,128)(2,1)}) custom-call(s32[1]{0:T(128)} %bitcast.core_ref, bf16[128,128]{1,0:T(8,128)(2,1)} %bitcast.19, bf16[128,128]{1,0:T(8,128)(2,1)} %copy-done.6, bf16[256,128]{1,0:T(8,128)(2,1)} %copy-done.4, bf16[256,128]{1,0:T(8,128)(2,1)} %copy-done.5, bf16[128,128]{1,0:T(8,128)(2,1)} %copy-done.8, ...), custom_call_target="tpu_custom_call" | custom-call | flops 2113929216 | bytes 2785284 | tf_op jit(solution)/shard_map/pallas_call | solution.py:286
  60.1 6.4 %all-to-all-done.parts_ref = bf16[8,16,4608]{2,1,0:T(8,128)(2,1)S(1)} async-done(((bf16[8,16,4608]{2,1,0:T(8,128)(2,1)}), bf16[8,16,4608]{2,1,0:T(8,128)(2,1)S(1)}, u32[]{:S(2)}, u32[]{:S(2)}) %all-to-all-start) | async-done | bytes 1179680 | tf_op jit(solution)/shard_map/all_to_all | solution.py:360
  66.4 0.9 %shard_map.76 = f32[576,128]{1,0:T(8,128)} custom-call(bf16[8,16,4608]{2,1,0:T(8,128)(2,1)S(1)} %all-to-all-done.parts_ref), custom_call_target="tpu_custom_call" | custom-call | flops 150994944 | bytes 1179648 | tf_op jit(solution)/shard_map/pallas_call | solution.py:286
  (4 shorter events, 0.0 us)
Async XLA Ops:
  0.6 7.6 %collective-permute-start.1 = (bf16[128,4608]{1,0:T(8,128)(2,1)}, bf16[128,4608]{1,0:T(8,128)(2,1)S(1)}, u32[]{:S(2)}, u32[]{:S(2)}) collective-permute-start(bf16[128,4608]{1,0:T(8,128)(2,1)} %bitcast.9), channel_id=1, source_target_pairs={{0,1},{1,0},{2,3},{3,2},{4,5},{5,4},{6,7},{7,6},{8,9},{9,8},{10,11... | collective-permute-start | bytes 3538952 | tf_op jit(solution)/shard_map/ppermute | solution.py:312
  6.7 2.9 %collective-permute-start.2 = (bf16[128,4608]{1,0:T(8,128)(2,1)S(1)}, bf16[128,4608]{1,0:T(8,128)(2,1)S(1)}, u32[]{:S(2)}, u32[]{:S(2)}) collective-permute-start(bf16[128,4608]{1,0:T(8,128)(2,1)S(1)} %get-tuple-element.23.t_ref.turned_ref), channel_id=1, source_target_pairs={{0,1},{1,0},{2,3},{3,2},{4,5},{5,4},{6,7},{7,6},{8,9},{9,8},{10,11... | collective-permute-start | bytes 3538952 | tf_op jit(solution)/shard_map/ppermute | solution.py:312
  6.8 4.9 %collective-permute-start = (bf16[128,128]{1,0:T(8,128)(2,1)S(1)}, bf16[128,128]{1,0:T(8,128)(2,1)S(1)}, u32[]{:S(2)}, u32[]{:S(2)}) collective-permute-start(bf16[128,128]{1,0:T(8,128)(2,1)S(1)} %get-tuple-element.21), channel_id=1, source_target_pairs={{0,31},{1,2},{2,1},{3,4},{4,3},{5,6},{6,5},{7,8},{8,7},{9,10},{10,... | collective-permute-start | bytes 98312 | tf_op jit(solution)/shard_map/ppermute | solution.py:312
  9.7 2.1 %copy-start = (bf16[1,1,128,4608]{3,2,1,0:T(8,128)(2,1)S(1)}, bf16[1,1,128,4608]{3,2,1,0:T(8,128)(2,1)}, u32[]{:S(2)}) copy-start(bf16[1,1,128,4608]{3,2,1,0:T(8,128)(2,1)} %param.5) | copy-start | bytes 3538948
  11.8 31.8 %copy-start.6 = (bf16[128,128]{1,0:T(8,128)(2,1)}, bf16[128,128]{1,0:T(8,128)(2,1)S(1)}, u32[]{:S(2)}) copy-start(bf16[128,128]{1,0:T(8,128)(2,1)S(1)} %collective-permute-done.come_ref.r0_ref) | copy-start | bytes 98308
  13.8 9.9 %collective-permute-start.3 = (bf16[256,128]{1,0:T(8,128)(2,1)S(1)}, bf16[256,128]{1,0:T(8,128)(2,1)S(1)}, u32[]{:S(2)}, u32[]{:S(2)}) collective-permute-start(bf16[256,128]{1,0:T(8,128)(2,1)S(1)} %get-tuple-element.27), channel_id=1, source_target_pairs={{0,2},{1,31},{2,4},{3,1},{4,6},{5,3},{6,8},{7,5},{8,10},{9,7},{10,... | collective-permute-start | bytes 196616 | tf_op jit(solution)/shard_map/ppermute | solution.py:312
  22.3 1.2 %collective-permute-start.4 = (bf16[128,128]{1,0:T(8,128)(2,1)S(1)}, bf16[128,128]{1,0:T(8,128)(2,1)S(1)}, u32[]{:S(2)}, u32[]{:S(2)}) collective-permute-start(bf16[128,128]{1,0:T(8,128)(2,1)S(1)} %get-tuple-element.22.keep_ref), channel_id=1, source_target_pairs={{0,1},{1,0},{2,3},{3,2},{4,5},{5,4},{6,7},{7,6},{8,9},{9,8},{10,11... | collective-permute-start | bytes 98312 | tf_op jit(solution)/shard_map/ppermute | solution.py:312
  22.3 1.4 %collective-permute-start.5 = (bf16[128,128]{1,0:T(8,128)(2,1)S(1)}, bf16[128,128]{1,0:T(8,128)(2,1)S(1)}, u32[]{:S(2)}, u32[]{:S(2)}) collective-permute-start(bf16[128,128]{1,0:T(8,128)(2,1)S(1)} %get-tuple-element.28), channel_id=1, source_target_pairs={{0,1},{1,0},{2,3},{3,2},{4,5},{5,4},{6,7},{7,6},{8,9},{9,8},{10,11... | collective-permute-start | bytes 98312 | tf_op jit(solution)/shard_map/ppermute | solution.py:312
  23.5 20.0 %copy-start.2 = (bf16[128,128]{1,0:T(8,128)(2,1)}, bf16[128,128]{1,0:T(8,128)(2,1)S(1)}, u32[]{:S(2)}) copy-start(bf16[128,128]{1,0:T(8,128)(2,1)S(1)} %collective-permute-done.4.m1_ref) | copy-start | bytes 98308
  23.7 19.9 %copy-start.3 = (bf16[128,128]{1,0:T(8,128)(2,1)}, bf16[128,128]{1,0:T(8,128)(2,1)S(1)}, u32[]{:S(2)}) copy-start(bf16[128,128]{1,0:T(8,128)(2,1)S(1)} %collective-permute-done.5.m2_ref) | copy-start | bytes 98308
  23.7 9.1 %copy-start.4 = (bf16[256,128]{1,0:T(8,128)(2,1)}, bf16[256,128]{1,0:T(8,128)(2,1)S(1)}, u32[]{:S(2)}) copy-start(bf16[256,128]{1,0:T(8,128)(2,1)S(1)} %collective-permute-done.3.come_ref.r1_ref) | copy-start | bytes 196612
  27.3 5.4 %collective-permute-start.7 = (bf16[256,128]{1,0:T(8,128)(2,1)S(1)}, bf16[256,128]{1,0:T(8,128)(2,1)S(1)}, u32[]{:S(2)}, u32[]{:S(2)}) collective-permute-start(bf16[256,128]{1,0:T(8,128)(2,1)S(1)} %get-tuple-element.30), channel_id=1, source_target_pairs={{0,1},{1,0},{2,3},{3,2},{4,5},{5,4},{6,7},{7,6},{8,9},{9,8},{10,11... | collective-permute-start | bytes 196616 | tf_op jit(solution)/shard_map/ppermute | solution.py:312
  28.9 5.5 %collective-permute-start.6 = (bf16[256,128]{1,0:T(8,128)(2,1)S(1)}, bf16[256,128]{1,0:T(8,128)(2,1)S(1)}, u32[]{:S(2)}, u32[]{:S(2)}) collective-permute-start(bf16[256,128]{1,0:T(8,128)(2,1)S(1)} %get-tuple-element.29), channel_id=1, source_target_pairs={{0,2},{1,31},{2,4},{3,1},{4,6},{5,3},{6,8},{7,5},{8,10},{9,7},{10,... | collective-permute-start | bytes 196616 | tf_op jit(solution)/shard_map/ppermute | solution.py:312
  32.7 1.6 %copy-start.7 = (bf16[256,128]{1,0:T(8,128)(2,1)}, bf16[256,128]{1,0:T(8,128)(2,1)S(1)}, u32[]{:S(2)}) copy-start(bf16[256,128]{1,0:T(8,128)(2,1)S(1)} %collective-permute-done.7.m3_ref) | copy-start | bytes 196612
  34.3 9.3 %copy-start.1 = (bf16[1,1,128,128]{3,2,1,0:T(8,128)(2,1)S(1)}, bf16[1,1,128,128]{3,2,1,0:T(8,128)(2,1)}, u32[]{:S(2)}) copy-start(bf16[1,1,128,128]{3,2,1,0:T(8,128)(2,1)} %param.4) | copy-start | bytes 98308
  34.3 9.2 %copy-start.5 = (bf16[256,128]{1,0:T(8,128)(2,1)}, bf16[256,128]{1,0:T(8,128)(2,1)S(1)}, u32[]{:S(2)}) copy-start(bf16[256,128]{1,0:T(8,128)(2,1)S(1)} %collective-permute-done.6.come_ref.r2_ref) | copy-start | bytes 196612
  36.4 7.1 %collective-permute-start.9 = (bf16[256,128]{1,0:T(8,128)(2,1)S(1)}, bf16[256,128]{1,0:T(8,128)(2,1)S(1)}, u32[]{:S(2)}, u32[]{:S(2)}) collective-permute-start(bf16[256,128]{1,0:T(8,128)(2,1)S(1)} %get-tuple-element.32), channel_id=1, source_target_pairs={{0,1},{1,0},{2,3},{3,2},{4,5},{5,4},{6,7},{7,6},{8,9},{9,8},{10,11... | collective-permute-start | bytes 196616 | tf_op jit(solution)/shard_map/ppermute | solution.py:312
  38.7 8.4 %collective-permute-start.8 = (bf16[128,128]{1,0:T(8,128)(2,1)S(1)}, bf16[128,128]{1,0:T(8,128)(2,1)S(1)}, u32[]{:S(2)}, u32[]{:S(2)}) collective-permute-start(bf16[128,128]{1,0:T(8,128)(2,1)S(1)} %get-tuple-element.31), channel_id=1, source_target_pairs={{1,31},{3,1},{5,3},{7,5},{9,7},{11,9},{13,11},{15,13},{17,15},{19,... | collective-permute-start | bytes 98312 | tf_op jit(solution)/shard_map/ppermute | solution.py:312
  47.1 1.7 %copy-start.9 = (bf16[256,128]{1,0:T(8,128)(2,1)}, bf16[256,128]{1,0:T(8,128)(2,1)S(1)}, u32[]{:S(2)}) copy-start(bf16[256,128]{1,0:T(8,128)(2,1)S(1)} %get-tuple-element.34.near_ref) | copy-start | bytes 196612
  47.1 1.7 %copy-start.8 = (bf16[128,128]{1,0:T(8,128)(2,1)}, bf16[128,128]{1,0:T(8,128)(2,1)S(1)}, u32[]{:S(2)}) copy-start(bf16[128,128]{1,0:T(8,128)(2,1)S(1)} %collective-permute-done.8.r3_ref) | copy-start | bytes 98308
  48.8 17.6 %all-to-all-start = ((bf16[8,16,4608]{2,1,0:T(8,128)(2,1)}), bf16[8,16,4608]{2,1,0:T(8,128)(2,1)S(1)}, u32[]{:S(2)}, u32[]{:S(2)}) async-start(bf16[8,16,4608]{2,1,0:T(8,128)(2,1)} %bitcast.22), calls=%async_computation | async-start | bytes 2359296 | tf_op jit(solution)/shard_map/all_to_all | solution.py:360

commit v5 on v4

v5 whole, which is shorter than its diff:
```python
import jax
import jax.numpy as jnp
from jax import lax
from jax.experimental import pallas as pl
from jax.experimental.pallas import tpu as pltpu
from jax.sharding import PartitionSpec as P


W = 128
BF = jnp.bfloat16
F32 = jnp.float32


def dot(a, b):
    return jnp.dot(a, b, preferred_element_type=F32)


def step(z, x_ref, y_ref):
    n = z.shape[0] // W
    total = None
    for t in range(x_ref.shape[1] // (2 * W)):
        cols = slice(2 * W * t, 2 * W * (t + 1))
        mid = dot(z, x_ref[:, cols]).astype(BF)
        tall = jnp.concatenate(
            [jnp.concatenate([mid[W * b : W * (b + 1), :W], mid[W * b : W * (b + 1), W:]], 0) for b in range(n)], 1
        )
        part = dot(y_ref[:, cols], tall)
        total = part if total is None else total + part
    return total.astype(BF)


def split(wide):
    return [wide[:, W * b : W * (b + 1)] for b in range(wide.shape[1] // W)]


def start_kernel(
    core_ref, proj_ref, edge_in, corner_in, cot_ref, mate_cot_ref, turned_ref, edge_ref, corner_ref, last_ref, send_ref,
    proj_vmem, wide_ref, cot_vmem, proj_sem, sem,
):
    pieces = proj_sem.shape[0]
    size = proj_ref.shape[0] // pieces
    loads = []
    for n in range(pieces):
        at = pl.ds(n * size, size)
        loads.append(pltpu.make_async_copy(proj_ref.at[at], proj_vmem.at[at], proj_sem.at[n]))
    others = [
        pltpu.make_async_copy(cot_ref, cot_vmem.at[0], sem.at[0]),
        pltpu.make_async_copy(mate_cot_ref, cot_vmem.at[1], sem.at[1]),
        pltpu.make_async_copy(corner_in, corner_ref, sem.at[2]),
        pltpu.make_async_copy(edge_in, edge_ref, sem.at[3]),
    ]
    for copy in loads + others:
        copy.start()
    for n, copy in enumerate(loads):
        copy.wait()
        at = slice(n * size, (n + 1) * size)
        wide_ref[at, :] = proj_vmem[at, :].astype(F32)
    planes = turned_ref.shape[1] // W
    for p in range(planes):
        turned_ref[:, W * p : W * (p + 1)] = wide_ref[pl.ds(p, W, stride=planes), :].T.astype(BF)
    for copy in others:
        copy.wait()

    @pl.when(core_ref[0] == 0)
    def _():
        last = cot_vmem[1].astype(F32).T.astype(BF)
        last_ref[...] = last
        send_ref[:W, :] = cot_vmem[0].astype(F32).T.astype(BF)
        send_ref[W:, :] = step(last, turned_ref, edge_ref)

    @pl.when(core_ref[0] != 0)
    def _():
        last_ref[...] = corner_ref[...]
        moved = step(corner_ref[...], edge_ref, turned_ref)
        send_ref[:W, :] = moved
        send_ref[W:, :] = moved


def by_role(core_ref, body, tensors):
    edge, turned, mate_edge, mate_turned = tensors

    @pl.when(core_ref[0] == 0)
    def _():
        body(edge, turned, mate_edge, mate_turned)

    @pl.when(core_ref[0] != 0)
    def _():
        body(turned, edge, mate_turned, mate_edge)


def ahead_kernel(
    core_ref, corner_ref, e_ref, t_ref, far_edge_ref, far_turned_ref, keep_ref, out_ref, me_ref, mt_ref, sem
):
    copies = [
        pltpu.make_async_copy(far_edge_ref, me_ref, sem.at[0]),
        pltpu.make_async_copy(far_turned_ref, mt_ref, sem.at[1]),
    ]
    for copy in copies:
        copy.start()

    @pl.when(core_ref[0] == 0)
    def _():
        keep_ref[...] = step(corner_ref[...], e_ref, t_ref)

    for copy in copies:
        copy.wait()

    @pl.when(core_ref[0] == 0)
    def _():
        out_ref[...] = step(keep_ref[...], me_ref, mt_ref)

    @pl.when(core_ref[0] != 0)
    def _():
        keep_ref[...] = jnp.zeros_like(keep_ref)
        out_ref[...] = jnp.zeros_like(out_ref)


def first_kernel(
    core_ref, come_ref, corner_ref, keep_ref, ahead_ref, e_ref, t_ref, me_ref, mt_ref, v_ref, near_ref, far_ref
):
    @pl.when(core_ref[0] == 0)
    def _():
        near = step(come_ref[:W, :], e_ref, t_ref)
        fill(near_ref, [keep_ref[...], near])
        fill(far_ref, [ahead_ref[...], step(near, me_ref, mt_ref)])
        fill(v_ref, [corner_ref[...], come_ref[:W, :]])

    @pl.when(core_ref[0] != 0)
    def _():
        near = jnp.concatenate(split(step(come_ref[...], t_ref, e_ref)), 0)
        near_ref[...] = near
        fill(far_ref, split(step(near, mt_ref, me_ref)))
        v_ref[...] = come_ref[...]


def double_kernel(core_ref, come_ref, e_ref, t_ref, me_ref, mt_ref, m1_ref, near_ref, far_ref):
    def body(x1, y1, x2, y2):
        near = jnp.concatenate(split(step(come_ref[...], x1, y1)), 0)
        near_ref[...] = near
        far_ref[...] = jnp.concatenate(split(step(near, x2, y2)), 0)

    by_role(core_ref, body, (e_ref, t_ref, me_ref, mt_ref))


def blocks(ref):
    return [ref[W * b : W * (b + 1), :] for b in range(ref.shape[0] // W)]


def fill(ref, parts):
    for b, part in enumerate(parts):
        ref[W * b : W * (b + 1), :] = part


def pairs_of(z_ref, x_ref, w_ref, put):
    n = z_ref.shape[0] // W
    for t in range(x_ref.shape[1] // (2 * W)):
        mid = dot(z_ref[...], x_ref[:, 2 * W * t : 2 * W * (t + 1)]).astype(BF)
        for half in range(2):
            flat = jnp.concatenate([mid[W * k : W * (k + 1), W * half : W * (half + 1)] for k in range(n)], 1)
            put(2 * t + half, dot(flat, w_ref[...]))


def place(core_ref, z_ref, w_ref, v, u):
    @pl.when(core_ref[0] == 0)
    def _():
        fill(z_ref, v)
        fill(w_ref, u)

    @pl.when(core_ref[0] != 0)
    def _():
        fill(z_ref, u)
        fill(w_ref, v)


def proj_early_kernel(core_ref, v_ref, r1_ref, m1_ref, m2_ref, edge_ref, out_ref, z_ref, w_ref):
    place(core_ref, z_ref, w_ref, [v_ref[W:, :]] + blocks(r1_ref), blocks(m2_ref)[::-1] + [m1_ref[W:, :]])

    def put(p, value):
        out_ref[:, W * p : W * (p + 1)] = value

    pairs_of(z_ref, edge_ref, w_ref, put)


def pass_kernel(value_ref, after_ref, out_ref):
    out_ref[...] = value_ref[...]


def proj_late_kernel(core_ref, r2_ref, m1_ref, last_ref, edge_ref, early_ref, out_ref, z_ref, w_ref):
    place(core_ref, z_ref, w_ref, blocks(r2_ref), [m1_ref[:W, :], last_ref[...]])

    def put(p, value):
        at = slice(W * p, W * (p + 1))
        out_ref[:, at] = early_ref[:, at] + value

    pairs_of(z_ref, edge_ref, w_ref, put)


def proj_last_kernel(
    core_ref, v_ref, m3_ref, e_ref, me_ref, mt_ref, sum_ref, near_ref, out_ref, z_ref, w_ref, stage_ref, sem
):
    def body(x1, y1, x2, y2):
        near_ref[...] = step(m3_ref[:W, :], y2, x2)

    by_role(core_ref, body, (None, None, me_ref, mt_ref))
    place(core_ref, z_ref, w_ref, [v_ref[:W, :]], [near_ref[...]])
    pieces = sem.shape[0]
    each = e_ref.shape[1] // W // pieces
    copies = []

    def put(p, value):
        at = slice(W * p, W * (p + 1))
        stage_ref[:, at] = (sum_ref[:, at] + value).astype(BF)
        if (p + 1) % each == 0:
            at = pl.ds(W * (p + 1 - each), W * each)
            copies.append(pltpu.make_async_copy(stage_ref.at[:, at], out_ref.at[:, at], sem.at[p // each]))
            copies[-1].start()

    pairs_of(z_ref, e_ref, w_ref, put)
    for copy in copies:
        copy.wait()


def edge_kernel(
    core_ref, v_ref, r1_ref, r2_ref, near_ref, m2_ref, m1_ref, last_ref, edge_ref, turned_ref,
    out_ref, grad_ref, z_ref, w_ref, sem,
):
    def halves(ref):
        return [ref.at[pl.ds(0, W)], ref.at[pl.ds(W, W)]]

    v = halves(v_ref) + halves(r1_ref) + halves(r2_ref)
    u = [near_ref] + halves(m2_ref)[::-1] + halves(m1_ref)[::-1] + [last_ref]

    def fetch(z_parts, w_parts):
        copies = []
        for n, part in enumerate(z_parts + w_parts):
            k = n % len(z_parts)
            to = z_ref if n < len(z_parts) else w_ref
            copies.append(pltpu.make_async_copy(part, to.at[pl.ds(W * k, W)], sem.at[n]))
        for copy in copies:
            copy.start()
        for copy in copies:
            copy.wait()

    @pl.when(core_ref[0] == 0)
    def _():
        fetch(u, v)

    @pl.when(core_ref[0] != 0)
    def _():
        fetch(v[::-1], u[::-1])

    def put(p, value):
        out_ref[:, W * p : W * (p + 1)] = value.T.astype(BF)

    pairs_of(z_ref, turned_ref, w_ref, put)
    grad_ref[...] = step(z_ref[:W, :], turned_ref, edge_ref).astype(F32).T.astype(BF)


def gather_kernel(parts_ref, out_ref):
    rows = parts_ref.shape[1]
    planes = parts_ref.shape[2] // W
    for p in range(planes):
        out_ref[pl.ds(p, rows, stride=planes), :] = jnp.sum(
            parts_ref[:, :, W * p : W * (p + 1)].astype(F32), axis=0
        )


def call(kernel, shapes, *args, scratch=(), sems=(), flops=0, far=(), free=(), far_outs=(), alias=None):
    def spec(n, arg):
        if n in far or n in free:
            return pl.BlockSpec(memory_space=pl.ANY)
        return pl.BlockSpec(memory_space=pltpu.SMEM if arg.dtype == jnp.int32 else pltpu.VMEM)

    moved = sum(arg.size * arg.dtype.itemsize for arg in args)
    single = len(shapes) == 1
    outs = [
        pltpu.HBM(shape, kind) if n in far_outs else jax.ShapeDtypeStruct(shape, kind)
        for n, (shape, kind) in enumerate(shapes)
    ]
    out_specs = [pl.BlockSpec(memory_space=pl.ANY if n in far_outs else pltpu.VMEM) for n in range(len(shapes))]
    in_specs = [spec(n, arg) for n, arg in enumerate(args)]
    args = [pltpu.with_memory_space_constraint(arg, pltpu.HBM) if n in far else arg for n, arg in enumerate(args)]
    return pl.pallas_call(
        kernel,
        out_shape=outs[0] if single else outs,
        in_specs=in_specs,
        out_specs=out_specs[0] if single else out_specs,
        scratch_shapes=[pltpu.VMEM(shape, kind) for shape, kind in scratch]
        + [pltpu.SemaphoreType.DMA((count,)) for count in sems],
        input_output_aliases=alias or {},
        compiler_params=pltpu.CompilerParams(vmem_limit_bytes=16 * 1024 * 1024),
        cost_estimate=pl.CostEstimate(flops=flops, bytes_accessed=moved, transcendentals=0),
    )(*args)


def shards(corners, edges, projectors, cotangent):
    corner = corners[0, 0]
    edge = edges[0, 0]
    projector = projectors[0]
    cot = cotangent[0, 0]
    width = edge.shape[1]
    rows = lax.axis_size("row")
    cols = lax.axis_size("col")
    core = (lax.axis_index("col") % 2).astype(jnp.int32).reshape(1)
    unit = 2 * W * W * width

    def send(value, to):
        pairs = [(i, to(i) % cols) for i in range(cols) if to(i) is not None]
        return lax.ppermute(value, "col", pairs)

    def swap(value):
        return send(value, lambda i: i ^ 1)

    def onward(value):
        return send(value, lambda i: i + 2 if i % 2 == 0 else i - 2)

    one, two = ((W, W), BF), ((2 * W, W), BF)
    whole, wide = ((W, width), BF), ((W, width), F32)

    def stacks(n):
        return [((n * W, W), BF), ((n * W, W), BF)]

    mate_cot = swap(cot)
    far_edge = swap(edge)
    turned, edge, corner, u0, first = call(
        start_kernel, [whole, whole, one, one, two], core, projector, edge, corner, cot, mate_cot,
        scratch=[((width, W), BF), ((width, W), F32), ((2, W, W), BF)], sems=(4, 4), flops=3 * unit,
        far=(1, 2, 3, 4), free=(5,),
    )
    r0 = send(first, lambda i: i - 1 if i % 2 == 0 else i + 1)
    far_turned = swap(turned)
    keep, ahead, mate_edge, mate_turned = call(
        ahead_kernel, [one, one, whole, whole], core, corner, edge, turned, far_edge, far_turned,
        sems=(2,), flops=4 * unit, free=(4, 5),
    )
    tensors = (edge, turned, mate_edge, mate_turned)
    v, near1, go1 = call(first_kernel, [two, two, two], core, r0, corner, keep, ahead, *tensors, flops=4 * unit)
    r1 = onward(go1)
    m1 = swap(near1)
    near2, go2 = call(double_kernel, [two, two], core, r1, *tensors, m1, flops=8 * unit)
    r2 = onward(go2)
    m2 = swap(near2)
    early = call(proj_early_kernel, [wide], core, v, r1, m1, m2, edge, scratch=stacks(3), flops=6 * unit)
    r2 = call(pass_kernel, [two], r2, early, free=(1,))
    m3 = swap(r2)
    late = call(proj_late_kernel, [wide], core, r2, m1, u0, edge, early, scratch=stacks(2), flops=4 * unit, alias={5: 0})
    near3, done = call(
        proj_last_kernel, [one, whole], core, v, m3, edge, mate_edge, mate_turned, late,
        scratch=stacks(1) + [whole], sems=(6,), flops=4 * unit, far_outs=(1,),
    )
    share = W // rows
    parts = lax.all_to_all(done.reshape(rows, share, width), "row", 0, 0, tiled=True)
    edge_grad, corner_grad = call(
        edge_kernel, [whole, one], core, v, r1, r2, near3, m2, m1, u0, edge, turned,
        scratch=stacks(6), sems=(12,), flops=14 * unit, far=range(1, 8),
    )
    proj = call(gather_kernel, [((share * width // W, W), F32)], parts, flops=unit)
    return (corner_grad[None, None], edge_grad[None, None], proj[None])


def solution(mesh):
    placed = (
        P("row", "col", None, None),
        P("row", "col", None, None),
        P("col", None, None),
        P("row", "col", None, None),
    )
    return jax.shard_map(
        shards,
        mesh=mesh,
        in_specs=placed,
        out_specs=(P("row", "col", None, None), P("row", "col", None, None), P("col", "row", None)),
        check_vma=False,
    )
```

time: 67.5 us -> 68.1 us (level)
  starting transfers between devices: 30.6 us -> 24.4 us
  waiting for transfers between devices: 9.22 us -> 15.3 us
  local copies, waits for them, and re-layouts: 0.04 us -> 1.99 us
  Pallas kernels: 26.6 us -> 25.3 us
    ppermute x10 -> x9, starting transfers between devices: 26.3 us -> 20.2 us  [send(): return lax.ppermute(value, 'col', pairs)]
    ppermute x10 -> x9, waiting for transfers between devices: 2.86 us -> 5.97 us  [send(): return lax.ppermute(value, 'col', pairs)]
    all_to_all x1, waiting for transfers between devices: 6.36 us -> 9.37 us  [shards(): lax.all_to_all(done.reshape(rows, share, width), 'row', 0, 0, tiled=True)]
    unnamed x20 -> x18, local copies, waits for them, and re-layouts: 0.04 us -> 1.99 us
    pallas_call x10, Pallas kernels: 26.6 us -> 25.3 us  [call(): pl.pallas_call(kernel, out_shape=outs[0] if single else outs, in_specs=in...]
  transfers between devices with their start and end apart: 11 -> 10, of which waited for: 5 -> 5; matrix products, arithmetic and copies ran while one was open for 0% -> 0% of each run, Pallas kernels for 24% -> 21%
where the time goes in v5:
time: 68.1 us; the launch traced here: 67.8 us
  Pallas kernels  25.3 us (37%)
  starting transfers between devices  24.4 us (36%)
  waiting for transfers between devices  15.3 us (22%)
  local copies, waits for them, and re-layouts  1.99 us (3%)
  between operations  0.79 us (1%)
    pallas_call x10, Pallas kernels, call(): pl.pallas_call(kernel, out_shape=outs[0] if single else outs, in_specs=in...  25.3 us
    ppermute x9, starting transfers between devices, send(): return lax.ppermute(value, 'col', pairs)  20.2 us
    all_to_all x1, waiting for transfers between devices, shards(): lax.all_to_all(done.reshape(rows, share, width), 'row', 0, 0, tiled=True)  9.37 us
    ppermute x9, waiting for transfers between devices, send(): return lax.ppermute(value, 'col', pairs)  5.97 us
    all_to_all x1, starting transfers between devices, shards(): lax.all_to_all(done.reshape(rows, share, width), 'row', 0, 0, tiled=True)  4.22 us
    unnamed x18, local copies, waits for them, and re-layouts  1.99 us
  transfers between devices with their start and end apart: 10, of which 5 were waited for; matrix products, arithmetic and copies ran while one was open for 0% of the time, Pallas kernels for 21%

profile of v5, /device:TPU:1, one launch (start us, length us, event | category | flops | bytes accessed | tf_op | source)
XLA Modules:
  0.0 67.8 jit_solution(17976966981878864256)
XLA Ops:
  0.6 3.3 %collective-permute-start = (bf16[128,128]{1,0:T(8,128)(2,1)}, bf16[128,128]{1,0:T(8,128)(2,1)S(1)}, u32[]{:S(2)}, u32[]{:S(2)}) collective-permute-start(bf16[128,128]{1,0:T(8,128)(2,1)} %bitcast.15), channel_id=1, source_target_pairs={{0,1},{1,0},{2,3},{3,2},{4,5},{5,4},{6,7},{7,6},{8,9},{9,8},{10,11... | collective-permute-start | bytes 98312 | tf_op jit(solution)/shard_map/ppermute | solution.py:309
  4.0 0.1 collective-permute-start.2
  4.1 1.0 %collective-permute-done.mate_cot_ref = bf16[128,128]{1,0:T(8,128)(2,1)S(1)} collective-permute-done((bf16[128,128]{1,0:T(8,128)(2,1)}, bf16[128,128]{1,0:T(8,128)(2,1)S(1)}, u32[]{:S(2)}, u32[]{:S(2)}) %collective-permute-start) | collective-permute-done | bytes 32800 | tf_op jit(solution)/shard_map/ppermute | solution.py:309
  5.0 0.0 copy-start.6
  5.0 0.6 copy-done.6
  5.6 0.0 copy-start.7
  5.6 0.8 %copy-done.7 = bf16[128,128]{1,0:T(8,128)(2,1)S(1)} copy-done((bf16[128,128]{1,0:T(8,128)(2,1)S(1)}, bf16[128,128]{1,0:T(8,128)(2,1)}, u32[]{:S(2)}) %copy-start.7) | copy-done | bytes 32792
  6.4 2.8 %shard_map.67 = (bf16[128,4608]{1,0:T(8,128)(2,1)S(1)}, bf16[128,4608]{1,0:T(8,128)(2,1)S(1)}, bf16[128,128]{1,0:T(8,128)(2,1)S(1)}, bf16[128,128]{1,0:T(8,128)(2,1)S(1)}, bf16[256,128]{1,0:T(8,128)(2,1)S(1)}) custom-call(s32[1]{0:T(128)} %bitcast.core_ref, bf16[4608,128]{1,0:T(8,128)(2,1)} %bitcast.10, bf16[128,4608]{1,0:T(8,128)(2,1)} %bitcast.12, ...), custom_call_target="tpu_custom_call" | custom-call | flops 452984832 | bytes 2457604 | tf_op jit(solution)/shard_map/pallas_call | solution.py:283
  9.2 0.0 copy-start.5
  9.2 0.5 collective-permute-start.3
  9.7 1.0 %collective-permute-start.1 = (bf16[256,128]{1,0:T(8,128)(2,1)S(1)}, bf16[256,128]{1,0:T(8,128)(2,1)S(1)}, u32[]{:S(2)}, u32[]{:S(2)}) collective-permute-start(bf16[256,128]{1,0:T(8,128)(2,1)S(1)} %get-tuple-element.21), channel_id=1, source_target_pairs={{0,31},{1,2},{2,1},{3,4},{4,3},{5,6},{6,5},{7,8},{8,7},{9,10},{10,... | collective-permute-start | bytes 196616 | tf_op jit(solution)/shard_map/ppermute | solution.py:309
  10.7 0.0 collective-permute-done.2.far_edge_ref
  10.7 1.5 %collective-permute-done.3.far_turned_ref = bf16[128,4608]{1,0:T(8,128)(2,1)S(1)} collective-permute-done((bf16[128,4608]{1,0:T(8,128)(2,1)S(1)}, bf16[128,4608]{1,0:T(8,128)(2,1)S(1)}, u32[]{:S(2)}, u32[]{:S(2)}) %collective-permute-start.3) | collective-permute-done | bytes 1179680 | tf_op jit(solution)/shard_map/ppermute | solution.py:309
  12.2 0.5 shard_map.68
  12.7 2.2 %collective-permute-done.1.come_ref = bf16[256,128]{1,0:T(8,128)(2,1)S(1)} collective-permute-done((bf16[256,128]{1,0:T(8,128)(2,1)S(1)}, bf16[256,128]{1,0:T(8,128)(2,1)S(1)}, u32[]{:S(2)}, u32[]{:S(2)}) %collective-permute-start.1) | collective-permute-done | bytes 65568 | tf_op jit(solution)/shard_map/ppermute | solution.py:309
  14.9 3.5 %shard_map.69 = (bf16[256,128]{1,0:T(8,128)(2,1)S(1)}, bf16[256,128]{1,0:T(8,128)(2,1)S(1)}, bf16[256,128]{1,0:T(8,128)(2,1)S(1)}) custom-call(s32[1]{0:T(128)} %bitcast.core_ref, bf16[256,128]{1,0:T(8,128)(2,1)S(1)} %collective-permute-done.1.come_ref, bf16[128,128]{1,0:T(8,128)(2,1)S(1)} %get-tuple-element.22.corner_ref, ...), custom_call_target="tpu_custom_call" | custom-call | flops 603979776 | bytes 4882436 | tf_op jit(solution)/shard_map/pallas_call | solution.py:283
  18.4 0.0 copy-start.1
  18.4 8.5 %collective-permute-start.4 = (bf16[256,128]{1,0:T(8,128)(2,1)S(1)}, bf16[256,128]{1,0:T(8,128)(2,1)S(1)}, u32[]{:S(2)}, u32[]{:S(2)}) collective-permute-start(bf16[256,128]{1,0:T(8,128)(2,1)S(1)} %get-tuple-element.30), channel_id=1, source_target_pairs={{0,2},{1,31},{2,4},{3,1},{4,6},{5,3},{6,8},{7,5},{8,10},{9,7},{10,... | collective-permute-start | bytes 196616 | tf_op jit(solution)/shard_map/ppermute | solution.py:309
  26.9 0.0 collective-permute-start.5
  26.9 1.3 %collective-permute-done.4.come_ref.r1_ref = bf16[256,128]{1,0:T(8,128)(2,1)S(1)} collective-permute-done((bf16[256,128]{1,0:T(8,128)(2,1)S(1)}, bf16[256,128]{1,0:T(8,128)(2,1)S(1)}, u32[]{:S(2)}, u32[]{:S(2)}) %collective-permute-start.4) | collective-permute-done | bytes 65568 | tf_op jit(solution)/shard_map/ppermute | solution.py:309
  28.3 0.0 copy-start.2
  28.3 0.0 collective-permute-done.5.m1_ref
  28.3 0.0 copy-start
  28.3 3.5 %shard_map.70 = (bf16[256,128]{1,0:T(8,128)(2,1)S(1)}, bf16[256,128]{1,0:T(8,128)(2,1)S(1)}) custom-call(s32[1]{0:T(128)} %bitcast.core_ref, bf16[256,128]{1,0:T(8,128)(2,1)S(1)} %collective-permute-done.4.come_ref.r1_ref, bf16[128,4608]{1,0:T(8,128)(2,1)S(1)} %get-tuple-element.23.e_ref.edge_ref, bf16[128,4608]{1,0:T(8,128)(2,1)S(1)} %get-tuple-element.24.t_ref.turned_ref, ...), custom_call_target="tpu_custom_call" | custom-call | flops 1207959552 | bytes 4849668 | tf_op jit(solution)/shard_map/pallas_call | solution.py:283
  31.8 1.0 %collective-permute-start.7 = (bf16[256,128]{1,0:T(8,128)(2,1)S(1)}, bf16[256,128]{1,0:T(8,128)(2,1)S(1)}, u32[]{:S(2)}, u32[]{:S(2)}) collective-permute-start(bf16[256,128]{1,0:T(8,128)(2,1)S(1)} %get-tuple-element.33), channel_id=1, source_target_pairs={{0,1},{1,0},{2,3},{3,2},{4,5},{5,4},{6,7},{7,6},{8,9},{9,8},{10,11... | collective-permute-start | bytes 196616 | tf_op jit(solution)/shard_map/ppermute | solution.py:309
  32.8 4.7 %collective-permute-start.6 = (bf16[256,128]{1,0:T(8,128)(2,1)S(1)}, bf16[256,128]{1,0:T(8,128)(2,1)S(1)}, u32[]{:S(2)}, u32[]{:S(2)}) collective-permute-start(bf16[256,128]{1,0:T(8,128)(2,1)S(1)} %get-tuple-element.32), channel_id=1, source_target_pairs={{0,2},{1,31},{2,4},{3,1},{4,6},{5,3},{6,8},{7,5},{8,10},{9,7},{10,... | collective-permute-start | bytes 196616 | tf_op jit(solution)/shard_map/ppermute | solution.py:309
  37.6 0.0 collective-permute-done.7.m2_ref
  37.6 0.0 copy-start.4
  37.6 0.0 copy-done.2
  37.6 2.2 %shard_map.71.after_ref.early_ref = f32[128,4608]{1,0:T(8,128)S(1)} custom-call(s32[1]{0:T(128)} %bitcast.core_ref, bf16[256,128]{1,0:T(8,128)(2,1)S(1)} %get-tuple-element.29.v_ref, bf16[256,128]{1,0:T(8,128)(2,1)S(1)} %collective-permute-done.4.come_ref.r1_ref, bf16[256,128]{1,0:T(8,128)(2,1)S(1)} %collective-permute-done.5.m1_ref, ...), custom_call_target="tpu_custom_call" | custom-call | flops 905969664 | bytes 1441796 | tf_op jit(solution)/shard_map/pallas_call | solution.py:283
  39.8 0.0 copy-done.4
  39.8 0.0 collective-permute-done.6.value_ref
  39.8 0.0 copy-start.3
  39.8 1.1 %collective-permute-start.8 = (bf16[256,128]{1,0:T(8,128)(2,1)S(1)}, bf16[256,128]{1,0:T(8,128)(2,1)S(1)}, u32[]{:S(2)}, u32[]{:S(2)}) collective-permute-start(bf16[256,128]{1,0:T(8,128)(2,1)S(1)} %shard_map.72.r2_ref), channel_id=1, source_target_pairs={{0,1},{1,0},{2,3},{3,2},{4,5},{5,4},{6,7},{7,6},{8,9},{9,8},{10,11... | collective-permute-start | bytes 196616 | tf_op jit(solution)/shard_map/ppermute | solution.py:309
  40.9 0.0 copy-done.5
  40.9 0.0 copy-done
  40.9 1.8 %shard_map.73.sum_ref = f32[128,4608]{1,0:T(8,128)S(1)} custom-call(s32[1]{0:T(128)} %bitcast.core_ref, bf16[256,128]{1,0:T(8,128)(2,1)S(1)} %shard_map.72.r2_ref, bf16[256,128]{1,0:T(8,128)(2,1)S(1)} %collective-permute-done.5.m1_ref, bf16[128,128]{1,0:T(8,128)(2,1)S(1)} %get-tuple-element.34.last_ref, ...), custom_call_target="tpu_custom_call", output_to_operand_aliasing={{}: (5, {})} | custom-call | flops 603979776 | bytes 3702788 | tf_op jit(solution)/shard_map/pallas_call | solution.py:283
  42.8 0.0 copy-done.3
  42.8 0.0 collective-permute-done.8.m3_ref
  42.8 0.0 copy-done.1
  42.8 2.9 %shard_map.74 = (bf16[128,128]{1,0:T(8,128)(2,1)S(1)}, bf16[128,4608]{1,0:T(8,128)(2,1)}) custom-call(s32[1]{0:T(128)} %bitcast.core_ref, bf16[256,128]{1,0:T(8,128)(2,1)S(1)} %get-tuple-element.29.v_ref, bf16[256,128]{1,0:T(8,128)(2,1)S(1)} %collective-permute-done.8.m3_ref, bf16[128,4608]{1,0:T(8,128)(2,1)S(1)} %get-tuple-element.23.e_ref.edge_ref, ...), custom_call_target="tpu_custom_call" | custom-call | flops 603979776 | bytes 6029316 | tf_op jit(solution)/shard_map/pallas_call | solution.py:283
  45.7 0.0 copy-start.8
  45.7 0.6 copy-done.8
  46.3 4.2 %all-to-all-start = ((bf16[8,16,4608]{2,1,0:T(8,128)(2,1)}), bf16[8,16,4608]{2,1,0:T(8,128)(2,1)S(1)}, u32[]{:S(2)}, u32[]{:S(2)}) async-start(bf16[8,16,4608]{2,1,0:T(8,128)(2,1)} %bitcast.9), calls=%async_computation | async-start | bytes 2359296 | tf_op jit(solution)/shard_map/all_to_all | solution.py:352
  50.6 7.0 %shard_map.75 = (bf16[128,4608]{1,0:T(8,128)(2,1)}, bf16[128,128]{1,0:T(8,128)(2,1)}) custom-call(s32[1]{0:T(128)} %bitcast.core_ref, bf16[256,128]{1,0:T(8,128)(2,1)} %copy-done.1, bf16[256,128]{1,0:T(8,128)(2,1)} %copy-done.2, bf16[256,128]{1,0:T(8,128)(2,1)} %copy-done.3, bf16[128,128]{1,0:T(8,128)(2,1)} %copy-done.8, bf16[256,128]{1,0:T(8,128)(2,1)} %copy-done.4, ...), custom_call_target="tpu_custom_call" | custom-call | flops 2113929216 | bytes 2752516 | tf_op jit(solution)/shard_map/pallas_call | solution.py:283
  57.6 9.4 %all-to-all-done.parts_ref = bf16[8,16,4608]{2,1,0:T(8,128)(2,1)S(1)} async-done(((bf16[8,16,4608]{2,1,0:T(8,128)(2,1)}), bf16[8,16,4608]{2,1,0:T(8,128)(2,1)S(1)}, u32[]{:S(2)}, u32[]{:S(2)}) %all-to-all-start) | async-done | bytes 1179680 | tf_op jit(solution)/shard_map/all_to_all | solution.py:352
  67.0 0.9 %shard_map.76 = f32[576,128]{1,0:T(8,128)} custom-call(bf16[8,16,4608]{2,1,0:T(8,128)(2,1)S(1)} %all-to-all-done.parts_ref), custom_call_target="tpu_custom_call" | custom-call | flops 150994944 | bytes 1179648 | tf_op jit(solution)/shard_map/pallas_call | solution.py:283
  (1 shorter events, 0.0 us)
Async XLA Ops:
  0.6 4.4 %collective-permute-start = (bf16[128,128]{1,0:T(8,128)(2,1)}, bf16[128,128]{1,0:T(8,128)(2,1)S(1)}, u32[]{:S(2)}, u32[]{:S(2)}) collective-permute-start(bf16[128,128]{1,0:T(8,128)(2,1)} %bitcast.15), channel_id=1, source_target_pairs={{0,1},{1,0},{2,3},{3,2},{4,5},{5,4},{6,7},{7,6},{8,9},{9,8},{10,11... | collective-permute-start | bytes 98312 | tf_op jit(solution)/shard_map/ppermute | solution.py:309
  4.0 6.7 %collective-permute-start.2 = (bf16[128,4608]{1,0:T(8,128)(2,1)}, bf16[128,4608]{1,0:T(8,128)(2,1)S(1)}, u32[]{:S(2)}, u32[]{:S(2)}) collective-permute-start(bf16[128,4608]{1,0:T(8,128)(2,1)} %bitcast.11), channel_id=1, source_target_pairs={{0,1},{1,0},{2,3},{3,2},{4,5},{5,4},{6,7},{7,6},{8,9},{9,8},{10,11... | collective-permute-start | bytes 3538952 | tf_op jit(solution)/shard_map/ppermute | solution.py:309
  5.0 0.6 copy-start.6
  5.6 0.8 %copy-start.7 = (bf16[128,128]{1,0:T(8,128)(2,1)S(1)}, bf16[128,128]{1,0:T(8,128)(2,1)}, u32[]{:S(2)}) copy-start(bf16[128,128]{1,0:T(8,128)(2,1)} %copy-done.6) | copy-start | bytes 98308
  9.2 31.7 %copy-start.5 = (bf16[128,128]{1,0:T(8,128)(2,1)}, bf16[128,128]{1,0:T(8,128)(2,1)S(1)}, u32[]{:S(2)}) copy-start(bf16[128,128]{1,0:T(8,128)(2,1)S(1)} %get-tuple-element.34.last_ref) | copy-start | bytes 98308
  9.2 3.0 %collective-permute-start.3 = (bf16[128,4608]{1,0:T(8,128)(2,1)S(1)}, bf16[128,4608]{1,0:T(8,128)(2,1)S(1)}, u32[]{:S(2)}, u32[]{:S(2)}) collective-permute-start(bf16[128,4608]{1,0:T(8,128)(2,1)S(1)} %get-tuple-element.24.t_ref.turned_ref), channel_id=1, source_target_pairs={{0,1},{1,0},{2,3},{3,2},{4,5},{5,4},{6,7},{7,6},{8,9},{9,8},{10,11... | collective-permute-start | bytes 3538952 | tf_op jit(solution)/shard_map/ppermute | solution.py:309
  9.7 5.2 %collective-permute-start.1 = (bf16[256,128]{1,0:T(8,128)(2,1)S(1)}, bf16[256,128]{1,0:T(8,128)(2,1)S(1)}, u32[]{:S(2)}, u32[]{:S(2)}) collective-permute-start(bf16[256,128]{1,0:T(8,128)(2,1)S(1)} %get-tuple-element.21), channel_id=1, source_target_pairs={{0,31},{1,2},{2,1},{3,4},{4,3},{5,6},{6,5},{7,8},{8,7},{9,10},{10,... | collective-permute-start | bytes 196616 | tf_op jit(solution)/shard_map/ppermute | solution.py:309
  18.4 24.3 %copy-start.1 = (bf16[256,128]{1,0:T(8,128)(2,1)}, bf16[256,128]{1,0:T(8,128)(2,1)S(1)}, u32[]{:S(2)}) copy-start(bf16[256,128]{1,0:T(8,128)(2,1)S(1)} %get-tuple-element.29.v_ref) | copy-start | bytes 196612
  18.4 9.8 %collective-permute-start.4 = (bf16[256,128]{1,0:T(8,128)(2,1)S(1)}, bf16[256,128]{1,0:T(8,128)(2,1)S(1)}, u32[]{:S(2)}, u32[]{:S(2)}) collective-permute-start(bf16[256,128]{1,0:T(8,128)(2,1)S(1)} %get-tuple-element.30), channel_id=1, source_target_pairs={{0,2},{1,31},{2,4},{3,1},{4,6},{5,3},{6,8},{7,5},{8,10},{9,7},{10,... | collective-permute-start | bytes 196616 | tf_op jit(solution)/shard_map/ppermute | solution.py:309
  26.9 1.3 %collective-permute-start.5 = (bf16[256,128]{1,0:T(8,128)(2,1)S(1)}, bf16[256,128]{1,0:T(8,128)(2,1)S(1)}, u32[]{:S(2)}, u32[]{:S(2)}) collective-permute-start(bf16[256,128]{1,0:T(8,128)(2,1)S(1)} %get-tuple-element.31), channel_id=1, source_target_pairs={{0,1},{1,0},{2,3},{3,2},{4,5},{5,4},{6,7},{7,6},{8,9},{9,8},{10,11... | collective-permute-start | bytes 196616 | tf_op jit(solution)/shard_map/ppermute | solution.py:309
  28.3 9.3 %copy-start.2 = (bf16[256,128]{1,0:T(8,128)(2,1)}, bf16[256,128]{1,0:T(8,128)(2,1)S(1)}, u32[]{:S(2)}) copy-start(bf16[256,128]{1,0:T(8,128)(2,1)S(1)} %collective-permute-done.4.come_ref.r1_ref) | copy-start | bytes 196612
  28.3 12.6 %copy-start = (bf16[256,128]{1,0:T(8,128)(2,1)}, bf16[256,128]{1,0:T(8,128)(2,1)S(1)}, u32[]{:S(2)}) copy-start(bf16[256,128]{1,0:T(8,128)(2,1)S(1)} %collective-permute-done.5.m1_ref) | copy-start | bytes 196612
  31.8 5.8 %collective-permute-start.7 = (bf16[256,128]{1,0:T(8,128)(2,1)S(1)}, bf16[256,128]{1,0:T(8,128)(2,1)S(1)}, u32[]{:S(2)}, u32[]{:S(2)}) collective-permute-start(bf16[256,128]{1,0:T(8,128)(2,1)S(1)} %get-tuple-element.33), channel_id=1, source_target_pairs={{0,1},{1,0},{2,3},{3,2},{4,5},{5,4},{6,7},{7,6},{8,9},{9,8},{10,11... | collective-permute-start | bytes 196616 | tf_op jit(solution)/shard_map/ppermute | solution.py:309
  32.8 7.0 %collective-permute-start.6 = (bf16[256,128]{1,0:T(8,128)(2,1)S(1)}, bf16[256,128]{1,0:T(8,128)(2,1)S(1)}, u32[]{:S(2)}, u32[]{:S(2)}) collective-permute-start(bf16[256,128]{1,0:T(8,128)(2,1)S(1)} %get-tuple-element.32), channel_id=1, source_target_pairs={{0,2},{1,31},{2,4},{3,1},{4,6},{5,3},{6,8},{7,5},{8,10},{9,7},{10,... | collective-permute-start | bytes 196616 | tf_op jit(solution)/shard_map/ppermute | solution.py:309
  37.6 2.2 %copy-start.4 = (bf16[256,128]{1,0:T(8,128)(2,1)}, bf16[256,128]{1,0:T(8,128)(2,1)S(1)}, u32[]{:S(2)}) copy-start(bf16[256,128]{1,0:T(8,128)(2,1)S(1)} %collective-permute-done.7.m2_ref) | copy-start | bytes 196612
  39.8 2.9 %copy-start.3 = (bf16[256,128]{1,0:T(8,128)(2,1)}, bf16[256,128]{1,0:T(8,128)(2,1)S(1)}, u32[]{:S(2)}) copy-start(bf16[256,128]{1,0:T(8,128)(2,1)S(1)} %shard_map.72.r2_ref) | copy-start | bytes 196612
  39.8 2.9 %collective-permute-start.8 = (bf16[256,128]{1,0:T(8,128)(2,1)S(1)}, bf16[256,128]{1,0:T(8,128)(2,1)S(1)}, u32[]{:S(2)}, u32[]{:S(2)}) collective-permute-start(bf16[256,128]{1,0:T(8,128)(2,1)S(1)} %shard_map.72.r2_ref), channel_id=1, source_target_pairs={{0,1},{1,0},{2,3},{3,2},{4,5},{5,4},{6,7},{7,6},{8,9},{9,8},{10,11... | collective-permute-start | bytes 196616 | tf_op jit(solution)/shard_map/ppermute | solution.py:309
  45.7 0.6 copy-start.8
  46.3 20.6 %all-to-all-start = ((bf16[8,16,4608]{2,1,0:T(8,128)(2,1)}), bf16[8,16,4608]{2,1,0:T(8,128)(2,1)S(1)}, u32[]{:S(2)}, u32[]{:S(2)}) async-start(bf16[8,16,4608]{2,1,0:T(8,128)(2,1)} %bitcast.9), calls=%async_computation | async-start | bytes 2359296 | tf_op jit(solution)/shard_map/all_to_all | solution.py:352

commit v6 on v5

--- a/solution.py
+++ b/solution.py
@@ -7,6 +7,7 @@
 
 
 W = 128
+H = W // 2
 BF = jnp.bfloat16
 F32 = jnp.float32
 
@@ -160,25 +161,70 @@
             put(2 * t + half, dot(flat, w_ref[...]))
 
 
+def block(ref, k):
+    return ref, W * k
+
+
 def place(core_ref, z_ref, w_ref, v, u):
-    @pl.when(core_ref[0] == 0)
-    def _():
-        fill(z_ref, v)
-        fill(w_ref, u)
-
-    @pl.when(core_ref[0] != 0)
-    def _():
-        fill(z_ref, u)
-        fill(w_ref, v)
-
-
-def proj_early_kernel(core_ref, v_ref, r1_ref, m1_ref, m2_ref, edge_ref, out_ref, z_ref, w_ref):
-    place(core_ref, z_ref, w_ref, [v_ref[W:, :]] + blocks(r1_ref), blocks(m2_ref)[::-1] + [m1_ref[W:, :]])
+    def put(corners, adjoints):
+        for n, ((c_ref, c_at), (a_ref, a_at)) in enumerate(zip(corners, adjoints)):
+            at = pl.multiple_of(c_at + H * core_ref[1], H)
+            z_ref[H * n : H * (n + 1), :] = c_ref[pl.ds(at, H), :]
+            w_ref[W * n : W * (n + 1), :] = a_ref[a_at : a_at + W, :]
+
+    @pl.when(core_ref[0] == 0)
+    def _():
+        put(v, u)
+
+    @pl.when(core_ref[0] != 0)
+    def _():
+        put(u, v)
+
+
+def terms_of(z_ref, x_ref, w_ref, put):
+    n = z_ref.shape[0] // H
+    for t in range(x_ref.shape[1] // (2 * W)):
+        mid = dot(z_ref[...], x_ref[:, 2 * W * t : 2 * W * (t + 1)]).astype(BF)
+        flat = jnp.concatenate(
+            [
+                jnp.concatenate([mid[H * k : H * (k + 1), W * half : W * (half + 1)] for k in range(n)], 1)
+                for half in range(2)
+            ],
+            0,
+        )
+        value = dot(flat, w_ref[...])
+        put(2 * t, value[:H, :])
+        put(2 * t + 1, value[H:, :])
+
+
+def adder(from_ref, to_ref):
+    def put(p, value):
+        at = slice(W * p, W * (p + 1))
+        to_ref[:, at] = from_ref[:, at] + value
+
+    return put
+
+
+def pack_kernel(v_ref, m1_ref, last_ref, out_ref):
+    out_ref[: 2 * W, :] = v_ref[...]
+    out_ref[2 * W : 4 * W, :] = m1_ref[...]
+    out_ref[4 * W :, :] = last_ref[...]
+
+
+def middle(v_ref, r1_ref, m1_ref, m2_ref):
+    v = [block(v_ref, 1), block(r1_ref, 0), block(r1_ref, 1)]
+    return v, [block(m2_ref, 1), block(m2_ref, 0), block(m1_ref, 1)]
+
+
+def proj_early_kernel(core_ref, v_ref, r1_ref, m1_ref, m2_ref, edge_ref, out_ref, pack_ref, z_ref, w_ref):
+    place(core_ref, z_ref, w_ref, *middle(v_ref, r1_ref, m1_ref, m2_ref))
+    pack_ref[: 2 * W, :] = r1_ref[...]
+    pack_ref[2 * W :, :] = m2_ref[...]
 
     def put(p, value):
         out_ref[:, W * p : W * (p + 1)] = value
 
-    pairs_of(z_ref, edge_ref, w_ref, put)
+    terms_of(z_ref, edge_ref, w_ref, put)
 
 
 def pass_kernel(value_ref, after_ref, out_ref):
@@ -186,25 +232,37 @@
 
 
 def proj_late_kernel(core_ref, r2_ref, m1_ref, last_ref, edge_ref, early_ref, out_ref, z_ref, w_ref):
-    place(core_ref, z_ref, w_ref, blocks(r2_ref), [m1_ref[:W, :], last_ref[...]])
-
-    def put(p, value):
-        at = slice(W * p, W * (p + 1))
-        out_ref[:, at] = early_ref[:, at] + value
-
-    pairs_of(z_ref, edge_ref, w_ref, put)
-
-
-def proj_last_kernel(
-    core_ref, v_ref, m3_ref, e_ref, me_ref, mt_ref, sum_ref, near_ref, out_ref, z_ref, w_ref, stage_ref, sem
-):
+    place(
+        core_ref, z_ref, w_ref, [block(r2_ref, 0), block(r2_ref, 1)], [block(m1_ref, 0), block(last_ref, 0)]
+    )
+    terms_of(z_ref, edge_ref, w_ref, adder(early_ref, out_ref))
+
+
+def near_kernel(core_ref, m3_ref, me_ref, mt_ref, after_ref, near_ref):
     def body(x1, y1, x2, y2):
         near_ref[...] = step(m3_ref[:W, :], y2, x2)
 
     by_role(core_ref, body, (None, None, me_ref, mt_ref))
-    place(core_ref, z_ref, w_ref, [v_ref[:W, :]], [near_ref[...]])
+
+
+def proj_other_kernel(
+    core_ref, v_ref, near_ref, pack1_ref, pack2_ref, r2_ref, edge_ref, other_edge_ref, sum_ref, out_ref,
+    z1_ref, w1_ref, z_ref, w_ref,
+):
+    place(core_ref, z1_ref, w1_ref, [block(v_ref, 0)], [block(near_ref, 0)])
+    terms_of(z1_ref, edge_ref, w1_ref, adder(sum_ref, out_ref))
+    v = [block(pack1_ref, 1), block(pack2_ref, 0), block(pack2_ref, 1), block(r2_ref, 0), block(r2_ref, 1)]
+    u = [block(pack2_ref, 3), block(pack2_ref, 2), block(pack1_ref, 3), block(pack1_ref, 2), block(pack1_ref, 4)]
+    place(core_ref, z_ref, w_ref, v, u)
+    terms_of(z_ref, other_edge_ref, w_ref, adder(out_ref, out_ref))
+
+
+def proj_last_kernel(
+    core_ref, pack1_ref, near_ref, other_edge_ref, sum_ref, out_ref, z_ref, w_ref, stage_ref, sem
+):
+    place(core_ref, z_ref, w_ref, [block(pack1_ref, 0)], [block(near_ref, 0)])
     pieces = sem.shape[0]
-    each = e_ref.shape[1] // W // pieces
+    each = stage_ref.shape[1] // W // pieces
     copies = []
 
     def put(p, value):
@@ -215,7 +273,7 @@
             copies.append(pltpu.make_async_copy(stage_ref.at[:, at], out_ref.at[:, at], sem.at[p // each]))
             copies[-1].start()
 
-    pairs_of(z_ref, e_ref, w_ref, put)
+    terms_of(z_ref, other_edge_ref, w_ref, put)
     for copy in copies:
         copy.wait()
 
@@ -301,7 +359,8 @@
     width = edge.shape[1]
     rows = lax.axis_size("row")
     cols = lax.axis_size("col")
-    core = (lax.axis_index("col") % 2).astype(jnp.int32).reshape(1)
+    across = rows // 2
+    core = jnp.stack([lax.axis_index("col") % 2, lax.axis_index("row") // across]).astype(jnp.int32)
     unit = 2 * W * W * width
 
     def send(value, to):
@@ -311,21 +370,26 @@
     def swap(value):
         return send(value, lambda i: i ^ 1)
 
+    def trade(value):
+        return lax.ppermute(value, "row", [(i, (i + across) % rows) for i in range(rows)])
+
     def onward(value):
         return send(value, lambda i: i + 2 if i % 2 == 0 else i - 2)
 
     one, two = ((W, W), BF), ((2 * W, W), BF)
-    whole, wide = ((W, width), BF), ((W, width), F32)
+    half = ((H, width), F32)
+    whole = ((W, width), BF)
 
     def stacks(n):
         return [((n * W, W), BF), ((n * W, W), BF)]
 
     mate_cot = swap(cot)
     far_edge = swap(edge)
+    other_edge = trade(edge)
     turned, edge, corner, u0, first = call(
         start_kernel, [whole, whole, one, one, two], core, projector, edge, corner, cot, mate_cot,
         scratch=[((width, W), BF), ((width, W), F32), ((2, W, W), BF)], sems=(4, 4), flops=3 * unit,
-        far=(1, 2, 3, 4), free=(5,),
+        far=(1, 2, 3, 4, 5),
     )
     r0 = send(first, lambda i: i - 1 if i % 2 == 0 else i + 1)
     far_turned = swap(turned)
@@ -337,22 +401,41 @@
     v, near1, go1 = call(first_kernel, [two, two, two], core, r0, corner, keep, ahead, *tensors, flops=4 * unit)
     r1 = onward(go1)
     m1 = swap(near1)
-    near2, go2 = call(double_kernel, [two, two], core, r1, *tensors, m1, flops=8 * unit)
+    pack1 = call(pack_kernel, [((5 * W, W), BF)], v, m1, u0)
+    near2, go2 = call(double_kernel, [two, two], core, r1, *tensors, pack1, flops=8 * unit)
+    other1 = trade(pack1)
     r2 = onward(go2)
     m2 = swap(near2)
-    early = call(proj_early_kernel, [wide], core, v, r1, m1, m2, edge, scratch=stacks(3), flops=6 * unit)
+
+    def halves(n):
+        return [((n * H, W), BF), ((n * W, W), BF)]
+
+    early, pack2 = call(
+        proj_early_kernel, [half, ((4 * W, W), BF)], core, v, r1, m1, m2, edge, scratch=halves(3), flops=3 * unit
+    )
+    other2 = trade(pack2)
     r2 = call(pass_kernel, [two], r2, early, free=(1,))
     m3 = swap(r2)
-    late = call(proj_late_kernel, [wide], core, r2, m1, u0, edge, early, scratch=stacks(2), flops=4 * unit, alias={5: 0})
-    near3, done = call(
-        proj_last_kernel, [one, whole], core, v, m3, edge, mate_edge, mate_turned, late,
-        scratch=stacks(1) + [whole], sems=(6,), flops=4 * unit, far_outs=(1,),
+    other3 = trade(r2)
+    late = call(proj_late_kernel, [half], core, r2, m1, u0, edge, early, scratch=halves(2), flops=2 * unit, alias={5: 0})
+    near3 = call(near_kernel, [one], core, m3, mate_edge, mate_turned, late, flops=2 * unit, free=(4,))
+    other4 = trade(near3)
+    late = call(
+        proj_other_kernel, [half], core, v, near3, other1, other2, other3, edge, other_edge, late,
+        scratch=halves(1) + halves(5), flops=6 * unit, alias={8: 0},
+    )
+    done = call(
+        proj_last_kernel, [((H, width), BF)], core, other1, other4, other_edge, late,
+        scratch=halves(1) + [((H, width), BF)], sems=(6,), flops=unit, far_outs=(0,),
     )
     share = W // rows
-    parts = lax.all_to_all(done.reshape(rows, share, width), "row", 0, 0, tiled=True)
+    groups = [list(range(across)), list(range(across, rows))]
+    parts = lax.all_to_all(
+        done.reshape(across, share, width), "row", 0, 0, tiled=True, axis_index_groups=groups
+    )
     edge_grad, corner_grad = call(
         edge_kernel, [whole, one], core, v, r1, r2, near3, m2, m1, u0, edge, turned,
-        scratch=stacks(6), sems=(12,), flops=14 * unit, far=range(1, 8),
+        scratch=stacks(6), sems=(12,), flops=14 * unit, far=(1, 2, 3, 5, 6, 7),
     )
     proj = call(gather_kernel, [((share * width // W, W), F32)], parts, flops=unit)
     return (corner_grad[None, None], edge_grad[None, None], proj[None])

time: 68.1 us -> 89.6 us (1.32); the launches traced: 67.8 us -> 88.1 us
  waiting for transfers between devices: 15.3 us -> 29.5 us
  Pallas kernels: 25.3 us -> 31.2 us
  starting transfers between devices: 24.4 us -> 25.8 us
  local copies, waits for them, and re-layouts: 1.99 us -> 0.64 us
    ppermute x9, waiting for transfers between devices: 5.97 us -> 28.5 us  [send(): return lax.ppermute(value, 'col', pairs)]
    all_to_all x1, waiting for transfers between devices: 9.37 us -> 0.99 us  [shards(): lax.all_to_all(done.reshape(across, share, width), 'row', 0, 0, tiled=Tru...]
    pallas_call x10 -> x13, Pallas kernels: 25.3 us -> 31.2 us  [call(): pl.pallas_call(kernel, out_shape=outs[0] if single else outs, in_specs=in...]
    ppermute x0 -> x5, starting transfers between devices: none -> 1.84 us  [trade(): lax.ppermute(value, 'row', [(i, (i + across) % rows) for i in range(rows)])]
    unnamed x18 -> x16, local copies, waits for them, and re-layouts: 1.99 us -> 0.64 us
  transfers between devices with their start and end apart: 10 -> 15, of which waited for: 5 -> 5; matrix products, arithmetic and copies ran while one was open for 0% -> 0% of each run, Pallas kernels for 21% -> 32%
where the time goes in v6:
time: 89.6 us; the launch traced here: 88.1 us
  Pallas kernels  31.2 us (35%)
  waiting for transfers between devices  29.5 us (33%)
  starting transfers between devices  25.8 us (29%)
    pallas_call x13, Pallas kernels, call(): pl.pallas_call(kernel, out_shape=outs[0] if single else outs, in_specs=in...  31.2 us
    ppermute x9, waiting for transfers between devices, send(): return lax.ppermute(value, 'col', pairs)  28.5 us
    ppermute x9, starting transfers between devices, send(): return lax.ppermute(value, 'col', pairs)  19.7 us
    all_to_all x1, starting transfers between devices, shards(): lax.all_to_all(done.reshape(across, share, width), 'row', 0, 0, tiled=Tru...  4.2 us
    ppermute x5, starting transfers between devices, trade(): lax.ppermute(value, 'row', [(i, (i + across) % rows) for i in range(rows)])  1.84 us
  transfers between devices with their start and end apart: 15, of which 5 were waited for; matrix products, arithmetic and copies ran while one was open for 0% of the time, Pallas kernels for 32%

profile of v6, /device:TPU:1, one launch (start us, length us, event | category | flops | bytes accessed | tf_op | source)
XLA Modules:
  0.0 88.1 jit_solution(12853640509016574365)
XLA Ops:
  0.6 3.3 %collective-permute-start = (bf16[128,128]{1,0:T(8,128)(2,1)}, bf16[128,128]{1,0:T(8,128)(2,1)S(1)}, u32[]{:S(2)}, u32[]{:S(2)}) collective-permute-start(bf16[128,128]{1,0:T(8,128)(2,1)} %bitcast.17), channel_id=1, source_target_pairs={{0,1},{1,0},{2,3},{3,2},{4,5},{5,4},{6,7},{7,6},{8,9},{9,8},{10,11... | collective-permute-start | bytes 98312 | tf_op jit(solution)/shard_map/ppermute | solution.py:368
  4.0 0.1 collective-permute-start.2
  4.1 0.1 pad_add_fusion.core_ref
  4.1 0.9 %collective-permute-done.mate_cot_ref = bf16[128,128]{1,0:T(8,128)(2,1)S(1)} collective-permute-done((bf16[128,128]{1,0:T(8,128)(2,1)}, bf16[128,128]{1,0:T(8,128)(2,1)S(1)}, u32[]{:S(2)}, u32[]{:S(2)}) %collective-permute-start) | collective-permute-done | bytes 32800 | tf_op jit(solution)/shard_map/ppermute | solution.py:368
  5.0 0.6 copy-done.7
  5.6 3.3 %shard_map.67 = (bf16[128,4608]{1,0:T(8,128)(2,1)S(1)}, bf16[128,4608]{1,0:T(8,128)(2,1)S(1)}, bf16[128,128]{1,0:T(8,128)(2,1)S(1)}, bf16[128,128]{1,0:T(8,128)(2,1)S(1)}, bf16[256,128]{1,0:T(8,128)(2,1)S(1)}) custom-call(s32[2]{0:T(128)S(1)} %pad_add_fusion.core_ref, bf16[4608,128]{1,0:T(8,128)(2,1)} %bitcast.11, bf16[128,4608]{1,0:T(8,128)(2,1)} %bitcast.13, ...), custom_call_target="tpu_custom_call" | custom-call | flops 452984832 | bytes 2457608 | tf_op jit(solution)/shard_map/pallas_call | solution.py:341
  9.0 0.0 copy-start.3
  9.0 0.5 collective-permute-start.3
  9.5 0.0 copy-done.6
  9.5 0.0 collective-permute-start.11
  9.5 2.2 %collective-permute-start.1 = (bf16[256,128]{1,0:T(8,128)(2,1)S(1)}, bf16[256,128]{1,0:T(8,128)(2,1)S(1)}, u32[]{:S(2)}, u32[]{:S(2)}) collective-permute-start(bf16[256,128]{1,0:T(8,128)(2,1)S(1)} %get-tuple-element.21), channel_id=1, source_target_pairs={{0,31},{1,2},{2,1},{3,4},{4,3},{5,6},{6,5},{7,8},{8,7},{9,10},{10,... | collective-permute-start | bytes 196616 | tf_op jit(solution)/shard_map/ppermute | solution.py:368
  11.7 0.0 collective-permute-done.2.far_edge_ref
  11.7 0.3 collective-permute-done.3.far_turned_ref
  12.0 1.1 %shard_map.68 = (bf16[128,128]{1,0:T(8,128)(2,1)S(1)}, bf16[128,128]{1,0:T(8,128)(2,1)S(1)}, bf16[128,4608]{1,0:T(8,128)(2,1)S(1)}, bf16[128,4608]{1,0:T(8,128)(2,1)S(1)}) custom-call(s32[2]{0:T(128)S(1)} %pad_add_fusion.core_ref, bf16[128,128]{1,0:T(8,128)(2,1)S(1)} %get-tuple-element.22.corner_ref, bf16[128,4608]{1,0:T(8,128)(2,1)S(1)} %get-tuple-element.23.e_ref.edge_ref, ...), custom_call_target="tpu_custom_call" | custom-call | flops 603979776 | bytes 4751368 | tf_op jit(solution)/shard_map/pallas_call | solution.py:341
  13.0 26.0 %collective-permute-done.1.come_ref = bf16[256,128]{1,0:T(8,128)(2,1)S(1)} collective-permute-done((bf16[256,128]{1,0:T(8,128)(2,1)S(1)}, bf16[256,128]{1,0:T(8,128)(2,1)S(1)}, u32[]{:S(2)}, u32[]{:S(2)}) %collective-permute-start.1) | collective-permute-done | bytes 65568 | tf_op jit(solution)/shard_map/ppermute | solution.py:368
  39.1 4.1 %shard_map.69 = (bf16[256,128]{1,0:T(8,128)(2,1)S(1)}, bf16[256,128]{1,0:T(8,128)(2,1)S(1)}, bf16[256,128]{1,0:T(8,128)(2,1)S(1)}) custom-call(s32[2]{0:T(128)S(1)} %pad_add_fusion.core_ref, bf16[256,128]{1,0:T(8,128)(2,1)S(1)} %collective-permute-done.1.come_ref, bf16[128,128]{1,0:T(8,128)(2,1)S(1)} %get-tuple-element.22.corner_ref, ...), custom_call_target="tpu_custom_call" | custom-call | flops 603979776 | bytes 4882440 | tf_op jit(solution)/shard_map/pallas_call | solution.py:341
  43.2 0.0 copy-start
  43.2 0.1 collective-permute-start.5
  43.3 4.9 %collective-permute-start.4 = (bf16[256,128]{1,0:T(8,128)(2,1)S(1)}, bf16[256,128]{1,0:T(8,128)(2,1)S(1)}, u32[]{:S(2)}, u32[]{:S(2)}) collective-permute-start(bf16[256,128]{1,0:T(8,128)(2,1)S(1)} %get-tuple-element.30), channel_id=1, source_target_pairs={{0,2},{1,31},{2,4},{3,1},{4,6},{5,3},{6,8},{7,5},{8,10},{9,7},{10,... | collective-permute-start | bytes 196616 | tf_op jit(solution)/shard_map/ppermute | solution.py:368
  48.3 0.0 collective-permute-done.5.m1_ref
  48.3 1.3 %collective-permute-done.4.come_ref.r1_ref = bf16[256,128]{1,0:T(8,128)(2,1)S(1)} collective-permute-done((bf16[256,128]{1,0:T(8,128)(2,1)S(1)}, bf16[256,128]{1,0:T(8,128)(2,1)S(1)}, u32[]{:S(2)}, u32[]{:S(2)}) %collective-permute-start.4) | collective-permute-done | bytes 65568 | tf_op jit(solution)/shard_map/ppermute | solution.py:368
  49.6 4.1 %shard_map.71 = (bf16[256,128]{1,0:T(8,128)(2,1)S(1)}, bf16[256,128]{1,0:T(8,128)(2,1)S(1)}) custom-call(s32[2]{0:T(128)S(1)} %pad_add_fusion.core_ref, bf16[256,128]{1,0:T(8,128)(2,1)S(1)} %collective-permute-done.4.come_ref.r1_ref, bf16[128,4608]{1,0:T(8,128)(2,1)S(1)} %get-tuple-element.23.e_ref.edge_ref, ...), custom_call_target="tpu_custom_call" | custom-call | flops 1207959552 | bytes 4947976 | tf_op jit(solution)/shard_map/pallas_call | solution.py:341
  53.7 2.2 %collective-permute-start.7 = (bf16[256,128]{1,0:T(8,128)(2,1)S(1)}, bf16[256,128]{1,0:T(8,128)(2,1)S(1)}, u32[]{:S(2)}, u32[]{:S(2)}) collective-permute-start(bf16[256,128]{1,0:T(8,128)(2,1)S(1)} %get-tuple-element.34), channel_id=1, source_target_pairs={{0,1},{1,0},{2,3},{3,2},{4,5},{5,4},{6,7},{7,6},{8,9},{9,8},{10,11... | collective-permute-start | bytes 196616 | tf_op jit(solution)/shard_map/ppermute | solution.py:368
  56.0 0.0 collective-permute-start.9
  56.0 4.2 %collective-permute-start.6 = (bf16[256,128]{1,0:T(8,128)(2,1)S(1)}, bf16[256,128]{1,0:T(8,128)(2,1)S(1)}, u32[]{:S(2)}, u32[]{:S(2)}) collective-permute-start(bf16[256,128]{1,0:T(8,128)(2,1)S(1)} %get-tuple-element.33), channel_id=1, source_target_pairs={{0,2},{1,31},{2,4},{3,1},{4,6},{5,3},{6,8},{7,5},{8,10},{9,7},{10,... | collective-permute-start | bytes 196616 | tf_op jit(solution)/shard_map/ppermute | solution.py:368
  60.2 0.0 collective-permute-done.7.m2_ref
  60.2 1.8 %shard_map.72 = (f32[64,4608]{1,0:T(8,128)S(1)}, bf16[512,128]{1,0:T(8,128)(2,1)S(1)}) custom-call(s32[2]{0:T(128)S(1)} %pad_add_fusion.core_ref, bf16[256,128]{1,0:T(8,128)(2,1)S(1)} %get-tuple-element.29.v_ref, bf16[256,128]{1,0:T(8,128)(2,1)S(1)} %collective-permute-done.4.come_ref.r1_ref, bf16[256,128]{1,0:T(8,128)(2,1)S(1)} %collective-permute-done.5.m1_ref, ...), custom_call_target="tpu_custom_call" | custom-call | flops 452984832 | bytes 1441800 | tf_op jit(solution)/shard_map/pallas_call | solution.py:341
  62.0 0.1 collective-permute-start.12
  62.1 0.0 collective-permute-done.6.value_ref
  62.1 2.1 %collective-permute-start.8 = (bf16[256,128]{1,0:T(8,128)(2,1)S(1)}, bf16[256,128]{1,0:T(8,128)(2,1)S(1)}, u32[]{:S(2)}, u32[]{:S(2)}) collective-permute-start(bf16[256,128]{1,0:T(8,128)(2,1)S(1)} %shard_map.73.r2_ref), channel_id=1, source_target_pairs={{0,1},{1,0},{2,3},{3,2},{4,5},{5,4},{6,7},{7,6},{8,9},{9,8},{10,11... | collective-permute-start | bytes 196616 | tf_op jit(solution)/shard_map/ppermute | solution.py:368
  64.3 1.6 %collective-permute-start.13 = (bf16[256,128]{1,0:T(8,128)(2,1)S(1)}, bf16[256,128]{1,0:T(8,128)(2,1)S(1)}, u32[]{:S(2)}, u32[]{:S(2)}) collective-permute-start(bf16[256,128]{1,0:T(8,128)(2,1)S(1)} %shard_map.73.r2_ref), channel_id=1, source_target_pairs={{0,128},{32,160},{64,192},{96,224},{128,0},{160,32},{192,64},{224,... | collective-permute-start | bytes 196616 | tf_op jit(solution)/shard_map/ppermute | solution.py:374
  65.9 1.6 %shard_map.74.after_ref.sum_ref = f32[64,4608]{1,0:T(8,128)S(1)} custom-call(s32[2]{0:T(128)S(1)} %pad_add_fusion.core_ref, bf16[256,128]{1,0:T(8,128)(2,1)S(1)} %shard_map.73.r2_ref, bf16[256,128]{1,0:T(8,128)(2,1)S(1)} %collective-permute-done.5.m1_ref, bf16[128,128]{1,0:T(8,128)(2,1)S(1)} %get-tuple-element.32.last_ref, ...), custom_call_target="tpu_custom_call", output_to_operand_aliasing={{}: (5, {})} | custom-call | flops 301989888 | bytes 2523144 | tf_op jit(solution)/shard_map/pallas_call | solution.py:341
  67.6 0.0 copy-done.2
  67.6 0.0 collective-permute-done.8.m3_ref
  67.6 1.8 %shard_map.75.near_ref = bf16[128,128]{1,0:T(8,128)(2,1)S(1)} custom-call(s32[2]{0:T(128)S(1)} %pad_add_fusion.core_ref, bf16[256,128]{1,0:T(8,128)(2,1)S(1)} %collective-permute-done.8.m3_ref, bf16[128,4608]{1,0:T(8,128)(2,1)S(1)} %get-tuple-element.27.me_ref, bf16[128,4608]{1,0:T(8,128)(2,1)S(1)} %get-tuple-element.28.mt_ref, ...), custom_call_target="tpu_custom_call" | custom-call | flops 301989888 | bytes 3604488 | tf_op jit(solution)/shard_map/pallas_call | solution.py:341
  69.4 0.1 collective-permute-start.10
  69.5 0.0 collective-permute-done.11.other_edge_ref
  69.5 0.0 collective-permute-done.13.r2_ref
  69.5 0.0 collective-permute-done.9.pack1_ref
  69.5 0.0 collective-permute-done.12.pack2_ref
  69.5 0.0 copy-done
  69.6 3.1 %shard_map.77.sum_ref = f32[64,4608]{1,0:T(8,128)S(1)} custom-call(s32[2]{0:T(128)S(1)} %pad_add_fusion.core_ref, bf16[256,128]{1,0:T(8,128)(2,1)S(1)} %get-tuple-element.29.v_ref, bf16[128,128]{1,0:T(8,128)(2,1)S(1)} %shard_map.75.near_ref, bf16[640,128]{1,0:T(8,128)(2,1)S(1)} %collective-permute-done.9.pack1_ref, ...), custom_call_target="tpu_custom_call", output_to_operand_aliasing={{}: (8, {})} | custom-call | flops 905969664 | bytes 3997704 | tf_op jit(solution)/shard_map/pallas_call | solution.py:341
  72.7 0.0 collective-permute-done.10.near_ref
  72.7 1.8 %shard_map.78 = bf16[64,4608]{1,0:T(8,128)(2,1)} custom-call(s32[2]{0:T(128)S(1)} %pad_add_fusion.core_ref, bf16[640,128]{1,0:T(8,128)(2,1)S(1)} %collective-permute-done.9.pack1_ref, bf16[128,128]{1,0:T(8,128)(2,1)S(1)} %collective-permute-done.10.near_ref, bf16[128,4608]{1,0:T(8,128)(2,1)S(1)} %collective-permute-done.11.other_edge_ref, ...), custom_call_target="tpu_custom_call" | custom-call | flops 150994944 | bytes 2555912 | tf_op jit(solution)/shard_map/pallas_call | solution.py:341
  74.5 4.2 %all-to-all-start = ((bf16[4,16,4608]{2,1,0:T(8,128)(2,1)}), bf16[4,16,4608]{2,1,0:T(8,128)(2,1)S(1)}, u32[]{:S(2)}, u32[]{:S(2)}) async-start(bf16[4,16,4608]{2,1,0:T(8,128)(2,1)} %bitcast.10), calls=%async_computation | async-start | bytes 1179648 | tf_op jit(solution)/shard_map/all_to_all | solution.py:433
  78.7 7.5 %shard_map.76 = (bf16[128,4608]{1,0:T(8,128)(2,1)}, bf16[128,128]{1,0:T(8,128)(2,1)}) custom-call(s32[2]{0:T(128)S(1)} %pad_add_fusion.core_ref, bf16[256,128]{1,0:T(8,128)(2,1)} %copy-done, bf16[256,128]{1,0:T(8,128)(2,1)} %copy-done.4, bf16[256,128]{1,0:T(8,128)(2,1)} %copy-done.2, bf16[128,128]{1,0:T(8,128)(2,1)S(1)} %shard_map.75.near_ref, ...), custom_call_target="tpu_custom_call" | custom-call | flops 2113929216 | bytes 2752520 | tf_op jit(solution)/shard_map/pallas_call | solution.py:341
  86.3 1.0 %all-to-all-done.parts_ref = bf16[4,16,4608]{2,1,0:T(8,128)(2,1)S(1)} async-done(((bf16[4,16,4608]{2,1,0:T(8,128)(2,1)}), bf16[4,16,4608]{2,1,0:T(8,128)(2,1)S(1)}, u32[]{:S(2)}, u32[]{:S(2)}) %all-to-all-start) | async-done | bytes 589856 | tf_op jit(solution)/shard_map/all_to_all | solution.py:433
  87.3 0.8 shard_map.79
  (12 shorter events, 0.0 us)
Async XLA Ops:
  0.6 4.4 %collective-permute-start = (bf16[128,128]{1,0:T(8,128)(2,1)}, bf16[128,128]{1,0:T(8,128)(2,1)S(1)}, u32[]{:S(2)}, u32[]{:S(2)}) collective-permute-start(bf16[128,128]{1,0:T(8,128)(2,1)} %bitcast.17), channel_id=1, source_target_pairs={{0,1},{1,0},{2,3},{3,2},{4,5},{5,4},{6,7},{7,6},{8,9},{9,8},{10,11... | collective-permute-start | bytes 98312 | tf_op jit(solution)/shard_map/ppermute | solution.py:368
  4.0 7.7 %collective-permute-start.2 = (bf16[128,4608]{1,0:T(8,128)(2,1)}, bf16[128,4608]{1,0:T(8,128)(2,1)S(1)}, u32[]{:S(2)}, u32[]{:S(2)}) collective-permute-start(bf16[128,4608]{1,0:T(8,128)(2,1)} %bitcast.12), channel_id=1, source_target_pairs={{0,1},{1,0},{2,3},{3,2},{4,5},{5,4},{6,7},{7,6},{8,9},{9,8},{10,11... | collective-permute-start | bytes 3538952 | tf_op jit(solution)/shard_map/ppermute | solution.py:368
  5.0 0.6 copy-start.7
  5.6 3.9 %copy-start.6 = (bf16[1,1,128,4608]{3,2,1,0:T(8,128)(2,1)S(1)}, bf16[1,1,128,4608]{3,2,1,0:T(8,128)(2,1)}, u32[]{:S(2)}) copy-start(bf16[1,1,128,4608]{3,2,1,0:T(8,128)(2,1)} %param.5) | copy-start | bytes 3538948
  9.0 56.9 %copy-start.3 = (bf16[128,128]{1,0:T(8,128)(2,1)}, bf16[128,128]{1,0:T(8,128)(2,1)S(1)}, u32[]{:S(2)}) copy-start(bf16[128,128]{1,0:T(8,128)(2,1)S(1)} %get-tuple-element.32.last_ref) | copy-start | bytes 98308
  9.0 3.0 %collective-permute-start.3 = (bf16[128,4608]{1,0:T(8,128)(2,1)S(1)}, bf16[128,4608]{1,0:T(8,128)(2,1)S(1)}, u32[]{:S(2)}, u32[]{:S(2)}) collective-permute-start(bf16[128,4608]{1,0:T(8,128)(2,1)S(1)} %get-tuple-element.24.t_ref.turned_ref), channel_id=1, source_target_pairs={{0,1},{1,0},{2,3},{3,2},{4,5},{5,4},{6,7},{7,6},{8,9},{9,8},{10,11... | collective-permute-start | bytes 3538952 | tf_op jit(solution)/shard_map/ppermute | solution.py:368
  9.5 60.0 %collective-permute-start.11 = (bf16[128,4608]{1,0:T(8,128)(2,1)S(1)}, bf16[128,4608]{1,0:T(8,128)(2,1)S(1)}, u32[]{:S(2)}, u32[]{:S(2)}) collective-permute-start(bf16[128,4608]{1,0:T(8,128)(2,1)S(1)} %bitcast.14), channel_id=1, source_target_pairs={{0,128},{32,160},{64,192},{96,224},{128,0},{160,32},{192,64},{224,... | collective-permute-start | bytes 3538952 | tf_op jit(solution)/shard_map/ppermute | solution.py:374
  9.5 29.6 %collective-permute-start.1 = (bf16[256,128]{1,0:T(8,128)(2,1)S(1)}, bf16[256,128]{1,0:T(8,128)(2,1)S(1)}, u32[]{:S(2)}, u32[]{:S(2)}) collective-permute-start(bf16[256,128]{1,0:T(8,128)(2,1)S(1)} %get-tuple-element.21), channel_id=1, source_target_pairs={{0,31},{1,2},{2,1},{3,4},{4,3},{5,6},{6,5},{7,8},{8,7},{9,10},{10,... | collective-permute-start | bytes 196616 | tf_op jit(solution)/shard_map/ppermute | solution.py:368
  43.2 26.3 %copy-start = (bf16[256,128]{1,0:T(8,128)(2,1)}, bf16[256,128]{1,0:T(8,128)(2,1)S(1)}, u32[]{:S(2)}) copy-start(bf16[256,128]{1,0:T(8,128)(2,1)S(1)} %get-tuple-element.29.v_ref) | copy-start | bytes 196612
  43.2 5.0 %collective-permute-start.5 = (bf16[256,128]{1,0:T(8,128)(2,1)S(1)}, bf16[256,128]{1,0:T(8,128)(2,1)S(1)}, u32[]{:S(2)}, u32[]{:S(2)}) collective-permute-start(bf16[256,128]{1,0:T(8,128)(2,1)S(1)} %get-tuple-element.31), channel_id=1, source_target_pairs={{0,1},{1,0},{2,3},{3,2},{4,5},{5,4},{6,7},{7,6},{8,9},{9,8},{10,11... | collective-permute-start | bytes 196616 | tf_op jit(solution)/shard_map/ppermute | solution.py:368
  43.3 6.3 %collective-permute-start.4 = (bf16[256,128]{1,0:T(8,128)(2,1)S(1)}, bf16[256,128]{1,0:T(8,128)(2,1)S(1)}, u32[]{:S(2)}, u32[]{:S(2)}) collective-permute-start(bf16[256,128]{1,0:T(8,128)(2,1)S(1)} %get-tuple-element.30), channel_id=1, source_target_pairs={{0,2},{1,31},{2,4},{3,1},{4,6},{5,3},{6,8},{7,5},{8,10},{9,7},{10,... | collective-permute-start | bytes 196616 | tf_op jit(solution)/shard_map/ppermute | solution.py:368
  48.3 17.7 %copy-start.1 = (bf16[256,128]{1,0:T(8,128)(2,1)}, bf16[256,128]{1,0:T(8,128)(2,1)S(1)}, u32[]{:S(2)}) copy-start(bf16[256,128]{1,0:T(8,128)(2,1)S(1)} %collective-permute-done.5.m1_ref) | copy-start | bytes 196612
  49.6 10.6 %copy-start.4 = (bf16[256,128]{1,0:T(8,128)(2,1)}, bf16[256,128]{1,0:T(8,128)(2,1)S(1)}, u32[]{:S(2)}) copy-start(bf16[256,128]{1,0:T(8,128)(2,1)S(1)} %collective-permute-done.4.come_ref.r1_ref) | copy-start | bytes 196612
  53.7 6.5 %collective-permute-start.7 = (bf16[256,128]{1,0:T(8,128)(2,1)S(1)}, bf16[256,128]{1,0:T(8,128)(2,1)S(1)}, u32[]{:S(2)}, u32[]{:S(2)}) collective-permute-start(bf16[256,128]{1,0:T(8,128)(2,1)S(1)} %get-tuple-element.34), channel_id=1, source_target_pairs={{0,1},{1,0},{2,3},{3,2},{4,5},{5,4},{6,7},{7,6},{8,9},{9,8},{10,11... | collective-permute-start | bytes 196616 | tf_op jit(solution)/shard_map/ppermute | solution.py:368
  56.0 13.6 %collective-permute-start.9 = (bf16[640,128]{1,0:T(8,128)(2,1)S(1)}, bf16[640,128]{1,0:T(8,128)(2,1)S(1)}, u32[]{:S(2)}, u32[]{:S(2)}) collective-permute-start(bf16[640,128]{1,0:T(8,128)(2,1)S(1)} %shard_map.70.m1_ref), channel_id=1, source_target_pairs={{0,128},{32,160},{64,192},{96,224},{128,0},{160,32},{192,64},{224,... | collective-permute-start | bytes 491528 | tf_op jit(solution)/shard_map/ppermute | solution.py:374
  56.0 6.1 %collective-permute-start.6 = (bf16[256,128]{1,0:T(8,128)(2,1)S(1)}, bf16[256,128]{1,0:T(8,128)(2,1)S(1)}, u32[]{:S(2)}, u32[]{:S(2)}) collective-permute-start(bf16[256,128]{1,0:T(8,128)(2,1)S(1)} %get-tuple-element.33), channel_id=1, source_target_pairs={{0,2},{1,31},{2,4},{3,1},{4,6},{5,3},{6,8},{7,5},{8,10},{9,7},{10,... | collective-permute-start | bytes 196616 | tf_op jit(solution)/shard_map/ppermute | solution.py:368
  60.2 1.9 %copy-start.5 = (bf16[256,128]{1,0:T(8,128)(2,1)}, bf16[256,128]{1,0:T(8,128)(2,1)S(1)}, u32[]{:S(2)}) copy-start(bf16[256,128]{1,0:T(8,128)(2,1)S(1)} %collective-permute-done.7.m2_ref) | copy-start | bytes 196612
  62.0 7.6 %collective-permute-start.12 = (bf16[512,128]{1,0:T(8,128)(2,1)S(1)}, bf16[512,128]{1,0:T(8,128)(2,1)S(1)}, u32[]{:S(2)}, u32[]{:S(2)}) collective-permute-start(bf16[512,128]{1,0:T(8,128)(2,1)S(1)} %get-tuple-element.38), channel_id=1, source_target_pairs={{0,128},{32,160},{64,192},{96,224},{128,0},{160,32},{192,64},{224,... | collective-permute-start | bytes 393224 | tf_op jit(solution)/shard_map/ppermute | solution.py:374
  62.1 5.5 %copy-start.2 = (bf16[256,128]{1,0:T(8,128)(2,1)}, bf16[256,128]{1,0:T(8,128)(2,1)S(1)}, u32[]{:S(2)}) copy-start(bf16[256,128]{1,0:T(8,128)(2,1)S(1)} %shard_map.73.r2_ref) | copy-start | bytes 196612
  62.1 5.5 %collective-permute-start.8 = (bf16[256,128]{1,0:T(8,128)(2,1)S(1)}, bf16[256,128]{1,0:T(8,128)(2,1)S(1)}, u32[]{:S(2)}, u32[]{:S(2)}) collective-permute-start(bf16[256,128]{1,0:T(8,128)(2,1)S(1)} %shard_map.73.r2_ref), channel_id=1, source_target_pairs={{0,1},{1,0},{2,3},{3,2},{4,5},{5,4},{6,7},{7,6},{8,9},{9,8},{10,11... | collective-permute-start | bytes 196616 | tf_op jit(solution)/shard_map/ppermute | solution.py:368
  64.3 5.3 %collective-permute-start.13 = (bf16[256,128]{1,0:T(8,128)(2,1)S(1)}, bf16[256,128]{1,0:T(8,128)(2,1)S(1)}, u32[]{:S(2)}, u32[]{:S(2)}) collective-permute-start(bf16[256,128]{1,0:T(8,128)(2,1)S(1)} %shard_map.73.r2_ref), channel_id=1, source_target_pairs={{0,128},{32,160},{64,192},{96,224},{128,0},{160,32},{192,64},{224,... | collective-permute-start | bytes 196616 | tf_op jit(solution)/shard_map/ppermute | solution.py:374
  69.4 3.3 %collective-permute-start.10 = (bf16[128,128]{1,0:T(8,128)(2,1)S(1)}, bf16[128,128]{1,0:T(8,128)(2,1)S(1)}, u32[]{:S(2)}, u32[]{:S(2)}) collective-permute-start(bf16[128,128]{1,0:T(8,128)(2,1)S(1)} %shard_map.75.near_ref), channel_id=1, source_target_pairs={{0,128},{32,160},{64,192},{96,224},{128,0},{160,32},{192,64},{224,... | collective-permute-start | bytes 98312 | tf_op jit(solution)/shard_map/ppermute | solution.py:374
  74.5 12.7 %all-to-all-start = ((bf16[4,16,4608]{2,1,0:T(8,128)(2,1)}), bf16[4,16,4608]{2,1,0:T(8,128)(2,1)S(1)}, u32[]{:S(2)}, u32[]{:S(2)}) async-start(bf16[4,16,4608]{2,1,0:T(8,128)(2,1)} %bitcast.10), calls=%async_computation | async-start | bytes 1179648 | tf_op jit(solution)/shard_map/all_to_all | solution.py:433

commit v7 on v6

--- a/solution.py
+++ b/solution.py
@@ -7,7 +7,7 @@
 
 
 W = 128
-H = W // 2
+PIECES = 3
 BF = jnp.bfloat16
 F32 = jnp.float32
 
@@ -35,9 +35,9 @@
 
 
 def start_kernel(
-    core_ref, proj_ref, edge_in, corner_in, cot_ref, mate_cot_ref, turned_ref, edge_ref, corner_ref, last_ref, send_ref,
-    proj_vmem, wide_ref, cot_vmem, proj_sem, sem,
+    core_ref, proj_ref, edge_in, corner_in, cot_ref, mate_cot_ref, turned_ref, edge_ref, corner_ref, last_ref, send_ref, mine_ref, *rest,
 ):
+    *give, proj_vmem, wide_ref, cot_vmem, proj_sem, sem = rest
     pieces = proj_sem.shape[0]
     size = proj_ref.shape[0] // pieces
     loads = []
@@ -62,6 +62,12 @@
     for copy in others:
         copy.wait()
 
+    part = mine_ref.shape[1]
+    mine_ref[...] = edge_ref[:, pl.ds(pl.multiple_of(part * core_ref[1], W), part)]
+    for n, ref in enumerate(give):
+        at = part * (1 - core_ref[1]) + n * ref.shape[1]
+        ref[...] = edge_ref[:, pl.ds(pl.multiple_of(at, W), ref.shape[1])]
+
     @pl.when(core_ref[0] == 0)
     def _():
         last = cot_vmem[1].astype(F32).T.astype(BF)
@@ -168,8 +174,7 @@
 def place(core_ref, z_ref, w_ref, v, u):
     def put(corners, adjoints):
         for n, ((c_ref, c_at), (a_ref, a_at)) in enumerate(zip(corners, adjoints)):
-            at = pl.multiple_of(c_at + H * core_ref[1], H)
-            z_ref[H * n : H * (n + 1), :] = c_ref[pl.ds(at, H), :]
+            z_ref[W * n : W * (n + 1), :] = c_ref[c_at : c_at + W, :]
             w_ref[W * n : W * (n + 1), :] = a_ref[a_at : a_at + W, :]
 
     @pl.when(core_ref[0] == 0)
@@ -181,25 +186,9 @@
         put(u, v)
 
 
-def terms_of(z_ref, x_ref, w_ref, put):
-    n = z_ref.shape[0] // H
-    for t in range(x_ref.shape[1] // (2 * W)):
-        mid = dot(z_ref[...], x_ref[:, 2 * W * t : 2 * W * (t + 1)]).astype(BF)
-        flat = jnp.concatenate(
-            [
-                jnp.concatenate([mid[H * k : H * (k + 1), W * half : W * (half + 1)] for k in range(n)], 1)
-                for half in range(2)
-            ],
-            0,
-        )
-        value = dot(flat, w_ref[...])
-        put(2 * t, value[:H, :])
-        put(2 * t + 1, value[H:, :])
-
-
-def adder(from_ref, to_ref):
+def adder(from_ref, to_ref, start=0):
     def put(p, value):
-        at = slice(W * p, W * (p + 1))
+        at = slice(start + W * p, start + W * (p + 1))
         to_ref[:, at] = from_ref[:, at] + value
 
     return put
@@ -224,7 +213,7 @@
     def put(p, value):
         out_ref[:, W * p : W * (p + 1)] = value
 
-    terms_of(z_ref, edge_ref, w_ref, put)
+    pairs_of(z_ref, edge_ref, w_ref, put)
 
 
 def pass_kernel(value_ref, after_ref, out_ref):
@@ -235,7 +224,7 @@
     place(
         core_ref, z_ref, w_ref, [block(r2_ref, 0), block(r2_ref, 1)], [block(m1_ref, 0), block(last_ref, 0)]
     )
-    terms_of(z_ref, edge_ref, w_ref, adder(early_ref, out_ref))
+    pairs_of(z_ref, edge_ref, w_ref, adder(early_ref, out_ref))
 
 
 def near_kernel(core_ref, m3_ref, me_ref, mt_ref, after_ref, near_ref):
@@ -246,34 +235,32 @@
 
 
 def proj_other_kernel(
-    core_ref, v_ref, near_ref, pack1_ref, pack2_ref, r2_ref, edge_ref, other_edge_ref, sum_ref, out_ref,
-    z1_ref, w1_ref, z_ref, w_ref,
+    core_ref, v_ref, near_ref, pack1_ref, pack2_ref, r2_ref, mine_ref, sum_ref, *rest
 ):
+    *other_refs, out_ref, z1_ref, w1_ref, z_ref, w_ref = rest
     place(core_ref, z1_ref, w1_ref, [block(v_ref, 0)], [block(near_ref, 0)])
-    terms_of(z1_ref, edge_ref, w1_ref, adder(sum_ref, out_ref))
+    pairs_of(z1_ref, mine_ref, w1_ref, adder(sum_ref, out_ref))
     v = [block(pack1_ref, 1), block(pack2_ref, 0), block(pack2_ref, 1), block(r2_ref, 0), block(r2_ref, 1)]
     u = [block(pack2_ref, 3), block(pack2_ref, 2), block(pack1_ref, 3), block(pack1_ref, 2), block(pack1_ref, 4)]
     place(core_ref, z_ref, w_ref, v, u)
-    terms_of(z_ref, other_edge_ref, w_ref, adder(out_ref, out_ref))
-
-
-def proj_last_kernel(
-    core_ref, pack1_ref, near_ref, other_edge_ref, sum_ref, out_ref, z_ref, w_ref, stage_ref, sem
-):
+    for n, ref in enumerate(other_refs):
+        pairs_of(z_ref, ref, w_ref, adder(out_ref, out_ref, n * ref.shape[1]))
+
+
+def proj_last_kernel(core_ref, pack1_ref, near_ref, sum_ref, *rest):
+    *other_refs, out_ref, z_ref, w_ref, stage_ref, sem = rest
     place(core_ref, z_ref, w_ref, [block(pack1_ref, 0)], [block(near_ref, 0)])
-    pieces = sem.shape[0]
-    each = stage_ref.shape[1] // W // pieces
     copies = []
-
-    def put(p, value):
-        at = slice(W * p, W * (p + 1))
-        stage_ref[:, at] = (sum_ref[:, at] + value).astype(BF)
-        if (p + 1) % each == 0:
-            at = pl.ds(W * (p + 1 - each), W * each)
-            copies.append(pltpu.make_async_copy(stage_ref.at[:, at], out_ref.at[:, at], sem.at[p // each]))
-            copies[-1].start()
-
-    terms_of(z_ref, other_edge_ref, w_ref, put)
+    for n, ref in enumerate(other_refs):
+
+        def put(p, value, at=n * ref.shape[1]):
+            at = slice(at + W * p, at + W * (p + 1))
+            stage_ref[:, at] = (sum_ref[:, at] + value).astype(BF)
+
+        pairs_of(z_ref, ref, w_ref, put)
+        at = pl.ds(n * ref.shape[1], ref.shape[1])
+        copies.append(pltpu.make_async_copy(stage_ref.at[:, at], out_ref.at[:, at], sem.at[n]))
+        copies[-1].start()
     for copy in copies:
         copy.wait()
 
@@ -315,12 +302,12 @@
 
 
 def gather_kernel(parts_ref, out_ref):
-    rows = parts_ref.shape[1]
-    planes = parts_ref.shape[2] // W
+    senders, rows, part = parts_ref.shape
+    planes = 2 * part // W
     for p in range(planes):
-        out_ref[pl.ds(p, rows, stride=planes), :] = jnp.sum(
-            parts_ref[:, :, W * p : W * (p + 1)].astype(F32), axis=0
-        )
+        half, at = divmod(W * p, part)
+        these = slice(senders // 2 * half, senders // 2 * (half + 1))
+        out_ref[pl.ds(p, rows, stride=planes), :] = jnp.sum(parts_ref[these, :, at : at + W].astype(F32), axis=0)
 
 
 def call(kernel, shapes, *args, scratch=(), sems=(), flops=0, far=(), free=(), far_outs=(), alias=None):
@@ -377,7 +364,9 @@
         return send(value, lambda i: i + 2 if i % 2 == 0 else i - 2)
 
     one, two = ((W, W), BF), ((2 * W, W), BF)
-    half = ((H, width), F32)
+    half_width = width // 2
+    half = ((W, half_width), F32)
+    piece = ((W, half_width // PIECES), BF)
     whole = ((W, width), BF)
 
     def stacks(n):
@@ -385,14 +374,14 @@
 
     mate_cot = swap(cot)
     far_edge = swap(edge)
-    other_edge = trade(edge)
-    turned, edge, corner, u0, first = call(
-        start_kernel, [whole, whole, one, one, two], core, projector, edge, corner, cot, mate_cot,
+    turned, edge, corner, u0, first, mine, *give = call(
+        start_kernel, [whole, whole, one, one, two, ((W, half_width), BF)] + [piece] * PIECES, core, projector, edge, corner, cot, mate_cot,
         scratch=[((width, W), BF), ((width, W), F32), ((2, W, W), BF)], sems=(4, 4), flops=3 * unit,
         far=(1, 2, 3, 4, 5),
     )
     r0 = send(first, lambda i: i - 1 if i % 2 == 0 else i + 1)
     far_turned = swap(turned)
+    other_edge = [trade(part) for part in give]
     keep, ahead, mate_edge, mate_turned = call(
         ahead_kernel, [one, one, whole, whole], core, corner, edge, turned, far_edge, far_turned,
         sems=(2,), flops=4 * unit, free=(4, 5),
@@ -408,31 +397,28 @@
     m2 = swap(near2)
 
     def halves(n):
-        return [((n * H, W), BF), ((n * W, W), BF)]
+        return [((n * W, W), BF), ((n * W, W), BF)]
 
     early, pack2 = call(
-        proj_early_kernel, [half, ((4 * W, W), BF)], core, v, r1, m1, m2, edge, scratch=halves(3), flops=3 * unit
+        proj_early_kernel, [half, ((4 * W, W), BF)], core, v, r1, m1, m2, mine, scratch=halves(3), flops=3 * unit
     )
     other2 = trade(pack2)
     r2 = call(pass_kernel, [two], r2, early, free=(1,))
     m3 = swap(r2)
     other3 = trade(r2)
-    late = call(proj_late_kernel, [half], core, r2, m1, u0, edge, early, scratch=halves(2), flops=2 * unit, alias={5: 0})
+    late = call(proj_late_kernel, [half], core, r2, m1, u0, mine, early, scratch=halves(2), flops=2 * unit, alias={5: 0})
     near3 = call(near_kernel, [one], core, m3, mate_edge, mate_turned, late, flops=2 * unit, free=(4,))
     other4 = trade(near3)
     late = call(
-        proj_other_kernel, [half], core, v, near3, other1, other2, other3, edge, other_edge, late,
-        scratch=halves(1) + halves(5), flops=6 * unit, alias={8: 0},
+        proj_other_kernel, [half], core, v, near3, other1, other2, other3, mine, late, *other_edge,
+        scratch=halves(1) + halves(5), flops=6 * unit, alias={7: 0},
     )
     done = call(
-        proj_last_kernel, [((H, width), BF)], core, other1, other4, other_edge, late,
-        scratch=halves(1) + [((H, width), BF)], sems=(6,), flops=unit, far_outs=(0,),
+        proj_last_kernel, [((W, half_width), BF)], core, other1, other4, late, *other_edge,
+        scratch=halves(1) + [((W, half_width), BF)], sems=(PIECES,), flops=unit, far_outs=(0,),
     )
     share = W // rows
-    groups = [list(range(across)), list(range(across, rows))]
-    parts = lax.all_to_all(
-        done.reshape(across, share, width), "row", 0, 0, tiled=True, axis_index_groups=groups
-    )
+    parts = lax.all_to_all(done.reshape(rows, share, half_width), "row", 0, 0, tiled=True)
     edge_grad, corner_grad = call(
         edge_kernel, [whole, one], core, v, r1, r2, near3, m2, m1, u0, edge, turned,
         scratch=stacks(6), sems=(12,), flops=14 * unit, far=(1, 2, 3, 5, 6, 7),

time: 89.6 us -> 73.3 us (0.82); the launches traced: 88.1 us -> 73.1 us
  waiting for transfers between devices: 29.5 us -> 11.7 us
  starting transfers between devices: 25.8 us -> 28.6 us
    ppermute x9, waiting for transfers between devices: 28.5 us -> 5.05 us  [send(): return lax.ppermute(value, 'col', pairs)]
    ppermute x5 -> x7, waiting for transfers between devices: 0.01 us -> 5.54 us  [trade(): lax.ppermute(value, 'row', [(i, (i + across) % rows) for i in range(rows)])]
    ppermute x5 -> x7, starting transfers between devices: 1.84 us -> 4.5 us  [trade(): lax.ppermute(value, 'row', [(i, (i + across) % rows) for i in range(rows)])]
  transfers between devices with their start and end apart: 15 -> 17, of which waited for: 5 -> 7; matrix products, arithmetic and copies ran while one was open for 0% -> 0% of each run, Pallas kernels for 32% -> 33%
where the time goes in v7:
time: 73.3 us; the launch traced here: 73.1 us
  Pallas kernels  31.2 us (43%)
  starting transfers between devices  28.6 us (39%)
  waiting for transfers between devices  11.7 us (16%)
  between operations  0.81 us (1%)
    pallas_call x13, Pallas kernels, call(): pl.pallas_call(kernel, out_shape=outs[0] if single else outs, in_specs=in...  31.2 us
    ppermute x9, starting transfers between devices, send(): return lax.ppermute(value, 'col', pairs)  19.9 us
    ppermute x7, waiting for transfers between devices, trade(): lax.ppermute(value, 'row', [(i, (i + across) % rows) for i in range(rows)])  5.54 us
    ppermute x9, waiting for transfers between devices, send(): return lax.ppermute(value, 'col', pairs)  5.05 us
    ppermute x7, starting transfers between devices, trade(): lax.ppermute(value, 'row', [(i, (i + across) % rows) for i in range(rows)])  4.5 us
    all_to_all x1, starting transfers between devices, shards(): lax.all_to_all(done.reshape(rows, share, half_width), 'row', 0, 0, tiled=...  4.25 us
  transfers between devices with their start and end apart: 17, of which 7 were waited for; matrix products, arithmetic and copies ran while one was open for 0% of the time, Pallas kernels for 33%

profile of v7, /device:TPU:1, one launch (start us, length us, event | category | flops | bytes accessed | tf_op | source)
XLA Modules:
  0.0 73.1 jit_solution(2105450215377588685)
XLA Ops:
  0.6 3.3 %collective-permute-start = (bf16[128,128]{1,0:T(8,128)(2,1)}, bf16[128,128]{1,0:T(8,128)(2,1)S(1)}, u32[]{:S(2)}, u32[]{:S(2)}) collective-permute-start(bf16[128,128]{1,0:T(8,128)(2,1)} %bitcast.16), channel_id=1, source_target_pairs={{0,1},{1,0},{2,3},{3,2},{4,5},{5,4},{6,7},{7,6},{8,9},{9,8},{10,11... | collective-permute-start | bytes 98312 | tf_op jit(solution)/shard_map/ppermute | solution.py:355
  4.0 0.1 collective-permute-start.2
  4.1 0.1 pad_add_fusion.core_ref
  4.1 0.9 %collective-permute-done.mate_cot_ref = bf16[128,128]{1,0:T(8,128)(2,1)S(1)} collective-permute-done((bf16[128,128]{1,0:T(8,128)(2,1)}, bf16[128,128]{1,0:T(8,128)(2,1)S(1)}, u32[]{:S(2)}, u32[]{:S(2)}) %collective-permute-start) | collective-permute-done | bytes 32800 | tf_op jit(solution)/shard_map/ppermute | solution.py:355
  5.0 0.6 copy-done.6
  5.6 3.4 %shard_map.67 = (bf16[128,4608]{1,0:T(8,128)(2,1)S(1)}, bf16[128,4608]{1,0:T(8,128)(2,1)S(1)}, bf16[128,128]{1,0:T(8,128)(2,1)S(1)}, bf16[128,128]{1,0:T(8,128)(...) custom-call(s32[2]{0:T(128)S(1)} %pad_add_fusion.core_ref, ...), custom_call_target="tpu_custom_call" | custom-call | flops 452984832 | bytes 2457608 | tf_op jit(solution)/shard_map/pallas_call | solution.py:328
  9.1 0.5 collective-permute-start.3
  9.6 1.0 %collective-permute-start.1 = (bf16[256,128]{1,0:T(8,128)(2,1)S(1)}, bf16[256,128]{1,0:T(8,128)(2,1)S(1)}, u32[]{:S(2)}, u32[]{:S(2)}) collective-permute-start(bf16[256,128]{1,0:T(8,128)(2,1)S(1)} %get-tuple-element.25), channel_id=1, source_target_pairs={{0,31},{1,2},{2,1},{3,4},{4,3},{5,6},{6,5},{7,8},{8,7},{9,10},{10,... | collective-permute-start | bytes 196616 | tf_op jit(solution)/shard_map/ppermute | solution.py:355
  10.6 0.0 collective-permute-done.2.far_edge_ref
  10.6 1.5 %collective-permute-done.3.far_turned_ref = bf16[128,4608]{1,0:T(8,128)(2,1)S(1)} collective-permute-done((bf16[128,4608]{1,0:T(8,128)(2,1)S(1)}, bf16[128,4608]{1,0:T(8,128)(2,1)S(1)}, u32[]{:S(2)}, u32[]{:S(2)}) %collective-permute-start.3) | collective-permute-done | bytes 1179680 | tf_op jit(solution)/shard_map/ppermute | solution.py:355
  12.0 1.1 %shard_map.68 = (bf16[128,128]{1,0:T(8,128)(2,1)S(1)}, bf16[128,128]{1,0:T(8,128)(2,1)S(1)}, bf16[128,4608]{1,0:T(8,128)(2,1)S(1)}, bf16[128,4608]{1,0:T(8,128)(2,1)S(1)}) custom-call(s32[2]{0:T(128)S(1)} %pad_add_fusion.core_ref, bf16[128,128]{1,0:T(8,128)(2,1)S(1)} %get-tuple-element.26.corner_ref, bf16[128,4608]{1,0:T(8,128)(2,1)S(1)} %get-tuple-element.27.e_ref.edge_ref, ...), custom_call_target="tpu_custom_call" | custom-call | flops 603979776 | bytes 4751368 | tf_op jit(solution)/shard_map/pallas_call | solution.py:328
  13.1 1.6 %collective-permute-done.1.come_ref = bf16[256,128]{1,0:T(8,128)(2,1)S(1)} collective-permute-done((bf16[256,128]{1,0:T(8,128)(2,1)S(1)}, bf16[256,128]{1,0:T(8,128)(2,1)S(1)}, u32[]{:S(2)}, u32[]{:S(2)}) %collective-permute-start.1) | collective-permute-done | bytes 65568 | tf_op jit(solution)/shard_map/ppermute | solution.py:355
  14.8 4.1 %shard_map.69 = (bf16[256,128]{1,0:T(8,128)(2,1)S(1)}, bf16[256,128]{1,0:T(8,128)(2,1)S(1)}, bf16[256,128]{1,0:T(8,128)(2,1)S(1)}) custom-call(s32[2]{0:T(128)S(1)} %pad_add_fusion.core_ref, bf16[256,128]{1,0:T(8,128)(2,1)S(1)} %collective-permute-done.1.come_ref, bf16[128,128]{1,0:T(8,128)(2,1)S(1)} %get-tuple-element.26.corner_ref, ...), custom_call_target="tpu_custom_call" | custom-call | flops 603979776 | bytes 4882440 | tf_op jit(solution)/shard_map/pallas_call | solution.py:328
  18.9 0.0 copy-start
  18.9 3.2 %collective-permute-start.5 = (bf16[256,128]{1,0:T(8,128)(2,1)S(1)}, bf16[256,128]{1,0:T(8,128)(2,1)S(1)}, u32[]{:S(2)}, u32[]{:S(2)}) collective-permute-start(bf16[256,128]{1,0:T(8,128)(2,1)S(1)} %get-tuple-element.35), channel_id=1, source_target_pairs={{0,1},{1,0},{2,3},{3,2},{4,5},{5,4},{6,7},{7,6},{8,9},{9,8},{10,11... | collective-permute-start | bytes 196616 | tf_op jit(solution)/shard_map/ppermute | solution.py:355
  22.1 5.6 %collective-permute-start.4 = (bf16[256,128]{1,0:T(8,128)(2,1)S(1)}, bf16[256,128]{1,0:T(8,128)(2,1)S(1)}, u32[]{:S(2)}, u32[]{:S(2)}) collective-permute-start(bf16[256,128]{1,0:T(8,128)(2,1)S(1)} %get-tuple-element.34), channel_id=1, source_target_pairs={{0,2},{1,31},{2,4},{3,1},{4,6},{5,3},{6,8},{7,5},{8,10},{9,7},{10,... | collective-permute-start | bytes 196616 | tf_op jit(solution)/shard_map/ppermute | solution.py:355
  27.7 0.3 collective-permute-start.13
  28.0 0.0 collective-permute-done.5.m1_ref
  28.0 1.0 %collective-permute-done.4.come_ref.r1_ref = bf16[256,128]{1,0:T(8,128)(2,1)S(1)} collective-permute-done((bf16[256,128]{1,0:T(8,128)(2,1)S(1)}, bf16[256,128]{1,0:T(8,128)(2,1)S(1)}, u32[]{:S(2)}, u32[]{:S(2)}) %collective-permute-start.4) | collective-permute-done | bytes 65568 | tf_op jit(solution)/shard_map/ppermute | solution.py:355
  29.0 4.1 %shard_map.71 = (bf16[256,128]{1,0:T(8,128)(2,1)S(1)}, bf16[256,128]{1,0:T(8,128)(2,1)S(1)}) custom-call(s32[2]{0:T(128)S(1)} %pad_add_fusion.core_ref, bf16[256,128]{1,0:T(8,128)(2,1)S(1)} %collective-permute-done.4.come_ref.r1_ref, bf16[128,4608]{1,0:T(8,128)(2,1)S(1)} %get-tuple-element.27.e_ref.edge_ref, ...), custom_call_target="tpu_custom_call" | custom-call | flops 1207959552 | bytes 4947976 | tf_op jit(solution)/shard_map/pallas_call | solution.py:328
  33.2 1.6 %collective-permute-start.7 = (bf16[256,128]{1,0:T(8,128)(2,1)S(1)}, bf16[256,128]{1,0:T(8,128)(2,1)S(1)}, u32[]{:S(2)}, u32[]{:S(2)}) collective-permute-start(bf16[256,128]{1,0:T(8,128)(2,1)S(1)} %get-tuple-element.38), channel_id=1, source_target_pairs={{0,1},{1,0},{2,3},{3,2},{4,5},{5,4},{6,7},{7,6},{8,9},{9,8},{10,11... | collective-permute-start | bytes 196616 | tf_op jit(solution)/shard_map/ppermute | solution.py:355
  34.8 4.1 %collective-permute-start.6 = (bf16[256,128]{1,0:T(8,128)(2,1)S(1)}, bf16[256,128]{1,0:T(8,128)(2,1)S(1)}, u32[]{:S(2)}, u32[]{:S(2)}) collective-permute-start(bf16[256,128]{1,0:T(8,128)(2,1)S(1)} %get-tuple-element.37), channel_id=1, source_target_pairs={{0,2},{1,31},{2,4},{3,1},{4,6},{5,3},{6,8},{7,5},{8,10},{9,7},{10,... | collective-permute-start | bytes 196616 | tf_op jit(solution)/shard_map/ppermute | solution.py:355
  38.9 0.3 collective-permute-start.14
  39.2 1.2 %collective-permute-start.15 = (bf16[128,768]{1,0:T(8,128)(2,1)S(1)}, bf16[128,768]{1,0:T(8,128)(2,1)S(1)}, u32[]{:S(2)}, u32[]{:S(2)}) collective-permute-start(bf16[128,768]{1,0:T(8,128)(2,1)S(1)} %get-tuple-element.46), channel_id=1, source_target_pairs={{0,128},{32,160},{64,192},{96,224},{128,0},{160,32},{192,64},{224,... | collective-permute-start | bytes 589832 | tf_op jit(solution)/shard_map/ppermute | solution.py:361
  40.3 0.0 collective-permute-done.7.m2_ref
  40.3 0.3 collective-permute-start.9
  40.6 1.8 %shard_map.72 = (f32[128,2304]{1,0:T(8,128)S(1)}, bf16[512,128]{1,0:T(8,128)(2,1)S(1)}) custom-call(s32[2]{0:T(128)S(1)} %pad_add_fusion.core_ref, bf16[256,128]{1,0:T(8,128)(2,1)S(1)} %get-tuple-element.33.v_ref, bf16[256,128]{1,0:T(8,128)(2,1)S(1)} %collective-permute-done.4.come_ref.r1_ref, bf16[256,128]{1,0:T(8,128)(2,1)S(1)} %collective-permute-done.5.m1_ref, ...), custom_call_target="tpu_custom_call" | custom-call | flops 452984832 | bytes 851976 | tf_op jit(solution)/shard_map/pallas_call | solution.py:328
  42.4 0.0 collective-permute-done.6.value_ref
  42.5 0.5 collective-permute-start.8
  43.0 0.0 collective-permute-done.13.rest_0_
  43.0 0.9 %collective-permute-start.11 = (bf16[512,128]{1,0:T(8,128)(2,1)S(1)}, bf16[512,128]{1,0:T(8,128)(2,1)S(1)}, u32[]{:S(2)}, u32[]{:S(2)}) collective-permute-start(bf16[512,128]{1,0:T(8,128)(2,1)S(1)} %get-tuple-element.43), channel_id=1, source_target_pairs={{0,128},{32,160},{64,192},{96,224},{128,0},{160,32},{192,64},{224,... | collective-permute-start | bytes 393224 | tf_op jit(solution)/shard_map/ppermute | solution.py:361
  43.8 0.0 collective-permute-done.8.m3_ref
  43.9 1.1 %collective-permute-start.12 = (bf16[256,128]{1,0:T(8,128)(2,1)S(1)}, bf16[256,128]{1,0:T(8,128)(2,1)S(1)}, u32[]{:S(2)}, u32[]{:S(2)}) collective-permute-start(bf16[256,128]{1,0:T(8,128)(2,1)S(1)} %shard_map.73.r2_ref), channel_id=1, source_target_pairs={{0,128},{32,160},{64,192},{96,224},{128,0},{160,32},{192,64},{224,... | collective-permute-start | bytes 196616 | tf_op jit(solution)/shard_map/ppermute | solution.py:361
  45.0 1.8 %shard_map.74.after_ref.sum_ref = f32[128,2304]{1,0:T(8,128)S(1)} custom-call(s32[2]{0:T(128)S(1)} %pad_add_fusion.core_ref, bf16[256,128]{1,0:T(8,128)(2,1)S(1)} %shard_map.73.r2_ref, bf16[256,128]{1,0:T(8,128)(2,1)S(1)} %collective-permute-done.5.m1_ref, bf16[128,128]{1,0:T(8,128)(2,1)S(1)} %get-tuple-element.36.last_ref, ...), custom_call_target="tpu_custom_call", output_to_operand_aliasing={{}: (5, {})} | custom-call | flops 301989888 | bytes 1933320 | tf_op jit(solution)/shard_map/pallas_call | solution.py:328
  46.8 1.6 %shard_map.75.near_ref = bf16[128,128]{1,0:T(8,128)(2,1)S(1)} custom-call(s32[2]{0:T(128)S(1)} %pad_add_fusion.core_ref, bf16[256,128]{1,0:T(8,128)(2,1)S(1)} %collective-permute-done.8.m3_ref, bf16[128,4608]{1,0:T(8,128)(2,1)S(1)} %get-tuple-element.31.me_ref, bf16[128,4608]{1,0:T(8,128)(2,1)S(1)} %get-tuple-element.32.mt_ref, ...), custom_call_target="tpu_custom_call" | custom-call | flops 301989888 | bytes 3604488 | tf_op jit(solution)/shard_map/pallas_call | solution.py:328
  48.4 0.0 collective-permute-done.14.rest_1_
  48.4 0.4 collective-permute-start.10
  48.8 1.2 %collective-permute-done.15.rest_2_ = bf16[128,768]{1,0:T(8,128)(2,1)S(1)} collective-permute-done((bf16[128,768]{1,0:T(8,128)(2,1)S(1)}, bf16[128,768]{1,0:T(8,128)(2,1)S(1)}, u32[]{:S(2)}, u32[]{:S(2)}) %collective-permute-start.15) | collective-permute-done | bytes 196640 | tf_op jit(solution)/shard_map/ppermute | solution.py:361
  50.1 4.3 %collective-permute-done.12.r2_ref = bf16[256,128]{1,0:T(8,128)(2,1)S(1)} collective-permute-done((bf16[256,128]{1,0:T(8,128)(2,1)S(1)}, bf16[256,128]{1,0:T(8,128)(2,1)S(1)}, u32[]{:S(2)}, u32[]{:S(2)}) %collective-permute-start.12) | collective-permute-done | bytes 65568 | tf_op jit(solution)/shard_map/ppermute | solution.py:361
  54.4 0.0 collective-permute-done.9.pack1_ref
  54.4 0.0 collective-permute-done.11.pack2_ref
  54.4 3.1 %shard_map.77.sum_ref = f32[128,2304]{1,0:T(8,128)S(1)} custom-call(s32[2]{0:T(128)S(1)} %pad_add_fusion.core_ref, bf16[256,128]{1,0:T(8,128)(2,1)S(1)} %get-tuple-element.33.v_ref, bf16[128,128]{1,0:T(8,128)(2,1)S(1)} %shard_map.75.near_ref, bf16[640,128]{1,0:T(8,128)(2,1)S(1)} %collective-permute-done.9.pack1_ref, ...), custom_call_target="tpu_custom_call", output_to_operand_aliasing={{}: (7, {})} | custom-call | flops 905969664 | bytes 2818056 | tf_op jit(solution)/shard_map/pallas_call | solution.py:328
  57.5 0.0 collective-permute-done.10.near_ref
  57.5 1.9 %shard_map.78 = bf16[128,2304]{1,0:T(8,128)(2,1)} custom-call(s32[2]{0:T(128)S(1)} %pad_add_fusion.core_ref, bf16[640,128]{1,0:T(8,128)(2,1)S(1)} %collective-permute-done.9.pack1_ref, bf16[128,128]{1,0:T(8,128)(2,1)S(1)} %collective-permute-done.10.near_ref, f32[128,2304]{1,0:T(8,128)S(1)} %shard_map.77.sum_ref, ...), custom_call_target="tpu_custom_call" | custom-call | flops 150994944 | bytes 1966088 | tf_op jit(solution)/shard_map/pallas_call | solution.py:328
  59.4 4.2 %all-to-all-start = ((bf16[8,16,2304]{2,1,0:T(8,128)(2,1)}), bf16[8,16,2304]{2,1,0:T(8,128)(2,1)S(1)}, u32[]{:S(2)}, u32[]{:S(2)}) async-start(bf16[8,16,2304]{2,1,0:T(8,128)(2,1)} %bitcast.10), calls=%async_computation | async-start | bytes 1179648 | tf_op jit(solution)/shard_map/all_to_all | solution.py:421
  63.6 7.5 %shard_map.76 = (bf16[128,4608]{1,0:T(8,128)(2,1)}, bf16[128,128]{1,0:T(8,128)(2,1)}) custom-call(s32[2]{0:T(128)S(1)} %pad_add_fusion.core_ref, bf16[256,128]{1,0:T(8,128)(2,1)} %copy-done, bf16[256,128]{1,0:T(8,128)(2,1)} %copy-done.4, bf16[256,128]{1,0:T(8,128)(2,1)} %copy-done.2, bf16[128,128]{1,0:T(8,128)(2,1)S(1)} %shard_map.75.near_ref, ...), custom_call_target="tpu_custom_call" | custom-call | flops 2113929216 | bytes 2752520 | tf_op jit(solution)/shard_map/pallas_call | solution.py:328
  71.2 1.1 %all-to-all-done.parts_ref = bf16[8,16,2304]{2,1,0:T(8,128)(2,1)S(1)} async-done(((bf16[8,16,2304]{2,1,0:T(8,128)(2,1)}), bf16[8,16,2304]{2,1,0:T(8,128)(2,1)S(1)}, u32[]{:S(2)}, u32[]{:S(2)}) %all-to-all-start) | async-done | bytes 589856 | tf_op jit(solution)/shard_map/all_to_all | solution.py:421
  72.3 0.8 %shard_map.79 = f32[576,128]{1,0:T(8,128)} custom-call(bf16[8,16,2304]{2,1,0:T(8,128)(2,1)S(1)} %all-to-all-done.parts_ref), custom_call_target="tpu_custom_call" | custom-call | flops 150994944 | bytes 589824 | tf_op jit(solution)/shard_map/pallas_call | solution.py:328
  (14 shorter events, 0.0 us)
Async XLA Ops:
  0.6 4.4 %collective-permute-start = (bf16[128,128]{1,0:T(8,128)(2,1)}, bf16[128,128]{1,0:T(8,128)(2,1)S(1)}, u32[]{:S(2)}, u32[]{:S(2)}) collective-permute-start(bf16[128,128]{1,0:T(8,128)(2,1)} %bitcast.16), channel_id=1, source_target_pairs={{0,1},{1,0},{2,3},{3,2},{4,5},{5,4},{6,7},{7,6},{8,9},{9,8},{10,11... | collective-permute-start | bytes 98312 | tf_op jit(solution)/shard_map/ppermute | solution.py:355
  4.0 6.6 %collective-permute-start.2 = (bf16[128,4608]{1,0:T(8,128)(2,1)}, bf16[128,4608]{1,0:T(8,128)(2,1)S(1)}, u32[]{:S(2)}, u32[]{:S(2)}) collective-permute-start(bf16[128,4608]{1,0:T(8,128)(2,1)} %bitcast.12), channel_id=1, source_target_pairs={{0,1},{1,0},{2,3},{3,2},{4,5},{5,4},{6,7},{7,6},{8,9},{9,8},{10,11... | collective-permute-start | bytes 3538952 | tf_op jit(solution)/shard_map/ppermute | solution.py:355
  5.0 0.6 copy-start.6
  9.1 35.9 %copy-start.3 = (bf16[128,128]{1,0:T(8,128)(2,1)}, bf16[128,128]{1,0:T(8,128)(2,1)S(1)}, u32[]{:S(2)}) copy-start(bf16[128,128]{1,0:T(8,128)(2,1)S(1)} %get-tuple-element.36.last_ref) | copy-start | bytes 98308
  9.1 3.0 %collective-permute-start.3 = (bf16[128,4608]{1,0:T(8,128)(2,1)S(1)}, bf16[128,4608]{1,0:T(8,128)(2,1)S(1)}, u32[]{:S(2)}, u32[]{:S(2)}) collective-permute-start(bf16[128,4608]{1,0:T(8,128)(2,1)S(1)} %get-tuple-element.28.t_ref.turned_ref), channel_id=1, source_target_pairs={{0,1},{1,0},{2,3},{3,2},{4,5},{5,4},{6,7},{7,6},{8,9},{9,8},{10,11... | collective-permute-start | bytes 3538952 | tf_op jit(solution)/shard_map/ppermute | solution.py:355
  9.6 5.2 %collective-permute-start.1 = (bf16[256,128]{1,0:T(8,128)(2,1)S(1)}, bf16[256,128]{1,0:T(8,128)(2,1)S(1)}, u32[]{:S(2)}, u32[]{:S(2)}) collective-permute-start(bf16[256,128]{1,0:T(8,128)(2,1)S(1)} %get-tuple-element.25), channel_id=1, source_target_pairs={{0,31},{1,2},{2,1},{3,4},{4,3},{5,6},{6,5},{7,8},{8,7},{9,10},{10,... | collective-permute-start | bytes 196616 | tf_op jit(solution)/shard_map/ppermute | solution.py:355
  18.9 35.5 %copy-start = (bf16[256,128]{1,0:T(8,128)(2,1)}, bf16[256,128]{1,0:T(8,128)(2,1)S(1)}, u32[]{:S(2)}) copy-start(bf16[256,128]{1,0:T(8,128)(2,1)S(1)} %get-tuple-element.33.v_ref) | copy-start | bytes 196612
  18.9 9.1 %collective-permute-start.5 = (bf16[256,128]{1,0:T(8,128)(2,1)S(1)}, bf16[256,128]{1,0:T(8,128)(2,1)S(1)}, u32[]{:S(2)}, u32[]{:S(2)}) collective-permute-start(bf16[256,128]{1,0:T(8,128)(2,1)S(1)} %get-tuple-element.35), channel_id=1, source_target_pairs={{0,1},{1,0},{2,3},{3,2},{4,5},{5,4},{6,7},{7,6},{8,9},{9,8},{10,11... | collective-permute-start | bytes 196616 | tf_op jit(solution)/shard_map/ppermute | solution.py:355
  22.1 6.9 %collective-permute-start.4 = (bf16[256,128]{1,0:T(8,128)(2,1)S(1)}, bf16[256,128]{1,0:T(8,128)(2,1)S(1)}, u32[]{:S(2)}, u32[]{:S(2)}) collective-permute-start(bf16[256,128]{1,0:T(8,128)(2,1)S(1)} %get-tuple-element.34), channel_id=1, source_target_pairs={{0,2},{1,31},{2,4},{3,1},{4,6},{5,3},{6,8},{7,5},{8,10},{9,7},{10,... | collective-permute-start | bytes 196616 | tf_op jit(solution)/shard_map/ppermute | solution.py:355
  27.7 15.3 %collective-permute-start.13 = (bf16[128,768]{1,0:T(8,128)(2,1)S(1)}, bf16[128,768]{1,0:T(8,128)(2,1)S(1)}, u32[]{:S(2)}, u32[]{:S(2)}) collective-permute-start(bf16[128,768]{1,0:T(8,128)(2,1)S(1)} %get-tuple-element.44), channel_id=1, source_target_pairs={{0,128},{32,160},{64,192},{96,224},{128,0},{160,32},{192,64},{224,... | collective-permute-start | bytes 589832 | tf_op jit(solution)/shard_map/ppermute | solution.py:361
  28.0 17.0 %copy-start.1 = (bf16[256,128]{1,0:T(8,128)(2,1)}, bf16[256,128]{1,0:T(8,128)(2,1)S(1)}, u32[]{:S(2)}) copy-start(bf16[256,128]{1,0:T(8,128)(2,1)S(1)} %collective-permute-done.5.m1_ref) | copy-start | bytes 196612
  29.0 11.6 %copy-start.4 = (bf16[256,128]{1,0:T(8,128)(2,1)}, bf16[256,128]{1,0:T(8,128)(2,1)S(1)}, u32[]{:S(2)}) copy-start(bf16[256,128]{1,0:T(8,128)(2,1)S(1)} %collective-permute-done.4.come_ref.r1_ref) | copy-start | bytes 196612
  33.2 7.2 %collective-permute-start.7 = (bf16[256,128]{1,0:T(8,128)(2,1)S(1)}, bf16[256,128]{1,0:T(8,128)(2,1)S(1)}, u32[]{:S(2)}, u32[]{:S(2)}) collective-permute-start(bf16[256,128]{1,0:T(8,128)(2,1)S(1)} %get-tuple-element.38), channel_id=1, source_target_pairs={{0,1},{1,0},{2,3},{3,2},{4,5},{5,4},{6,7},{7,6},{8,9},{9,8},{10,11... | collective-permute-start | bytes 196616 | tf_op jit(solution)/shard_map/ppermute | solution.py:355
  34.8 7.7 %collective-permute-start.6 = (bf16[256,128]{1,0:T(8,128)(2,1)S(1)}, bf16[256,128]{1,0:T(8,128)(2,1)S(1)}, u32[]{:S(2)}, u32[]{:S(2)}) collective-permute-start(bf16[256,128]{1,0:T(8,128)(2,1)S(1)} %get-tuple-element.37), channel_id=1, source_target_pairs={{0,2},{1,31},{2,4},{3,1},{4,6},{5,3},{6,8},{7,5},{8,10},{9,7},{10,... | collective-permute-start | bytes 196616 | tf_op jit(solution)/shard_map/ppermute | solution.py:355
  38.9 9.5 %collective-permute-start.14 = (bf16[128,768]{1,0:T(8,128)(2,1)S(1)}, bf16[128,768]{1,0:T(8,128)(2,1)S(1)}, u32[]{:S(2)}, u32[]{:S(2)}) collective-permute-start(bf16[128,768]{1,0:T(8,128)(2,1)S(1)} %get-tuple-element.45), channel_id=1, source_target_pairs={{0,128},{32,160},{64,192},{96,224},{128,0},{160,32},{192,64},{224,... | collective-permute-start | bytes 589832 | tf_op jit(solution)/shard_map/ppermute | solution.py:361
  39.2 10.9 %collective-permute-start.15 = (bf16[128,768]{1,0:T(8,128)(2,1)S(1)}, bf16[128,768]{1,0:T(8,128)(2,1)S(1)}, u32[]{:S(2)}, u32[]{:S(2)}) collective-permute-start(bf16[128,768]{1,0:T(8,128)(2,1)S(1)} %get-tuple-element.46), channel_id=1, source_target_pairs={{0,128},{32,160},{64,192},{96,224},{128,0},{160,32},{192,64},{224,... | collective-permute-start | bytes 589832 | tf_op jit(solution)/shard_map/ppermute | solution.py:361
  40.3 2.2 %copy-start.5 = (bf16[256,128]{1,0:T(8,128)(2,1)}, bf16[256,128]{1,0:T(8,128)(2,1)S(1)}, u32[]{:S(2)}) copy-start(bf16[256,128]{1,0:T(8,128)(2,1)S(1)} %collective-permute-done.7.m2_ref) | copy-start | bytes 196612
  40.3 14.0 %collective-permute-start.9 = (bf16[640,128]{1,0:T(8,128)(2,1)S(1)}, bf16[640,128]{1,0:T(8,128)(2,1)S(1)}, u32[]{:S(2)}, u32[]{:S(2)}) collective-permute-start(bf16[640,128]{1,0:T(8,128)(2,1)S(1)} %shard_map.70.m1_ref), channel_id=1, source_target_pairs={{0,128},{32,160},{64,192},{96,224},{128,0},{160,32},{192,64},{224,... | collective-permute-start | bytes 491528 | tf_op jit(solution)/shard_map/ppermute | solution.py:361
  42.5 4.3 %copy-start.2 = (bf16[256,128]{1,0:T(8,128)(2,1)}, bf16[256,128]{1,0:T(8,128)(2,1)S(1)}, u32[]{:S(2)}) copy-start(bf16[256,128]{1,0:T(8,128)(2,1)S(1)} %shard_map.73.r2_ref) | copy-start | bytes 196612
  42.5 1.4 %collective-permute-start.8 = (bf16[256,128]{1,0:T(8,128)(2,1)S(1)}, bf16[256,128]{1,0:T(8,128)(2,1)S(1)}, u32[]{:S(2)}, u32[]{:S(2)}) collective-permute-start(bf16[256,128]{1,0:T(8,128)(2,1)S(1)} %shard_map.73.r2_ref), channel_id=1, source_target_pairs={{0,1},{1,0},{2,3},{3,2},{4,5},{5,4},{6,7},{7,6},{8,9},{9,8},{10,11... | collective-permute-start | bytes 196616 | tf_op jit(solution)/shard_map/ppermute | solution.py:355
  43.0 11.4 %collective-permute-start.11 = (bf16[512,128]{1,0:T(8,128)(2,1)S(1)}, bf16[512,128]{1,0:T(8,128)(2,1)S(1)}, u32[]{:S(2)}, u32[]{:S(2)}) collective-permute-start(bf16[512,128]{1,0:T(8,128)(2,1)S(1)} %get-tuple-element.43), channel_id=1, source_target_pairs={{0,128},{32,160},{64,192},{96,224},{128,0},{160,32},{192,64},{224,... | collective-permute-start | bytes 393224 | tf_op jit(solution)/shard_map/ppermute | solution.py:361
  43.9 10.5 %collective-permute-start.12 = (bf16[256,128]{1,0:T(8,128)(2,1)S(1)}, bf16[256,128]{1,0:T(8,128)(2,1)S(1)}, u32[]{:S(2)}, u32[]{:S(2)}) collective-permute-start(bf16[256,128]{1,0:T(8,128)(2,1)S(1)} %shard_map.73.r2_ref), channel_id=1, source_target_pairs={{0,128},{32,160},{64,192},{96,224},{128,0},{160,32},{192,64},{224,... | collective-permute-start | bytes 196616 | tf_op jit(solution)/shard_map/ppermute | solution.py:361
  48.4 9.1 %collective-permute-start.10 = (bf16[128,128]{1,0:T(8,128)(2,1)S(1)}, bf16[128,128]{1,0:T(8,128)(2,1)S(1)}, u32[]{:S(2)}, u32[]{:S(2)}) collective-permute-start(bf16[128,128]{1,0:T(8,128)(2,1)S(1)} %shard_map.75.near_ref), channel_id=1, source_target_pairs={{0,128},{32,160},{64,192},{96,224},{128,0},{160,32},{192,64},{224,... | collective-permute-start | bytes 98312 | tf_op jit(solution)/shard_map/ppermute | solution.py:361
  59.4 12.9 %all-to-all-start = ((bf16[8,16,2304]{2,1,0:T(8,128)(2,1)}), bf16[8,16,2304]{2,1,0:T(8,128)(2,1)S(1)}, u32[]{:S(2)}, u32[]{:S(2)}) async-start(bf16[8,16,2304]{2,1,0:T(8,128)(2,1)} %bitcast.10), calls=%async_computation | async-start | bytes 1179648 | tf_op jit(solution)/shard_map/all_to_all | solution.py:421

commit v8 on v5

--- a/solution.py
+++ b/solution.py
@@ -33,8 +33,8 @@
     return [wide[:, W * b : W * (b + 1)] for b in range(wide.shape[1] // W)]
 
 
-def start_kernel(
-    core_ref, proj_ref, edge_in, corner_in, cot_ref, mate_cot_ref, turned_ref, edge_ref, corner_ref, last_ref, send_ref,
+def turn_kernel(
+    proj_ref, edge_in, corner_in, cot_ref, turned_ref, edge_ref, corner_ref, cot_t_ref,
     proj_vmem, wide_ref, cot_vmem, proj_sem, sem,
 ):
     pieces = proj_sem.shape[0]
@@ -44,10 +44,9 @@
         at = pl.ds(n * size, size)
         loads.append(pltpu.make_async_copy(proj_ref.at[at], proj_vmem.at[at], proj_sem.at[n]))
     others = [
-        pltpu.make_async_copy(cot_ref, cot_vmem.at[0], sem.at[0]),
-        pltpu.make_async_copy(mate_cot_ref, cot_vmem.at[1], sem.at[1]),
-        pltpu.make_async_copy(corner_in, corner_ref, sem.at[2]),
-        pltpu.make_async_copy(edge_in, edge_ref, sem.at[3]),
+        pltpu.make_async_copy(cot_ref, cot_vmem, sem.at[0]),
+        pltpu.make_async_copy(corner_in, corner_ref, sem.at[1]),
+        pltpu.make_async_copy(edge_in, edge_ref, sem.at[2]),
     ]
     for copy in loads + others:
         copy.start()
@@ -60,12 +59,15 @@
         turned_ref[:, W * p : W * (p + 1)] = wide_ref[pl.ds(p, W, stride=planes), :].T.astype(BF)
     for copy in others:
         copy.wait()
-
-    @pl.when(core_ref[0] == 0)
-    def _():
-        last = cot_vmem[1].astype(F32).T.astype(BF)
+    cot_t_ref[...] = cot_vmem[...].astype(F32).T.astype(BF)
+
+
+def own_kernel(core_ref, corner_ref, cot_t_ref, mate_cot_ref, edge_ref, turned_ref, last_ref, send_ref, same_ref):
+    @pl.when(core_ref[0] == 0)
+    def _():
+        last = mate_cot_ref[...].astype(F32).T.astype(BF)
         last_ref[...] = last
-        send_ref[:W, :] = cot_vmem[0].astype(F32).T.astype(BF)
+        send_ref[:W, :] = cot_t_ref[...]
         send_ref[W:, :] = step(last, turned_ref, edge_ref)
 
     @pl.when(core_ref[0] != 0)
@@ -196,16 +198,18 @@
 
 
 def proj_last_kernel(
-    core_ref, v_ref, m3_ref, e_ref, me_ref, mt_ref, sum_ref, near_ref, out_ref, z_ref, w_ref, stage_ref, sem
+    core_ref, v_ref, m3_ref, e_ref, me_ref, mt_ref, sum_ref, near_out_ref, out_ref,
+    near_ref, z_ref, w_ref, stage_ref, sem, near_sem,
 ):
     def body(x1, y1, x2, y2):
         near_ref[...] = step(m3_ref[:W, :], y2, x2)
 
     by_role(core_ref, body, (None, None, me_ref, mt_ref))
+    copies = [pltpu.make_async_copy(near_ref, near_out_ref, near_sem.at[0])]
+    copies[0].start()
     place(core_ref, z_ref, w_ref, [v_ref[:W, :]], [near_ref[...]])
     pieces = sem.shape[0]
     each = e_ref.shape[1] // W // pieces
-    copies = []
 
     def put(p, value):
         at = slice(W * p, W * (p + 1))
@@ -322,10 +326,12 @@
 
     mate_cot = swap(cot)
     far_edge = swap(edge)
-    turned, edge, corner, u0, first = call(
-        start_kernel, [whole, whole, one, one, two], core, projector, edge, corner, cot, mate_cot,
-        scratch=[((width, W), BF), ((width, W), F32), ((2, W, W), BF)], sems=(4, 4), flops=3 * unit,
-        far=(1, 2, 3, 4), free=(5,),
+    turned, edge, corner, cot_t = call(
+        turn_kernel, [whole, whole, one, one], projector, edge, corner, cot,
+        scratch=[((width, W), BF), ((width, W), F32), ((W, W), BF)], sems=(4, 3), flops=unit, far=(0, 1, 2, 3),
+    )
+    u0, first, turned = call(
+        own_kernel, [one, two, whole], core, corner, cot_t, mate_cot, edge, turned, flops=2 * unit, alias={5: 2}
     )
     r0 = send(first, lambda i: i - 1 if i % 2 == 0 else i + 1)
     far_turned = swap(turned)
@@ -346,7 +352,7 @@
     late = call(proj_late_kernel, [wide], core, r2, m1, u0, edge, early, scratch=stacks(2), flops=4 * unit, alias={5: 0})
     near3, done = call(
         proj_last_kernel, [one, whole], core, v, m3, edge, mate_edge, mate_turned, late,
-        scratch=stacks(1) + [whole], sems=(6,), flops=4 * unit, far_outs=(1,),
+        scratch=[one] + stacks(1) + [whole], sems=(18, 1), flops=4 * unit, far_outs=(0, 1),
     )
     share = W // rows
     parts = lax.all_to_all(done.reshape(rows, share, width), "row", 0, 0, tiled=True)

time: 68.1 us -> 66.2 us (0.972)
  local copies, waits for them, and re-layouts: 1.99 us -> 0.03 us
  waiting for transfers between devices: 15.3 us -> 14.4 us
  Pallas kernels: 25.3 us -> 26.1 us
    unnamed x18 -> x12, local copies, waits for them, and re-layouts: 1.99 us -> 0.03 us
    ppermute x9, waiting for transfers between devices: 5.97 us -> 5.01 us  [send(): return lax.ppermute(value, 'col', pairs)]
    pallas_call x10 -> x11, Pallas kernels: 25.3 us -> 26.1 us  [call(): pl.pallas_call(kernel, out_shape=outs[0] if single else outs, in_specs=in...]
  transfers between devices with their start and end apart: 10 -> 10, of which waited for: 5 -> 4; matrix products, arithmetic and copies ran while one was open for 0% -> 0% of each run, Pallas kernels for 21% -> 23%
where the time goes in v8:
time: 66.2 us; the launch traced here: 65.9 us
  Pallas kernels  26.1 us (39%)
  starting transfers between devices  24.5 us (37%)
  waiting for transfers between devices  14.4 us (22%)
  between operations  0.79 us (1%)
    pallas_call x11, Pallas kernels, call(): pl.pallas_call(kernel, out_shape=outs[0] if single else outs, in_specs=in...  26.1 us
    ppermute x9, starting transfers between devices, send(): return lax.ppermute(value, 'col', pairs)  20.3 us
    all_to_all x1, waiting for transfers between devices, shards(): lax.all_to_all(done.reshape(rows, share, width), 'row', 0, 0, tiled=True)  9.38 us
    ppermute x9, waiting for transfers between devices, send(): return lax.ppermute(value, 'col', pairs)  5.01 us
    all_to_all x1, starting transfers between devices, shards(): lax.all_to_all(done.reshape(rows, share, width), 'row', 0, 0, tiled=True)  4.22 us
  transfers between devices with their start and end apart: 10, of which 4 were waited for; matrix products, arithmetic and copies ran while one was open for 0% of the time, Pallas kernels for 23%

profile of v8, /device:TPU:1, one launch (start us, length us, event | category | flops | bytes accessed | tf_op | source)
XLA Modules:
  0.0 65.9 jit_solution(14699761562306416633)
XLA Ops:
  0.6 3.3 %collective-permute-start = (bf16[128,128]{1,0:T(8,128)(2,1)}, bf16[128,128]{1,0:T(8,128)(2,1)}, u32[]{:S(2)}, u32[]{:S(2)}) collective-permute-start(bf16[128,128]{1,0:T(8,128)(2,1)} %bitcast.15), channel_id=1, source_target_pairs={{0,1},{1,0},{2,3},{3,2},{4,5},{5,4},{6,7},{7,6},{8,9},{9,8},{10,11... | collective-permute-start | bytes 98312 | tf_op jit(solution)/shard_map/ppermute | solution.py:313
  4.0 0.1 collective-permute-start.2
  4.1 1.8 %shard_map.67 = (bf16[128,4608]{1,0:T(8,128)(2,1)S(1)}, bf16[128,4608]{1,0:T(8,128)(2,1)S(1)}, bf16[128,128]{1,0:T(8,128)(2,1)S(1)}, bf16[128,128]{1,0:T(8,128)(2,1)S(1)}) custom-call(bf16[4608,128]{1,0:T(8,128)(2,1)} %bitcast.9, bf16[128,4608]{1,0:T(8,128)(2,1)} %bitcast.11, bf16[128,128]{1,0:T(8,128)(2,1)} %bitcast.14, bf16[128,128]{1,0:T(8,128)(2,1)} %bitcast.16), custom_call_target="tpu_custom_call" | custom-call | flops 150994944 | bytes 2424832 | tf_op jit(solution)/shard_map/pallas_call | solution.py:287
  5.9 0.0 collective-permute-done.mate_cot_ref
  5.9 1.8 %shard_map.68 = (bf16[128,128]{1,0:T(8,128)(2,1)S(1)}, bf16[256,128]{1,0:T(8,128)(2,1)S(1)}, bf16[128,4608]{1,0:T(8,128)(2,1)S(1)}) custom-call(s32[1]{0:T(128)} %bitcast.core_ref, bf16[128,128]{1,0:T(8,128)(2,1)S(1)} %get-tuple-element.23.corner_ref, bf16[128,128]{1,0:T(8,128)(2,1)S(1)} %get-tuple-element.24.cot_t_ref, ...), custom_call_target="tpu_custom_call", output_to_operand_aliasing={{2}: (5, {})} | custom-call | flops 301989888 | bytes 2457604 | tf_op jit(solution)/shard_map/pallas_call | solution.py:287
  7.7 0.0 copy-start.5
  7.7 0.6 collective-permute-start.3
  8.3 1.0 %collective-permute-start.1 = (bf16[256,128]{1,0:T(8,128)(2,1)S(1)}, bf16[256,128]{1,0:T(8,128)(2,1)S(1)}, u32[]{:S(2)}, u32[]{:S(2)}) collective-permute-start(bf16[256,128]{1,0:T(8,128)(2,1)S(1)} %get-tuple-element.27), channel_id=1, source_target_pairs={{0,31},{1,2},{2,1},{3,4},{4,3},{5,6},{6,5},{7,8},{8,7},{9,10},{10,... | collective-permute-start | bytes 196616 | tf_op jit(solution)/shard_map/ppermute | solution.py:313
  9.3 0.0 collective-permute-done.2.far_edge_ref
  9.3 1.5 %collective-permute-done.3.far_turned_ref = bf16[128,4608]{1,0:T(8,128)(2,1)S(1)} collective-permute-done((bf16[128,4608]{1,0:T(8,128)(2,1)S(1)}, bf16[128,4608]{1,0:T(8,128)(2,1)S(1)}, u32[]{:S(2)}, u32[]{:S(2)}) %collective-permute-start.3) | collective-permute-done | bytes 1179680 | tf_op jit(solution)/shard_map/ppermute | solution.py:313
  10.8 0.5 shard_map.69
  11.3 2.2 %collective-permute-done.1.come_ref = bf16[256,128]{1,0:T(8,128)(2,1)S(1)} collective-permute-done((bf16[256,128]{1,0:T(8,128)(2,1)S(1)}, bf16[256,128]{1,0:T(8,128)(2,1)S(1)}, u32[]{:S(2)}, u32[]{:S(2)}) %collective-permute-start.1) | collective-permute-done | bytes 65568 | tf_op jit(solution)/shard_map/ppermute | solution.py:313
  13.5 3.5 %shard_map.70 = (bf16[256,128]{1,0:T(8,128)(2,1)S(1)}, bf16[256,128]{1,0:T(8,128)(2,1)S(1)}, bf16[256,128]{1,0:T(8,128)(2,1)S(1)}) custom-call(s32[1]{0:T(128)} %bitcast.core_ref, bf16[256,128]{1,0:T(8,128)(2,1)S(1)} %collective-permute-done.1.come_ref, bf16[128,128]{1,0:T(8,128)(2,1)S(1)} %get-tuple-element.23.corner_ref, ...), custom_call_target="tpu_custom_call" | custom-call | flops 603979776 | bytes 4882436 | tf_op jit(solution)/shard_map/pallas_call | solution.py:287
  17.0 0.0 copy-start.1
  17.0 8.5 %collective-permute-start.4 = (bf16[256,128]{1,0:T(8,128)(2,1)S(1)}, bf16[256,128]{1,0:T(8,128)(2,1)S(1)}, u32[]{:S(2)}, u32[]{:S(2)}) collective-permute-start(bf16[256,128]{1,0:T(8,128)(2,1)S(1)} %get-tuple-element.34), channel_id=1, source_target_pairs={{0,2},{1,31},{2,4},{3,1},{4,6},{5,3},{6,8},{7,5},{8,10},{9,7},{10,... | collective-permute-start | bytes 196616 | tf_op jit(solution)/shard_map/ppermute | solution.py:313
  25.5 0.0 collective-permute-start.5
  25.5 1.3 %collective-permute-done.4.come_ref.r1_ref = bf16[256,128]{1,0:T(8,128)(2,1)S(1)} collective-permute-done((bf16[256,128]{1,0:T(8,128)(2,1)S(1)}, bf16[256,128]{1,0:T(8,128)(2,1)S(1)}, u32[]{:S(2)}, u32[]{:S(2)}) %collective-permute-start.4) | collective-permute-done | bytes 65568 | tf_op jit(solution)/shard_map/ppermute | solution.py:313
  26.8 0.0 copy-start.2
  26.8 0.0 collective-permute-done.5.m1_ref
  26.9 0.0 copy-start
  26.9 3.5 %shard_map.71 = (bf16[256,128]{1,0:T(8,128)(2,1)S(1)}, bf16[256,128]{1,0:T(8,128)(2,1)S(1)}) custom-call(s32[1]{0:T(128)} %bitcast.core_ref, bf16[256,128]{1,0:T(8,128)(2,1)S(1)} %collective-permute-done.4.come_ref.r1_ref, bf16[128,4608]{1,0:T(8,128)(2,1)S(1)} %get-tuple-element.25.edge_ref.e_ref, bf16[128,4608]{1,0:T(8,128)(2,1)S(1)} %get-tuple-element.28.t_ref.turned_ref, ...), custom_call_target="tpu_custom_call" | custom-call | flops 1207959552 | bytes 4849668 | tf_op jit(solution)/shard_map/pallas_call | solution.py:287
  30.4 1.0 %collective-permute-start.7 = (bf16[256,128]{1,0:T(8,128)(2,1)S(1)}, bf16[256,128]{1,0:T(8,128)(2,1)S(1)}, u32[]{:S(2)}, u32[]{:S(2)}) collective-permute-start(bf16[256,128]{1,0:T(8,128)(2,1)S(1)} %get-tuple-element.37), channel_id=1, source_target_pairs={{0,1},{1,0},{2,3},{3,2},{4,5},{5,4},{6,7},{7,6},{8,9},{9,8},{10,11... | collective-permute-start | bytes 196616 | tf_op jit(solution)/shard_map/ppermute | solution.py:313
  31.4 4.7 %collective-permute-start.6 = (bf16[256,128]{1,0:T(8,128)(2,1)S(1)}, bf16[256,128]{1,0:T(8,128)(2,1)S(1)}, u32[]{:S(2)}, u32[]{:S(2)}) collective-permute-start(bf16[256,128]{1,0:T(8,128)(2,1)S(1)} %get-tuple-element.36), channel_id=1, source_target_pairs={{0,2},{1,31},{2,4},{3,1},{4,6},{5,3},{6,8},{7,5},{8,10},{9,7},{10,... | collective-permute-start | bytes 196616 | tf_op jit(solution)/shard_map/ppermute | solution.py:313
  36.2 0.0 collective-permute-done.7.m2_ref
  36.2 0.0 copy-start.4
  36.2 0.0 copy-done.2
  36.2 2.2 %shard_map.72.after_ref.early_ref = f32[128,4608]{1,0:T(8,128)S(1)} custom-call(s32[1]{0:T(128)} %bitcast.core_ref, bf16[256,128]{1,0:T(8,128)(2,1)S(1)} %get-tuple-element.33.v_ref, bf16[256,128]{1,0:T(8,128)(2,1)S(1)} %collective-permute-done.4.come_ref.r1_ref, bf16[256,128]{1,0:T(8,128)(2,1)S(1)} %collective-permute-done.5.m1_ref, ...), custom_call_target="tpu_custom_call" | custom-call | flops 905969664 | bytes 1441796 | tf_op jit(solution)/shard_map/pallas_call | solution.py:287
  38.4 0.0 copy-done.4
  38.4 0.0 collective-permute-done.6.value_ref
  38.4 0.0 copy-start.3
  38.4 1.1 %collective-permute-start.8 = (bf16[256,128]{1,0:T(8,128)(2,1)S(1)}, bf16[256,128]{1,0:T(8,128)(2,1)S(1)}, u32[]{:S(2)}, u32[]{:S(2)}) collective-permute-start(bf16[256,128]{1,0:T(8,128)(2,1)S(1)} %shard_map.73.r2_ref), channel_id=1, source_target_pairs={{0,1},{1,0},{2,3},{3,2},{4,5},{5,4},{6,7},{7,6},{8,9},{9,8},{10,11... | collective-permute-start | bytes 196616 | tf_op jit(solution)/shard_map/ppermute | solution.py:313
  39.5 0.0 copy-done.5
  39.5 0.0 copy-done
  39.5 1.8 %shard_map.74.sum_ref = f32[128,4608]{1,0:T(8,128)S(1)} custom-call(s32[1]{0:T(128)} %bitcast.core_ref, bf16[256,128]{1,0:T(8,128)(2,1)S(1)} %shard_map.73.r2_ref, bf16[256,128]{1,0:T(8,128)(2,1)S(1)} %collective-permute-done.5.m1_ref, bf16[128,128]{1,0:T(8,128)(2,1)S(1)} %get-tuple-element.38.last_ref, ...), custom_call_target="tpu_custom_call", output_to_operand_aliasing={{}: (5, {})} | custom-call | flops 603979776 | bytes 3702788 | tf_op jit(solution)/shard_map/pallas_call | solution.py:287
  41.3 0.0 copy-done.3
  41.4 0.0 collective-permute-done.8.m3_ref
  41.4 0.0 copy-done.1
  41.4 3.0 %shard_map.75 = (bf16[128,128]{1,0:T(8,128)(2,1)}, bf16[128,4608]{1,0:T(8,128)(2,1)}) custom-call(s32[1]{0:T(128)} %bitcast.core_ref, bf16[256,128]{1,0:T(8,128)(2,1)S(1)} %get-tuple-element.33.v_ref, bf16[256,128]{1,0:T(8,128)(2,1)S(1)} %collective-permute-done.8.m3_ref, bf16[128,4608]{1,0:T(8,128)(2,1)S(1)} %get-tuple-element.25.edge_ref.e_ref, ...), custom_call_target="tpu_custom_call" | custom-call | flops 603979776 | bytes 6029316 | tf_op jit(solution)/shard_map/pallas_call | solution.py:287
  44.4 4.2 %all-to-all-start = ((bf16[8,16,4608]{2,1,0:T(8,128)(2,1)}), bf16[8,16,4608]{2,1,0:T(8,128)(2,1)S(1)}, u32[]{:S(2)}, u32[]{:S(2)}) async-start(bf16[8,16,4608]{2,1,0:T(8,128)(2,1)} %bitcast.12), calls=%async_computation | async-start | bytes 2359296 | tf_op jit(solution)/shard_map/all_to_all | solution.py:358
  48.6 7.0 %shard_map.76 = (bf16[128,4608]{1,0:T(8,128)(2,1)}, bf16[128,128]{1,0:T(8,128)(2,1)}) custom-call(s32[1]{0:T(128)} %bitcast.core_ref, bf16[256,128]{1,0:T(8,128)(2,1)} %copy-done.1, bf16[256,128]{1,0:T(8,128)(2,1)} %copy-done.2, bf16[256,128]{1,0:T(8,128)(2,1)} %copy-done.3, bf16[128,128]{1,0:T(8,128)(2,1)} %get-tuple-element.39.near_ref, ...), custom_call_target="tpu_custom_call" | custom-call | flops 2113929216 | bytes 2752516 | tf_op jit(solution)/shard_map/pallas_call | solution.py:287
  55.6 9.4 %all-to-all-done.parts_ref = bf16[8,16,4608]{2,1,0:T(8,128)(2,1)S(1)} async-done(((bf16[8,16,4608]{2,1,0:T(8,128)(2,1)}), bf16[8,16,4608]{2,1,0:T(8,128)(2,1)S(1)}, u32[]{:S(2)}, u32[]{:S(2)}) %all-to-all-start) | async-done | bytes 1179680 | tf_op jit(solution)/shard_map/all_to_all | solution.py:358
  65.0 0.9 %shard_map.77 = f32[576,128]{1,0:T(8,128)} custom-call(bf16[8,16,4608]{2,1,0:T(8,128)(2,1)S(1)} %all-to-all-done.parts_ref), custom_call_target="tpu_custom_call" | custom-call | flops 150994944 | bytes 1179648 | tf_op jit(solution)/shard_map/pallas_call | solution.py:287
  (1 shorter events, 0.0 us)
Async XLA Ops:
  0.6 5.3 %collective-permute-start = (bf16[128,128]{1,0:T(8,128)(2,1)}, bf16[128,128]{1,0:T(8,128)(2,1)}, u32[]{:S(2)}, u32[]{:S(2)}) collective-permute-start(bf16[128,128]{1,0:T(8,128)(2,1)} %bitcast.15), channel_id=1, source_target_pairs={{0,1},{1,0},{2,3},{3,2},{4,5},{5,4},{6,7},{7,6},{8,9},{9,8},{10,11... | collective-permute-start | bytes 98312 | tf_op jit(solution)/shard_map/ppermute | solution.py:313
  4.0 5.3 %collective-permute-start.2 = (bf16[128,4608]{1,0:T(8,128)(2,1)}, bf16[128,4608]{1,0:T(8,128)(2,1)S(1)}, u32[]{:S(2)}, u32[]{:S(2)}) collective-permute-start(bf16[128,4608]{1,0:T(8,128)(2,1)} %bitcast.10), channel_id=1, source_target_pairs={{0,1},{1,0},{2,3},{3,2},{4,5},{5,4},{6,7},{7,6},{8,9},{9,8},{10,11... | collective-permute-start | bytes 3538952 | tf_op jit(solution)/shard_map/ppermute | solution.py:313
  7.7 31.8 %copy-start.5 = (bf16[128,128]{1,0:T(8,128)(2,1)}, bf16[128,128]{1,0:T(8,128)(2,1)S(1)}, u32[]{:S(2)}) copy-start(bf16[128,128]{1,0:T(8,128)(2,1)S(1)} %get-tuple-element.38.last_ref) | copy-start | bytes 98308
  7.7 3.0 %collective-permute-start.3 = (bf16[128,4608]{1,0:T(8,128)(2,1)S(1)}, bf16[128,4608]{1,0:T(8,128)(2,1)S(1)}, u32[]{:S(2)}, u32[]{:S(2)}) collective-permute-start(bf16[128,4608]{1,0:T(8,128)(2,1)S(1)} %get-tuple-element.28.t_ref.turned_ref), channel_id=1, source_target_pairs={{0,1},{1,0},{2,3},{3,2},{4,5},{5,4},{6,7},{7,6},{8,9},{9,8},{10,11... | collective-permute-start | bytes 3538952 | tf_op jit(solution)/shard_map/ppermute | solution.py:313
  8.3 5.2 %collective-permute-start.1 = (bf16[256,128]{1,0:T(8,128)(2,1)S(1)}, bf16[256,128]{1,0:T(8,128)(2,1)S(1)}, u32[]{:S(2)}, u32[]{:S(2)}) collective-permute-start(bf16[256,128]{1,0:T(8,128)(2,1)S(1)} %get-tuple-element.27), channel_id=1, source_target_pairs={{0,31},{1,2},{2,1},{3,4},{4,3},{5,6},{6,5},{7,8},{8,7},{9,10},{10,... | collective-permute-start | bytes 196616 | tf_op jit(solution)/shard_map/ppermute | solution.py:313
  17.0 24.4 %copy-start.1 = (bf16[256,128]{1,0:T(8,128)(2,1)}, bf16[256,128]{1,0:T(8,128)(2,1)S(1)}, u32[]{:S(2)}) copy-start(bf16[256,128]{1,0:T(8,128)(2,1)S(1)} %get-tuple-element.33.v_ref) | copy-start | bytes 196612
  17.0 9.8 %collective-permute-start.4 = (bf16[256,128]{1,0:T(8,128)(2,1)S(1)}, bf16[256,128]{1,0:T(8,128)(2,1)S(1)}, u32[]{:S(2)}, u32[]{:S(2)}) collective-permute-start(bf16[256,128]{1,0:T(8,128)(2,1)S(1)} %get-tuple-element.34), channel_id=1, source_target_pairs={{0,2},{1,31},{2,4},{3,1},{4,6},{5,3},{6,8},{7,5},{8,10},{9,7},{10,... | collective-permute-start | bytes 196616 | tf_op jit(solution)/shard_map/ppermute | solution.py:313
  25.5 1.3 %collective-permute-start.5 = (bf16[256,128]{1,0:T(8,128)(2,1)S(1)}, bf16[256,128]{1,0:T(8,128)(2,1)S(1)}, u32[]{:S(2)}, u32[]{:S(2)}) collective-permute-start(bf16[256,128]{1,0:T(8,128)(2,1)S(1)} %get-tuple-element.35), channel_id=1, source_target_pairs={{0,1},{1,0},{2,3},{3,2},{4,5},{5,4},{6,7},{7,6},{8,9},{9,8},{10,11... | collective-permute-start | bytes 196616 | tf_op jit(solution)/shard_map/ppermute | solution.py:313
  26.8 9.3 %copy-start.2 = (bf16[256,128]{1,0:T(8,128)(2,1)}, bf16[256,128]{1,0:T(8,128)(2,1)S(1)}, u32[]{:S(2)}) copy-start(bf16[256,128]{1,0:T(8,128)(2,1)S(1)} %collective-permute-done.4.come_ref.r1_ref) | copy-start | bytes 196612
  26.9 12.6 %copy-start = (bf16[256,128]{1,0:T(8,128)(2,1)}, bf16[256,128]{1,0:T(8,128)(2,1)S(1)}, u32[]{:S(2)}) copy-start(bf16[256,128]{1,0:T(8,128)(2,1)S(1)} %collective-permute-done.5.m1_ref) | copy-start | bytes 196612
  30.4 5.8 %collective-permute-start.7 = (bf16[256,128]{1,0:T(8,128)(2,1)S(1)}, bf16[256,128]{1,0:T(8,128)(2,1)S(1)}, u32[]{:S(2)}, u32[]{:S(2)}) collective-permute-start(bf16[256,128]{1,0:T(8,128)(2,1)S(1)} %get-tuple-element.37), channel_id=1, source_target_pairs={{0,1},{1,0},{2,3},{3,2},{4,5},{5,4},{6,7},{7,6},{8,9},{9,8},{10,11... | collective-permute-start | bytes 196616 | tf_op jit(solution)/shard_map/ppermute | solution.py:313
  31.4 7.0 %collective-permute-start.6 = (bf16[256,128]{1,0:T(8,128)(2,1)S(1)}, bf16[256,128]{1,0:T(8,128)(2,1)S(1)}, u32[]{:S(2)}, u32[]{:S(2)}) collective-permute-start(bf16[256,128]{1,0:T(8,128)(2,1)S(1)} %get-tuple-element.36), channel_id=1, source_target_pairs={{0,2},{1,31},{2,4},{3,1},{4,6},{5,3},{6,8},{7,5},{8,10},{9,7},{10,... | collective-permute-start | bytes 196616 | tf_op jit(solution)/shard_map/ppermute | solution.py:313
  36.2 2.2 %copy-start.4 = (bf16[256,128]{1,0:T(8,128)(2,1)}, bf16[256,128]{1,0:T(8,128)(2,1)S(1)}, u32[]{:S(2)}) copy-start(bf16[256,128]{1,0:T(8,128)(2,1)S(1)} %collective-permute-done.7.m2_ref) | copy-start | bytes 196612
  38.4 2.9 %copy-start.3 = (bf16[256,128]{1,0:T(8,128)(2,1)}, bf16[256,128]{1,0:T(8,128)(2,1)S(1)}, u32[]{:S(2)}) copy-start(bf16[256,128]{1,0:T(8,128)(2,1)S(1)} %shard_map.73.r2_ref) | copy-start | bytes 196612
  38.4 2.9 %collective-permute-start.8 = (bf16[256,128]{1,0:T(8,128)(2,1)S(1)}, bf16[256,128]{1,0:T(8,128)(2,1)S(1)}, u32[]{:S(2)}, u32[]{:S(2)}) collective-permute-start(bf16[256,128]{1,0:T(8,128)(2,1)S(1)} %shard_map.73.r2_ref), channel_id=1, source_target_pairs={{0,1},{1,0},{2,3},{3,2},{4,5},{5,4},{6,7},{7,6},{8,9},{9,8},{10,11... | collective-permute-start | bytes 196616 | tf_op jit(solution)/shard_map/ppermute | solution.py:313
  44.4 20.6 %all-to-all-start = ((bf16[8,16,4608]{2,1,0:T(8,128)(2,1)}), bf16[8,16,4608]{2,1,0:T(8,128)(2,1)S(1)}, u32[]{:S(2)}, u32[]{:S(2)}) async-start(bf16[8,16,4608]{2,1,0:T(8,128)(2,1)} %bitcast.12), calls=%async_computation | async-start | bytes 2359296 | tf_op jit(solution)/shard_map/all_to_all | solution.py:358

commit v9 on v8

--- a/solution.py
+++ b/solution.py
@@ -260,16 +260,23 @@
     grad_ref[...] = step(z_ref[:W, :], turned_ref, edge_ref).astype(F32).T.astype(BF)
 
 
-def gather_kernel(parts_ref, out_ref):
+def gather_kernel(parts_ref, out_ref, in_ref, sem):
     rows = parts_ref.shape[1]
     planes = parts_ref.shape[2] // W
+    pieces = sem.shape[0]
+    each = planes // pieces
+    copies = []
+    for n in range(pieces):
+        at = pl.ds(n * each * W, each * W)
+        copies.append(pltpu.make_async_copy(parts_ref.at[:, :, at], in_ref.at[:, :, at], sem.at[n]))
+        copies[-1].start()
     for p in range(planes):
-        out_ref[pl.ds(p, rows, stride=planes), :] = jnp.sum(
-            parts_ref[:, :, W * p : W * (p + 1)].astype(F32), axis=0
-        )
-
-
-def call(kernel, shapes, *args, scratch=(), sems=(), flops=0, far=(), free=(), far_outs=(), alias=None):
+        if p % each == 0:
+            copies[p // each].wait()
+        out_ref[pl.ds(p, rows, stride=planes), :] = jnp.sum(in_ref[:, :, W * p : W * (p + 1)].astype(F32), axis=0)
+
+
+def call(kernel, shapes, *args, scratch=(), sems=(), flops=0, far=(), free=(), far_outs=(), alias=None, room=16):
     def spec(n, arg):
         if n in far or n in free:
             return pl.BlockSpec(memory_space=pl.ANY)
@@ -292,7 +299,7 @@
         scratch_shapes=[pltpu.VMEM(shape, kind) for shape, kind in scratch]
         + [pltpu.SemaphoreType.DMA((count,)) for count in sems],
         input_output_aliases=alias or {},
-        compiler_params=pltpu.CompilerParams(vmem_limit_bytes=16 * 1024 * 1024),
+        compiler_params=pltpu.CompilerParams(vmem_limit_bytes=room * 1024 * 1024),
         cost_estimate=pl.CostEstimate(flops=flops, bytes_accessed=moved, transcendentals=0),
     )(*args)
 
@@ -358,9 +365,12 @@
     parts = lax.all_to_all(done.reshape(rows, share, width), "row", 0, 0, tiled=True)
     edge_grad, corner_grad = call(
         edge_kernel, [whole, one], core, v, r1, r2, near3, m2, m1, u0, edge, turned,
-        scratch=stacks(6), sems=(12,), flops=14 * unit, far=range(1, 8),
-    )
-    proj = call(gather_kernel, [((share * width // W, W), F32)], parts, flops=unit)
+        scratch=stacks(6), sems=(12,), flops=14 * unit, room=63, far=range(1, 8),
+    )
+    proj = call(
+        gather_kernel, [((share * width // W, W), F32)], parts,
+        scratch=[((rows, share, width), BF)], sems=(6,), flops=unit, far=(0,),
+    )
     return (corner_grad[None, None], edge_grad[None, None], proj[None])
 
 

time: 66.2 us -> 67.2 us (1.015)
  Pallas kernels: 26.1 us -> 28.6 us
  waiting for transfers between devices: 14.4 us -> 12.9 us
    pallas_call x11, Pallas kernels: 26.1 us -> 28.6 us  [call(): pl.pallas_call(kernel, out_shape=outs[0] if single else outs, in_specs=in...]
    all_to_all x1, waiting for transfers between devices: 9.38 us -> 7.89 us  [shards(): lax.all_to_all(done.reshape(rows, share, width), 'row', 0, 0, tiled=True)]
  transfers between devices with their start and end apart: 10 -> 10, of which waited for: 4 -> 4; matrix products, arithmetic and copies ran while one was open for 0% -> 0% of each run, Pallas kernels for 23% -> 24%
where the time goes in v9:
time: 67.2 us; the launch traced here: 66.9 us
  Pallas kernels  28.6 us (43%)
  starting transfers between devices  24.3 us (36%)
  waiting for transfers between devices  12.9 us (19%)
  between operations  1.01 us (2%)
    pallas_call x11, Pallas kernels, call(): pl.pallas_call(kernel, out_shape=outs[0] if single else outs, in_specs=in...  28.6 us
    ppermute x9, starting transfers between devices, send(): return lax.ppermute(value, 'col', pairs)  20.1 us
    all_to_all x1, waiting for transfers between devices, shards(): lax.all_to_all(done.reshape(rows, share, width), 'row', 0, 0, tiled=True)  7.89 us
    ppermute x9, waiting for transfers between devices, send(): return lax.ppermute(value, 'col', pairs)  5.01 us
    all_to_all x1, starting transfers between devices, shards(): lax.all_to_all(done.reshape(rows, share, width), 'row', 0, 0, tiled=True)  4.27 us
  transfers between devices with their start and end apart: 10, of which 4 were waited for; matrix products, arithmetic and copies ran while one was open for 0% of the time, Pallas kernels for 24%

profile of v9, /device:TPU:1, one launch (start us, length us, event | category | flops | bytes accessed | tf_op | source)
XLA Modules:
  0.0 66.9 jit_solution(10793730938527908208)
XLA Ops:
  0.6 3.3 %collective-permute-start = (bf16[128,128]{1,0:T(8,128)(2,1)}, bf16[128,128]{1,0:T(8,128)(2,1)S(1)}, u32[]{:S(2)}, u32[]{:S(2)}) collective-permute-start(bf16[128,128]{1,0:T(8,128)(2,1)} %bitcast.15), channel_id=1, source_target_pairs={{0,1},{1,0},{2,3},{3,2},{4,5},{5,4},{6,7},{7,6},{8,9},{9,8},{10,11... | collective-permute-start | bytes 98312 | tf_op jit(solution)/shard_map/ppermute | solution.py:320
  4.0 0.1 collective-permute-start.2
  4.1 1.8 %shard_map.67 = (bf16[128,4608]{1,0:T(8,128)(2,1)S(1)}, bf16[128,4608]{1,0:T(8,128)(2,1)S(1)}, bf16[128,128]{1,0:T(8,128)(2,1)S(1)}, bf16[128,128]{1,0:T(8,128)(2,1)S(1)}) custom-call(bf16[4608,128]{1,0:T(8,128)(2,1)} %bitcast.9, bf16[128,4608]{1,0:T(8,128)(2,1)} %bitcast.11, bf16[128,128]{1,0:T(8,128)(2,1)} %bitcast.14, bf16[128,128]{1,0:T(8,128)(2,1)} %bitcast.16), custom_call_target="tpu_custom_call" | custom-call | flops 150994944 | bytes 2424832 | tf_op jit(solution)/shard_map/pallas_call | solution.py:294
  5.9 0.0 copy-start
  5.9 0.0 collective-permute-done.mate_cot_ref
  5.9 1.1 %shard_map.68 = (bf16[128,128]{1,0:T(8,128)(2,1)S(1)}, bf16[256,128]{1,0:T(8,128)(2,1)S(1)}, bf16[128,4608]{1,0:T(8,128)(2,1)S(1)}) custom-call(s32[1]{0:T(128)} %bitcast.core_ref, bf16[128,128]{1,0:T(8,128)(2,1)S(1)} %get-tuple-element.23.corner_ref, bf16[128,128]{1,0:T(8,128)(2,1)S(1)} %get-tuple-element.24.cot_t_ref, ...), custom_call_target="tpu_custom_call", output_to_operand_aliasing={{2}: (5, {})} | custom-call | flops 301989888 | bytes 2457604 | tf_op jit(solution)/shard_map/pallas_call | solution.py:294
  7.0 0.0 copy-start.1
  7.0 0.0 copy-start.7
  7.0 0.6 collective-permute-start.3
  7.5 1.0 %collective-permute-start.1 = (bf16[256,128]{1,0:T(8,128)(2,1)S(1)}, bf16[256,128]{1,0:T(8,128)(2,1)S(1)}, u32[]{:S(2)}, u32[]{:S(2)}) collective-permute-start(bf16[256,128]{1,0:T(8,128)(2,1)S(1)} %get-tuple-element.27), channel_id=1, source_target_pairs={{0,31},{1,2},{2,1},{3,4},{4,3},{5,6},{6,5},{7,8},{8,7},{9,10},{10,... | collective-permute-start | bytes 196616 | tf_op jit(solution)/shard_map/ppermute | solution.py:320
  8.5 0.0 collective-permute-done.2.far_edge_ref
  8.5 1.5 %collective-permute-done.3.far_turned_ref = bf16[128,4608]{1,0:T(8,128)(2,1)S(1)} collective-permute-done((bf16[128,4608]{1,0:T(8,128)(2,1)S(1)}, bf16[128,4608]{1,0:T(8,128)(2,1)S(1)}, u32[]{:S(2)}, u32[]{:S(2)}) %collective-permute-start.3) | collective-permute-done | bytes 1179680 | tf_op jit(solution)/shard_map/ppermute | solution.py:320
  10.0 0.5 shard_map.69
  10.6 2.2 %collective-permute-done.1.come_ref = bf16[256,128]{1,0:T(8,128)(2,1)S(1)} collective-permute-done((bf16[256,128]{1,0:T(8,128)(2,1)S(1)}, bf16[256,128]{1,0:T(8,128)(2,1)S(1)}, u32[]{:S(2)}, u32[]{:S(2)}) %collective-permute-start.1) | collective-permute-done | bytes 65568 | tf_op jit(solution)/shard_map/ppermute | solution.py:320
  12.7 3.6 %shard_map.70 = (bf16[256,128]{1,0:T(8,128)(2,1)S(1)}, bf16[256,128]{1,0:T(8,128)(2,1)S(1)}, bf16[256,128]{1,0:T(8,128)(2,1)S(1)}) custom-call(s32[1]{0:T(128)} %bitcast.core_ref, bf16[256,128]{1,0:T(8,128)(2,1)S(1)} %collective-permute-done.1.come_ref, bf16[128,128]{1,0:T(8,128)(2,1)S(1)} %get-tuple-element.23.corner_ref, ...), custom_call_target="tpu_custom_call" | custom-call | flops 603979776 | bytes 4882436 | tf_op jit(solution)/shard_map/pallas_call | solution.py:294
  16.3 0.0 copy-start.3
  16.4 8.5 %collective-permute-start.4 = (bf16[256,128]{1,0:T(8,128)(2,1)S(1)}, bf16[256,128]{1,0:T(8,128)(2,1)S(1)}, u32[]{:S(2)}, u32[]{:S(2)}) collective-permute-start(bf16[256,128]{1,0:T(8,128)(2,1)S(1)} %get-tuple-element.34), channel_id=1, source_target_pairs={{0,2},{1,31},{2,4},{3,1},{4,6},{5,3},{6,8},{7,5},{8,10},{9,7},{10,... | collective-permute-start | bytes 196616 | tf_op jit(solution)/shard_map/ppermute | solution.py:320
  24.8 0.0 collective-permute-start.5
  24.8 1.3 %collective-permute-done.4.come_ref.r1_ref = bf16[256,128]{1,0:T(8,128)(2,1)S(1)} collective-permute-done((bf16[256,128]{1,0:T(8,128)(2,1)S(1)}, bf16[256,128]{1,0:T(8,128)(2,1)S(1)}, u32[]{:S(2)}, u32[]{:S(2)}) %collective-permute-start.4) | collective-permute-done | bytes 65568 | tf_op jit(solution)/shard_map/ppermute | solution.py:320
  26.2 0.0 copy-start.4
  26.2 0.0 collective-permute-done.5.m1_ref
  26.2 0.0 copy-done.1
  26.2 0.0 copy-start.2
  26.2 3.8 %shard_map.71 = (bf16[256,128]{1,0:T(8,128)(2,1)S(1)}, bf16[256,128]{1,0:T(8,128)(2,1)S(1)}) custom-call(s32[1]{0:T(128)} %bitcast.core_ref, bf16[256,128]{1,0:T(8,128)(2,1)S(1)} %collective-permute-done.4.come_ref.r1_ref, bf16[128,4608]{1,0:T(8,128)(2,1)S(1)} %get-tuple-element.25.edge_ref.e_ref, bf16[128,4608]{1,0:T(8,128)(2,1)S(1)} %get-tuple-element.28.t_ref.turned_ref, ...), custom_call_target="tpu_custom_call" | custom-call | flops 1207959552 | bytes 4849668 | tf_op jit(solution)/shard_map/pallas_call | solution.py:294
  30.0 0.8 %collective-permute-start.7 = (bf16[256,128]{1,0:T(8,128)(2,1)S(1)}, bf16[256,128]{1,0:T(8,128)(2,1)S(1)}, u32[]{:S(2)}, u32[]{:S(2)}) collective-permute-start(bf16[256,128]{1,0:T(8,128)(2,1)S(1)} %get-tuple-element.37), channel_id=1, source_target_pairs={{0,1},{1,0},{2,3},{3,2},{4,5},{5,4},{6,7},{7,6},{8,9},{9,8},{10,11... | collective-permute-start | bytes 196616 | tf_op jit(solution)/shard_map/ppermute | solution.py:320
  30.8 4.7 %collective-permute-start.6 = (bf16[256,128]{1,0:T(8,128)(2,1)S(1)}, bf16[256,128]{1,0:T(8,128)(2,1)S(1)}, u32[]{:S(2)}, u32[]{:S(2)}) collective-permute-start(bf16[256,128]{1,0:T(8,128)(2,1)S(1)} %get-tuple-element.36), channel_id=1, source_target_pairs={{0,2},{1,31},{2,4},{3,1},{4,6},{5,3},{6,8},{7,5},{8,10},{9,7},{10,... | collective-permute-start | bytes 196616 | tf_op jit(solution)/shard_map/ppermute | solution.py:320
  35.5 0.0 collective-permute-done.7.m2_ref
  35.5 0.0 copy-start.6
  35.5 0.0 copy-done.4
  35.5 2.2 %shard_map.72.after_ref.early_ref = f32[128,4608]{1,0:T(8,128)S(1)} custom-call(s32[1]{0:T(128)} %bitcast.core_ref, bf16[256,128]{1,0:T(8,128)(2,1)S(1)} %get-tuple-element.33.v_ref, bf16[256,128]{1,0:T(8,128)(2,1)S(1)} %collective-permute-done.4.come_ref.r1_ref, bf16[256,128]{1,0:T(8,128)(2,1)S(1)} %collective-permute-done.5.m1_ref, ...), custom_call_target="tpu_custom_call" | custom-call | flops 905969664 | bytes 1441796 | tf_op jit(solution)/shard_map/pallas_call | solution.py:294
  37.8 0.0 copy-done.6
  37.8 0.0 collective-permute-done.6.value_ref
  37.8 0.0 copy-start.5
  37.8 1.0 %collective-permute-start.8 = (bf16[256,128]{1,0:T(8,128)(2,1)S(1)}, bf16[256,128]{1,0:T(8,128)(2,1)S(1)}, u32[]{:S(2)}, u32[]{:S(2)}) collective-permute-start(bf16[256,128]{1,0:T(8,128)(2,1)S(1)} %shard_map.73.r2_ref), channel_id=1, source_target_pairs={{0,1},{1,0},{2,3},{3,2},{4,5},{5,4},{6,7},{7,6},{8,9},{9,8},{10,11... | collective-permute-start | bytes 196616 | tf_op jit(solution)/shard_map/ppermute | solution.py:320
  38.9 0.0 copy-done.7
  38.9 0.0 copy-done.2
  38.9 1.9 %shard_map.74.sum_ref = f32[128,4608]{1,0:T(8,128)S(1)} custom-call(s32[1]{0:T(128)} %bitcast.core_ref, bf16[256,128]{1,0:T(8,128)(2,1)S(1)} %shard_map.73.r2_ref, bf16[256,128]{1,0:T(8,128)(2,1)S(1)} %collective-permute-done.5.m1_ref, bf16[128,128]{1,0:T(8,128)(2,1)S(1)} %get-tuple-element.38.last_ref, ...), custom_call_target="tpu_custom_call", output_to_operand_aliasing={{}: (5, {})} | custom-call | flops 603979776 | bytes 3702788 | tf_op jit(solution)/shard_map/pallas_call | solution.py:294
  40.7 0.0 copy-done.5
  40.7 0.0 collective-permute-done.8.m3_ref
  40.7 0.0 copy-done
  40.8 0.0 copy-done.3
  40.8 3.0 %shard_map.75 = (bf16[128,128]{1,0:T(8,128)(2,1)}, bf16[128,4608]{1,0:T(8,128)(2,1)}) custom-call(s32[1]{0:T(128)} %bitcast.core_ref, bf16[256,128]{1,0:T(8,128)(2,1)S(1)} %get-tuple-element.33.v_ref, bf16[256,128]{1,0:T(8,128)(2,1)S(1)} %collective-permute-done.8.m3_ref, bf16[128,4608]{1,0:T(8,128)(2,1)S(1)} %get-tuple-element.25.edge_ref.e_ref, ...), custom_call_target="tpu_custom_call" | custom-call | flops 603979776 | bytes 6029316 | tf_op jit(solution)/shard_map/pallas_call | solution.py:294
  43.8 4.3 %all-to-all-start = ((bf16[8,16,4608]{2,1,0:T(8,128)(2,1)}), bf16[8,16,4608]{2,1,0:T(8,128)(2,1)}, u32[]{:S(2)}, u32[]{:S(2)}) async-start(bf16[8,16,4608]{2,1,0:T(8,128)(2,1)} %bitcast.12), calls=%async_computation | async-start | bytes 2359296 | tf_op jit(solution)/shard_map/all_to_all | solution.py:365
  48.1 8.6 %shard_map.76 = (bf16[128,4608]{1,0:T(8,128)(2,1)}, bf16[128,128]{1,0:T(8,128)(2,1)}) custom-call(s32[1]{0:T(128)} %bitcast.core_ref, bf16[256,128]{1,0:T(8,128)(2,1)} %copy-done.3, bf16[256,128]{1,0:T(8,128)(2,1)} %copy-done.4, bf16[256,128]{1,0:T(8,128)(2,1)} %copy-done.5, bf16[128,128]{1,0:T(8,128)(2,1)} %get-tuple-element.39.near_ref, ...), custom_call_target="tpu_custom_call" | custom-call | flops 2113929216 | bytes 2752516 | tf_op jit(solution)/shard_map/pallas_call | solution.py:294
  56.7 7.9 %all-to-all-done.parts_ref = bf16[8,16,4608]{2,1,0:T(8,128)(2,1)} async-done(((bf16[8,16,4608]{2,1,0:T(8,128)(2,1)}), bf16[8,16,4608]{2,1,0:T(8,128)(2,1)}, u32[]{:S(2)}, u32[]{:S(2)}) %all-to-all-start) | async-done | bytes 1179680 | tf_op jit(solution)/shard_map/all_to_all | solution.py:365
  64.6 2.1 %shard_map.77 = f32[576,128]{1,0:T(8,128)} custom-call(bf16[8,16,4608]{2,1,0:T(8,128)(2,1)} %all-to-all-done.parts_ref), custom_call_target="tpu_custom_call" | custom-call | flops 150994944 | bytes 1179648 | tf_op jit(solution)/shard_map/pallas_call | solution.py:294
  (1 shorter events, 0.0 us)
Async XLA Ops:
  0.6 5.3 %collective-permute-start = (bf16[128,128]{1,0:T(8,128)(2,1)}, bf16[128,128]{1,0:T(8,128)(2,1)S(1)}, u32[]{:S(2)}, u32[]{:S(2)}) collective-permute-start(bf16[128,128]{1,0:T(8,128)(2,1)} %bitcast.15), channel_id=1, source_target_pairs={{0,1},{1,0},{2,3},{3,2},{4,5},{5,4},{6,7},{7,6},{8,9},{9,8},{10,11... | collective-permute-start | bytes 98312 | tf_op jit(solution)/shard_map/ppermute | solution.py:320
  4.0 4.6 %collective-permute-start.2 = (bf16[128,4608]{1,0:T(8,128)(2,1)}, bf16[128,4608]{1,0:T(8,128)(2,1)S(1)}, u32[]{:S(2)}, u32[]{:S(2)}) collective-permute-start(bf16[128,4608]{1,0:T(8,128)(2,1)} %bitcast.10), channel_id=1, source_target_pairs={{0,1},{1,0},{2,3},{3,2},{4,5},{5,4},{6,7},{7,6},{8,9},{9,8},{10,11... | collective-permute-start | bytes 3538952 | tf_op jit(solution)/shard_map/ppermute | solution.py:320
  5.9 34.9 %copy-start = (bf16[128,4608]{1,0:T(8,128)(2,1)}, bf16[128,4608]{1,0:T(8,128)(2,1)S(1)}, u32[]{:S(2)}) copy-start(bf16[128,4608]{1,0:T(8,128)(2,1)S(1)} %get-tuple-element.25.edge_ref.e_ref) | copy-start | bytes 3538948
  7.0 19.2 %copy-start.1 = (bf16[128,4608]{1,0:T(8,128)(2,1)}, bf16[128,4608]{1,0:T(8,128)(2,1)S(1)}, u32[]{:S(2)}) copy-start(bf16[128,4608]{1,0:T(8,128)(2,1)S(1)} %get-tuple-element.28.t_ref.turned_ref) | copy-start | bytes 3538948
  7.0 31.9 %copy-start.7 = (bf16[128,128]{1,0:T(8,128)(2,1)}, bf16[128,128]{1,0:T(8,128)(2,1)S(1)}, u32[]{:S(2)}) copy-start(bf16[128,128]{1,0:T(8,128)(2,1)S(1)} %get-tuple-element.38.last_ref) | copy-start | bytes 98308
  7.0 3.0 %collective-permute-start.3 = (bf16[128,4608]{1,0:T(8,128)(2,1)S(1)}, bf16[128,4608]{1,0:T(8,128)(2,1)S(1)}, u32[]{:S(2)}, u32[]{:S(2)}) collective-permute-start(bf16[128,4608]{1,0:T(8,128)(2,1)S(1)} %get-tuple-element.28.t_ref.turned_ref), channel_id=1, source_target_pairs={{0,1},{1,0},{2,3},{3,2},{4,5},{5,4},{6,7},{7,6},{8,9},{9,8},{10,11... | collective-permute-start | bytes 3538952 | tf_op jit(solution)/shard_map/ppermute | solution.py:320
  7.5 5.2 %collective-permute-start.1 = (bf16[256,128]{1,0:T(8,128)(2,1)S(1)}, bf16[256,128]{1,0:T(8,128)(2,1)S(1)}, u32[]{:S(2)}, u32[]{:S(2)}) collective-permute-start(bf16[256,128]{1,0:T(8,128)(2,1)S(1)} %get-tuple-element.27), channel_id=1, source_target_pairs={{0,31},{1,2},{2,1},{3,4},{4,3},{5,6},{6,5},{7,8},{8,7},{9,10},{10,... | collective-permute-start | bytes 196616 | tf_op jit(solution)/shard_map/ppermute | solution.py:320
  16.3 24.4 %copy-start.3 = (bf16[256,128]{1,0:T(8,128)(2,1)}, bf16[256,128]{1,0:T(8,128)(2,1)S(1)}, u32[]{:S(2)}) copy-start(bf16[256,128]{1,0:T(8,128)(2,1)S(1)} %get-tuple-element.33.v_ref) | copy-start | bytes 196612
  16.4 9.8 %collective-permute-start.4 = (bf16[256,128]{1,0:T(8,128)(2,1)S(1)}, bf16[256,128]{1,0:T(8,128)(2,1)S(1)}, u32[]{:S(2)}, u32[]{:S(2)}) collective-permute-start(bf16[256,128]{1,0:T(8,128)(2,1)S(1)} %get-tuple-element.34), channel_id=1, source_target_pairs={{0,2},{1,31},{2,4},{3,1},{4,6},{5,3},{6,8},{7,5},{8,10},{9,7},{10,... | collective-permute-start | bytes 196616 | tf_op jit(solution)/shard_map/ppermute | solution.py:320
  24.8 1.3 %collective-permute-start.5 = (bf16[256,128]{1,0:T(8,128)(2,1)S(1)}, bf16[256,128]{1,0:T(8,128)(2,1)S(1)}, u32[]{:S(2)}, u32[]{:S(2)}) collective-permute-start(bf16[256,128]{1,0:T(8,128)(2,1)S(1)} %get-tuple-element.35), channel_id=1, source_target_pairs={{0,1},{1,0},{2,3},{3,2},{4,5},{5,4},{6,7},{7,6},{8,9},{9,8},{10,11... | collective-permute-start | bytes 196616 | tf_op jit(solution)/shard_map/ppermute | solution.py:320
  26.2 9.4 %copy-start.4 = (bf16[256,128]{1,0:T(8,128)(2,1)}, bf16[256,128]{1,0:T(8,128)(2,1)S(1)}, u32[]{:S(2)}) copy-start(bf16[256,128]{1,0:T(8,128)(2,1)S(1)} %collective-permute-done.4.come_ref.r1_ref) | copy-start | bytes 196612
  26.2 12.7 %copy-start.2 = (bf16[256,128]{1,0:T(8,128)(2,1)}, bf16[256,128]{1,0:T(8,128)(2,1)S(1)}, u32[]{:S(2)}) copy-start(bf16[256,128]{1,0:T(8,128)(2,1)S(1)} %collective-permute-done.5.m1_ref) | copy-start | bytes 196612
  30.0 5.6 %collective-permute-start.7 = (bf16[256,128]{1,0:T(8,128)(2,1)S(1)}, bf16[256,128]{1,0:T(8,128)(2,1)S(1)}, u32[]{:S(2)}, u32[]{:S(2)}) collective-permute-start(bf16[256,128]{1,0:T(8,128)(2,1)S(1)} %get-tuple-element.37), channel_id=1, source_target_pairs={{0,1},{1,0},{2,3},{3,2},{4,5},{5,4},{6,7},{7,6},{8,9},{9,8},{10,11... | collective-permute-start | bytes 196616 | tf_op jit(solution)/shard_map/ppermute | solution.py:320
  30.8 7.0 %collective-permute-start.6 = (bf16[256,128]{1,0:T(8,128)(2,1)S(1)}, bf16[256,128]{1,0:T(8,128)(2,1)S(1)}, u32[]{:S(2)}, u32[]{:S(2)}) collective-permute-start(bf16[256,128]{1,0:T(8,128)(2,1)S(1)} %get-tuple-element.36), channel_id=1, source_target_pairs={{0,2},{1,31},{2,4},{3,1},{4,6},{5,3},{6,8},{7,5},{8,10},{9,7},{10,... | collective-permute-start | bytes 196616 | tf_op jit(solution)/shard_map/ppermute | solution.py:320
  35.5 2.2 %copy-start.6 = (bf16[256,128]{1,0:T(8,128)(2,1)}, bf16[256,128]{1,0:T(8,128)(2,1)S(1)}, u32[]{:S(2)}) copy-start(bf16[256,128]{1,0:T(8,128)(2,1)S(1)} %collective-permute-done.7.m2_ref) | copy-start | bytes 196612
  37.8 2.9 %copy-start.5 = (bf16[256,128]{1,0:T(8,128)(2,1)}, bf16[256,128]{1,0:T(8,128)(2,1)S(1)}, u32[]{:S(2)}) copy-start(bf16[256,128]{1,0:T(8,128)(2,1)S(1)} %shard_map.73.r2_ref) | copy-start | bytes 196612
  37.8 2.9 %collective-permute-start.8 = (bf16[256,128]{1,0:T(8,128)(2,1)S(1)}, bf16[256,128]{1,0:T(8,128)(2,1)S(1)}, u32[]{:S(2)}, u32[]{:S(2)}) collective-permute-start(bf16[256,128]{1,0:T(8,128)(2,1)S(1)} %shard_map.73.r2_ref), channel_id=1, source_target_pairs={{0,1},{1,0},{2,3},{3,2},{4,5},{5,4},{6,7},{7,6},{8,9},{9,8},{10,11... | collective-permute-start | bytes 196616 | tf_op jit(solution)/shard_map/ppermute | solution.py:320
  43.8 20.8 %all-to-all-start = ((bf16[8,16,4608]{2,1,0:T(8,128)(2,1)}), bf16[8,16,4608]{2,1,0:T(8,128)(2,1)}, u32[]{:S(2)}, u32[]{:S(2)}) async-start(bf16[8,16,4608]{2,1,0:T(8,128)(2,1)} %bitcast.12), calls=%async_computation | async-start | bytes 2359296 | tf_op jit(solution)/shard_map/all_to_all | solution.py:365

commit v10 on v8

--- a/solution.py
+++ b/solution.py
@@ -198,15 +198,17 @@
 
 
 def proj_last_kernel(
-    core_ref, v_ref, m3_ref, e_ref, me_ref, mt_ref, sum_ref, near_out_ref, out_ref,
-    near_ref, z_ref, w_ref, stage_ref, sem, near_sem,
-):
+    core_ref, v_ref, m3_ref, e_ref, me_ref, mt_ref, sum_ref, near_out_ref, *rest
+):
+    *out_refs, near_ref, z_ref, w_ref, stage_ref, sem, near_sem = rest
+
     def body(x1, y1, x2, y2):
         near_ref[...] = step(m3_ref[:W, :], y2, x2)
 
     by_role(core_ref, body, (None, None, me_ref, mt_ref))
     copies = [pltpu.make_async_copy(near_ref, near_out_ref, near_sem.at[0])]
     copies[0].start()
+    share = out_refs[0].shape[0]
     place(core_ref, z_ref, w_ref, [v_ref[:W, :]], [near_ref[...]])
     pieces = sem.shape[0]
     each = e_ref.shape[1] // W // pieces
@@ -216,8 +218,12 @@
         stage_ref[:, at] = (sum_ref[:, at] + value).astype(BF)
         if (p + 1) % each == 0:
             at = pl.ds(W * (p + 1 - each), W * each)
-            copies.append(pltpu.make_async_copy(stage_ref.at[:, at], out_ref.at[:, at], sem.at[p // each]))
-            copies[-1].start()
+            for k, ref in enumerate(out_refs):
+                mine = pl.multiple_of(share * (core_ref[1] ^ k), share)
+                copies.append(
+                    pltpu.make_async_copy(stage_ref.at[pl.ds(mine, share), at], ref.at[:, at], sem.at[p // each, k])
+                )
+                copies[-1].start()
 
     pairs_of(z_ref, e_ref, w_ref, put)
     for copy in copies:
@@ -260,13 +266,13 @@
     grad_ref[...] = step(z_ref[:W, :], turned_ref, edge_ref).astype(F32).T.astype(BF)
 
 
-def gather_kernel(parts_ref, out_ref):
-    rows = parts_ref.shape[1]
-    planes = parts_ref.shape[2] // W
+def gather_kernel(*refs):
+    *parts, out_ref = refs
+    rows = parts[0].shape[0]
+    planes = parts[0].shape[1] // W
     for p in range(planes):
-        out_ref[pl.ds(p, rows, stride=planes), :] = jnp.sum(
-            parts_ref[:, :, W * p : W * (p + 1)].astype(F32), axis=0
-        )
+        total = sum(part[:, W * p : W * (p + 1)].astype(F32) for part in parts)
+        out_ref[pl.ds(p, rows, stride=planes), :] = total
 
 
 def call(kernel, shapes, *args, scratch=(), sems=(), flops=0, far=(), free=(), far_outs=(), alias=None):
@@ -290,7 +296,7 @@
         in_specs=in_specs,
         out_specs=out_specs[0] if single else out_specs,
         scratch_shapes=[pltpu.VMEM(shape, kind) for shape, kind in scratch]
-        + [pltpu.SemaphoreType.DMA((count,)) for count in sems],
+        + [pltpu.SemaphoreType.DMA(count if isinstance(count, tuple) else (count,)) for count in sems],
         input_output_aliases=alias or {},
         compiler_params=pltpu.CompilerParams(vmem_limit_bytes=16 * 1024 * 1024),
         cost_estimate=pl.CostEstimate(flops=flops, bytes_accessed=moved, transcendentals=0),
@@ -305,7 +311,8 @@
     width = edge.shape[1]
     rows = lax.axis_size("row")
     cols = lax.axis_size("col")
-    core = (lax.axis_index("col") % 2).astype(jnp.int32).reshape(1)
+    core = jnp.stack([lax.axis_index("col") % 2, lax.axis_index("row")]).astype(jnp.int32)
+    share = W // rows
     unit = 2 * W * W * width
 
     def send(value, to):
@@ -350,17 +357,18 @@
     r2 = call(pass_kernel, [two], r2, early, free=(1,))
     m3 = swap(r2)
     late = call(proj_late_kernel, [wide], core, r2, m1, u0, edge, early, scratch=stacks(2), flops=4 * unit, alias={5: 0})
-    near3, done = call(
-        proj_last_kernel, [one, whole], core, v, m3, edge, mate_edge, mate_turned, late,
-        scratch=[one] + stacks(1) + [whole], sems=(18, 1), flops=4 * unit, far_outs=(0, 1),
-    )
-    share = W // rows
-    parts = lax.all_to_all(done.reshape(rows, share, width), "row", 0, 0, tiled=True)
+    near3, *done = call(
+        proj_last_kernel, [one] + [((share, width), BF)] * rows, core, v, m3, edge, mate_edge, mate_turned, late,
+        scratch=[one] + stacks(1) + [whole], sems=((6, rows), 1), flops=4 * unit, far_outs=range(rows + 1),
+    )
+    parts = done[:1] + [
+        lax.ppermute(done[k], "row", [(i, i ^ k) for i in range(rows)]) for k in range(1, rows)
+    ]
     edge_grad, corner_grad = call(
         edge_kernel, [whole, one], core, v, r1, r2, near3, m2, m1, u0, edge, turned,
         scratch=stacks(6), sems=(12,), flops=14 * unit, far=range(1, 8),
     )
-    proj = call(gather_kernel, [((share * width // W, W), F32)], parts, flops=unit)
+    proj = call(gather_kernel, [((share * width // W, W), F32)], *parts, flops=unit)
     return (corner_grad[None, None], edge_grad[None, None], proj[None])
 
 

time: 66.2 us -> 72.7 us (1.098)
  the two profiles are of different devices: /device:TPU:1 before, /device:TPU:26 now
where the time goes in v10:
time: 72.7 us; the launch traced here: 72.5 us
  starting transfers between devices  32 us (44%)
  Pallas kernels  30.9 us (43%)
  waiting for transfers between devices  8.63 us (12%)
  between operations  0.88 us (1%)
    pallas_call x11, Pallas kernels, call(): pl.pallas_call(kernel, out_shape=outs[0] if single else outs, in_specs=in...  30.9 us
    ppermute x7, starting transfers between devices, shards(): lax.ppermute(done[k], 'row', [(i, i ^ k) for i in range(rows)])  17.7 us
    ppermute x9, starting transfers between devices, send(): return lax.ppermute(value, 'col', pairs)  14.4 us
    ppermute x9, waiting for transfers between devices, send(): return lax.ppermute(value, 'col', pairs)  7.16 us
    ppermute x7, waiting for transfers between devices, shards(): lax.ppermute(done[k], 'row', [(i, i ^ k) for i in range(rows)])  1.47 us
  transfers between devices with their start and end apart: 16, of which 5 were waited for; matrix products, arithmetic and copies ran while one was open for 0% of the time, Pallas kernels for 27%

profile of v10, /device:TPU:26, one launch (start us, length us, event | category | flops | bytes accessed | tf_op | source)
XLA Modules:
  0.0 72.5 jit_solution(14306219564027651054)
XLA Ops:
  0.6 0.1 collective-permute-start
  0.7 0.5 collective-permute-start.2
  1.2 0.1 pad_add_fusion.core_ref
  1.3 1.8 %shard_map.67 = (bf16[128,4608]{1,0:T(8,128)(2,1)S(1)}, bf16[128,4608]{1,0:T(8,128)(2,1)S(1)}, bf16[128,128]{1,0:T(8,128)(2,1)S(1)}, bf16[128,128]{1,0:T(8,128)(2,1)S(1)}) custom-call(bf16[4608,128]{1,0:T(8,128)(2,1)} %bitcast.9, bf16[128,4608]{1,0:T(8,128)(2,1)} %bitcast.11, bf16[128,128]{1,0:T(8,128)(2,1)} %bitcast.13, bf16[128,128]{1,0:T(8,128)(2,1)} %bitcast.15), custom_call_target="tpu_custom_call" | custom-call | flops 150994944 | bytes 2424832 | tf_op jit(solution)/shard_map/pallas_call | solution.py:293
  3.1 0.0 collective-permute-done.mate_cot_ref
  3.1 1.6 %shard_map.68 = (bf16[128,128]{1,0:T(8,128)(2,1)S(1)}, bf16[256,128]{1,0:T(8,128)(2,1)S(1)}, bf16[128,4608]{1,0:T(8,128)(2,1)S(1)}) custom-call(s32[2]{0:T(128)S(1)} %pad_add_fusion.core_ref, bf16[128,128]{1,0:T(8,128)(2,1)S(1)} %get-tuple-element.30.corner_ref, bf16[128,128]{1,0:T(8,128)(2,1)S(1)} %get-tuple-element.31.cot_t_ref, ...), custom_call_target="tpu_custom_call", output_to_operand_aliasing={{2}: (5, {})} | custom-call | flops 301989888 | bytes 2457608 | tf_op jit(solution)/shard_map/pallas_call | solution.py:293
  4.8 0.0 copy-start.6
  4.8 0.1 collective-permute-start.3
  4.9 7.5 %collective-permute-start.1 = (bf16[256,128]{1,0:T(8,128)(2,1)S(1)}, bf16[256,128]{1,0:T(8,128)(2,1)S(1)}, u32[]{:S(2)}, u32[]{:S(2)}) collective-permute-start(bf16[256,128]{1,0:T(8,128)(2,1)S(1)} %get-tuple-element.34), channel_id=1, source_target_pairs={{0,31},{1,2},{2,1},{3,4},{4,3},{5,6},{6,5},{7,8},{8,7},{9,10},{10,... | collective-permute-start | bytes 196616 | tf_op jit(solution)/shard_map/ppermute | solution.py:320
  12.4 0.0 collective-permute-done.2.far_edge_ref
  12.4 0.0 collective-permute-done.3.far_turned_ref
  12.4 3.1 %shard_map.69 = (bf16[128,128]{1,0:T(8,128)(2,1)S(1)}, bf16[128,128]{1,0:T(8,128)(2,1)S(1)}, bf16[128,4608]{1,0:T(8,128)(2,1)S(1)}, bf16[128,4608]{1,0:T(8,128)(2,1)S(1)}) custom-call(s32[2]{0:T(128)S(1)} %pad_add_fusion.core_ref, bf16[128,128]{1,0:T(8,128)(2,1)S(1)} %get-tuple-element.30.corner_ref, bf16[128,4608]{1,0:T(8,128)(2,1)S(1)} %get-tuple-element.32.edge_ref.e_ref, ...), custom_call_target="tpu_custom_call" | custom-call | flops 603979776 | bytes 4751368 | tf_op jit(solution)/shard_map/pallas_call | solution.py:293
  15.6 0.0 collective-permute-done.1.come_ref
  15.6 2.6 %shard_map.70 = (bf16[256,128]{1,0:T(8,128)(2,1)S(1)}, bf16[256,128]{1,0:T(8,128)(2,1)S(1)}, bf16[256,128]{1,0:T(8,128)(2,1)S(1)}) custom-call(s32[2]{0:T(128)S(1)} %pad_add_fusion.core_ref, bf16[256,128]{1,0:T(8,128)(2,1)S(1)} %collective-permute-done.1.come_ref, bf16[128,128]{1,0:T(8,128)(2,1)S(1)} %get-tuple-element.30.corner_ref, ...), custom_call_target="tpu_custom_call" | custom-call | flops 603979776 | bytes 4882440 | tf_op jit(solution)/shard_map/pallas_call | solution.py:293
  18.2 0.0 copy-start.1
  18.2 0.1 collective-permute-start.4
  18.3 5.8 %collective-permute-start.5 = (bf16[256,128]{1,0:T(8,128)(2,1)S(1)}, bf16[256,128]{1,0:T(8,128)(2,1)S(1)}, u32[]{:S(2)}, u32[]{:S(2)}) collective-permute-start(bf16[256,128]{1,0:T(8,128)(2,1)S(1)} %get-tuple-element.42), channel_id=1, source_target_pairs={{0,1},{1,0},{2,3},{3,2},{4,5},{5,4},{6,7},{7,6},{8,9},{9,8},{10,11... | collective-permute-start | bytes 196616 | tf_op jit(solution)/shard_map/ppermute | solution.py:320
  24.1 2.1 %collective-permute-done.4.come_ref.r1_ref = bf16[256,128]{1,0:T(8,128)(2,1)S(1)} collective-permute-done((bf16[256,128]{1,0:T(8,128)(2,1)S(1)}, bf16[256,128]{1,0:T(8,128)(2,1)S(1)}, u32[]{:S(2)}, u32[]{:S(2)}) %collective-permute-start.4) | collective-permute-done | bytes 65568 | tf_op jit(solution)/shard_map/ppermute | solution.py:320
  26.1 0.0 collective-permute-done.5.m1_ref
  26.1 4.3 %shard_map.71 = (bf16[256,128]{1,0:T(8,128)(2,1)S(1)}, bf16[256,128]{1,0:T(8,128)(2,1)S(1)}) custom-call(s32[2]{0:T(128)S(1)} %pad_add_fusion.core_ref, bf16[256,128]{1,0:T(8,128)(2,1)S(1)} %collective-permute-done.4.come_ref.r1_ref, bf16[128,4608]{1,0:T(8,128)(2,1)S(1)} %get-tuple-element.32.edge_ref.e_ref, ...), custom_call_target="tpu_custom_call" | custom-call | flops 1207959552 | bytes 4849672 | tf_op jit(solution)/shard_map/pallas_call | solution.py:293
  30.5 0.1 collective-permute-start.7
  30.6 0.1 collective-permute-start.6
  30.7 1.1 %collective-permute-done.7.m2_ref = bf16[256,128]{1,0:T(8,128)(2,1)S(1)} collective-permute-done((bf16[256,128]{1,0:T(8,128)(2,1)S(1)}, bf16[256,128]{1,0:T(8,128)(2,1)S(1)}, u32[]{:S(2)}, u32[]{:S(2)}) %collective-permute-start.7) | collective-permute-done | bytes 65568 | tf_op jit(solution)/shard_map/ppermute | solution.py:320
  31.8 0.0 copy-done.2
  31.8 2.8 %shard_map.72.after_ref.early_ref = f32[128,4608]{1,0:T(8,128)S(1)} custom-call(s32[2]{0:T(128)S(1)} %pad_add_fusion.core_ref, bf16[256,128]{1,0:T(8,128)(2,1)S(1)} %get-tuple-element.40.v_ref, bf16[256,128]{1,0:T(8,128)(2,1)S(1)} %collective-permute-done.4.come_ref.r1_ref, bf16[256,128]{1,0:T(8,128)(2,1)S(1)} %collective-permute-done.5.m1_ref, ...), custom_call_target="tpu_custom_call" | custom-call | flops 905969664 | bytes 1441800 | tf_op jit(solution)/shard_map/pallas_call | solution.py:293
  34.6 0.0 copy-done.5
  34.6 3.9 %collective-permute-done.6.value_ref = bf16[256,128]{1,0:T(8,128)(2,1)S(1)} collective-permute-done((bf16[256,128]{1,0:T(8,128)(2,1)S(1)}, bf16[256,128]{1,0:T(8,128)(2,1)S(1)}, u32[]{:S(2)}, u32[]{:S(2)}) %collective-permute-start.6) | collective-permute-done | bytes 65568 | tf_op jit(solution)/shard_map/ppermute | solution.py:320
  38.5 0.1 collective-permute-start.8
  38.6 0.0 copy-done.6
  38.7 2.4 %shard_map.74.sum_ref = f32[128,4608]{1,0:T(8,128)S(1)} custom-call(s32[2]{0:T(128)S(1)} %pad_add_fusion.core_ref, bf16[256,128]{1,0:T(8,128)(2,1)S(1)} %shard_map.73.r2_ref, bf16[256,128]{1,0:T(8,128)(2,1)S(1)} %collective-permute-done.5.m1_ref, bf16[128,128]{1,0:T(8,128)(2,1)S(1)} %get-tuple-element.45.last_ref, ...), custom_call_target="tpu_custom_call", output_to_operand_aliasing={{}: (5, {})} | custom-call | flops 603979776 | bytes 3702792 | tf_op jit(solution)/shard_map/pallas_call | solution.py:293
  41.1 0.0 collective-permute-done.8.m3_ref
  41.1 3.8 %shard_map.75 = (bf16[128,128]{1,0:T(8,128)(2,1)}, bf16[16,4608]{1,0:T(8,128)(2,1)}, bf16[16,4608]{1,0:T(8,128)(2,1)}, bf16[16,4608]{1,0:T(8,128)(2,1)}, bf16[16...) custom-call(s32[2]{0:T(128)S(1)} %pad_add_fusion.core_ref, ...), custom_call_target="tpu_custom_call" | custom-call | flops 603979776 | bytes 6029320 | tf_op jit(solution)/shard_map/pallas_call | solution.py:293
  44.9 0.8 %collective-permute-start.9 = (bf16[16,4608]{1,0:T(8,128)(2,1)}, bf16[16,4608]{1,0:T(8,128)(2,1)S(1)}, u32[]{:S(2)}, u32[]{:S(2)}) collective-permute-start(bf16[16,4608]{1,0:T(8,128)(2,1)} %get-tuple-element.50), channel_id=1, source_target_pairs={{0,32},{32,0},{64,96},{96,64},{128,160},{160,128},{192,224},{224,1... | collective-permute-start | bytes 442376 | tf_op jit(solution)/shard_map/ppermute | solution.py:365
  45.8 0.9 %collective-permute-start.10 = (bf16[16,4608]{1,0:T(8,128)(2,1)}, bf16[16,4608]{1,0:T(8,128)(2,1)S(1)}, u32[]{:S(2)}, u32[]{:S(2)}) collective-permute-start(bf16[16,4608]{1,0:T(8,128)(2,1)} %get-tuple-element.51), channel_id=1, source_target_pairs={{0,64},{32,96},{64,0},{96,32},{128,192},{160,224},{192,128},{224,1... | collective-permute-start | bytes 442376 | tf_op jit(solution)/shard_map/ppermute | solution.py:365
  46.7 3.0 %collective-permute-start.11 = (bf16[16,4608]{1,0:T(8,128)(2,1)}, bf16[16,4608]{1,0:T(8,128)(2,1)S(1)}, u32[]{:S(2)}, u32[]{:S(2)}) collective-permute-start(bf16[16,4608]{1,0:T(8,128)(2,1)} %get-tuple-element.52), channel_id=1, source_target_pairs={{0,96},{32,64},{64,32},{96,0},{128,224},{160,192},{192,160},{224,1... | collective-permute-start | bytes 442376 | tf_op jit(solution)/shard_map/ppermute | solution.py:365
  49.7 1.4 %collective-permute-start.12 = (bf16[16,4608]{1,0:T(8,128)(2,1)}, bf16[16,4608]{1,0:T(8,128)(2,1)S(1)}, u32[]{:S(2)}, u32[]{:S(2)}) collective-permute-start(bf16[16,4608]{1,0:T(8,128)(2,1)} %get-tuple-element.53), channel_id=1, source_target_pairs={{0,128},{32,160},{64,192},{96,224},{128,0},{160,32},{192,64},{224,... | collective-permute-start | bytes 442376 | tf_op jit(solution)/shard_map/ppermute | solution.py:365
  51.2 0.0 collective-permute-start.13
  51.2 0.7 collective-permute-done.9.refs_1_
  51.9 2.1 %collective-permute-start.14 = (bf16[16,4608]{1,0:T(8,128)(2,1)}, bf16[16,4608]{1,0:T(8,128)(2,1)S(1)}, u32[]{:S(2)}, u32[]{:S(2)}) collective-permute-start(bf16[16,4608]{1,0:T(8,128)(2,1)} %get-tuple-element.55), channel_id=1, source_target_pairs={{0,192},{32,224},{64,128},{96,160},{128,64},{160,96},{192,0},{224,... | collective-permute-start | bytes 442376 | tf_op jit(solution)/shard_map/ppermute | solution.py:365
  54.0 0.7 %collective-permute-done.10.refs_2_ = bf16[16,4608]{1,0:T(8,128)(2,1)S(1)} collective-permute-done((bf16[16,4608]{1,0:T(8,128)(2,1)}, bf16[16,4608]{1,0:T(8,128)(2,1)S(1)}, u32[]{:S(2)}, u32[]{:S(2)}) %collective-permute-start.10) | collective-permute-done | bytes 147488 | tf_op jit(solution)/shard_map/ppermute | solution.py:365
  54.7 9.3 %collective-permute-start.15 = (bf16[16,4608]{1,0:T(8,128)(2,1)}, bf16[16,4608]{1,0:T(8,128)(2,1)S(1)}, u32[]{:S(2)}, u32[]{:S(2)}) collective-permute-start(bf16[16,4608]{1,0:T(8,128)(2,1)} %get-tuple-element.56), channel_id=1, source_target_pairs={{0,224},{32,192},{64,160},{96,128},{128,96},{160,64},{192,32},{224... | collective-permute-start | bytes 442376 | tf_op jit(solution)/shard_map/ppermute | solution.py:365
  64.1 7.6 %shard_map.76 = (bf16[128,4608]{1,0:T(8,128)(2,1)}, bf16[128,128]{1,0:T(8,128)(2,1)}) custom-call(s32[2]{0:T(128)S(1)} %pad_add_fusion.core_ref, bf16[256,128]{1,0:T(8,128)(2,1)} %copy-done.1, bf16[256,128]{1,0:T(8,128)(2,1)} %copy-done.2, bf16[256,128]{1,0:T(8,128)(2,1)} %copy-done.3, bf16[128,128]{1,0:T(8,128)(2,1)} %get-tuple-element.46.near_ref, ...), custom_call_target="tpu_custom_call" | custom-call | flops 2113929216 | bytes 2752520 | tf_op jit(solution)/shard_map/pallas_call | solution.py:293
  71.6 0.0 collective-permute-done.11.refs_3_
  71.6 0.0 collective-permute-done.12.refs_4_
  71.6 0.0 collective-permute-done.13.refs_5_
  71.7 0.0 collective-permute-done.14.refs_6_
  71.7 0.0 collective-permute-done.15.refs_7_
  71.7 0.9 %shard_map.77 = f32[576,128]{1,0:T(8,128)} custom-call(bf16[16,4608]{1,0:T(8,128)(2,1)S(1)} %copy-done.4, bf16[16,4608]{1,0:T(8,128)(2,1)S(1)} %collective-permute-done.9.refs_1_, bf16[16,4608]{1,0:T(8,128)(2,1)S(1)} %collective-permute-done.10.refs_2_, bf16[16,4608]{1,0:T(8,128)(2,1)S(1)} %collective-permute-done.11.refs_3_, ...), custom_call_target="tpu_custom_call" | custom-call | flops 150994944 | bytes 1179648 | tf_op jit(solution)/shard_map/pallas_call | solution.py:293
  (10 shorter events, 0.0 us)
Async XLA Ops:
  0.6 2.5 %collective-permute-start = (bf16[128,128]{1,0:T(8,128)(2,1)}, bf16[128,128]{1,0:T(8,128)(2,1)S(1)}, u32[]{:S(2)}, u32[]{:S(2)}) collective-permute-start(bf16[128,128]{1,0:T(8,128)(2,1)} %bitcast.14), channel_id=1, source_target_pairs={{0,1},{1,0},{2,3},{3,2},{4,5},{5,4},{6,7},{7,6},{8,9},{9,8},{10,11... | collective-permute-start | bytes 98312 | tf_op jit(solution)/shard_map/ppermute | solution.py:320
  0.7 11.7 %collective-permute-start.2 = (bf16[128,4608]{1,0:T(8,128)(2,1)}, bf16[128,4608]{1,0:T(8,128)(2,1)S(1)}, u32[]{:S(2)}, u32[]{:S(2)}) collective-permute-start(bf16[128,4608]{1,0:T(8,128)(2,1)} %bitcast.10), channel_id=1, source_target_pairs={{0,1},{1,0},{2,3},{3,2},{4,5},{5,4},{6,7},{7,6},{8,9},{9,8},{10,11... | collective-permute-start | bytes 3538952 | tf_op jit(solution)/shard_map/ppermute | solution.py:320
  4.8 33.8 %copy-start.6 = (bf16[128,128]{1,0:T(8,128)(2,1)}, bf16[128,128]{1,0:T(8,128)(2,1)S(1)}, u32[]{:S(2)}) copy-start(bf16[128,128]{1,0:T(8,128)(2,1)S(1)} %get-tuple-element.45.last_ref) | copy-start | bytes 98308
  4.8 7.6 %collective-permute-start.3 = (bf16[128,4608]{1,0:T(8,128)(2,1)S(1)}, bf16[128,4608]{1,0:T(8,128)(2,1)S(1)}, u32[]{:S(2)}, u32[]{:S(2)}) collective-permute-start(bf16[128,4608]{1,0:T(8,128)(2,1)S(1)} %get-tuple-element.35.t_ref.turned_ref), channel_id=1, source_target_pairs={{0,1},{1,0},{2,3},{3,2},{4,5},{5,4},{6,7},{7,6},{8,9},{9,8},{10,11... | collective-permute-start | bytes 3538952 | tf_op jit(solution)/shard_map/ppermute | solution.py:320
  4.9 10.6 %collective-permute-start.1 = (bf16[256,128]{1,0:T(8,128)(2,1)S(1)}, bf16[256,128]{1,0:T(8,128)(2,1)S(1)}, u32[]{:S(2)}, u32[]{:S(2)}) collective-permute-start(bf16[256,128]{1,0:T(8,128)(2,1)S(1)} %get-tuple-element.34), channel_id=1, source_target_pairs={{0,31},{1,2},{2,1},{3,4},{4,3},{5,6},{6,5},{7,8},{8,7},{9,10},{10,... | collective-permute-start | bytes 196616 | tf_op jit(solution)/shard_map/ppermute | solution.py:320
  18.2 22.9 %copy-start.1 = (bf16[256,128]{1,0:T(8,128)(2,1)}, bf16[256,128]{1,0:T(8,128)(2,1)S(1)}, u32[]{:S(2)}) copy-start(bf16[256,128]{1,0:T(8,128)(2,1)S(1)} %get-tuple-element.40.v_ref) | copy-start | bytes 196612
  18.2 8.0 %collective-permute-start.4 = (bf16[256,128]{1,0:T(8,128)(2,1)S(1)}, bf16[256,128]{1,0:T(8,128)(2,1)S(1)}, u32[]{:S(2)}, u32[]{:S(2)}) collective-permute-start(bf16[256,128]{1,0:T(8,128)(2,1)S(1)} %get-tuple-element.41), channel_id=1, source_target_pairs={{0,2},{1,31},{2,4},{3,1},{4,6},{5,3},{6,8},{7,5},{8,10},{9,7},{10,... | collective-permute-start | bytes 196616 | tf_op jit(solution)/shard_map/ppermute | solution.py:320
  18.3 7.9 %collective-permute-start.5 = (bf16[256,128]{1,0:T(8,128)(2,1)S(1)}, bf16[256,128]{1,0:T(8,128)(2,1)S(1)}, u32[]{:S(2)}, u32[]{:S(2)}) collective-permute-start(bf16[256,128]{1,0:T(8,128)(2,1)S(1)} %get-tuple-element.42), channel_id=1, source_target_pairs={{0,1},{1,0},{2,3},{3,2},{4,5},{5,4},{6,7},{7,6},{8,9},{9,8},{10,11... | collective-permute-start | bytes 196616 | tf_op jit(solution)/shard_map/ppermute | solution.py:320
  26.1 5.7 %copy-start.2 = (bf16[256,128]{1,0:T(8,128)(2,1)}, bf16[256,128]{1,0:T(8,128)(2,1)S(1)}, u32[]{:S(2)}) copy-start(bf16[256,128]{1,0:T(8,128)(2,1)S(1)} %collective-permute-done.4.come_ref.r1_ref) | copy-start | bytes 196612
  26.1 12.5 %copy-start = (bf16[256,128]{1,0:T(8,128)(2,1)}, bf16[256,128]{1,0:T(8,128)(2,1)S(1)}, u32[]{:S(2)}) copy-start(bf16[256,128]{1,0:T(8,128)(2,1)S(1)} %collective-permute-done.5.m1_ref) | copy-start | bytes 196612
  30.5 1.3 %collective-permute-start.7 = (bf16[256,128]{1,0:T(8,128)(2,1)S(1)}, bf16[256,128]{1,0:T(8,128)(2,1)S(1)}, u32[]{:S(2)}, u32[]{:S(2)}) collective-permute-start(bf16[256,128]{1,0:T(8,128)(2,1)S(1)} %get-tuple-element.44), channel_id=1, source_target_pairs={{0,1},{1,0},{2,3},{3,2},{4,5},{5,4},{6,7},{7,6},{8,9},{9,8},{10,11... | collective-permute-start | bytes 196616 | tf_op jit(solution)/shard_map/ppermute | solution.py:320
  30.6 8.0 %collective-permute-start.6 = (bf16[256,128]{1,0:T(8,128)(2,1)S(1)}, bf16[256,128]{1,0:T(8,128)(2,1)S(1)}, u32[]{:S(2)}, u32[]{:S(2)}) collective-permute-start(bf16[256,128]{1,0:T(8,128)(2,1)S(1)} %get-tuple-element.43), channel_id=1, source_target_pairs={{0,2},{1,31},{2,4},{3,1},{4,6},{5,3},{6,8},{7,5},{8,10},{9,7},{10,... | collective-permute-start | bytes 196616 | tf_op jit(solution)/shard_map/ppermute | solution.py:320
  31.8 2.8 %copy-start.5 = (bf16[256,128]{1,0:T(8,128)(2,1)}, bf16[256,128]{1,0:T(8,128)(2,1)S(1)}, u32[]{:S(2)}) copy-start(bf16[256,128]{1,0:T(8,128)(2,1)S(1)} %collective-permute-done.7.m2_ref) | copy-start | bytes 196612
  38.5 2.5 %copy-start.3 = (bf16[256,128]{1,0:T(8,128)(2,1)}, bf16[256,128]{1,0:T(8,128)(2,1)S(1)}, u32[]{:S(2)}) copy-start(bf16[256,128]{1,0:T(8,128)(2,1)S(1)} %shard_map.73.r2_ref) | copy-start | bytes 196612
  38.5 2.6 %collective-permute-start.8 = (bf16[256,128]{1,0:T(8,128)(2,1)S(1)}, bf16[256,128]{1,0:T(8,128)(2,1)S(1)}, u32[]{:S(2)}, u32[]{:S(2)}) collective-permute-start(bf16[256,128]{1,0:T(8,128)(2,1)S(1)} %shard_map.73.r2_ref), channel_id=1, source_target_pairs={{0,1},{1,0},{2,3},{3,2},{4,5},{5,4},{6,7},{7,6},{8,9},{9,8},{10,11... | collective-permute-start | bytes 196616 | tf_op jit(solution)/shard_map/ppermute | solution.py:320
  44.9 6.9 %collective-permute-start.9 = (bf16[16,4608]{1,0:T(8,128)(2,1)}, bf16[16,4608]{1,0:T(8,128)(2,1)S(1)}, u32[]{:S(2)}, u32[]{:S(2)}) collective-permute-start(bf16[16,4608]{1,0:T(8,128)(2,1)} %get-tuple-element.50), channel_id=1, source_target_pairs={{0,32},{32,0},{64,96},{96,64},{128,160},{160,128},{192,224},{224,1... | collective-permute-start | bytes 442376 | tf_op jit(solution)/shard_map/ppermute | solution.py:365
  45.8 9.0 %collective-permute-start.10 = (bf16[16,4608]{1,0:T(8,128)(2,1)}, bf16[16,4608]{1,0:T(8,128)(2,1)S(1)}, u32[]{:S(2)}, u32[]{:S(2)}) collective-permute-start(bf16[16,4608]{1,0:T(8,128)(2,1)} %get-tuple-element.51), channel_id=1, source_target_pairs={{0,64},{32,96},{64,0},{96,32},{128,192},{160,224},{192,128},{224,1... | collective-permute-start | bytes 442376 | tf_op jit(solution)/shard_map/ppermute | solution.py:365
  46.7 24.9 %collective-permute-start.11 = (bf16[16,4608]{1,0:T(8,128)(2,1)}, bf16[16,4608]{1,0:T(8,128)(2,1)S(1)}, u32[]{:S(2)}, u32[]{:S(2)}) collective-permute-start(bf16[16,4608]{1,0:T(8,128)(2,1)} %get-tuple-element.52), channel_id=1, source_target_pairs={{0,96},{32,64},{64,32},{96,0},{128,224},{160,192},{192,160},{224,1... | collective-permute-start | bytes 442376 | tf_op jit(solution)/shard_map/ppermute | solution.py:365
  49.7 21.9 %collective-permute-start.12 = (bf16[16,4608]{1,0:T(8,128)(2,1)}, bf16[16,4608]{1,0:T(8,128)(2,1)S(1)}, u32[]{:S(2)}, u32[]{:S(2)}) collective-permute-start(bf16[16,4608]{1,0:T(8,128)(2,1)} %get-tuple-element.53), channel_id=1, source_target_pairs={{0,128},{32,160},{64,192},{96,224},{128,0},{160,32},{192,64},{224,... | collective-permute-start | bytes 442376 | tf_op jit(solution)/shard_map/ppermute | solution.py:365
  51.2 20.5 %collective-permute-start.13 = (bf16[16,4608]{1,0:T(8,128)(2,1)}, bf16[16,4608]{1,0:T(8,128)(2,1)S(1)}, u32[]{:S(2)}, u32[]{:S(2)}) collective-permute-start(bf16[16,4608]{1,0:T(8,128)(2,1)} %get-tuple-element.54), channel_id=1, source_target_pairs={{0,160},{32,128},{64,224},{96,192},{128,32},{160,0},{192,96},{224,... | collective-permute-start | bytes 442376 | tf_op jit(solution)/shard_map/ppermute | solution.py:365
  51.9 19.8 %collective-permute-start.14 = (bf16[16,4608]{1,0:T(8,128)(2,1)}, bf16[16,4608]{1,0:T(8,128)(2,1)S(1)}, u32[]{:S(2)}, u32[]{:S(2)}) collective-permute-start(bf16[16,4608]{1,0:T(8,128)(2,1)} %get-tuple-element.55), channel_id=1, source_target_pairs={{0,192},{32,224},{64,128},{96,160},{128,64},{160,96},{192,0},{224,... | collective-permute-start | bytes 442376 | tf_op jit(solution)/shard_map/ppermute | solution.py:365
  54.7 16.9 %collective-permute-start.15 = (bf16[16,4608]{1,0:T(8,128)(2,1)}, bf16[16,4608]{1,0:T(8,128)(2,1)S(1)}, u32[]{:S(2)}, u32[]{:S(2)}) collective-permute-start(bf16[16,4608]{1,0:T(8,128)(2,1)} %get-tuple-element.56), channel_id=1, source_target_pairs={{0,224},{32,192},{64,160},{96,128},{128,96},{160,64},{192,32},{224... | collective-permute-start | bytes 442376 | tf_op jit(solution)/shard_map/ppermute | solution.py:365
  64.1 7.6 %copy-start.4 = (bf16[16,4608]{1,0:T(8,128)(2,1)S(1)}, bf16[16,4608]{1,0:T(8,128)(2,1)}, u32[]{:S(2)}) copy-start(bf16[16,4608]{1,0:T(8,128)(2,1)} %get-tuple-element.49.refs_0_) | copy-start | bytes 442372

commit v11 on v8

--- a/solution.py
+++ b/solution.py
@@ -62,10 +62,15 @@
     cot_t_ref[...] = cot_vmem[...].astype(F32).T.astype(BF)
 
 
-def own_kernel(core_ref, corner_ref, cot_t_ref, mate_cot_ref, edge_ref, turned_ref, last_ref, send_ref, same_ref):
-    @pl.when(core_ref[0] == 0)
-    def _():
-        last = mate_cot_ref[...].astype(F32).T.astype(BF)
+def own_kernel(
+    core_ref, corner_ref, cot_t_ref, mate_cot_ref, edge_ref, turned_ref, last_ref, send_ref, same_ref, mate_ref, sem
+):
+    @pl.when(core_ref[0] == 0)
+    def _():
+        copy = pltpu.make_async_copy(mate_cot_ref, mate_ref, sem.at[0])
+        copy.start()
+        copy.wait()
+        last = mate_ref[...].astype(F32).T.astype(BF)
         last_ref[...] = last
         send_ref[:W, :] = cot_t_ref[...]
         send_ref[W:, :] = step(last, turned_ref, edge_ref)
@@ -331,7 +336,8 @@
         scratch=[((width, W), BF), ((width, W), F32), ((W, W), BF)], sems=(4, 3), flops=unit, far=(0, 1, 2, 3),
     )
     u0, first, turned = call(
-        own_kernel, [one, two, whole], core, corner, cot_t, mate_cot, edge, turned, flops=2 * unit, alias={5: 2}
+        own_kernel, [one, two, whole], core, corner, cot_t, mate_cot, edge, turned,
+        scratch=[one], sems=(1,), flops=2 * unit, free=(3,), alias={5: 2},
     )
     r0 = send(first, lambda i: i - 1 if i % 2 == 0 else i + 1)
     far_turned = swap(turned)

time: 66.2 us -> 66.2 us (level)
  starting transfers between devices: 24.5 us -> 25.3 us
  Pallas kernels: 26.1 us -> 25.4 us
    pallas_call x11, Pallas kernels: 26.1 us -> 25.4 us  [call(): pl.pallas_call(kernel, out_shape=outs[0] if single else outs, in_specs=in...]
    ppermute x9, starting transfers between devices: 20.3 us -> 21 us  [send(): return lax.ppermute(value, 'col', pairs)]
  transfers between devices with their start and end apart: 10 -> 10, of which waited for: 4 -> 4; matrix products, arithmetic and copies ran while one was open for 0% -> 0% of each run, Pallas kernels for 23% -> 22%
where the time goes in v11:
time: 66.2 us; the launch traced here: 65.9 us
  Pallas kernels  25.4 us (38%)
  starting transfers between devices  25.3 us (38%)
  waiting for transfers between devices  14.4 us (22%)
  between operations  0.79 us (1%)
    pallas_call x11, Pallas kernels, call(): pl.pallas_call(kernel, out_shape=outs[0] if single else outs, in_specs=in...  25.4 us
    ppermute x9, starting transfers between devices, send(): return lax.ppermute(value, 'col', pairs)  21 us
    all_to_all x1, waiting for transfers between devices, shards(): lax.all_to_all(done.reshape(rows, share, width), 'row', 0, 0, tiled=True)  9.38 us
    ppermute x9, waiting for transfers between devices, send(): return lax.ppermute(value, 'col', pairs)  5.01 us
    all_to_all x1, starting transfers between devices, shards(): lax.all_to_all(done.reshape(rows, share, width), 'row', 0, 0, tiled=True)  4.24 us
  transfers between devices with their start and end apart: 10, of which 4 were waited for; matrix products, arithmetic and copies ran while one was open for 0% of the time, Pallas kernels for 22%

profile of v11, /device:TPU:1, one launch (start us, length us, event | category | flops | bytes accessed | tf_op | source)
XLA Modules:
  0.0 65.9 jit_solution(6037025626095233160)
XLA Ops:
  0.6 3.3 %collective-permute-start = (bf16[128,128]{1,0:T(8,128)(2,1)}, bf16[128,128]{1,0:T(8,128)(2,1)}, u32[]{:S(2)}, u32[]{:S(2)}) collective-permute-start(bf16[128,128]{1,0:T(8,128)(2,1)} %bitcast.15), channel_id=1, source_target_pairs={{0,1},{1,0},{2,3},{3,2},{4,5},{5,4},{6,7},{7,6},{8,9},{9,8},{10,11... | collective-permute-start | bytes 98312 | tf_op jit(solution)/shard_map/ppermute | solution.py:318
  4.0 0.1 collective-permute-start.2
  4.1 1.8 %shard_map.67 = (bf16[128,4608]{1,0:T(8,128)(2,1)S(1)}, bf16[128,4608]{1,0:T(8,128)(2,1)S(1)}, bf16[128,128]{1,0:T(8,128)(2,1)S(1)}, bf16[128,128]{1,0:T(8,128)(2,1)S(1)}) custom-call(bf16[4608,128]{1,0:T(8,128)(2,1)} %bitcast.9, bf16[128,4608]{1,0:T(8,128)(2,1)} %bitcast.11, bf16[128,128]{1,0:T(8,128)(2,1)} %bitcast.14, bf16[128,128]{1,0:T(8,128)(2,1)} %bitcast.16), custom_call_target="tpu_custom_call" | custom-call | flops 150994944 | bytes 2424832 | tf_op jit(solution)/shard_map/pallas_call | solution.py:292
  5.9 0.0 collective-permute-done.mate_cot_ref
  5.9 1.1 %shard_map.68 = (bf16[128,128]{1,0:T(8,128)(2,1)S(1)}, bf16[256,128]{1,0:T(8,128)(2,1)S(1)}, bf16[128,4608]{1,0:T(8,128)(2,1)S(1)}) custom-call(s32[1]{0:T(128)} %bitcast.core_ref, bf16[128,128]{1,0:T(8,128)(2,1)S(1)} %get-tuple-element.23.corner_ref, bf16[128,128]{1,0:T(8,128)(2,1)S(1)} %get-tuple-element.24.cot_t_ref, ...), custom_call_target="tpu_custom_call", output_to_operand_aliasing={{2}: (5, {})} | custom-call | flops 301989888 | bytes 2457604 | tf_op jit(solution)/shard_map/pallas_call | solution.py:292
  7.0 0.0 copy-start.5
  7.0 1.3 %collective-permute-start.3 = (bf16[128,4608]{1,0:T(8,128)(2,1)S(1)}, bf16[128,4608]{1,0:T(8,128)(2,1)S(1)}, u32[]{:S(2)}, u32[]{:S(2)}) collective-permute-start(bf16[128,4608]{1,0:T(8,128)(2,1)S(1)} %get-tuple-element.28.t_ref.turned_ref), channel_id=1, source_target_pairs={{0,1},{1,0},{2,3},{3,2},{4,5},{5,4},{6,7},{7,6},{8,9},{9,8},{10,11... | collective-permute-start | bytes 3538952 | tf_op jit(solution)/shard_map/ppermute | solution.py:318
  8.3 1.0 %collective-permute-start.1 = (bf16[256,128]{1,0:T(8,128)(2,1)S(1)}, bf16[256,128]{1,0:T(8,128)(2,1)S(1)}, u32[]{:S(2)}, u32[]{:S(2)}) collective-permute-start(bf16[256,128]{1,0:T(8,128)(2,1)S(1)} %get-tuple-element.27), channel_id=1, source_target_pairs={{0,31},{1,2},{2,1},{3,4},{4,3},{5,6},{6,5},{7,8},{8,7},{9,10},{10,... | collective-permute-start | bytes 196616 | tf_op jit(solution)/shard_map/ppermute | solution.py:318
  9.3 0.0 collective-permute-done.2.far_edge_ref
  9.3 1.5 %collective-permute-done.3.far_turned_ref = bf16[128,4608]{1,0:T(8,128)(2,1)S(1)} collective-permute-done((bf16[128,4608]{1,0:T(8,128)(2,1)S(1)}, bf16[128,4608]{1,0:T(8,128)(2,1)S(1)}, u32[]{:S(2)}, u32[]{:S(2)}) %collective-permute-start.3) | collective-permute-done | bytes 1179680 | tf_op jit(solution)/shard_map/ppermute | solution.py:318
  10.8 0.5 shard_map.69
  11.3 2.2 %collective-permute-done.1.come_ref = bf16[256,128]{1,0:T(8,128)(2,1)S(1)} collective-permute-done((bf16[256,128]{1,0:T(8,128)(2,1)S(1)}, bf16[256,128]{1,0:T(8,128)(2,1)S(1)}, u32[]{:S(2)}, u32[]{:S(2)}) %collective-permute-start.1) | collective-permute-done | bytes 65568 | tf_op jit(solution)/shard_map/ppermute | solution.py:318
  13.5 3.5 %shard_map.70 = (bf16[256,128]{1,0:T(8,128)(2,1)S(1)}, bf16[256,128]{1,0:T(8,128)(2,1)S(1)}, bf16[256,128]{1,0:T(8,128)(2,1)S(1)}) custom-call(s32[1]{0:T(128)} %bitcast.core_ref, bf16[256,128]{1,0:T(8,128)(2,1)S(1)} %collective-permute-done.1.come_ref, bf16[128,128]{1,0:T(8,128)(2,1)S(1)} %get-tuple-element.23.corner_ref, ...), custom_call_target="tpu_custom_call" | custom-call | flops 603979776 | bytes 4882436 | tf_op jit(solution)/shard_map/pallas_call | solution.py:292
  17.0 0.0 copy-start.1
  17.0 8.5 %collective-permute-start.4 = (bf16[256,128]{1,0:T(8,128)(2,1)S(1)}, bf16[256,128]{1,0:T(8,128)(2,1)S(1)}, u32[]{:S(2)}, u32[]{:S(2)}) collective-permute-start(bf16[256,128]{1,0:T(8,128)(2,1)S(1)} %get-tuple-element.34), channel_id=1, source_target_pairs={{0,2},{1,31},{2,4},{3,1},{4,6},{5,3},{6,8},{7,5},{8,10},{9,7},{10,... | collective-permute-start | bytes 196616 | tf_op jit(solution)/shard_map/ppermute | solution.py:318
  25.5 0.0 collective-permute-start.5
  25.5 1.3 %collective-permute-done.4.come_ref.r1_ref = bf16[256,128]{1,0:T(8,128)(2,1)S(1)} collective-permute-done((bf16[256,128]{1,0:T(8,128)(2,1)S(1)}, bf16[256,128]{1,0:T(8,128)(2,1)S(1)}, u32[]{:S(2)}, u32[]{:S(2)}) %collective-permute-start.4) | collective-permute-done | bytes 65568 | tf_op jit(solution)/shard_map/ppermute | solution.py:318
  26.9 0.0 copy-start.2
  26.9 0.0 collective-permute-done.5.m1_ref
  26.9 0.0 copy-start
  26.9 3.5 %shard_map.71 = (bf16[256,128]{1,0:T(8,128)(2,1)S(1)}, bf16[256,128]{1,0:T(8,128)(2,1)S(1)}) custom-call(s32[1]{0:T(128)} %bitcast.core_ref, bf16[256,128]{1,0:T(8,128)(2,1)S(1)} %collective-permute-done.4.come_ref.r1_ref, bf16[128,4608]{1,0:T(8,128)(2,1)S(1)} %get-tuple-element.25.edge_ref.e_ref, bf16[128,4608]{1,0:T(8,128)(2,1)S(1)} %get-tuple-element.28.t_ref.turned_ref, ...), custom_call_target="tpu_custom_call" | custom-call | flops 1207959552 | bytes 4849668 | tf_op jit(solution)/shard_map/pallas_call | solution.py:292
  30.4 1.0 %collective-permute-start.7 = (bf16[256,128]{1,0:T(8,128)(2,1)S(1)}, bf16[256,128]{1,0:T(8,128)(2,1)S(1)}, u32[]{:S(2)}, u32[]{:S(2)}) collective-permute-start(bf16[256,128]{1,0:T(8,128)(2,1)S(1)} %get-tuple-element.37), channel_id=1, source_target_pairs={{0,1},{1,0},{2,3},{3,2},{4,5},{5,4},{6,7},{7,6},{8,9},{9,8},{10,11... | collective-permute-start | bytes 196616 | tf_op jit(solution)/shard_map/ppermute | solution.py:318
  31.4 4.7 %collective-permute-start.6 = (bf16[256,128]{1,0:T(8,128)(2,1)S(1)}, bf16[256,128]{1,0:T(8,128)(2,1)S(1)}, u32[]{:S(2)}, u32[]{:S(2)}) collective-permute-start(bf16[256,128]{1,0:T(8,128)(2,1)S(1)} %get-tuple-element.36), channel_id=1, source_target_pairs={{0,2},{1,31},{2,4},{3,1},{4,6},{5,3},{6,8},{7,5},{8,10},{9,7},{10,... | collective-permute-start | bytes 196616 | tf_op jit(solution)/shard_map/ppermute | solution.py:318
  36.2 0.0 collective-permute-done.7.m2_ref
  36.2 0.0 copy-start.4
  36.2 0.0 copy-done.2
  36.2 2.2 %shard_map.72.after_ref.early_ref = f32[128,4608]{1,0:T(8,128)S(1)} custom-call(s32[1]{0:T(128)} %bitcast.core_ref, bf16[256,128]{1,0:T(8,128)(2,1)S(1)} %get-tuple-element.33.v_ref, bf16[256,128]{1,0:T(8,128)(2,1)S(1)} %collective-permute-done.4.come_ref.r1_ref, bf16[256,128]{1,0:T(8,128)(2,1)S(1)} %collective-permute-done.5.m1_ref, ...), custom_call_target="tpu_custom_call" | custom-call | flops 905969664 | bytes 1441796 | tf_op jit(solution)/shard_map/pallas_call | solution.py:292
  38.4 0.0 copy-done.4
  38.4 0.0 collective-permute-done.6.value_ref
  38.4 0.0 copy-start.3
  38.4 1.1 %collective-permute-start.8 = (bf16[256,128]{1,0:T(8,128)(2,1)S(1)}, bf16[256,128]{1,0:T(8,128)(2,1)S(1)}, u32[]{:S(2)}, u32[]{:S(2)}) collective-permute-start(bf16[256,128]{1,0:T(8,128)(2,1)S(1)} %shard_map.73.r2_ref), channel_id=1, source_target_pairs={{0,1},{1,0},{2,3},{3,2},{4,5},{5,4},{6,7},{7,6},{8,9},{9,8},{10,11... | collective-permute-start | bytes 196616 | tf_op jit(solution)/shard_map/ppermute | solution.py:318
  39.5 0.0 copy-done.5
  39.5 0.0 copy-done
  39.5 1.8 %shard_map.74.sum_ref = f32[128,4608]{1,0:T(8,128)S(1)} custom-call(s32[1]{0:T(128)} %bitcast.core_ref, bf16[256,128]{1,0:T(8,128)(2,1)S(1)} %shard_map.73.r2_ref, bf16[256,128]{1,0:T(8,128)(2,1)S(1)} %collective-permute-done.5.m1_ref, bf16[128,128]{1,0:T(8,128)(2,1)S(1)} %get-tuple-element.38.last_ref, ...), custom_call_target="tpu_custom_call", output_to_operand_aliasing={{}: (5, {})} | custom-call | flops 603979776 | bytes 3702788 | tf_op jit(solution)/shard_map/pallas_call | solution.py:292
  41.3 0.0 copy-done.3
  41.4 0.0 collective-permute-done.8.m3_ref
  41.4 0.0 copy-done.1
  41.4 3.0 %shard_map.75 = (bf16[128,128]{1,0:T(8,128)(2,1)}, bf16[128,4608]{1,0:T(8,128)(2,1)}) custom-call(s32[1]{0:T(128)} %bitcast.core_ref, bf16[256,128]{1,0:T(8,128)(2,1)S(1)} %get-tuple-element.33.v_ref, bf16[256,128]{1,0:T(8,128)(2,1)S(1)} %collective-permute-done.8.m3_ref, bf16[128,4608]{1,0:T(8,128)(2,1)S(1)} %get-tuple-element.25.edge_ref.e_ref, ...), custom_call_target="tpu_custom_call" | custom-call | flops 603979776 | bytes 6029316 | tf_op jit(solution)/shard_map/pallas_call | solution.py:292
  44.4 4.2 %all-to-all-start = ((bf16[8,16,4608]{2,1,0:T(8,128)(2,1)}), bf16[8,16,4608]{2,1,0:T(8,128)(2,1)S(1)}, u32[]{:S(2)}, u32[]{:S(2)}) async-start(bf16[8,16,4608]{2,1,0:T(8,128)(2,1)} %bitcast.12), calls=%async_computation | async-start | bytes 2359296 | tf_op jit(solution)/shard_map/all_to_all | solution.py:364
  48.6 7.0 %shard_map.76 = (bf16[128,4608]{1,0:T(8,128)(2,1)}, bf16[128,128]{1,0:T(8,128)(2,1)}) custom-call(s32[1]{0:T(128)} %bitcast.core_ref, bf16[256,128]{1,0:T(8,128)(2,1)} %copy-done.1, bf16[256,128]{1,0:T(8,128)(2,1)} %copy-done.2, bf16[256,128]{1,0:T(8,128)(2,1)} %copy-done.3, bf16[128,128]{1,0:T(8,128)(2,1)} %get-tuple-element.39.near_ref, ...), custom_call_target="tpu_custom_call" | custom-call | flops 2113929216 | bytes 2752516 | tf_op jit(solution)/shard_map/pallas_call | solution.py:292
  55.6 9.4 %all-to-all-done.parts_ref = bf16[8,16,4608]{2,1,0:T(8,128)(2,1)S(1)} async-done(((bf16[8,16,4608]{2,1,0:T(8,128)(2,1)}), bf16[8,16,4608]{2,1,0:T(8,128)(2,1)S(1)}, u32[]{:S(2)}, u32[]{:S(2)}) %all-to-all-start) | async-done | bytes 1179680 | tf_op jit(solution)/shard_map/all_to_all | solution.py:364
  65.0 0.9 %shard_map.77 = f32[576,128]{1,0:T(8,128)} custom-call(bf16[8,16,4608]{2,1,0:T(8,128)(2,1)S(1)} %all-to-all-done.parts_ref), custom_call_target="tpu_custom_call" | custom-call | flops 150994944 | bytes 1179648 | tf_op jit(solution)/shard_map/pallas_call | solution.py:292
  (1 shorter events, 0.0 us)
Async XLA Ops:
  0.6 5.3 %collective-permute-start = (bf16[128,128]{1,0:T(8,128)(2,1)}, bf16[128,128]{1,0:T(8,128)(2,1)}, u32[]{:S(2)}, u32[]{:S(2)}) collective-permute-start(bf16[128,128]{1,0:T(8,128)(2,1)} %bitcast.15), channel_id=1, source_target_pairs={{0,1},{1,0},{2,3},{3,2},{4,5},{5,4},{6,7},{7,6},{8,9},{9,8},{10,11... | collective-permute-start | bytes 98312 | tf_op jit(solution)/shard_map/ppermute | solution.py:318
  4.0 5.3 %collective-permute-start.2 = (bf16[128,4608]{1,0:T(8,128)(2,1)}, bf16[128,4608]{1,0:T(8,128)(2,1)S(1)}, u32[]{:S(2)}, u32[]{:S(2)}) collective-permute-start(bf16[128,4608]{1,0:T(8,128)(2,1)} %bitcast.10), channel_id=1, source_target_pairs={{0,1},{1,0},{2,3},{3,2},{4,5},{5,4},{6,7},{7,6},{8,9},{9,8},{10,11... | collective-permute-start | bytes 3538952 | tf_op jit(solution)/shard_map/ppermute | solution.py:318
  7.0 32.5 %copy-start.5 = (bf16[128,128]{1,0:T(8,128)(2,1)}, bf16[128,128]{1,0:T(8,128)(2,1)S(1)}, u32[]{:S(2)}) copy-start(bf16[128,128]{1,0:T(8,128)(2,1)S(1)} %get-tuple-element.38.last_ref) | copy-start | bytes 98308
  7.0 3.8 %collective-permute-start.3 = (bf16[128,4608]{1,0:T(8,128)(2,1)S(1)}, bf16[128,4608]{1,0:T(8,128)(2,1)S(1)}, u32[]{:S(2)}, u32[]{:S(2)}) collective-permute-start(bf16[128,4608]{1,0:T(8,128)(2,1)S(1)} %get-tuple-element.28.t_ref.turned_ref), channel_id=1, source_target_pairs={{0,1},{1,0},{2,3},{3,2},{4,5},{5,4},{6,7},{7,6},{8,9},{9,8},{10,11... | collective-permute-start | bytes 3538952 | tf_op jit(solution)/shard_map/ppermute | solution.py:318
  8.3 5.2 %collective-permute-start.1 = (bf16[256,128]{1,0:T(8,128)(2,1)S(1)}, bf16[256,128]{1,0:T(8,128)(2,1)S(1)}, u32[]{:S(2)}, u32[]{:S(2)}) collective-permute-start(bf16[256,128]{1,0:T(8,128)(2,1)S(1)} %get-tuple-element.27), channel_id=1, source_target_pairs={{0,31},{1,2},{2,1},{3,4},{4,3},{5,6},{6,5},{7,8},{8,7},{9,10},{10,... | collective-permute-start | bytes 196616 | tf_op jit(solution)/shard_map/ppermute | solution.py:318
  17.0 24.3 %copy-start.1 = (bf16[256,128]{1,0:T(8,128)(2,1)}, bf16[256,128]{1,0:T(8,128)(2,1)S(1)}, u32[]{:S(2)}) copy-start(bf16[256,128]{1,0:T(8,128)(2,1)S(1)} %get-tuple-element.33.v_ref) | copy-start | bytes 196612
  17.0 9.8 %collective-permute-start.4 = (bf16[256,128]{1,0:T(8,128)(2,1)S(1)}, bf16[256,128]{1,0:T(8,128)(2,1)S(1)}, u32[]{:S(2)}, u32[]{:S(2)}) collective-permute-start(bf16[256,128]{1,0:T(8,128)(2,1)S(1)} %get-tuple-element.34), channel_id=1, source_target_pairs={{0,2},{1,31},{2,4},{3,1},{4,6},{5,3},{6,8},{7,5},{8,10},{9,7},{10,... | collective-permute-start | bytes 196616 | tf_op jit(solution)/shard_map/ppermute | solution.py:318
  25.5 1.3 %collective-permute-start.5 = (bf16[256,128]{1,0:T(8,128)(2,1)S(1)}, bf16[256,128]{1,0:T(8,128)(2,1)S(1)}, u32[]{:S(2)}, u32[]{:S(2)}) collective-permute-start(bf16[256,128]{1,0:T(8,128)(2,1)S(1)} %get-tuple-element.35), channel_id=1, source_target_pairs={{0,1},{1,0},{2,3},{3,2},{4,5},{5,4},{6,7},{7,6},{8,9},{9,8},{10,11... | collective-permute-start | bytes 196616 | tf_op jit(solution)/shard_map/ppermute | solution.py:318
  26.9 9.3 %copy-start.2 = (bf16[256,128]{1,0:T(8,128)(2,1)}, bf16[256,128]{1,0:T(8,128)(2,1)S(1)}, u32[]{:S(2)}) copy-start(bf16[256,128]{1,0:T(8,128)(2,1)S(1)} %collective-permute-done.4.come_ref.r1_ref) | copy-start | bytes 196612
  26.9 12.6 %copy-start = (bf16[256,128]{1,0:T(8,128)(2,1)}, bf16[256,128]{1,0:T(8,128)(2,1)S(1)}, u32[]{:S(2)}) copy-start(bf16[256,128]{1,0:T(8,128)(2,1)S(1)} %collective-permute-done.5.m1_ref) | copy-start | bytes 196612
  30.4 5.8 %collective-permute-start.7 = (bf16[256,128]{1,0:T(8,128)(2,1)S(1)}, bf16[256,128]{1,0:T(8,128)(2,1)S(1)}, u32[]{:S(2)}, u32[]{:S(2)}) collective-permute-start(bf16[256,128]{1,0:T(8,128)(2,1)S(1)} %get-tuple-element.37), channel_id=1, source_target_pairs={{0,1},{1,0},{2,3},{3,2},{4,5},{5,4},{6,7},{7,6},{8,9},{9,8},{10,11... | collective-permute-start | bytes 196616 | tf_op jit(solution)/shard_map/ppermute | solution.py:318
  31.4 7.0 %collective-permute-start.6 = (bf16[256,128]{1,0:T(8,128)(2,1)S(1)}, bf16[256,128]{1,0:T(8,128)(2,1)S(1)}, u32[]{:S(2)}, u32[]{:S(2)}) collective-permute-start(bf16[256,128]{1,0:T(8,128)(2,1)S(1)} %get-tuple-element.36), channel_id=1, source_target_pairs={{0,2},{1,31},{2,4},{3,1},{4,6},{5,3},{6,8},{7,5},{8,10},{9,7},{10,... | collective-permute-start | bytes 196616 | tf_op jit(solution)/shard_map/ppermute | solution.py:318
  36.2 2.2 %copy-start.4 = (bf16[256,128]{1,0:T(8,128)(2,1)}, bf16[256,128]{1,0:T(8,128)(2,1)S(1)}, u32[]{:S(2)}) copy-start(bf16[256,128]{1,0:T(8,128)(2,1)S(1)} %collective-permute-done.7.m2_ref) | copy-start | bytes 196612
  38.4 2.9 %copy-start.3 = (bf16[256,128]{1,0:T(8,128)(2,1)}, bf16[256,128]{1,0:T(8,128)(2,1)S(1)}, u32[]{:S(2)}) copy-start(bf16[256,128]{1,0:T(8,128)(2,1)S(1)} %shard_map.73.r2_ref) | copy-start | bytes 196612
  38.4 2.9 %collective-permute-start.8 = (bf16[256,128]{1,0:T(8,128)(2,1)S(1)}, bf16[256,128]{1,0:T(8,128)(2,1)S(1)}, u32[]{:S(2)}, u32[]{:S(2)}) collective-permute-start(bf16[256,128]{1,0:T(8,128)(2,1)S(1)} %shard_map.73.r2_ref), channel_id=1, source_target_pairs={{0,1},{1,0},{2,3},{3,2},{4,5},{5,4},{6,7},{7,6},{8,9},{9,8},{10,11... | collective-permute-start | bytes 196616 | tf_op jit(solution)/shard_map/ppermute | solution.py:318
  44.4 20.6 %all-to-all-start = ((bf16[8,16,4608]{2,1,0:T(8,128)(2,1)}), bf16[8,16,4608]{2,1,0:T(8,128)(2,1)S(1)}, u32[]{:S(2)}, u32[]{:S(2)}) async-start(bf16[8,16,4608]{2,1,0:T(8,128)(2,1)} %bitcast.12), calls=%async_computation | async-start | bytes 2359296 | tf_op jit(solution)/shard_map/all_to_all | solution.py:364
